TPU v7x, 32 devices: a whole 2x2x4 slice. The times are simulated.
32 devices in a mesh: groups: 2 (over y), row: 8 (over z, core), col: 2 (over x).
Axes of the slice: x: 2, y: 2, z: 4, core: 2. Of those that a mesh axis runs over, the one named last changes fastest.
Arguments:
- pair_rep: bfloat16 [192, 96, 128], P(('groups', 'row'), 'col'), parts along dimension 0, may hold values from -6 to 6
- token_mask: int32 [192], P('groups'), parts along dimension 0, may hold values 0 or 1
- out_project: bfloat16 [128, 512], replicated, may hold values from -0.5 to 0.5
- out_gating: bfloat16 [128, 128], replicated, may hold values from -0.5 to 0.5
- out_final: bfloat16 [128, 128], replicated, may hold values from -0.5 to 0.5
- in_project: bfloat16 [128, 512], replicated, may hold values from -0.5 to 0.5
- in_gating: bfloat16 [128, 128], replicated, may hold values from -0.5 to 0.5
- in_final: bfloat16 [128, 128], replicated, may hold values from -0.5 to 0.5
Outputs:
- updated_pair: bfloat16 [192, 96, 128], P(('groups', 'row'), 'col'), parts along dimension 0
There are 2 independent parts, one for each index of `groups`. A program takes and returns all parts, laid end to end along the dimension named above; an argument that names none is the same for every part. Nothing has to cross between parts.
All inputs are finite; a program needn't handle non-finite values.
Results may differ from a plain program's by a relative error of at most 0.012.
Values may be sent and summed in bfloat16 or wider, within the bound.
No kernel may reach another device: no remote copies, remote signals or barrier semaphores. Data moves between devices by JAX's collectives and lax.ppermute only.
A program may use at most 64 MiB of HBM per device.

v0:
```python
import jax
import jax.numpy as jnp
from jax import lax
from jax.sharding import PartitionSpec as P


def layer_norm(values):
    center = jnp.mean(values, axis=-1, keepdims=True)
    spread = jnp.mean((values - center) ** 2, axis=-1, keepdims=True)
    return (values - center) / jnp.sqrt(spread + 1e-05)


def project(pair_block, row_weights, col_weights, w_project, w_gating):
    hidden = w_project.shape[1] // 4
    normed = layer_norm(pair_block.astype(jnp.float32)).astype(jnp.bfloat16)
    projected = jnp.dot(normed, w_project, preferred_element_type=jnp.float32)
    pair_mask = (row_weights[:, None] * col_weights[None, :])[:, :, None]
    left_proj = (
        pair_mask * jax.nn.sigmoid(projected[..., hidden : 2 * hidden]) * projected[..., :hidden]
    ).astype(jnp.bfloat16)
    right_proj = (
        pair_mask
        * jax.nn.sigmoid(projected[..., 3 * hidden :])
        * projected[..., 2 * hidden : 3 * hidden]
    ).astype(jnp.bfloat16)
    gate_value = jax.nn.sigmoid(jnp.dot(normed, w_gating, preferred_element_type=jnp.float32))
    return (left_proj, right_proj, gate_value)


def finish(pair_block, gate_value, product, w_final):
    mixed_rows = layer_norm(product).astype(jnp.bfloat16)
    return (
        pair_block.astype(jnp.float32)
        + gate_value * jnp.dot(mixed_rows, w_final, preferred_element_type=jnp.float32)
    ).astype(jnp.bfloat16)


def on_device(
    pair_rep, token_mask, out_project, out_gating, out_final, in_project, in_gating, in_final
):
    row_count = pair_rep.shape[0]
    col_count = pair_rep.shape[1]
    mask_values = token_mask.astype(jnp.float32)
    row_weights = lax.dynamic_slice_in_dim(
        mask_values, lax.axis_index("row") * row_count, row_count, 0
    )
    col_weights = lax.dynamic_slice_in_dim(
        mask_values, lax.axis_index("col") * col_count, col_count, 0
    )
    left_proj, right_proj, gate_value = project(
        pair_rep, row_weights, col_weights, out_project, out_gating
    )
    col_panel = lax.all_gather(right_proj, "row", axis=0, tiled=True)
    row_panel = lax.all_gather(left_proj, "col", axis=1, tiled=True)
    mirrored = lax.all_to_all(col_panel, "col", split_axis=0, concat_axis=1, tiled=True)
    product = jnp.einsum("ikc,jkc->ijc", row_panel, mirrored, preferred_element_type=jnp.float32)
    first_pass = finish(pair_rep, gate_value, product, out_final)
    left_next, right_next, gate_next = project(
        first_pass, row_weights, col_weights, in_project, in_gating
    )
    row_panel_next = lax.all_gather(left_next, "col", axis=1, tiled=True)
    column_left = lax.all_to_all(row_panel_next, "row", split_axis=1, concat_axis=0, tiled=True)
    product_next = jnp.einsum(
        "kic,kjc->ijc",
        column_left,
        lax.all_gather(right_next, "row", axis=0, tiled=True),
        preferred_element_type=jnp.float32,
    )
    return finish(first_pass, gate_next, product_next, in_final)


def solution(mesh):
    return jax.shard_map(
        on_device,
        mesh=mesh,
        in_specs=(P(("groups", "row"), "col", None), P("groups"), P(), P(), P(), P(), P(), P()),
        out_specs=P(("groups", "row"), "col", None),
        check_vma=False,
    )
```

profile of v0, /device:TPU:0, one launch (start us, length us, event | category | flops | bytes accessed | tf_op | source)
XLA Modules:
  0.0 112.4 jit_solution(3461679144124965293)
XLA Ops:
  6.5 0.7 convert_element_type.43
  7.4 1.1 convert_reduce_fusion
  8.5 1.2 %fusion.15 = f32[12,48]{1,0:T(8,128)S(1)} fusion(bf16[12,48,128]{2,1,0:T(8,128)(2,1)} %param.8, f32[12,48]{1,0:T(8,128)S(1)} %broadcast_multiply_fusion.4), kind=kLoop, calls=%fused_computation.27 | loop fusion | flops 294336 | bytes 152064 | tf_op jit(solution)/shard_map/reduce_sum | solution.py:9
  9.7 1.3 %fusion.39 = f32[12,48,512]{2,1,0:T(8,128)S(1)} fusion(bf16[128,512]{1,0:T(8,128)(2,1)S(1)} %copy-done, bf16[12,48,128]{2,1,0:T(8,128)(2,1)} %param.8, f32[12,48]{1,0:T(8,128)S(1)} %add_sqrt_fusion.3, f32[12,48]{1,0:T(8,128)S(1)} %broadcast_multiply_fusion.4), kind=kOutput, calls=%fused_computation.61 | convolution fusion | flops 75792384 | bytes 1462784 | tf_op jit(solution)/shard_map/dot_general | solution.py:16
  11.0 0.9 fusion.27
  11.9 25.5 %all-gather.3.cloned.1.call-done = bf16[96,48,128]{2,1,0:T(8,128)(2,1)} async-done(((bf16[12,48,128]{2,1,0:T(8,128)(2,1)}), bf16[96,48,128]{2,1,0:T(8,128)(2,1)}) %all-gather.3.cloned.1.call-update) | async-done | bytes 1179664 | tf_op jit(solution)/shard_map/all_gather | solution.py:53
  37.4 3.6 %all-to-all-start = ((bf16[96,48,128]{2,1,0:T(8,128)(2,1)}), bf16[96,48,128]{2,1,0:T(8,128)(2,1)S(1)}, u32[]{:S(2)}, u32[]{:S(2)}) async-start(bf16[96,48,128]{2,1,0:T(8,128)(2,1)} %all-gather.3.cloned.1.call-done), calls=%async_computation | async-start | bytes 2359296 | tf_op jit(solution)/shard_map/all_to_all | solution.py:55
  41.1 18.7 %all_gather.13 = bf16[12,96,128]{2,1,0:T(8,128)(2,1)S(1)} all-gather(bf16[12,48,128]{2,1,0:T(8,128)(2,1)S(1)} %get-tuple-element.7), channel_id=1, replica_groups=mesh['groups'=2,'row'=8,'col'=2] {'col'}, dimensions={1}, use_global_device_ids=true | all-gather | bytes 442368 | tf_op jit(solution)/shard_map/all_gather | solution.py:54
  59.8 0.4 copy.34
  60.3 1.1 fusion.7
  61.5 1.0 copy.33
  62.5 0.9 fusion.47
  63.8 0.6 copy-done.5
  65.5 0.9 fusion.17
  66.4 5.8 %all_gather.15 = bf16[12,96,128]{2,1,0:T(8,128)(2,1)S(1)} all-gather(bf16[12,48,128]{2,1,0:T(8,128)(2,1)S(1)} %get-tuple-element.5), channel_id=1, replica_groups=mesh['groups'=2,'row'=8,'col'=2] {'col'}, dimensions={1}, use_global_device_ids=true | all-gather | bytes 442368 | tf_op jit(solution)/shard_map/all_gather | solution.py:61
  72.2 0.9 copy.36
  73.1 3.5 %all-to-all-start.1 = ((bf16[12,96,128]{2,0,1:T(8,128)(2,1)}), bf16[12,96,128]{2,0,1:T(8,128)(2,1)S(1)}, u32[]{:S(2)}, u32[]{:S(2)}) async-start(bf16[12,96,128]{2,0,1:T(8,128)(2,1)} %copy.36), calls=%async_computation.1 | async-start | bytes 786432 | tf_op jit(solution)/shard_map/all_to_all | solution.py:62
  76.6 1.1 fusion.4
  77.7 17.3 %all-to-all-done.1 = bf16[12,96,128]{2,0,1:T(8,128)(2,1)S(1)} async-done(((bf16[12,96,128]{2,0,1:T(8,128)(2,1)}), bf16[12,96,128]{2,0,1:T(8,128)(2,1)S(1)}, u32[]{:S(2)}, u32[]{:S(2)}) %all-to-all-start.1) | async-done | bytes 294944 | tf_op jit(solution)/shard_map/all_to_all | solution.py:62
  95.1 1.2 %copy.40 = bf16[96,12,128]{0,1,2:T(8,128)(2,1)} copy(bf16[96,12,128]{2,0,1:T(8,128)(2,1)S(1)} %all_to_all.33) | data formatting | bytes 589824 | tf_op jit(solution)/shard_map/all_to_all | solution.py:62
  96.3 5.3 %copy.39 = bf16[96,48,128]{1,0,2:T(8,128)(2,1)S(1)} copy(bf16[96,48,128]{2,1,0:T(8,128)(2,1)} %all-gather.5.cloned.1.call-done) | data formatting | bytes 2359296 | tf_op jit(solution)/shard_map/all_gather | solution.py:66
  101.6 2.0 %fusion.49 = (f32[12,48]{1,0:T(8,128)S(1)}, f32[12,48,128]{1,0,2:T(8,128)S(1)}) fusion(bf16[96,48,128]{1,0,2:T(8,128)(2,1)S(1)} %copy.39, bf16[96,12,128]{0,1,2:T(8,128)(2,1)} %copy.40), kind=kOutput, calls=%fused_computation.78 | convolution fusion | flops 14228928 | bytes 1771776 | tf_op jit(solution)/shard_map/kic,kjc->ijc/dot_general | solution.py:63
  104.0 0.6 copy-done.2
  104.7 0.9 fusion.10
  (51 shorter events, 2.3 us)
Async XLA Ops:
  6.5 3.2 %copy-start = (bf16[128,512]{1,0:T(8,128)(2,1)S(1)}, bf16[128,512]{1,0:T(8,128)(2,1)}, u32[]{:S(2)}) copy-start(bf16[128,512]{1,0:T(8,128)(2,1)} %param.10) | copy-start | bytes 393220
  6.5 30.9 %all-gather.3.cloned.1.call-start = ((), (), s32[]{:S(2)}) async-start(), calls=%async_computation.2 | async-start | bytes 1327104 | tf_op jit(solution)/shard_map/all_gather | solution.py:53
  9.7 2.1 %copy-start.7 = (f32[12,48]{1,0:T(8,128)}, f32[12,48]{1,0:T(8,128)S(1)}, u32[]{:S(2)}) copy-start(f32[12,48]{1,0:T(8,128)S(1)} %broadcast_multiply_fusion) | copy-start | bytes 6916
  37.4 24.0 %all-to-all-start = ((bf16[96,48,128]{2,1,0:T(8,128)(2,1)}), bf16[96,48,128]{2,1,0:T(8,128)(2,1)S(1)}, u32[]{:S(2)}, u32[]{:S(2)}) async-start(bf16[96,48,128]{2,1,0:T(8,128)(2,1)} %all-gather.3.cloned.1.call-done), calls=%async_computation | async-start | bytes 2359296 | tf_op jit(solution)/shard_map/all_to_all | solution.py:55
  41.0 19.3 %copy-start.3 = (bf16[12,48,128]{2,1,0:T(8,128)(2,1)S(1)}, bf16[12,48,128]{2,1,0:T(8,128)(2,1)}, u32[]{:S(2)}) copy-start(bf16[12,48,128]{2,1,0:T(8,128)(2,1)} %param.8) | copy-start | bytes 442372
  41.0 19.3 %copy-start.11 = (bf16[128,128]{1,0:T(8,128)(2,1)S(1)}, bf16[128,128]{1,0:T(8,128)(2,1)}, u32[]{:S(2)}) copy-start(bf16[128,128]{1,0:T(8,128)(2,1)} %param.11) | copy-start | bytes 98308
  41.1 55.3 %all-gather.5.cloned.1.call-start = ((), (), s32[]{:S(2)}) async-start(), calls=%async_computation.3 | async-start | bytes 1327104 | tf_op jit(solution)/shard_map/all_gather | solution.py:66
  63.4 1.0 copy-start.5
  63.5 1.0 copy-start.9
  63.7 1.4 %copy-start.6 = (bf16[128,512]{1,0:T(8,128)(2,1)S(1)}, bf16[128,512]{1,0:T(8,128)(2,1)}, u32[]{:S(2)}) copy-start(bf16[128,512]{1,0:T(8,128)(2,1)} %param.13) | copy-start | bytes 393220
  64.8 11.8 %copy-start.1 = (f32[12,48,128]{2,1,0:T(8,128)}, f32[12,48,128]{2,1,0:T(8,128)S(1)}, u32[]{:S(2)}) copy-start(f32[12,48,128]{2,1,0:T(8,128)S(1)} %get-tuple-element.12) | copy-start | bytes 884740
  64.8 0.7 copy-start.8
  66.4 10.2 %copy-start.12 = (bf16[128,128]{1,0:T(8,128)(2,1)S(1)}, bf16[128,128]{1,0:T(8,128)(2,1)}, u32[]{:S(2)}) copy-start(bf16[128,128]{1,0:T(8,128)(2,1)} %param.14) | copy-start | bytes 98308
  73.1 21.9 %all-to-all-start.1 = ((bf16[12,96,128]{2,0,1:T(8,128)(2,1)}), bf16[12,96,128]{2,0,1:T(8,128)(2,1)S(1)}, u32[]{:S(2)}, u32[]{:S(2)}) async-start(bf16[12,96,128]{2,0,1:T(8,128)(2,1)} %copy.36), calls=%async_computation.1 | async-start | bytes 786432 | tf_op jit(solution)/shard_map/all_to_all | solution.py:62
  103.6 1.0 copy-start.2
  103.6 1.1 copy-start.4
  103.6 1.1 copy-start.10
Sparse Core Ops, SparseCore 0:
  12.0 25.3 all-gather.2
  66.5 28.9 all-gather.4
where the time goes:
time: 113 us; the launch traced here: 112 us
  waiting for transfers between devices  42.8 us (38%)
  blocking collectives  24.6 us (22%)
  between operations  13.7 us (12%)
  local copies, waits for them, and re-layouts  10.5 us (9%)
  matrix products  8.03 us (7%)
  starting transfers between devices  7.11 us (6%)
  other arithmetic  5.69 us (5%)
    all_gather x1, waiting for transfers between devices, on_device(): col_panel = lax.all_gather(right_proj, 'row', axis=0, tiled=True)  25.5 us
    all_gather x1, blocking collectives, on_device(): row_panel = lax.all_gather(left_proj, 'col', axis=1, tiled=True)  18.7 us
    all_to_all x1, waiting for transfers between devices, on_device(): lax.all_to_all(row_panel_next, 'row', split_axis=1, concat_axis=0, tiled=...  17.3 us
    all_gather x1, blocking collectives, on_device(): row_panel_next = lax.all_gather(left_next, 'col', axis=1, tiled=True)  5.84 us
    all_gather x1, local copies, waits for them, and re-layouts, on_device(): lax.all_gather(right_next, 'row', axis=0, tiled=True)  5.29 us
    all_to_all x1, starting transfers between devices, on_device(): lax.all_to_all(col_panel, 'col', split_axis=0, concat_axis=1, tiled=True)  3.6 us
    all_to_all x1, starting transfers between devices, on_device(): lax.all_to_all(row_panel_next, 'row', split_axis=1, concat_axis=0, tiled=...  3.47 us
  transfers between devices with their start and end apart: 4, of which 2 were waited for; matrix products, arithmetic and copies ran while one was open for 4% of the time, Pallas kernels for 0%

commit v1 on v0

v1 whole, which is shorter than its diff:
```python
import functools

import jax
import jax.numpy as jnp
from jax import lax
from jax.experimental import pallas as pl
from jax.experimental.pallas import tpu as pltpu
from jax.sharding import PartitionSpec as P

F32, BF16 = jnp.float32, jnp.bfloat16
VMEM = pl.BlockSpec(memory_space=pltpu.VMEM)
LIMIT = 40 * 1024 * 1024


def call(kernel, outs, args, scratch=(), flops=10_000_000, name=None):
    single = not isinstance(outs, (list, tuple))
    outs = [outs] if single else list(outs)
    moved = sum(a.size * a.dtype.itemsize for a in args) + sum(
        o.size * o.dtype.itemsize for o in outs
    )
    result = pl.pallas_call(
        kernel,
        out_shape=outs,
        in_specs=[VMEM] * len(args),
        out_specs=[VMEM] * len(outs),
        scratch_shapes=list(scratch),
        compiler_params=pltpu.CompilerParams(vmem_limit_bytes=LIMIT),
        cost_estimate=pl.CostEstimate(flops=flops, bytes_accessed=moved, transcendentals=0),
        name=name,
    )(*args)
    return result[0] if single else result


def shape(dims, dtype):
    return jax.ShapeDtypeStruct(dims, dtype)


def sigmoid(v):
    return 0.5 * jnp.tanh(0.5 * v) + 0.5


def layer_norm(v):
    center = jnp.mean(v, axis=-1, keepdims=True)
    shifted = v - center
    spread = jnp.mean(shifted * shifted, axis=-1, keepdims=True)
    return shifted * lax.rsqrt(spread + 1e-05)


def place():
    row = lax.axis_index("row")
    return row // 2, row % 2, lax.axis_index("col")


def token_weights(mask_row, start, count):
    tokens = mask_row.shape[1]
    lane = lax.broadcasted_iota(jnp.int32, (count, tokens), 1)
    row = lax.broadcasted_iota(jnp.int32, (count, tokens), 0)
    hot = jnp.where(lane == row + start, mask_row, 0.0).astype(BF16)
    return jnp.dot(hot, jnp.ones((tokens, 128), BF16), preferred_element_type=F32)


def gated(normed, w, mask_ref, rows, cols):
    hidden = w.shape[1] // 2
    projected = jnp.dot(normed, w, preferred_element_type=F32)
    value = sigmoid(projected[:, hidden:]) * projected[:, :hidden]
    mask_row = mask_ref[...].astype(F32)
    row_w = token_weights(mask_row, lax.axis_index("row") * rows, -(-rows // 8) * 8)
    col_w = token_weights(mask_row, lax.axis_index("col") * cols, cols)
    weights = row_w[:rows, None, :] * col_w[None, :, :]
    return value * weights.reshape(rows * cols, 128)


def right_kernel(half, pair_ref, mask_ref, w_ref, right_ref):
    rows, cols, chan = pair_ref.shape
    normed = layer_norm(pair_ref[...].astype(F32)).astype(BF16).reshape(rows * cols, chan)
    width = w_ref.shape[1] // 2
    w = w_ref[:, half * width : (half + 1) * width]
    value = gated(normed, w, mask_ref, rows, cols)
    right_ref[...] = value.astype(BF16).reshape(right_ref.shape)


def gate_kernel(pair_ref, w_ref, gate_ref):
    rows, cols, chan = pair_ref.shape
    normed = layer_norm(pair_ref[...].astype(F32)).astype(BF16).reshape(rows * cols, chan)
    gate = sigmoid(jnp.dot(normed, w_ref[...], preferred_element_type=F32))
    gate_ref[...] = gate.reshape(gate_ref.shape)


def outgoing_kernel(own_left, core_left, *refs):
    rights, (mine_ref, other_ref, r_scr, l_scr) = refs[:-4], refs[-4:]
    rows, cols, chan = own_left.shape
    count = len(rights)
    width = count * rows
    z, _, _ = place()
    low = z % count
    for m, ref in enumerate(rights):
        base = (low ^ m) * rows
        for j in range(rows):
            r_scr[pl.ds(base + j, cols, stride=width), :] = ref[j].astype(F32)
    for out_ref, left in ((mine_ref, own_left), (other_ref, core_left)):
        l_scr[...] = left[...].astype(F32).reshape(rows * cols, chan)

        def step(block, totals):
            for u in range(8):
                k = block * 8 + u
                right = r_scr[pl.ds(pl.multiple_of(k * width, 8), width), :]
                totals = tuple(
                    t + l_scr[pl.ds(i * cols + k, 1), :] * right for i, t in enumerate(totals)
                )
            return totals

        zero = jnp.zeros((width, chan), F32)
        totals = lax.fori_loop(0, cols // 8, step, (zero,) * rows)
        for i, t in enumerate(totals):
            out_ref[i] = t.astype(out_ref.dtype)


def first_kernel(cols_n, *refs):
    own, others = refs[0], refs[1 : 2 * cols_n]
    pair_ref, gate_ref, mask_ref, final_ref, w_ref = refs[2 * cols_n : 2 * cols_n + 5]
    first_ref, mine_ref, other_ref, scr, half_scr = refs[2 * cols_n + 5 :]
    rows, cols, chan = pair_ref.shape
    _, core, _ = place()
    same = own[...].astype(F32)
    for ref in others[: cols_n - 1]:
        same = same + ref[...].astype(F32)
    cross = others[cols_n - 1][...].astype(F32)
    for ref in others[cols_n:]:
        cross = cross + ref[...].astype(F32)
    pieces = cols // (2 * rows)
    for value, side in ((same, core), (cross, 1 - core)):
        half_scr[...] = value.reshape(half_scr.shape)
        for i in range(rows):
            for q in range(pieces):
                part = half_scr[pl.ds((i * pieces + q) * rows, rows), :]
                scr[pl.ds(i * cols + (2 * q + side) * rows, rows), :] = part
    mixed = layer_norm(scr[...]).astype(BF16)
    update = jnp.dot(mixed, final_ref[...], preferred_element_type=F32)
    pair = pair_ref[...].astype(F32).reshape(rows * cols, chan)
    first = (pair + gate_ref[...].reshape(rows * cols, chan) * update).astype(BF16)
    first_ref[...] = first.reshape(first_ref.shape)
    normed = layer_norm(first.astype(F32)).astype(BF16)
    w = w_ref[:, : w_ref.shape[1] // 2]
    scr[...] = gated(normed, w, mask_ref, rows, cols)
    for out_ref, side in ((mine_ref, core), (other_ref, 1 - core)):
        for i in range(rows):
            for q in range(pieces):
                part = scr[pl.ds(i * cols + (2 * q + side) * rows, rows), :]
                half_scr[pl.ds((i * pieces + q) * rows, rows), :] = part
        out_ref[...] = half_scr[...].astype(BF16).reshape(out_ref.shape)


def incoming_kernel(cols_n, steps, *refs):
    own_right, core_right = refs[:2]
    lefts = refs[2 : 2 + 2 * cols_n]
    outs = refs[2 + 2 * cols_n : 2 + 2 * cols_n + len(steps)]
    l_scr, r_scr = refs[-2:]
    rows, cols, chan = own_right.shape
    width = lefts[0].shape[1]
    pieces = width // rows
    z, _, x = place()
    for n, ref in enumerate((own_right, core_right)):
        r_scr[pl.ds(n * rows * cols, rows * cols), :] = ref[...].astype(F32).reshape(-1, chan)
    for n, ref in enumerate(lefts):
        l_scr[pl.ds(n * rows * width, rows * width), :] = ref[...].astype(F32).reshape(-1, chan)
    for m, out_ref in zip(steps, outs):
        target = z ^ m
        base = ((target // pieces) ^ x) * (2 * rows * width) + (target % pieces) * rows
        for group in range(0, rows, 6):

            def step(k, totals):
                right = r_scr[pl.ds(pl.multiple_of(k * cols, 8), cols), :]
                return tuple(
                    t + l_scr[pl.ds(base + k * width + group + i, 1), :] * right
                    for i, t in enumerate(totals)
                )

            zero = jnp.zeros((cols, chan), F32)
            totals = lax.fori_loop(0, 2 * rows, step, (zero,) * 6, unroll=4)
            for i, t in enumerate(totals):
                out_ref[group + i] = t.astype(out_ref.dtype)


def last_kernel(*refs):
    parts, (first_ref, gate_ref, final_ref, out_ref) = refs[:-4], refs[-4:]
    rows, cols, chan = first_ref.shape
    product = parts[0][...].astype(F32)
    for ref in parts[1:]:
        product = product + ref[...].astype(F32)
    mixed = layer_norm(product).astype(BF16).reshape(rows * cols, chan)
    update = jnp.dot(mixed, final_ref[...], preferred_element_type=F32)
    first = first_ref[...].astype(F32).reshape(rows * cols, chan)
    result = first + gate_ref[...].reshape(rows * cols, chan) * update
    out_ref[...] = result.astype(BF16).reshape(out_ref.shape)


def on_device(
    rows_n,
    cols_n,
    pair_rep,
    token_mask,
    out_project,
    out_gating,
    out_final,
    in_project,
    in_gating,
    in_final,
):
    rows, cols, chan = pair_rep.shape
    chips = rows_n // 2
    pieces = cols // (2 * rows)
    mask = token_mask.reshape(1, -1)
    block = shape((rows, cols, chan), BF16)
    block32 = shape((rows, cols, chan), F32)
    half = (rows, pieces * rows, chan)

    def along_row(v, bits):
        return lax.ppermute(v, "row", [(i, i ^ bits) for i in range(rows_n)])

    def shift(v, dx, core):
        pairs = [
            (r * cols_n + c, (r ^ core) * cols_n + (c ^ dx))
            for r in range(rows_n)
            for c in range(cols_n)
        ]
        return lax.ppermute(v, ("row", "col"), pairs)

    z, _, x = place()
    offset = (z // pieces) ^ x

    project = lambda pair, w, half: call(
        functools.partial(right_kernel, half), block, [pair, mask, w], flops=100_000_000
    )
    right = project(pair_rep, out_project, 1)
    rights = [right] + [None] * (chips - 1)
    for m in reversed(range(1, chips)):
        rights[m] = along_row(right, 2 * m)
    left = project(pair_rep, out_project, 0)
    core_left = along_row(left, 1)
    gate = call(gate_kernel, block32, [pair_rep, out_gating], flops=50_000_000)
    mine, other = [], []
    for h in range(cols_n):
        a, b = call(
            outgoing_kernel,
            [shape(half, F32), shape(half, BF16)],
            [left, core_left] + rights[h * pieces : (h + 1) * pieces],
            scratch=[
                pltpu.VMEM((cols * pieces * rows, chan), F32),
                pltpu.VMEM((rows * cols, chan), F32),
            ],
            flops=500_000_000,
        )
        mine.append(a)
        other.append(b)

    def pick(options, dx):
        return lax.select_n(offset ^ dx, *options)

    same = [pick(mine, 0)]
    for dx in range(1, cols_n):
        same.append(shift(pick(mine, dx).astype(BF16), dx, 0))
    cross = [shift(pick(other, dx), dx, 1) for dx in range(cols_n)]
    first, left_mine, left_other = call(
        functools.partial(first_kernel, cols_n),
        [block, shape(half, BF16), shape(half, BF16)],
        same + cross + [pair_rep, gate, mask, out_final, in_project],
        scratch=[
            pltpu.VMEM((rows * cols, chan), F32),
            pltpu.VMEM((rows * pieces * rows, chan), F32),
        ],
        flops=200_000_000,
    )

    lefts = []
    for dx in range(cols_n):
        lefts.append(left_mine if dx == 0 else shift(left_mine, dx, 0))
        lefts.append(shift(left_other, dx, 1))
    right = project(first, in_project, 1)
    core_right = along_row(right, 1)

    def partial_products(steps):
        return call(
            functools.partial(incoming_kernel, cols_n, steps),
            [block32 if m == 0 else block for m in steps],
            [right, core_right] + lefts,
            scratch=[
                pltpu.VMEM((2 * cols_n * rows * pieces * rows, chan), F32),
                pltpu.VMEM((2 * rows * cols, chan), F32),
            ],
            flops=200_000_000 * len(steps),
        )

    far = list(range(pieces, chips))
    parts = [None] * chips
    for m, value in zip(far, partial_products(far)):
        parts[m] = along_row(value, 2 * m)
    near = list(range(1, pieces))
    for m, value in zip(near, partial_products(near)):
        parts[m] = along_row(value, 2 * m)
    parts[0] = partial_products([0])[0]
    gate = call(gate_kernel, block32, [first, in_gating], flops=50_000_000)
    return call(last_kernel, block, parts + [first, gate, in_final], flops=100_000_000)


def solution(mesh):
    return jax.shard_map(
        functools.partial(on_device, mesh.shape["row"], mesh.shape["col"]),
        mesh=mesh,
        in_specs=(P(("groups", "row"), "col", None), P("groups"), P(), P(), P(), P(), P(), P()),
        out_specs=P(("groups", "row"), "col", None),
        check_vma=False,
    )
```

time: 113 us -> 54.6 us (0.48)
  blocking collectives: 24.6 us -> 0 us
  waiting for transfers between devices: 42.8 us -> 25.9 us
  between operations: 13.7 us -> 0.17 us
  Pallas kernels: 0 us -> 9.12 us
  starting transfers between devices: 7.11 us -> 15.8 us
  matrix products: 8.03 us -> 0 us
  local copies, waits for them, and re-layouts: 10.5 us -> 3.25 us
  other arithmetic: 5.69 us -> 0.06 us
    ppermute x0 -> x14, waiting for transfers between devices: none -> 25.9 us  [the longest x8 17.9 us: along_row(): return lax.ppermute(v, 'row', [(i, i ^ bits) for i in range(rows_n)])]
    all_gather x2 -> x0, waiting for transfers between devices: 25.5 us -> none  [the longest x1 25.5 us: on_device(): col_panel = lax.all_gather(right_proj, 'row', axis=0, tiled=True)]
    all_gather x2 -> x0, blocking collectives: 24.6 us -> none  [the longest x1 18.7 us: on_device(): row_panel = lax.all_gather(left_proj, 'col', axis=1, tiled=True)]
    all_to_all x2 -> x0, waiting for transfers between devices: 17.3 us -> none  [the longest x1 17.3 us: on_device(): lax.all_to_all(row_panel_next, 'row', split_axis=1, concat_axis=0, tiled=...]
    ppermute x0 -> x14, starting transfers between devices: none -> 15.8 us  [the longest x8 11.3 us: along_row(): return lax.ppermute(v, 'row', [(i, i ^ bits) for i in range(rows_n)])]
    pallas_call x0 -> x12, Pallas kernels: none -> 9.12 us  [call(): pl.pallas_call(kernel, out_shape=outs, in_specs=[VMEM] * len(args), out_s...]
    dot_general x8 -> x0, matrix products: 8.03 us -> none  [the longest x2 2.2 us: project(): jnp.dot(normed, w_gating, preferred_element_type=jnp.float32)]
    all_to_all x2 -> x0, starting transfers between devices: 7.07 us -> none  [the longest x1 3.6 us: on_device(): lax.all_to_all(col_panel, 'col', split_axis=0, concat_axis=1, tiled=True)]
  transfers between devices with their start and end apart: 4 -> 14, of which waited for: 2 -> 8; matrix products, arithmetic and copies ran while one was open for 4% -> 0% of each run, Pallas kernels for 0% -> 7%
where the time goes in v1:
time: 54.6 us; the launch traced here: 54.3 us
  waiting for transfers between devices  25.9 us (47%)
  starting transfers between devices  15.8 us (29%)
  Pallas kernels  9.12 us (17%)
  local copies, waits for them, and re-layouts  3.25 us (6%)
    ppermute x8, waiting for transfers between devices, along_row(): return lax.ppermute(v, 'row', [(i, i ^ bits) for i in range(rows_n)])  17.9 us
    ppermute x8, starting transfers between devices, along_row(): return lax.ppermute(v, 'row', [(i, i ^ bits) for i in range(rows_n)])  11.3 us
    pallas_call x12, Pallas kernels, call(): pl.pallas_call(kernel, out_shape=outs, in_specs=[VMEM] * len(args), out_s...  9.12 us
    ppermute x6, waiting for transfers between devices, shift(): return lax.ppermute(v, ('row', 'col'), pairs)  8.01 us
    ppermute x6, starting transfers between devices, shift(): return lax.ppermute(v, ('row', 'col'), pairs)  4.48 us
    unnamed x18, local copies, waits for them, and re-layouts  3.25 us
  transfers between devices with their start and end apart: 14, of which 8 were waited for; matrix products, arithmetic and copies ran while one was open for 0% of the time, Pallas kernels for 7%

profile of v1, /device:TPU:0, one launch (start us, length us, event | category | flops | bytes accessed | tf_op | source)
XLA Modules:
  0.0 54.3 jit_solution(18310633913968015042)
XLA Ops:
  0.7 0.9 %copy-done = bf16[12,48,128]{2,1,0:T(8,128)(2,1)S(1)} copy-done((bf16[12,48,128]{2,1,0:T(8,128)(2,1)S(1)}, bf16[12,48,128]{2,1,0:T(8,128)(2,1)}, u32[]{:S(2)}) %copy-start) | copy-done | bytes 147480
  1.6 0.9 %copy-done.3 = bf16[128,512]{1,0:T(8,128)(2,1)S(1)} copy-done((bf16[128,512]{1,0:T(8,128)(2,1)S(1)}, bf16[128,512]{1,0:T(8,128)(2,1)}, u32[]{:S(2)}) %copy-start.3) | copy-done | bytes 131096
  3.9 2.7 %collective-permute-start.1 = (bf16[12,48,128]{2,1,0:T(8,128)(2,1)S(1)}, bf16[12,48,128]{2,1,0:T(8,128)(2,1)S(1)}, u32[]{:S(2)}, u32[]{:S(2)}) collective-permute-start(bf16[12,48,128]{2,1,0:T(8,128)(2,1)S(1)} %shard_map.83.refs_0_), channel_id=1, source_target_pairs={{0,4},{2,6},{4,0},{6,2},{8,12},{10,14},{12,8},{14,10},{1,5},{3,7},... | collective-permute-start | bytes 442376 | tf_op jit(solution)/shard_map/ppermute | solution.py:218
  6.6 2.6 %collective-permute-start.2 = (bf16[12,48,128]{2,1,0:T(8,128)(2,1)S(1)}, bf16[12,48,128]{2,1,0:T(8,128)(2,1)S(1)}, u32[]{:S(2)}, u32[]{:S(2)}) collective-permute-start(bf16[12,48,128]{2,1,0:T(8,128)(2,1)S(1)} %shard_map.83.refs_0_), channel_id=1, source_target_pairs={{0,8},{2,10},{4,12},{6,14},{8,0},{10,2},{12,4},{14,6},{1,9},{3,11}... | collective-permute-start | bytes 442376 | tf_op jit(solution)/shard_map/ppermute | solution.py:218
  9.2 0.8 %copy-done.6 = bf16[128,128]{1,0:T(8,128)(2,1)S(1)} copy-done((bf16[128,128]{1,0:T(8,128)(2,1)S(1)}, bf16[128,128]{1,0:T(8,128)(2,1)}, u32[]{:S(2)}) %copy-start.6) | copy-done | bytes 32792
  10.3 3.5 %collective-permute-done.1.refs_1_ = bf16[12,48,128]{2,1,0:T(8,128)(2,1)S(1)} collective-permute-done((bf16[12,48,128]{2,1,0:T(8,128)(2,1)S(1)}, bf16[12,48,128]{2,1,0:T(8,128)(2,1)S(1)}, u32[]{:S(2)}, u32[]{:S(2)}) %collective-permute-start.1) | collective-permute-done | bytes 147488 | tf_op jit(solution)/shard_map/ppermute | solution.py:218
  13.8 1.2 %shard_map.84 = (f32[12,24,128]{2,1,0:T(8,128)S(1)}, bf16[12,24,128]{2,1,0:T(8,128)(2,1)S(1)}) custom-call(bf16[12,48,128]{2,1,0:T(8,128)(2,1)S(1)} %shard_map.82.own_left, bf16[12,48,128]{2,1,0:T(8,128)(2,1)S(1)} %collective-permute-done.core_left, bf16[12,48,128]{2,1,0:T(8,128)(2,1)S(1)} %shard_map.83.refs_0_, ...), custom_call_target="tpu_custom_call" | custom-call | flops 500000000 | bytes 811008 | tf_op jit(solution)/shard_map/pallas_call | solution.py:21
  15.0 5.5 %collective-permute-done.2.refs_0_ = bf16[12,48,128]{2,1,0:T(8,128)(2,1)S(1)} collective-permute-done((bf16[12,48,128]{2,1,0:T(8,128)(2,1)S(1)}, bf16[12,48,128]{2,1,0:T(8,128)(2,1)S(1)}, u32[]{:S(2)}, u32[]{:S(2)}) %collective-permute-start.2) | collective-permute-done | bytes 147488 | tf_op jit(solution)/shard_map/ppermute | solution.py:218
  20.5 1.2 %shard_map.85 = (f32[12,24,128]{2,1,0:T(8,128)S(1)}, bf16[12,24,128]{2,1,0:T(8,128)(2,1)S(1)}) custom-call(bf16[12,48,128]{2,1,0:T(8,128)(2,1)S(1)} %shard_map.82.own_left, bf16[12,48,128]{2,1,0:T(8,128)(2,1)S(1)} %collective-permute-done.core_left, bf16[12,48,128]{2,1,0:T(8,128)(2,1)S(1)} %collective-permute-done.2.refs_0_, ...), custom_call_target="tpu_custom_call" | custom-call | flops 500000000 | bytes 811008 | tf_op jit(solution)/shard_map/pallas_call | solution.py:21
  21.8 1.6 %collective-permute-start.6 = (bf16[12,24,128]{2,1,0:T(8,128)(2,1)S(1)}, bf16[12,24,128]{2,1,0:T(8,128)(2,1)S(1)}, u32[]{:S(2)}, u32[]{:S(2)}) collective-permute-start(bf16[12,24,128]{2,1,0:T(8,128)(2,1)S(1)} %get-tuple-element.23), channel_id=1, source_target_pairs={{0,3},{1,2},{2,1},{3,0},{4,7},{5,6},{6,5},{7,4},{8,11},{9,10},{10,... | collective-permute-start | bytes 221192 | tf_op jit(solution)/shard_map/ppermute | solution.py:226
  24.1 1.9 %collective-permute-done.6.refs_3_ = bf16[12,24,128]{2,1,0:T(8,128)(2,1)S(1)} collective-permute-done((bf16[12,24,128]{2,1,0:T(8,128)(2,1)S(1)}, bf16[12,24,128]{2,1,0:T(8,128)(2,1)S(1)}, u32[]{:S(2)}, u32[]{:S(2)}) %collective-permute-start.6) | collective-permute-done | bytes 73760 | tf_op jit(solution)/shard_map/ppermute | solution.py:226
  26.0 2.0 %collective-permute-done.4.refs_1_ = bf16[12,24,128]{2,1,0:T(8,128)(2,1)S(1)} collective-permute-done((bf16[12,24,128]{2,1,0:T(8,128)(2,1)S(1)}, bf16[12,24,128]{2,1,0:T(8,128)(2,1)S(1)}, u32[]{:S(2)}, u32[]{:S(2)}) %collective-permute-start.4) | collective-permute-done | bytes 73760 | tf_op jit(solution)/shard_map/ppermute | solution.py:226
  28.1 0.9 %shard_map.87 = (bf16[12,48,128]{2,1,0:T(8,128)(2,1)S(1)}, bf16[12,24,128]{2,1,0:T(8,128)(2,1)S(1)}, bf16[12,24,128]{2,1,0:T(8,128)(2,1)S(1)}) custom-call(f32[12,24,128]{2,1,0:T(8,128)S(1)} %broadcast_select_fusion.2.refs_0_, bf16[12,24,128]{2,1,0:T(8,128)(2,1)S(1)} %collective-permute-done.4.refs_1_, ...), custom_call_target="tpu_custom_call" | custom-call | flops 200000000 | bytes 1270144 | tf_op jit(solution)/shard_map/pallas_call | solution.py:21
  29.5 1.6 %collective-permute-start.10 = (bf16[12,24,128]{2,1,0:T(8,128)(2,1)S(1)}, bf16[12,24,128]{2,1,0:T(8,128)(2,1)S(1)}, u32[]{:S(2)}, u32[]{:S(2)}) collective-permute-start(bf16[12,24,128]{2,1,0:T(8,128)(2,1)S(1)} %get-tuple-element.20), channel_id=1, source_target_pairs={{0,3},{1,2},{2,1},{3,0},{4,7},{5,6},{6,5},{7,4},{8,11},{9,10},{10,... | collective-permute-start | bytes 221192 | tf_op jit(solution)/shard_map/ppermute | solution.py:226
  31.7 2.0 %collective-permute-done.10.refs_5_ = bf16[12,24,128]{2,1,0:T(8,128)(2,1)S(1)} collective-permute-done((bf16[12,24,128]{2,1,0:T(8,128)(2,1)S(1)}, bf16[12,24,128]{2,1,0:T(8,128)(2,1)S(1)}, u32[]{:S(2)}, u32[]{:S(2)}) %collective-permute-start.10) | collective-permute-done | bytes 73760 | tf_op jit(solution)/shard_map/ppermute | solution.py:226
  33.7 2.1 %collective-permute-done.9.refs_4_ = bf16[12,24,128]{2,1,0:T(8,128)(2,1)S(1)} collective-permute-done((bf16[12,24,128]{2,1,0:T(8,128)(2,1)S(1)}, bf16[12,24,128]{2,1,0:T(8,128)(2,1)S(1)}, u32[]{:S(2)}, u32[]{:S(2)}) %collective-permute-start.9) | collective-permute-done | bytes 73760 | tf_op jit(solution)/shard_map/ppermute | solution.py:226
  35.8 1.3 %shard_map.91 = (bf16[12,48,128]{2,1,0:T(8,128)(2,1)S(1)}, bf16[12,48,128]{2,1,0:T(8,128)(2,1)S(1)}) custom-call(bf16[12,48,128]{2,1,0:T(8,128)(2,1)S(1)} %shard_map.88.refs_0_, bf16[12,48,128]{2,1,0:T(8,128)(2,1)S(1)} %collective-permute-done.7.refs_1_, bf16[12,24,128]{2,1,0:T(8,128)(2,1)S(1)} %get-tuple-element.19.refs_2_, ...), custom_call_target="tpu_custom_call" | custom-call | flops 400000000 | bytes 884736 | tf_op jit(solution)/shard_map/pallas_call | solution.py:21
  37.1 4.1 %collective-permute-start.12 = (bf16[12,48,128]{2,1,0:T(8,128)(2,1)S(1)}, bf16[12,48,128]{2,1,0:T(8,128)(2,1)S(1)}, u32[]{:S(2)}, u32[]{:S(2)}) collective-permute-start(bf16[12,48,128]{2,1,0:T(8,128)(2,1)S(1)} %get-tuple-element.21), channel_id=1, source_target_pairs={{0,8},{2,10},{4,12},{6,14},{8,0},{10,2},{12,4},{14,6},{1,9},{3,11}... | collective-permute-start | bytes 442376 | tf_op jit(solution)/shard_map/ppermute | solution.py:218
  41.2 1.4 %collective-permute-start.13 = (bf16[12,48,128]{2,1,0:T(8,128)(2,1)S(1)}, bf16[12,48,128]{2,1,0:T(8,128)(2,1)S(1)}, u32[]{:S(2)}, u32[]{:S(2)}) collective-permute-start(bf16[12,48,128]{2,1,0:T(8,128)(2,1)S(1)} %get-tuple-element.22), channel_id=1, source_target_pairs={{0,12},{2,14},{4,8},{6,10},{8,4},{10,6},{12,0},{14,2},{1,13},{3,15... | collective-permute-start | bytes 442376 | tf_op jit(solution)/shard_map/ppermute | solution.py:218
  42.6 0.7 %shard_map.90 = bf16[12,48,128]{2,1,0:T(8,128)(2,1)S(1)} custom-call(bf16[12,48,128]{2,1,0:T(8,128)(2,1)S(1)} %shard_map.88.refs_0_, bf16[12,48,128]{2,1,0:T(8,128)(2,1)S(1)} %collective-permute-done.7.refs_1_, bf16[12,24,128]{2,1,0:T(8,128)(2,1)S(1)} %get-tuple-element.19.refs_2_, bf16[12,24,128]{2,1,0:T(8,128)(2,1)S(1)} %collective-permute-done.8.refs_3_, ...), custom_call_target="tpu_custom_call" | custom-call | flops 200000000 | bytes 737280 | tf_op jit(solution)/shard_map/pallas_call | solution.py:21
  43.7 0.7 %shard_map.89.refs_0_ = f32[12,48,128]{2,1,0:T(8,128)S(1)} custom-call(bf16[12,48,128]{2,1,0:T(8,128)(2,1)S(1)} %shard_map.88.refs_0_, bf16[12,48,128]{2,1,0:T(8,128)(2,1)S(1)} %collective-permute-done.7.refs_1_, bf16[12,24,128]{2,1,0:T(8,128)(2,1)S(1)} %get-tuple-element.19.refs_2_, bf16[12,24,128]{2,1,0:T(8,128)(2,1)S(1)} %collective-permute-done.8.refs_3_, ...), custom_call_target="tpu_custom_call" | custom-call | flops 200000000 | bytes 884736 | tf_op jit(solution)/shard_map/pallas_call | solution.py:21
  44.4 7.8 %collective-permute-done.12.refs_2_ = bf16[12,48,128]{2,1,0:T(8,128)(2,1)S(1)} collective-permute-done((bf16[12,48,128]{2,1,0:T(8,128)(2,1)S(1)}, bf16[12,48,128]{2,1,0:T(8,128)(2,1)S(1)}, u32[]{:S(2)}, u32[]{:S(2)}) %collective-permute-start.12) | collective-permute-done | bytes 147488 | tf_op jit(solution)/shard_map/ppermute | solution.py:218
  52.2 1.1 %collective-permute-done.11.refs_1_ = bf16[12,48,128]{2,1,0:T(8,128)(2,1)S(1)} collective-permute-done((bf16[12,48,128]{2,1,0:T(8,128)(2,1)S(1)}, bf16[12,48,128]{2,1,0:T(8,128)(2,1)S(1)}, u32[]{:S(2)}, u32[]{:S(2)}) %collective-permute-start.11) | collective-permute-done | bytes 147488 | tf_op jit(solution)/shard_map/ppermute | solution.py:218
  53.3 1.0 %shard_map.93 = bf16[12,48,128]{2,1,0:T(8,128)(2,1)} custom-call(f32[12,48,128]{2,1,0:T(8,128)S(1)} %shard_map.89.refs_0_, bf16[12,48,128]{2,1,0:T(8,128)(2,1)S(1)} %collective-permute-done.11.refs_1_, bf16[12,48,128]{2,1,0:T(8,128)(2,1)S(1)} %collective-permute-done.12.refs_2_, bf16[12,48,128]{2,1,0:T(8,128)(2,1)S(1)} %collective-permute-done.13.refs_3_, ...), custom_call_target="tpu_custom_call" | custom-call | flops 100000000 | bytes 1359872 | tf_op jit(solution)/shard_map/pallas_call | solution.py:21
  (37 shorter events, 4.8 us)
Async XLA Ops:
  0.0 0.7 %copy-start.8 = (s32[96]{0:T(128)S(1)}, s32[96]{0:T(128)}, u32[]{:S(2)}) copy-start(s32[96]{0:T(128)} %param.9) | copy-start | bytes 1156
  0.7 0.9 %copy-start = (bf16[12,48,128]{2,1,0:T(8,128)(2,1)S(1)}, bf16[12,48,128]{2,1,0:T(8,128)(2,1)}, u32[]{:S(2)}) copy-start(bf16[12,48,128]{2,1,0:T(8,128)(2,1)} %refs_4_.1) | copy-start | bytes 442372
  1.6 0.9 %copy-start.3 = (bf16[128,512]{1,0:T(8,128)(2,1)S(1)}, bf16[128,512]{1,0:T(8,128)(2,1)}, u32[]{:S(2)}) copy-start(bf16[128,512]{1,0:T(8,128)(2,1)} %w_ref.6) | copy-start | bytes 393220
  2.9 6.2 %copy-start.1 = (bf16[12,48,128]{2,1,0:T(8,128)(2,1)S(1)}, bf16[12,48,128]{2,1,0:T(8,128)(2,1)}, u32[]{:S(2)}) copy-start(bf16[12,48,128]{2,1,0:T(8,128)(2,1)} %refs_4_.1) | copy-start | bytes 442372
  2.9 7.4 %collective-permute-start = (bf16[12,48,128]{2,1,0:T(8,128)(2,1)S(1)}, bf16[12,48,128]{2,1,0:T(8,128)(2,1)S(1)}, u32[]{:S(2)}, u32[]{:S(2)}) collective-permute-start(bf16[12,48,128]{2,1,0:T(8,128)(2,1)S(1)} %shard_map.82.own_left), channel_id=1, source_target_pairs={{0,2},{2,0},{4,6},{6,4},{8,10},{10,8},{12,14},{14,12},{1,3},{3,1},... | collective-permute-start | bytes 442376 | tf_op jit(solution)/shard_map/ppermute | solution.py:218
  3.9 9.9 %collective-permute-start.1 = (bf16[12,48,128]{2,1,0:T(8,128)(2,1)S(1)}, bf16[12,48,128]{2,1,0:T(8,128)(2,1)S(1)}, u32[]{:S(2)}, u32[]{:S(2)}) collective-permute-start(bf16[12,48,128]{2,1,0:T(8,128)(2,1)S(1)} %shard_map.83.refs_0_), channel_id=1, source_target_pairs={{0,4},{2,6},{4,0},{6,2},{8,12},{10,14},{12,8},{14,10},{1,5},{3,7},... | collective-permute-start | bytes 442376 | tf_op jit(solution)/shard_map/ppermute | solution.py:218
  6.6 13.9 %collective-permute-start.2 = (bf16[12,48,128]{2,1,0:T(8,128)(2,1)S(1)}, bf16[12,48,128]{2,1,0:T(8,128)(2,1)S(1)}, u32[]{:S(2)}, u32[]{:S(2)}) collective-permute-start(bf16[12,48,128]{2,1,0:T(8,128)(2,1)S(1)} %shard_map.83.refs_0_), channel_id=1, source_target_pairs={{0,8},{2,10},{4,12},{6,14},{8,0},{10,2},{12,4},{14,6},{1,9},{3,11}... | collective-permute-start | bytes 442376 | tf_op jit(solution)/shard_map/ppermute | solution.py:218
  9.2 11.4 %collective-permute-start.3 = (bf16[12,48,128]{2,1,0:T(8,128)(2,1)S(1)}, bf16[12,48,128]{2,1,0:T(8,128)(2,1)S(1)}, u32[]{:S(2)}, u32[]{:S(2)}) collective-permute-start(bf16[12,48,128]{2,1,0:T(8,128)(2,1)S(1)} %shard_map.83.refs_0_), channel_id=1, source_target_pairs={{0,12},{2,14},{4,8},{6,10},{8,4},{10,6},{12,0},{14,2},{1,13},{3,15... | collective-permute-start | bytes 442376 | tf_op jit(solution)/shard_map/ppermute | solution.py:218
  9.2 0.8 %copy-start.6 = (bf16[128,128]{1,0:T(8,128)(2,1)S(1)}, bf16[128,128]{1,0:T(8,128)(2,1)}, u32[]{:S(2)}) copy-start(bf16[128,128]{1,0:T(8,128)(2,1)} %w_ref.7) | copy-start | bytes 98308
  21.8 2.4 %collective-permute-start.5 = (bf16[12,24,128]{2,1,0:T(8,128)(2,1)S(1)}, bf16[12,24,128]{2,1,0:T(8,128)(2,1)S(1)}, u32[]{:S(2)}, u32[]{:S(2)}) collective-permute-start(bf16[12,24,128]{2,1,0:T(8,128)(2,1)S(1)} %get-tuple-element.24), channel_id=1, source_target_pairs={{0,2},{1,3},{2,0},{3,1},{4,6},{5,7},{6,4},{7,5},{8,10},{9,11},{10,... | collective-permute-start | bytes 221192 | tf_op jit(solution)/shard_map/ppermute | solution.py:226
  21.8 4.2 %collective-permute-start.6 = (bf16[12,24,128]{2,1,0:T(8,128)(2,1)S(1)}, bf16[12,24,128]{2,1,0:T(8,128)(2,1)S(1)}, u32[]{:S(2)}, u32[]{:S(2)}) collective-permute-start(bf16[12,24,128]{2,1,0:T(8,128)(2,1)S(1)} %get-tuple-element.23), channel_id=1, source_target_pairs={{0,3},{1,2},{2,1},{3,0},{4,7},{5,6},{6,5},{7,4},{8,11},{9,10},{10,... | collective-permute-start | bytes 221192 | tf_op jit(solution)/shard_map/ppermute | solution.py:226
  23.5 4.6 %copy-start.2 = (bf16[128,512]{1,0:T(8,128)(2,1)S(1)}, bf16[128,512]{1,0:T(8,128)(2,1)}, u32[]{:S(2)}) copy-start(bf16[128,512]{1,0:T(8,128)(2,1)} %w_ref.8) | copy-start | bytes 393220
  23.5 4.6 %copy-start.4 = (bf16[128,128]{1,0:T(8,128)(2,1)S(1)}, bf16[128,128]{1,0:T(8,128)(2,1)}, u32[]{:S(2)}) copy-start(bf16[128,128]{1,0:T(8,128)(2,1)} %refs_7_.1) | copy-start | bytes 98308
  23.5 4.6 %collective-permute-start.4 = (bf16[12,24,128]{2,1,0:T(8,128)(2,1)S(1)}, bf16[12,24,128]{2,1,0:T(8,128)(2,1)S(1)}, u32[]{:S(2)}, u32[]{:S(2)}) collective-permute-start(bf16[12,24,128]{2,1,0:T(8,128)(2,1)S(1)} %select_convert_fusion), channel_id=1, source_target_pairs={{0,1},{1,0},{2,3},{3,2},{4,5},{5,4},{6,7},{7,6},{8,9},{9,8},{10,11... | collective-permute-start | bytes 221192 | tf_op jit(solution)/shard_map/ppermute | solution.py:226
  29.5 6.4 %collective-permute-start.7 = (bf16[12,48,128]{2,1,0:T(8,128)(2,1)S(1)}, bf16[12,48,128]{2,1,0:T(8,128)(2,1)S(1)}, u32[]{:S(2)}, u32[]{:S(2)}) collective-permute-start(bf16[12,48,128]{2,1,0:T(8,128)(2,1)S(1)} %shard_map.88.refs_0_), channel_id=1, source_target_pairs={{0,2},{2,0},{4,6},{6,4},{8,10},{10,8},{12,14},{14,12},{1,3},{3,1},... | collective-permute-start | bytes 442376 | tf_op jit(solution)/shard_map/ppermute | solution.py:218
  29.5 4.2 %collective-permute-start.10 = (bf16[12,24,128]{2,1,0:T(8,128)(2,1)S(1)}, bf16[12,24,128]{2,1,0:T(8,128)(2,1)S(1)}, u32[]{:S(2)}, u32[]{:S(2)}) collective-permute-start(bf16[12,24,128]{2,1,0:T(8,128)(2,1)S(1)} %get-tuple-element.20), channel_id=1, source_target_pairs={{0,3},{1,2},{2,1},{3,0},{4,7},{5,6},{6,5},{7,4},{8,11},{9,10},{10,... | collective-permute-start | bytes 221192 | tf_op jit(solution)/shard_map/ppermute | solution.py:226
  31.1 2.6 %collective-permute-start.8 = (bf16[12,24,128]{2,1,0:T(8,128)(2,1)S(1)}, bf16[12,24,128]{2,1,0:T(8,128)(2,1)S(1)}, u32[]{:S(2)}, u32[]{:S(2)}) collective-permute-start(bf16[12,24,128]{2,1,0:T(8,128)(2,1)S(1)} %get-tuple-element.20), channel_id=1, source_target_pairs={{0,2},{1,3},{2,0},{3,1},{4,6},{5,7},{6,4},{7,5},{8,10},{9,11},{10,... | collective-permute-start | bytes 221192 | tf_op jit(solution)/shard_map/ppermute | solution.py:226
  31.2 4.6 %collective-permute-start.9 = (bf16[12,24,128]{2,1,0:T(8,128)(2,1)S(1)}, bf16[12,24,128]{2,1,0:T(8,128)(2,1)S(1)}, u32[]{:S(2)}, u32[]{:S(2)}) collective-permute-start(bf16[12,24,128]{2,1,0:T(8,128)(2,1)S(1)} %get-tuple-element.19.refs_2_), channel_id=1, source_target_pairs={{0,1},{1,0},{2,3},{3,2},{4,5},{5,4},{6,7},{7,6},{8,9},{9,8},{10,11... | collective-permute-start | bytes 221192 | tf_op jit(solution)/shard_map/ppermute | solution.py:226
  37.1 15.1 %collective-permute-start.12 = (bf16[12,48,128]{2,1,0:T(8,128)(2,1)S(1)}, bf16[12,48,128]{2,1,0:T(8,128)(2,1)S(1)}, u32[]{:S(2)}, u32[]{:S(2)}) collective-permute-start(bf16[12,48,128]{2,1,0:T(8,128)(2,1)S(1)} %get-tuple-element.21), channel_id=1, source_target_pairs={{0,8},{2,10},{4,12},{6,14},{8,0},{10,2},{12,4},{14,6},{1,9},{3,11}... | collective-permute-start | bytes 442376 | tf_op jit(solution)/shard_map/ppermute | solution.py:218
  41.2 2.1 %copy-start.7 = (bf16[128,128]{1,0:T(8,128)(2,1)S(1)}, bf16[128,128]{1,0:T(8,128)(2,1)}, u32[]{:S(2)}) copy-start(bf16[128,128]{1,0:T(8,128)(2,1)} %w_ref.9) | copy-start | bytes 98308
  41.2 11.0 %collective-permute-start.13 = (bf16[12,48,128]{2,1,0:T(8,128)(2,1)S(1)}, bf16[12,48,128]{2,1,0:T(8,128)(2,1)S(1)}, u32[]{:S(2)}, u32[]{:S(2)}) collective-permute-start(bf16[12,48,128]{2,1,0:T(8,128)(2,1)S(1)} %get-tuple-element.22), channel_id=1, source_target_pairs={{0,12},{2,14},{4,8},{6,10},{8,4},{10,6},{12,0},{14,2},{1,13},{3,15... | collective-permute-start | bytes 442376 | tf_op jit(solution)/shard_map/ppermute | solution.py:218
  43.2 10.1 %collective-permute-start.11 = (bf16[12,48,128]{2,1,0:T(8,128)(2,1)S(1)}, bf16[12,48,128]{2,1,0:T(8,128)(2,1)S(1)}, u32[]{:S(2)}, u32[]{:S(2)}) collective-permute-start(bf16[12,48,128]{2,1,0:T(8,128)(2,1)S(1)} %shard_map.90), channel_id=1, source_target_pairs={{0,4},{2,6},{4,0},{6,2},{8,12},{10,14},{12,8},{14,10},{1,5},{3,7},... | collective-permute-start | bytes 442376 | tf_op jit(solution)/shard_map/ppermute | solution.py:218
  43.7 9.6 %copy-start.5 = (bf16[128,128]{1,0:T(8,128)(2,1)S(1)}, bf16[128,128]{1,0:T(8,128)(2,1)}, u32[]{:S(2)}) copy-start(bf16[128,128]{1,0:T(8,128)(2,1)} %refs_6_.1) | copy-start | bytes 98308

commit v2 on v1

--- a/solution.py
+++ b/solution.py
@@ -12,7 +12,7 @@
 LIMIT = 40 * 1024 * 1024
 
 
-def call(kernel, outs, args, scratch=(), flops=10_000_000, name=None):
+def call(kernel, outs, args, scratch=(), flops=10_000_000, outside=()):
     single = not isinstance(outs, (list, tuple))
     outs = [outs] if single else list(outs)
     moved = sum(a.size * a.dtype.itemsize for a in args) + sum(
@@ -21,12 +21,13 @@
     result = pl.pallas_call(
         kernel,
         out_shape=outs,
-        in_specs=[VMEM] * len(args),
+        in_specs=[
+            pl.BlockSpec(memory_space=pl.ANY) if n in outside else VMEM for n in range(len(args))
+        ],
         out_specs=[VMEM] * len(outs),
         scratch_shapes=list(scratch),
         compiler_params=pltpu.CompilerParams(vmem_limit_bytes=LIMIT),
         cost_estimate=pl.CostEstimate(flops=flops, bytes_accessed=moved, transcendentals=0),
-        name=name,
     )(*args)
     return result[0] if single else result
 
@@ -59,31 +60,84 @@
     return jnp.dot(hot, jnp.ones((tokens, 128), BF16), preferred_element_type=F32)
 
 
-def gated(normed, w, mask_ref, rows, cols):
+def gated(normed, w, mask_ref, rows, cols, x):
     hidden = w.shape[1] // 2
     projected = jnp.dot(normed, w, preferred_element_type=F32)
     value = sigmoid(projected[:, hidden:]) * projected[:, :hidden]
     mask_row = mask_ref[...].astype(F32)
     row_w = token_weights(mask_row, lax.axis_index("row") * rows, -(-rows // 8) * 8)
-    col_w = token_weights(mask_row, lax.axis_index("col") * cols, cols)
+    col_w = token_weights(mask_row, x * cols, cols)
     weights = row_w[:rows, None, :] * col_w[None, :, :]
     return value * weights.reshape(rows * cols, 128)
 
 
-def right_kernel(half, pair_ref, mask_ref, w_ref, right_ref):
-    rows, cols, chan = pair_ref.shape
-    normed = layer_norm(pair_ref[...].astype(F32)).astype(BF16).reshape(rows * cols, chan)
-    width = w_ref.shape[1] // 2
-    w = w_ref[:, half * width : (half + 1) * width]
-    value = gated(normed, w, mask_ref, rows, cols)
+def normed_of(pair):
+    rows, cols, chan = pair.shape
+    return layer_norm(pair.astype(F32)).astype(BF16).reshape(rows * cols, chan)
+
+
+def opening_kernel(pair_hbm, mask_hbm, w_hbm, right_ref, pair_scr, mask_scr, w_scr, sems):
+    rows, cols, chan = pair_scr.shape
+    width = w_scr.shape[1]
+    copies = [
+        pltpu.make_async_copy(pair_hbm, pair_scr, sems.at[0]),
+        pltpu.make_async_copy(w_hbm.at[:, pl.ds(width, width)], w_scr, sems.at[1]),
+        pltpu.make_async_copy(mask_hbm, mask_scr, sems.at[2]),
+    ]
+    for copy in copies:
+        copy.start()
+    for copy in copies:
+        copy.wait()
+    value = gated(
+        normed_of(pair_scr[...]), w_scr[...], mask_scr, rows, cols, lax.axis_index("col")
+    )
     right_ref[...] = value.astype(BF16).reshape(right_ref.shape)
 
 
+def left_kernel(pair_ref, mask_ref, w_ref, right_hbm, left_ref):
+    del right_hbm
+    rows, cols, _ = pair_ref.shape
+    w = w_ref[:, : w_ref.shape[1] // 2]
+    value = gated(normed_of(pair_ref[...]), w, mask_ref, rows, cols, lax.axis_index("col"))
+    left_ref[...] = value.astype(BF16).reshape(left_ref.shape)
+
+
+def right_kernel(*refs):
+    firsts, (mask_ref, w_ref, right_ref, own_ref) = refs[:-4], refs[-4:]
+    rows, cols, _ = own_ref.shape
+    pieces = cols // (2 * rows)
+    z, _, x = place()
+    for h, ref in enumerate(firsts):
+
+        @pl.when(((z // pieces) ^ h) == x)
+        def _():
+            own_ref[...] = ref[...]
+
+    w = w_ref[:, w_ref.shape[1] // 2 :]
+    value = gated(normed_of(own_ref[...]), w, mask_ref, rows, cols, x)
+    right_ref[...] = value.astype(BF16).reshape(right_ref.shape)
+
+
+def gates_kernel(cols_n, *refs):
+    pairs, w_ref, outs = refs[:cols_n], refs[cols_n], refs[cols_n + 1 :]
+    rows, cols, _ = pairs[0].shape
+    pieces = cols // (2 * rows)
+    z, _, x = place()
+    for h in range(cols_n):
+        pair_ref, gate_ref = outs[2 * h : 2 * h + 2]
+        for dx in range(cols_n):
+
+            @pl.when(((z // pieces) ^ x ^ h) == dx)
+            def _():
+                pair_ref[...] = pairs[dx][...]
+
+        gate = jnp.dot(normed_of(pair_ref[...]), w_ref[...], preferred_element_type=F32)
+        gate_ref[...] = sigmoid(gate).reshape(gate_ref.shape)
+
+
 def gate_kernel(pair_ref, w_ref, gate_ref):
-    rows, cols, chan = pair_ref.shape
-    normed = layer_norm(pair_ref[...].astype(F32)).astype(BF16).reshape(rows * cols, chan)
-    gate = sigmoid(jnp.dot(normed, w_ref[...], preferred_element_type=F32))
-    gate_ref[...] = gate.reshape(gate_ref.shape)
+    gate = jnp.dot(normed_of(pair_ref[...]), w_ref[...], preferred_element_type=F32)
+    gate_ref[...] = sigmoid(gate).reshape(gate_ref.shape)
 
 
 def outgoing_kernel(own_left, core_left, *refs):
@@ -115,20 +169,17 @@
             out_ref[i] = t.astype(out_ref.dtype)
 
 
-def first_kernel(cols_n, *refs):
-    own, others = refs[0], refs[1 : 2 * cols_n]
+def first_kernel(cols_n, h, *refs):
+    parts = refs[: 2 * cols_n]
     pair_ref, gate_ref, mask_ref, final_ref, w_ref = refs[2 * cols_n : 2 * cols_n + 5]
     first_ref, mine_ref, other_ref, scr, half_scr = refs[2 * cols_n + 5 :]
     rows, cols, chan = pair_ref.shape
-    _, core, _ = place()
-    same = own[...].astype(F32)
-    for ref in others[: cols_n - 1]:
-        same = same + ref[...].astype(F32)
-    cross = others[cols_n - 1][...].astype(F32)
-    for ref in others[cols_n:]:
-        cross = cross + ref[...].astype(F32)
     pieces = cols // (2 * rows)
-    for value, side in ((same, core), (cross, 1 - core)):
+    z, core, _ = place()
+    for group, side in ((parts[:cols_n], core), (parts[cols_n:], 1 - core)):
+        value = group[0][...].astype(F32)
+        for ref in group[1:]:
+            value = value + ref[...].astype(F32)
         half_scr[...] = value.reshape(half_scr.shape)
         for i in range(rows):
             for q in range(pieces):
@@ -141,7 +192,7 @@
     first_ref[...] = first.reshape(first_ref.shape)
     normed = layer_norm(first.astype(F32)).astype(BF16)
     w = w_ref[:, : w_ref.shape[1] // 2]
-    scr[...] = gated(normed, w, mask_ref, rows, cols)
+    scr[...] = gated(normed, w, mask_ref, rows, cols, (z // pieces) ^ h)
     for out_ref, side in ((mine_ref, core), (other_ref, 1 - core)):
         for i in range(rows):
             for q in range(pieces):
@@ -150,22 +201,23 @@
         out_ref[...] = half_scr[...].astype(BF16).reshape(out_ref.shape)
 
 
-def incoming_kernel(cols_n, steps, *refs):
+def incoming_kernel(steps, *refs):
     own_right, core_right = refs[:2]
-    lefts = refs[2 : 2 + 2 * cols_n]
-    outs = refs[2 + 2 * cols_n : 2 + 2 * cols_n + len(steps)]
+    count = (len(refs) - 4 - len(steps)) // 2
+    lefts = refs[2 : 2 + 2 * count]
+    outs = refs[2 + 2 * count : -2]
     l_scr, r_scr = refs[-2:]
     rows, cols, chan = own_right.shape
     width = lefts[0].shape[1]
     pieces = width // rows
-    z, _, x = place()
+    z, _, _ = place()
     for n, ref in enumerate((own_right, core_right)):
         r_scr[pl.ds(n * rows * cols, rows * cols), :] = ref[...].astype(F32).reshape(-1, chan)
     for n, ref in enumerate(lefts):
         l_scr[pl.ds(n * rows * width, rows * width), :] = ref[...].astype(F32).reshape(-1, chan)
     for m, out_ref in zip(steps, outs):
-        target = z ^ m
-        base = ((target // pieces) ^ x) * (2 * rows * width) + (target % pieces) * rows
+        block = m // pieces - steps[0] // pieces
+        base = block * (2 * rows * width) + ((z ^ m) % pieces) * rows
         for group in range(0, rows, 6):
 
             def step(k, totals):
@@ -225,24 +277,42 @@
         ]
         return lax.ppermute(v, ("row", "col"), pairs)
 
-    z, _, x = place()
-    offset = (z // pieces) ^ x
-
-    project = lambda pair, w, half: call(
-        functools.partial(right_kernel, half), block, [pair, mask, w], flops=100_000_000
-    )
-    right = project(pair_rep, out_project, 1)
+    right = call(
+        opening_kernel,
+        block,
+        [pair_rep, mask, out_project],
+        scratch=[
+            pltpu.VMEM(pair_rep.shape, BF16),
+            pltpu.VMEM(mask.shape, jnp.int32),
+            pltpu.VMEM((chan, out_project.shape[1] // 2), BF16),
+            pltpu.SemaphoreType.DMA((3,)),
+        ],
+        flops=100_000_000,
+        outside=(0, 1, 2),
+    )
     rights = [right] + [None] * (chips - 1)
     for m in reversed(range(1, chips)):
         rights[m] = along_row(right, 2 * m)
-    left = project(pair_rep, out_project, 0)
+    left = call(
+        left_kernel,
+        block,
+        [pair_rep, mask, out_project, right],
+        flops=100_000_000,
+        outside=(3,),
+    )
     core_left = along_row(left, 1)
-    gate = call(gate_kernel, block32, [pair_rep, out_gating], flops=50_000_000)
-    mine, other = [], []
+    pairs = [pair_rep] + [shift(pair_rep, dx, 0) for dx in range(1, cols_n)]
+    gates = call(
+        functools.partial(gates_kernel, cols_n),
+        [block, block32] * cols_n,
+        pairs + [out_gating],
+        flops=100_000_000,
+    )
+    firsts, lefts = [], []
     for h in range(cols_n):
-        a, b = call(
+        mine, other = call(
             outgoing_kernel,
-            [shape(half, F32), shape(half, BF16)],
+            [shape(half, BF16), shape(half, BF16)],
             [left, core_left] + rights[h * pieces : (h + 1) * pieces],
             scratch=[
                 pltpu.VMEM((cols * pieces * rows, chan), F32),
@@ -250,41 +320,34 @@
             ],
             flops=500_000_000,
         )
-        mine.append(a)
-        other.append(b)
-
-    def pick(options, dx):
-        return lax.select_n(offset ^ dx, *options)
-
-    same = [pick(mine, 0)]
-    for dx in range(1, cols_n):
-        same.append(shift(pick(mine, dx).astype(BF16), dx, 0))
-    cross = [shift(pick(other, dx), dx, 1) for dx in range(cols_n)]
-    first, left_mine, left_other = call(
-        functools.partial(first_kernel, cols_n),
-        [block, shape(half, BF16), shape(half, BF16)],
-        same + cross + [pair_rep, gate, mask, out_final, in_project],
-        scratch=[
-            pltpu.VMEM((rows * cols, chan), F32),
-            pltpu.VMEM((rows * pieces * rows, chan), F32),
-        ],
-        flops=200_000_000,
-    )
-
-    lefts = []
-    for dx in range(cols_n):
-        lefts.append(left_mine if dx == 0 else shift(left_mine, dx, 0))
-        lefts.append(shift(left_other, dx, 1))
-    right = project(first, in_project, 1)
+        parts = [mine] + [shift(mine, dx, 0) for dx in range(1, cols_n)]
+        parts += [shift(other, dx, 1) for dx in range(cols_n)]
+        first, left_mine, left_other = call(
+            functools.partial(first_kernel, cols_n, h),
+            [block, shape(half, BF16), shape(half, BF16)],
+            parts + list(gates[2 * h : 2 * h + 2]) + [mask, out_final, in_project],
+            scratch=[
+                pltpu.VMEM((rows * cols, chan), F32),
+                pltpu.VMEM((rows * pieces * rows, chan), F32),
+            ],
+            flops=200_000_000,
+        )
+        firsts.append(first)
+        lefts.append([left_mine, along_row(left_other, 1)])
+
+    right, first = call(
+        right_kernel, [block, block], firsts + [mask, in_project], flops=100_000_000
+    )
     core_right = along_row(right, 1)
 
     def partial_products(steps):
+        used = lefts[steps[0] // pieces : steps[-1] // pieces + 1]
         return call(
-            functools.partial(incoming_kernel, cols_n, steps),
+            functools.partial(incoming_kernel, steps),
             [block32 if m == 0 else block for m in steps],
-            [right, core_right] + lefts,
+            [right, core_right] + sum(used, []),
             scratch=[
-                pltpu.VMEM((2 * cols_n * rows * pieces * rows, chan), F32),
+                pltpu.VMEM((2 * len(used) * rows * pieces * rows, chan), F32),
                 pltpu.VMEM((2 * rows * cols, chan), F32),
             ],
             flops=200_000_000 * len(steps),

time: 54.6 us -> 52 us (0.952)
  waiting for transfers between devices: 25.9 us -> 21.3 us
  Pallas kernels: 9.12 us -> 13.3 us
  local copies, waits for them, and re-layouts: 3.25 us -> 1.58 us
    ppermute x6 -> x7, waiting for transfers between devices: 8.01 us -> 1.02 us  [shift(): return lax.ppermute(v, ('row', 'col'), pairs)]
    pallas_call x12 -> x13, Pallas kernels: 9.12 us -> 13.3 us  [call(): pl.pallas_call(kernel, out_shape=outs, in_specs=[pl.BlockSpec(memory_spac...]
    ppermute x8 -> x10, waiting for transfers between devices: 17.9 us -> 20.3 us  [along_row(): return lax.ppermute(v, 'row', [(i, i ^ bits) for i in range(rows_n)])]
    unnamed x18 -> x14, local copies, waits for them, and re-layouts: 3.25 us -> 1.58 us
    ppermute x8 -> x10, starting transfers between devices: 11.3 us -> 10 us  [along_row(): return lax.ppermute(v, 'row', [(i, i ^ bits) for i in range(rows_n)])]
    ppermute x6 -> x7, starting transfers between devices: 4.48 us -> 5.43 us  [shift(): return lax.ppermute(v, ('row', 'col'), pairs)]
  transfers between devices with their start and end apart: 14 -> 17, of which waited for: 8 -> 7; matrix products, arithmetic and copies ran while one was open for 0% -> 0% of each run, Pallas kernels for 7% -> 16%
where the time goes in v2:
time: 52 us; the launch traced here: 51.8 us
  waiting for transfers between devices  21.3 us (41%)
  starting transfers between devices  15.4 us (30%)
  Pallas kernels  13.3 us (26%)
  local copies, waits for them, and re-layouts  1.58 us (3%)
    ppermute x10, waiting for transfers between devices, along_row(): return lax.ppermute(v, 'row', [(i, i ^ bits) for i in range(rows_n)])  20.3 us
    pallas_call x13, Pallas kernels, call(): pl.pallas_call(kernel, out_shape=outs, in_specs=[pl.BlockSpec(memory_spac...  13.3 us
    ppermute x10, starting transfers between devices, along_row(): return lax.ppermute(v, 'row', [(i, i ^ bits) for i in range(rows_n)])  10 us
    ppermute x7, starting transfers between devices, shift(): return lax.ppermute(v, ('row', 'col'), pairs)  5.43 us
    unnamed x14, local copies, waits for them, and re-layouts  1.58 us
  transfers between devices with their start and end apart: 17, of which 7 were waited for; matrix products, arithmetic and copies ran while one was open for 0% of the time, Pallas kernels for 16%

profile of v2, /device:TPU:0, one launch (start us, length us, event | category | flops | bytes accessed | tf_op | source)
XLA Modules:
  0.0 51.8 jit_solution(10772174906868102560)
XLA Ops:
  0.7 0.9 %copy-done.1 = bf16[128,512]{1,0:T(8,128)(2,1)S(1)} copy-done((bf16[128,512]{1,0:T(8,128)(2,1)S(1)}, bf16[128,512]{1,0:T(8,128)(2,1)}, u32[]{:S(2)}) %copy-start.1) | copy-done | bytes 131096
  1.6 1.4 %shard_map.82.right_hbm.refs_0_ = bf16[12,48,128]{2,1,0:T(8,128)(2,1)S(1)} custom-call(bf16[12,48,128]{2,1,0:T(8,128)(2,1)} %refs_0_.1, s32[1,96]{1,0:T(1,128)S(1)} %bitcast.1, bf16[128,512]{1,0:T(8,128)(2,1)S(1)} %copy-done.1), custom_call_target="tpu_custom_call" | custom-call | flops 100000000 | bytes 426368 | tf_op jit(solution)/shard_map/pallas_call | solution.py:21
  3.0 1.4 %shard_map.83.own_left = bf16[12,48,128]{2,1,0:T(8,128)(2,1)S(1)} custom-call(bf16[12,48,128]{2,1,0:T(8,128)(2,1)} %refs_0_.1, s32[1,96]{1,0:T(1,128)S(1)} %bitcast.2, bf16[128,512]{1,0:T(8,128)(2,1)S(1)} %copy-done.1, bf16[12,48,128]{2,1,0:T(8,128)(2,1)S(1)} %shard_map.82.right_hbm.refs_0_), custom_call_target="tpu_custom_call" | custom-call | flops 100000000 | bytes 573824 | tf_op jit(solution)/shard_map/pallas_call | solution.py:21
  4.8 2.6 %collective-permute-start.1 = (bf16[12,48,128]{2,1,0:T(8,128)(2,1)S(1)}, bf16[12,48,128]{2,1,0:T(8,128)(2,1)S(1)}, u32[]{:S(2)}, u32[]{:S(2)}) collective-permute-start(bf16[12,48,128]{2,1,0:T(8,128)(2,1)S(1)} %shard_map.82.right_hbm.refs_0_), channel_id=1, source_target_pairs={{0,4},{2,6},{4,0},{6,2},{8,12},{10,14},{12,8},{14,10},{1,5},{3,7},... | collective-permute-start | bytes 442376 | tf_op jit(solution)/shard_map/ppermute | solution.py:270
  7.5 2.5 %collective-permute-start.7 = (bf16[12,48,128]{2,1,0:T(8,128)(2,1)S(1)}, bf16[12,48,128]{2,1,0:T(8,128)(2,1)S(1)}, u32[]{:S(2)}, u32[]{:S(2)}) collective-permute-start(bf16[12,48,128]{2,1,0:T(8,128)(2,1)S(1)} %shard_map.82.right_hbm.refs_0_), channel_id=1, source_target_pairs={{0,12},{2,14},{4,8},{6,10},{8,4},{10,6},{12,0},{14,2},{1,13},{3,15... | collective-permute-start | bytes 442376 | tf_op jit(solution)/shard_map/ppermute | solution.py:270
  10.1 1.5 %collective-permute-start.5 = (bf16[12,48,128]{2,1,0:T(8,128)(2,1)}, bf16[12,48,128]{2,1,0:T(8,128)(2,1)S(1)}, u32[]{:S(2)}, u32[]{:S(2)}) collective-permute-start(bf16[12,48,128]{2,1,0:T(8,128)(2,1)} %refs_0_.1), channel_id=1, source_target_pairs={{0,1},{1,0},{2,3},{3,2},{4,5},{5,4},{6,7},{7,6},{8,9},{9,8},{10,11... | collective-permute-start | bytes 442376 | tf_op jit(solution)/shard_map/ppermute | solution.py:278
  11.9 1.2 %shard_map.84 = (bf16[12,24,128]{2,1,0:T(8,128)(2,1)S(1)}, bf16[12,24,128]{2,1,0:T(8,128)(2,1)S(1)}) custom-call(bf16[12,48,128]{2,1,0:T(8,128)(2,1)S(1)} %shard_map.83.own_left, bf16[12,48,128]{2,1,0:T(8,128)(2,1)S(1)} %collective-permute-done.core_left, bf16[12,48,128]{2,1,0:T(8,128)(2,1)S(1)} %shard_map.82.right_hbm.refs_0_, ...), custom_call_target="tpu_custom_call" | custom-call | flops 500000000 | bytes 737280 | tf_op jit(solution)/shard_map/pallas_call | solution.py:21
  13.2 1.7 %collective-permute-start.2 = (bf16[12,24,128]{2,1,0:T(8,128)(2,1)S(1)}, bf16[12,24,128]{2,1,0:T(8,128)(2,1)S(1)}, u32[]{:S(2)}, u32[]{:S(2)}) collective-permute-start(bf16[12,24,128]{2,1,0:T(8,128)(2,1)S(1)} %get-tuple-element.23.refs_0_), channel_id=1, source_target_pairs={{0,1},{1,0},{2,3},{3,2},{4,5},{5,4},{6,7},{7,6},{8,9},{9,8},{10,11... | collective-permute-start | bytes 221192 | tf_op jit(solution)/shard_map/ppermute | solution.py:278
  14.9 3.0 %collective-permute-done.7.refs_1_ = bf16[12,48,128]{2,1,0:T(8,128)(2,1)S(1)} collective-permute-done((bf16[12,48,128]{2,1,0:T(8,128)(2,1)S(1)}, bf16[12,48,128]{2,1,0:T(8,128)(2,1)S(1)}, u32[]{:S(2)}, u32[]{:S(2)}) %collective-permute-start.7) | collective-permute-done | bytes 147488 | tf_op jit(solution)/shard_map/ppermute | solution.py:270
  17.9 5.9 %collective-permute-done.6.refs_0_ = bf16[12,48,128]{2,1,0:T(8,128)(2,1)S(1)} collective-permute-done((bf16[12,48,128]{2,1,0:T(8,128)(2,1)S(1)}, bf16[12,48,128]{2,1,0:T(8,128)(2,1)S(1)}, u32[]{:S(2)}, u32[]{:S(2)}) %collective-permute-start.6) | collective-permute-done | bytes 147488 | tf_op jit(solution)/shard_map/ppermute | solution.py:270
  23.7 1.2 %shard_map.87 = (bf16[12,24,128]{2,1,0:T(8,128)(2,1)S(1)}, bf16[12,24,128]{2,1,0:T(8,128)(2,1)S(1)}) custom-call(bf16[12,48,128]{2,1,0:T(8,128)(2,1)S(1)} %shard_map.83.own_left, bf16[12,48,128]{2,1,0:T(8,128)(2,1)S(1)} %collective-permute-done.core_left, bf16[12,48,128]{2,1,0:T(8,128)(2,1)S(1)} %collective-permute-done.6.refs_0_, ...), custom_call_target="tpu_custom_call" | custom-call | flops 500000000 | bytes 737280 | tf_op jit(solution)/shard_map/pallas_call | solution.py:21
  25.0 1.6 %collective-permute-start.8 = (bf16[12,24,128]{2,1,0:T(8,128)(2,1)S(1)}, bf16[12,24,128]{2,1,0:T(8,128)(2,1)S(1)}, u32[]{:S(2)}, u32[]{:S(2)}) collective-permute-start(bf16[12,24,128]{2,1,0:T(8,128)(2,1)S(1)} %get-tuple-element.28.refs_0_), channel_id=1, source_target_pairs={{0,1},{1,0},{2,3},{3,2},{4,5},{5,4},{6,7},{7,6},{8,9},{9,8},{10,11... | collective-permute-start | bytes 221192 | tf_op jit(solution)/shard_map/ppermute | solution.py:278
  27.2 1.8 %shard_map.85 = (bf16[12,48,128]{2,1,0:T(8,128)(2,1)S(1)}, f32[12,48,128]{2,1,0:T(8,128)S(1)}, bf16[12,48,128]{2,1,0:T(8,128)(2,1)S(1)}, f32[12,48,128]{2,1,0:T(8,128)S(1)}) custom-call(bf16[12,48,128]{2,1,0:T(8,128)(2,1)} %refs_0_.1, bf16[12,48,128]{2,1,0:T(8,128)(2,1)S(1)} %collective-permute-done.5.refs_1_, bf16[128,128]{1,0:T(8,128)(2,1)S(1)} %copy-done.6), custom_call_target="tpu_custom_call" | custom-call | flops 100000000 | bytes 1212416 | tf_op jit(solution)/shard_map/pallas_call | solution.py:21
  29.0 0.9 %shard_map.86 = (bf16[12,48,128]{2,1,0:T(8,128)(2,1)S(1)}, bf16[12,24,128]{2,1,0:T(8,128)(2,1)S(1)}, bf16[12,24,128]{2,1,0:T(8,128)(2,1)S(1)}) custom-call(bf16[12,24,128]{2,1,0:T(8,128)(2,1)S(1)} %get-tuple-element.23.refs_0_, bf16[12,24,128]{2,1,0:T(8,128)(2,1)S(1)} %collective-permute-done.2.refs_1_, ...), custom_call_target="tpu_custom_call" | custom-call | flops 200000000 | bytes 1196416 | tf_op jit(solution)/shard_map/pallas_call | solution.py:21
  30.0 1.0 %collective-permute-done.10.refs_3_ = bf16[12,24,128]{2,1,0:T(8,128)(2,1)S(1)} collective-permute-done((bf16[12,24,128]{2,1,0:T(8,128)(2,1)S(1)}, bf16[12,24,128]{2,1,0:T(8,128)(2,1)S(1)}, u32[]{:S(2)}, u32[]{:S(2)}) %collective-permute-start.10) | collective-permute-done | bytes 73760 | tf_op jit(solution)/shard_map/ppermute | solution.py:278
  31.0 0.9 %shard_map.88 = (bf16[12,48,128]{2,1,0:T(8,128)(2,1)S(1)}, bf16[12,24,128]{2,1,0:T(8,128)(2,1)S(1)}, bf16[12,24,128]{2,1,0:T(8,128)(2,1)S(1)}) custom-call(bf16[12,24,128]{2,1,0:T(8,128)(2,1)S(1)} %get-tuple-element.28.refs_0_, bf16[12,24,128]{2,1,0:T(8,128)(2,1)S(1)} %collective-permute-done.8.refs_1_, ...), custom_call_target="tpu_custom_call" | custom-call | flops 200000000 | bytes 1196416 | tf_op jit(solution)/shard_map/pallas_call | solution.py:21
  33.1 0.9 %collective-permute-done.14.refs_3_ = bf16[12,24,128]{2,1,0:T(8,128)(2,1)S(1)} collective-permute-done((bf16[12,24,128]{2,1,0:T(8,128)(2,1)S(1)}, bf16[12,24,128]{2,1,0:T(8,128)(2,1)S(1)}, u32[]{:S(2)}, u32[]{:S(2)}) %collective-permute-start.14) | collective-permute-done | bytes 73760 | tf_op jit(solution)/shard_map/ppermute | solution.py:270
  33.9 1.3 %shard_map.92 = (bf16[12,48,128]{2,1,0:T(8,128)(2,1)S(1)}, bf16[12,48,128]{2,1,0:T(8,128)(2,1)S(1)}) custom-call(bf16[12,48,128]{2,1,0:T(8,128)(2,1)S(1)} %get-tuple-element.33.refs_0_, bf16[12,48,128]{2,1,0:T(8,128)(2,1)S(1)} %collective-permute-done.11.refs_1_, bf16[12,24,128]{2,1,0:T(8,128)(2,1)S(1)} %get-tuple-element.36.refs_2_, ...), custom_call_target="tpu_custom_call" | custom-call | flops 400000000 | bytes 737280 | tf_op jit(solution)/shard_map/pallas_call | solution.py:21
  35.3 2.7 %collective-permute-start.16 = (bf16[12,48,128]{2,1,0:T(8,128)(2,1)S(1)}, bf16[12,48,128]{2,1,0:T(8,128)(2,1)S(1)}, u32[]{:S(2)}, u32[]{:S(2)}) collective-permute-start(bf16[12,48,128]{2,1,0:T(8,128)(2,1)S(1)} %get-tuple-element.39), channel_id=1, source_target_pairs={{0,12},{2,14},{4,8},{6,10},{8,4},{10,6},{12,0},{14,2},{1,13},{3,15... | collective-permute-start | bytes 442376 | tf_op jit(solution)/shard_map/ppermute | solution.py:270
  38.0 0.7 %shard_map.91 = bf16[12,48,128]{2,1,0:T(8,128)(2,1)S(1)} custom-call(bf16[12,48,128]{2,1,0:T(8,128)(2,1)S(1)} %get-tuple-element.33.refs_0_, bf16[12,48,128]{2,1,0:T(8,128)(2,1)S(1)} %collective-permute-done.11.refs_1_, bf16[12,24,128]{2,1,0:T(8,128)(2,1)S(1)} %get-tuple-element.34.refs_2_, bf16[12,24,128]{2,1,0:T(8,128)(2,1)S(1)} %collective-permute-done.12.refs_3_), custom_call_target="tpu_custom_call" | custom-call | flops 200000000 | bytes 589824 | tf_op jit(solution)/shard_map/pallas_call | solution.py:21
  38.7 0.8 %collective-permute-start.13 = (bf16[12,48,128]{2,1,0:T(8,128)(2,1)S(1)}, bf16[12,48,128]{2,1,0:T(8,128)(2,1)S(1)}, u32[]{:S(2)}, u32[]{:S(2)}) collective-permute-start(bf16[12,48,128]{2,1,0:T(8,128)(2,1)S(1)} %shard_map.91), channel_id=1, source_target_pairs={{0,4},{2,6},{4,0},{6,2},{8,12},{10,14},{12,8},{14,10},{1,5},{3,7},... | collective-permute-start | bytes 442376 | tf_op jit(solution)/shard_map/ppermute | solution.py:270
  40.6 8.1 %collective-permute-done.15.refs_2_ = bf16[12,48,128]{2,1,0:T(8,128)(2,1)S(1)} collective-permute-done((bf16[12,48,128]{2,1,0:T(8,128)(2,1)S(1)}, bf16[12,48,128]{2,1,0:T(8,128)(2,1)S(1)}, u32[]{:S(2)}, u32[]{:S(2)}) %collective-permute-start.15) | collective-permute-done | bytes 147488 | tf_op jit(solution)/shard_map/ppermute | solution.py:270
  48.7 2.0 %collective-permute-done.13.refs_1_ = bf16[12,48,128]{2,1,0:T(8,128)(2,1)S(1)} collective-permute-done((bf16[12,48,128]{2,1,0:T(8,128)(2,1)S(1)}, bf16[12,48,128]{2,1,0:T(8,128)(2,1)S(1)}, u32[]{:S(2)}, u32[]{:S(2)}) %collective-permute-start.13) | collective-permute-done | bytes 147488 | tf_op jit(solution)/shard_map/ppermute | solution.py:270
  50.7 1.0 %shard_map.94 = bf16[12,48,128]{2,1,0:T(8,128)(2,1)} custom-call(f32[12,48,128]{2,1,0:T(8,128)S(1)} %shard_map.90.refs_0_, bf16[12,48,128]{2,1,0:T(8,128)(2,1)S(1)} %collective-permute-done.13.refs_1_, bf16[12,48,128]{2,1,0:T(8,128)(2,1)S(1)} %collective-permute-done.15.refs_2_, bf16[12,48,128]{2,1,0:T(8,128)(2,1)S(1)} %collective-permute-done.16.refs_3_, ...), custom_call_target="tpu_custom_call" | custom-call | flops 100000000 | bytes 1359872 | tf_op jit(solution)/shard_map/pallas_call | solution.py:21
  (37 shorter events, 4.6 us)
Async XLA Ops:
  0.0 0.7 %copy-start.5 = (s32[96]{0:T(128)S(1)}, s32[96]{0:T(128)}, u32[]{:S(2)}) copy-start(s32[96]{0:T(128)} %param.9) | copy-start | bytes 1156
  0.7 0.9 %copy-start.1 = (bf16[128,512]{1,0:T(8,128)(2,1)S(1)}, bf16[128,512]{1,0:T(8,128)(2,1)}, u32[]{:S(2)}) copy-start(bf16[128,512]{1,0:T(8,128)(2,1)} %w_ref.2) | copy-start | bytes 393220
  4.3 7.3 %collective-permute-start = (bf16[12,48,128]{2,1,0:T(8,128)(2,1)S(1)}, bf16[12,48,128]{2,1,0:T(8,128)(2,1)S(1)}, u32[]{:S(2)}, u32[]{:S(2)}) collective-permute-start(bf16[12,48,128]{2,1,0:T(8,128)(2,1)S(1)} %shard_map.83.own_left), channel_id=1, source_target_pairs={{0,2},{2,0},{4,6},{6,4},{8,10},{10,8},{12,14},{14,12},{1,3},{3,1},... | collective-permute-start | bytes 442376 | tf_op jit(solution)/shard_map/ppermute | solution.py:270
  4.8 7.1 %collective-permute-start.1 = (bf16[12,48,128]{2,1,0:T(8,128)(2,1)S(1)}, bf16[12,48,128]{2,1,0:T(8,128)(2,1)S(1)}, u32[]{:S(2)}, u32[]{:S(2)}) collective-permute-start(bf16[12,48,128]{2,1,0:T(8,128)(2,1)S(1)} %shard_map.82.right_hbm.refs_0_), channel_id=1, source_target_pairs={{0,4},{2,6},{4,0},{6,2},{8,12},{10,14},{12,8},{14,10},{1,5},{3,7},... | collective-permute-start | bytes 442376 | tf_op jit(solution)/shard_map/ppermute | solution.py:270
  7.5 10.4 %collective-permute-start.7 = (bf16[12,48,128]{2,1,0:T(8,128)(2,1)S(1)}, bf16[12,48,128]{2,1,0:T(8,128)(2,1)S(1)}, u32[]{:S(2)}, u32[]{:S(2)}) collective-permute-start(bf16[12,48,128]{2,1,0:T(8,128)(2,1)S(1)} %shard_map.82.right_hbm.refs_0_), channel_id=1, source_target_pairs={{0,12},{2,14},{4,8},{6,10},{8,4},{10,6},{12,0},{14,2},{1,13},{3,15... | collective-permute-start | bytes 442376 | tf_op jit(solution)/shard_map/ppermute | solution.py:270
  10.0 13.8 %collective-permute-start.6 = (bf16[12,48,128]{2,1,0:T(8,128)(2,1)S(1)}, bf16[12,48,128]{2,1,0:T(8,128)(2,1)S(1)}, u32[]{:S(2)}, u32[]{:S(2)}) collective-permute-start(bf16[12,48,128]{2,1,0:T(8,128)(2,1)S(1)} %shard_map.82.right_hbm.refs_0_), channel_id=1, source_target_pairs={{0,8},{2,10},{4,12},{6,14},{8,0},{10,2},{12,4},{14,6},{1,9},{3,11}... | collective-permute-start | bytes 442376 | tf_op jit(solution)/shard_map/ppermute | solution.py:270
  10.1 16.4 %collective-permute-start.5 = (bf16[12,48,128]{2,1,0:T(8,128)(2,1)}, bf16[12,48,128]{2,1,0:T(8,128)(2,1)S(1)}, u32[]{:S(2)}, u32[]{:S(2)}) collective-permute-start(bf16[12,48,128]{2,1,0:T(8,128)(2,1)} %refs_0_.1), channel_id=1, source_target_pairs={{0,1},{1,0},{2,3},{3,2},{4,5},{5,4},{6,7},{7,6},{8,9},{9,8},{10,11... | collective-permute-start | bytes 442376 | tf_op jit(solution)/shard_map/ppermute | solution.py:278
  13.2 13.4 %collective-permute-start.2 = (bf16[12,24,128]{2,1,0:T(8,128)(2,1)S(1)}, bf16[12,24,128]{2,1,0:T(8,128)(2,1)S(1)}, u32[]{:S(2)}, u32[]{:S(2)}) collective-permute-start(bf16[12,24,128]{2,1,0:T(8,128)(2,1)S(1)} %get-tuple-element.23.refs_0_), channel_id=1, source_target_pairs={{0,1},{1,0},{2,3},{3,2},{4,5},{5,4},{6,7},{7,6},{8,9},{9,8},{10,11... | collective-permute-start | bytes 221192 | tf_op jit(solution)/shard_map/ppermute | solution.py:278
  14.9 12.3 %copy-start.6 = (bf16[128,128]{1,0:T(8,128)(2,1)S(1)}, bf16[128,128]{1,0:T(8,128)(2,1)}, u32[]{:S(2)}) copy-start(bf16[128,128]{1,0:T(8,128)(2,1)} %refs_2_.1) | copy-start | bytes 98308
  14.9 14.1 %collective-permute-start.4 = (bf16[12,24,128]{2,1,0:T(8,128)(2,1)S(1)}, bf16[12,24,128]{2,1,0:T(8,128)(2,1)S(1)}, u32[]{:S(2)}, u32[]{:S(2)}) collective-permute-start(bf16[12,24,128]{2,1,0:T(8,128)(2,1)S(1)} %get-tuple-element.24), channel_id=1, source_target_pairs={{0,3},{1,2},{2,1},{3,0},{4,7},{5,6},{6,5},{7,4},{8,11},{9,10},{10,... | collective-permute-start | bytes 221192 | tf_op jit(solution)/shard_map/ppermute | solution.py:278
  17.9 11.1 %collective-permute-start.3 = (bf16[12,24,128]{2,1,0:T(8,128)(2,1)S(1)}, bf16[12,24,128]{2,1,0:T(8,128)(2,1)S(1)}, u32[]{:S(2)}, u32[]{:S(2)}) collective-permute-start(bf16[12,24,128]{2,1,0:T(8,128)(2,1)S(1)} %get-tuple-element.24), channel_id=1, source_target_pairs={{0,2},{1,3},{2,0},{3,1},{4,6},{5,7},{6,4},{7,5},{8,10},{9,11},{10,... | collective-permute-start | bytes 221192 | tf_op jit(solution)/shard_map/ppermute | solution.py:278
  25.0 5.0 %collective-permute-start.8 = (bf16[12,24,128]{2,1,0:T(8,128)(2,1)S(1)}, bf16[12,24,128]{2,1,0:T(8,128)(2,1)S(1)}, u32[]{:S(2)}, u32[]{:S(2)}) collective-permute-start(bf16[12,24,128]{2,1,0:T(8,128)(2,1)S(1)} %get-tuple-element.28.refs_0_), channel_id=1, source_target_pairs={{0,1},{1,0},{2,3},{3,2},{4,5},{5,4},{6,7},{7,6},{8,9},{9,8},{10,11... | collective-permute-start | bytes 221192 | tf_op jit(solution)/shard_map/ppermute | solution.py:278
  26.5 2.5 %copy-start = (bf16[128,512]{1,0:T(8,128)(2,1)S(1)}, bf16[128,512]{1,0:T(8,128)(2,1)}, u32[]{:S(2)}) copy-start(bf16[128,512]{1,0:T(8,128)(2,1)} %refs_3_.1) | copy-start | bytes 393220
  26.5 2.5 %copy-start.2 = (bf16[128,128]{1,0:T(8,128)(2,1)S(1)}, bf16[128,128]{1,0:T(8,128)(2,1)}, u32[]{:S(2)}) copy-start(bf16[128,128]{1,0:T(8,128)(2,1)} %refs_7_.3) | copy-start | bytes 98308
  26.5 4.4 %collective-permute-start.10 = (bf16[12,24,128]{2,1,0:T(8,128)(2,1)S(1)}, bf16[12,24,128]{2,1,0:T(8,128)(2,1)S(1)}, u32[]{:S(2)}, u32[]{:S(2)}) collective-permute-start(bf16[12,24,128]{2,1,0:T(8,128)(2,1)S(1)} %get-tuple-element.29), channel_id=1, source_target_pairs={{0,3},{1,2},{2,1},{3,0},{4,7},{5,6},{6,5},{7,4},{8,11},{9,10},{10,... | collective-permute-start | bytes 221192 | tf_op jit(solution)/shard_map/ppermute | solution.py:278
  26.5 4.4 %collective-permute-start.9 = (bf16[12,24,128]{2,1,0:T(8,128)(2,1)S(1)}, bf16[12,24,128]{2,1,0:T(8,128)(2,1)S(1)}, u32[]{:S(2)}, u32[]{:S(2)}) collective-permute-start(bf16[12,24,128]{2,1,0:T(8,128)(2,1)S(1)} %get-tuple-element.29), channel_id=1, source_target_pairs={{0,2},{1,3},{2,0},{3,1},{4,6},{5,7},{6,4},{7,5},{8,10},{9,11},{10,... | collective-permute-start | bytes 221192 | tf_op jit(solution)/shard_map/ppermute | solution.py:278
  32.4 1.5 %collective-permute-start.11 = (bf16[12,48,128]{2,1,0:T(8,128)(2,1)S(1)}, bf16[12,48,128]{2,1,0:T(8,128)(2,1)S(1)}, u32[]{:S(2)}, u32[]{:S(2)}) collective-permute-start(bf16[12,48,128]{2,1,0:T(8,128)(2,1)S(1)} %get-tuple-element.33.refs_0_), channel_id=1, source_target_pairs={{0,2},{2,0},{4,6},{6,4},{8,10},{10,8},{12,14},{14,12},{1,3},{3,1},... | collective-permute-start | bytes 442376 | tf_op jit(solution)/shard_map/ppermute | solution.py:270
  32.5 1.5 %collective-permute-start.14 = (bf16[12,24,128]{2,1,0:T(8,128)(2,1)S(1)}, bf16[12,24,128]{2,1,0:T(8,128)(2,1)S(1)}, u32[]{:S(2)}, u32[]{:S(2)}) collective-permute-start(bf16[12,24,128]{2,1,0:T(8,128)(2,1)S(1)} %get-tuple-element.37), channel_id=1, source_target_pairs={{0,2},{2,0},{4,6},{6,4},{8,10},{10,8},{12,14},{14,12},{1,3},{3,1},... | collective-permute-start | bytes 221192 | tf_op jit(solution)/shard_map/ppermute | solution.py:270
  33.0 5.0 %collective-permute-start.12 = (bf16[12,24,128]{2,1,0:T(8,128)(2,1)S(1)}, bf16[12,24,128]{2,1,0:T(8,128)(2,1)S(1)}, u32[]{:S(2)}, u32[]{:S(2)}) collective-permute-start(bf16[12,24,128]{2,1,0:T(8,128)(2,1)S(1)} %get-tuple-element.35), channel_id=1, source_target_pairs={{0,2},{2,0},{4,6},{6,4},{8,10},{10,8},{12,14},{14,12},{1,3},{3,1},... | collective-permute-start | bytes 221192 | tf_op jit(solution)/shard_map/ppermute | solution.py:270
  35.2 13.5 %collective-permute-start.15 = (bf16[12,48,128]{2,1,0:T(8,128)(2,1)S(1)}, bf16[12,48,128]{2,1,0:T(8,128)(2,1)S(1)}, u32[]{:S(2)}, u32[]{:S(2)}) collective-permute-start(bf16[12,48,128]{2,1,0:T(8,128)(2,1)S(1)} %get-tuple-element.38), channel_id=1, source_target_pairs={{0,8},{2,10},{4,12},{6,14},{8,0},{10,2},{12,4},{14,6},{1,9},{3,11}... | collective-permute-start | bytes 442376 | tf_op jit(solution)/shard_map/ppermute | solution.py:270
  35.3 13.4 %collective-permute-start.16 = (bf16[12,48,128]{2,1,0:T(8,128)(2,1)S(1)}, bf16[12,48,128]{2,1,0:T(8,128)(2,1)S(1)}, u32[]{:S(2)}, u32[]{:S(2)}) collective-permute-start(bf16[12,48,128]{2,1,0:T(8,128)(2,1)S(1)} %get-tuple-element.39), channel_id=1, source_target_pairs={{0,12},{2,14},{4,8},{6,10},{8,4},{10,6},{12,0},{14,2},{1,13},{3,15... | collective-permute-start | bytes 442376 | tf_op jit(solution)/shard_map/ppermute | solution.py:270
  38.0 1.5 %copy-start.4 = (bf16[128,128]{1,0:T(8,128)(2,1)S(1)}, bf16[128,128]{1,0:T(8,128)(2,1)}, u32[]{:S(2)}) copy-start(bf16[128,128]{1,0:T(8,128)(2,1)} %w_ref.3) | copy-start | bytes 98308
  38.7 12.1 %collective-permute-start.13 = (bf16[12,48,128]{2,1,0:T(8,128)(2,1)S(1)}, bf16[12,48,128]{2,1,0:T(8,128)(2,1)S(1)}, u32[]{:S(2)}, u32[]{:S(2)}) collective-permute-start(bf16[12,48,128]{2,1,0:T(8,128)(2,1)S(1)} %shard_map.91), channel_id=1, source_target_pairs={{0,4},{2,6},{4,0},{6,2},{8,12},{10,14},{12,8},{14,10},{1,5},{3,7},... | collective-permute-start | bytes 442376 | tf_op jit(solution)/shard_map/ppermute | solution.py:270
  39.9 10.8 %copy-start.3 = (bf16[128,128]{1,0:T(8,128)(2,1)S(1)}, bf16[128,128]{1,0:T(8,128)(2,1)}, u32[]{:S(2)}) copy-start(bf16[128,128]{1,0:T(8,128)(2,1)} %refs_6_.1) | copy-start | bytes 98308

commit v3 on v2

--- a/solution.py
+++ b/solution.py
@@ -10,9 +10,14 @@
 F32, BF16 = jnp.float32, jnp.bfloat16
 VMEM = pl.BlockSpec(memory_space=pltpu.VMEM)
 LIMIT = 40 * 1024 * 1024
-
-
-def call(kernel, outs, args, scratch=(), flops=10_000_000, outside=()):
+FULL = 63 * 1024 * 1024
+
+
+def after(kernel, count, *refs):
+    kernel(*refs[count:])
+
+
+def call(kernel, outs, args, scratch=(), flops=10_000_000, outside=(), limit=LIMIT):
     single = not isinstance(outs, (list, tuple))
     outs = [outs] if single else list(outs)
     moved = sum(a.size * a.dtype.itemsize for a in args) + sum(
@@ -26,7 +31,7 @@
         ],
         out_specs=[VMEM] * len(outs),
         scratch_shapes=list(scratch),
-        compiler_params=pltpu.CompilerParams(vmem_limit_bytes=LIMIT),
+        compiler_params=pltpu.CompilerParams(vmem_limit_bytes=limit),
         cost_estimate=pl.CostEstimate(flops=flops, bytes_accessed=moved, transcendentals=0),
     )(*args)
     return result[0] if single else result
@@ -76,11 +81,11 @@
     return layer_norm(pair.astype(F32)).astype(BF16).reshape(rows * cols, chan)
 
 
-def opening_kernel(pair_hbm, mask_hbm, w_hbm, right_ref, pair_scr, mask_scr, w_scr, sems):
-    rows, cols, chan = pair_scr.shape
+def opening_kernel(pair_hbm, mask_hbm, w_hbm, right_ref, pair_ref, mask_scr, w_scr, sems):
+    rows, cols, chan = pair_ref.shape
     width = w_scr.shape[1]
     copies = [
-        pltpu.make_async_copy(pair_hbm, pair_scr, sems.at[0]),
+        pltpu.make_async_copy(pair_hbm, pair_ref, sems.at[0]),
         pltpu.make_async_copy(w_hbm.at[:, pl.ds(width, width)], w_scr, sems.at[1]),
         pltpu.make_async_copy(mask_hbm, mask_scr, sems.at[2]),
     ]
@@ -89,33 +94,17 @@
     for copy in copies:
         copy.wait()
     value = gated(
-        normed_of(pair_scr[...]), w_scr[...], mask_scr, rows, cols, lax.axis_index("col")
+        normed_of(pair_ref[...]), w_scr[...], mask_scr, rows, cols, lax.axis_index("col")
     )
     right_ref[...] = value.astype(BF16).reshape(right_ref.shape)
 
 
-def left_kernel(pair_ref, mask_ref, w_ref, right_hbm, left_ref):
-    del right_hbm
+def left_kernel(pair_ref, mask_ref, w_ref, left_ref, copy_ref):
     rows, cols, _ = pair_ref.shape
     w = w_ref[:, : w_ref.shape[1] // 2]
     value = gated(normed_of(pair_ref[...]), w, mask_ref, rows, cols, lax.axis_index("col"))
     left_ref[...] = value.astype(BF16).reshape(left_ref.shape)
-
-
-def right_kernel(*refs):
-    firsts, (mask_ref, w_ref, right_ref, own_ref) = refs[:-4], refs[-4:]
-    rows, cols, _ = own_ref.shape
-    pieces = cols // (2 * rows)
-    z, _, x = place()
-    for h, ref in enumerate(firsts):
-
-        @pl.when(((z // pieces) ^ h) == x)
-        def _():
-            own_ref[...] = ref[...]
-
-    w = w_ref[:, w_ref.shape[1] // 2 :]
-    value = gated(normed_of(own_ref[...]), w, mask_ref, rows, cols, x)
-    right_ref[...] = value.astype(BF16).reshape(right_ref.shape)
+    copy_ref[...] = pair_ref[...]
 
 
 def gates_kernel(cols_n, *refs):
@@ -140,65 +129,83 @@
     gate_ref[...] = sigmoid(gate).reshape(gate_ref.shape)
 
 
-def outgoing_kernel(own_left, core_left, *refs):
-    rights, (mine_ref, other_ref, r_scr, l_scr) = refs[:-4], refs[-4:]
+def outgoing_kernel(runs, own_left, core_left, *refs):
+    rights, (mine_ref, other_ref, r_scr, l_scr, o_scr) = refs[:-5], refs[-5:]
     rows, cols, chan = own_left.shape
-    count = len(rights)
-    width = count * rows
     z, _, _ = place()
-    low = z % count
-    for m, ref in enumerate(rights):
-        base = (low ^ m) * rows
-        for j in range(rows):
-            r_scr[pl.ds(base + j, cols, stride=width), :] = ref[j].astype(F32)
     for out_ref, left in ((mine_ref, own_left), (other_ref, core_left)):
         l_scr[...] = left[...].astype(F32).reshape(rows * cols, chan)
-
-        def step(block, totals):
-            for u in range(8):
-                k = block * 8 + u
-                right = r_scr[pl.ds(pl.multiple_of(k * width, 8), width), :]
-                totals = tuple(
-                    t + l_scr[pl.ds(i * cols + k, 1), :] * right for i, t in enumerate(totals)
-                )
-            return totals
-
-        zero = jnp.zeros((width, chan), F32)
-        totals = lax.fori_loop(0, cols // 8, step, (zero,) * rows)
-        for i, t in enumerate(totals):
-            out_ref[i] = t.astype(out_ref.dtype)
-
-
-def first_kernel(cols_n, h, *refs):
-    parts = refs[: 2 * cols_n]
-    pair_ref, gate_ref, mask_ref, final_ref, w_ref = refs[2 * cols_n : 2 * cols_n + 5]
-    first_ref, mine_ref, other_ref, scr, half_scr = refs[2 * cols_n + 5 :]
+        done = 0
+        for count in runs:
+            used = count * rows
+            width = -(-used // 8) * 8
+            if out_ref is mine_ref or len(runs) > 1:
+                for m, ref in enumerate(rights[done : done + count]):
+                    base = ((z % count) ^ m) * rows
+                    for j in range(rows):
+                        r_scr[pl.ds(base + j, cols, stride=width), :] = ref[j].astype(F32)
+
+            def step(block, totals):
+                for u in range(8):
+                    k = block * 8 + u
+                    right = r_scr[pl.ds(pl.multiple_of(k * width, 8), width), :]
+                    totals = tuple(
+                        t + l_scr[pl.ds(i * cols + k, 1), :] * right for i, t in enumerate(totals)
+                    )
+                return totals
+
+            zero = jnp.zeros((width, chan), F32)
+            totals = lax.fori_loop(0, cols // 8, step, (zero,) * rows)
+            for i, t in enumerate(totals):
+                o_scr[pl.ds(rows * done * rows + i * used, used), :] = t[:used]
+            done += count
+        out_ref[...] = o_scr[...].astype(BF16)
+
+
+def first_kernel(cols_n, h, groups, *refs):
+    parts, refs = refs[: 2 * cols_n * len(groups)], refs[2 * cols_n * len(groups) :]
+    pair_ref, gate_ref, mask_ref, final_ref, w_ref = refs[:5]
+    earlier, refs = refs[5:-6], refs[-6:]
+    first_ref, right_ref, mine_ref, other_ref, scr, half_scr = refs
     rows, cols, chan = pair_ref.shape
     pieces = cols // (2 * rows)
-    z, core, _ = place()
-    for group, side in ((parts[:cols_n], core), (parts[cols_n:], 1 - core)):
-        value = group[0][...].astype(F32)
-        for ref in group[1:]:
-            value = value + ref[...].astype(F32)
-        half_scr[...] = value.reshape(half_scr.shape)
-        for i in range(rows):
-            for q in range(pieces):
-                part = half_scr[pl.ds((i * pieces + q) * rows, rows), :]
-                scr[pl.ds(i * cols + (2 * q + side) * rows, rows), :] = part
+    z, core, x = place()
+    for n, (begin, start, count) in enumerate(groups):
+        group = parts[2 * cols_n * n : 2 * cols_n * (n + 1)]
+        size = rows * count * rows
+        for some, side in ((group[:cols_n], core), (group[cols_n:], 1 - core)):
+            value = some[0][pl.ds(begin, size), :].astype(F32)
+            for ref in some[1:]:
+                value = value + ref[pl.ds(begin, size), :].astype(F32)
+            half_scr[pl.ds(0, size), :] = value
+            for i in range(rows):
+                for p in range(count):
+                    q = p if count == pieces else (z % pieces) ^ start
+                    part = half_scr[pl.ds((i * count + p) * rows, rows), :]
+                    scr[pl.ds(i * cols + (2 * q + side) * rows, rows), :] = part
     mixed = layer_norm(scr[...]).astype(BF16)
     update = jnp.dot(mixed, final_ref[...], preferred_element_type=F32)
     pair = pair_ref[...].astype(F32).reshape(rows * cols, chan)
     first = (pair + gate_ref[...].reshape(rows * cols, chan) * update).astype(BF16)
     first_ref[...] = first.reshape(first_ref.shape)
     normed = layer_norm(first.astype(F32)).astype(BF16)
-    w = w_ref[:, : w_ref.shape[1] // 2]
-    scr[...] = gated(normed, w, mask_ref, rows, cols, (z // pieces) ^ h)
+    width = w_ref.shape[1] // 2
+    block = (z // pieces) ^ h
+    scr[...] = gated(normed, w_ref[:, :width], mask_ref, rows, cols, block)
     for out_ref, side in ((mine_ref, core), (other_ref, 1 - core)):
         for i in range(rows):
             for q in range(pieces):
                 part = scr[pl.ds(i * cols + (2 * q + side) * rows, rows), :]
                 half_scr[pl.ds((i * pieces + q) * rows, rows), :] = part
         out_ref[...] = half_scr[...].astype(BF16).reshape(out_ref.shape)
+    right = gated(normed, w_ref[:, width:], mask_ref, rows, cols, block)
+    right_ref[...] = right.astype(BF16).reshape(right_ref.shape)
+    for g in range(len(earlier) // 2):
+
+        @pl.when(((z // pieces) ^ g) == x)
+        def _():
+            first_ref[...] = earlier[2 * g][...]
+            right_ref[...] = earlier[2 * g + 1][...]
 
 
 def incoming_kernel(steps, *refs):
@@ -289,62 +296,75 @@
         ],
         flops=100_000_000,
         outside=(0, 1, 2),
-    )
-    rights = [right] + [None] * (chips - 1)
-    for m in reversed(range(1, chips)):
-        rights[m] = along_row(right, 2 * m)
-    left = call(
-        left_kernel,
-        block,
-        [pair_rep, mask, out_project, right],
+        limit=FULL,
+    )
+    rights = {0: right}
+    bit = chips // 2
+    while bit:
+        for m in list(rights):
+            rights[m | bit] = along_row(rights[m], 2 * bit)
+        bit //= 2
+    left, pair_copy = call(
+        functools.partial(after, left_kernel, 1),
+        [block, block],
+        [right, pair_rep, mask, out_project],
         flops=100_000_000,
-        outside=(3,),
-    )
-    core_left = along_row(left, 1)
-    pairs = [pair_rep] + [shift(pair_rep, dx, 0) for dx in range(1, cols_n)]
+        outside=(0,),
+    )
+    pairs = [pair_copy] + [shift(pair_copy, dx, 0) for dx in range(1, cols_n)]
     gates = call(
         functools.partial(gates_kernel, cols_n),
         [block, block32] * cols_n,
         pairs + [out_gating],
         flops=100_000_000,
     )
+    core_left = along_row(left, 1)
+    runs = [pieces] * (cols_n - 1) + [1] * (pieces - 1)
+    exchanged = []
+    for counts, blocks in ((runs, list(range(chips - 1))), ([1], [chips - 1])):
+        out = shape((rows * len(blocks) * rows, chan), BF16)
+        mine, other = call(
+            functools.partial(outgoing_kernel, counts),
+            [out, out],
+            [left, core_left] + [rights[m] for m in blocks],
+            scratch=[
+                pltpu.VMEM((cols * (-(-max(counts) * rows // 8) * 8), chan), F32),
+                pltpu.VMEM((rows * cols, chan), F32),
+                pltpu.VMEM(out.shape, F32),
+            ],
+            flops=250_000_000 * len(blocks),
+        )
+        parts = [mine] + [shift(mine, dx, 0) for dx in range(1, cols_n)]
+        exchanged.append(parts + [shift(other, dx, 1) for dx in range(cols_n)])
     firsts, lefts = [], []
     for h in range(cols_n):
-        mine, other = call(
-            outgoing_kernel,
-            [shape(half, BF16), shape(half, BF16)],
-            [left, core_left] + rights[h * pieces : (h + 1) * pieces],
-            scratch=[
-                pltpu.VMEM((cols * pieces * rows, chan), F32),
-                pltpu.VMEM((rows * cols, chan), F32),
-            ],
-            flops=500_000_000,
-        )
-        parts = [mine] + [shift(mine, dx, 0) for dx in range(1, cols_n)]
-        parts += [shift(other, dx, 1) for dx in range(cols_n)]
-        first, left_mine, left_other = call(
-            functools.partial(first_kernel, cols_n, h),
-            [block, shape(half, BF16), shape(half, BF16)],
-            parts + list(gates[2 * h : 2 * h + 2]) + [mask, out_final, in_project],
+        area = rows * rows
+        if h < cols_n - 1:
+            groups, parts, earlier = [(h * pieces * area, 0, pieces)], exchanged[0], []
+        else:
+            groups = [((h * pieces + p) * area, p, 1) for p in range(pieces - 1)]
+            groups.append((0, pieces - 1, 1))
+            parts, earlier = exchanged[0] * (pieces - 1) + exchanged[1], firsts
+        first, right, left_mine, left_other = call(
+            functools.partial(first_kernel, cols_n, h, groups),
+            [block, block, shape(half, BF16), shape(half, BF16)],
+            parts + list(gates[2 * h : 2 * h + 2]) + [mask, out_final, in_project] + earlier,
             scratch=[
                 pltpu.VMEM((rows * cols, chan), F32),
                 pltpu.VMEM((rows * pieces * rows, chan), F32),
             ],
-            flops=200_000_000,
+            flops=300_000_000,
         )
-        firsts.append(first)
+        firsts += [first, right]
         lefts.append([left_mine, along_row(left_other, 1)])
 
-    right, first = call(
-        right_kernel, [block, block], firsts + [mask, in_project], flops=100_000_000
-    )
     core_right = along_row(right, 1)
 
     def partial_products(steps):
         used = lefts[steps[0] // pieces : steps[-1] // pieces + 1]
         return call(
             functools.partial(incoming_kernel, steps),
-            [block32 if m == 0 else block for m in steps],
+            [block if m else block32 for m in steps],
             [right, core_right] + sum(used, []),
             scratch=[
                 pltpu.VMEM((2 * len(used) * rows * pieces * rows, chan), F32),
@@ -353,11 +373,10 @@
             flops=200_000_000 * len(steps),
         )
 
-    far = list(range(pieces, chips))
     parts = [None] * chips
+    far, near = list(range(pieces, chips)), list(range(1, pieces))
     for m, value in zip(far, partial_products(far)):
         parts[m] = along_row(value, 2 * m)
-    near = list(range(1, pieces))
     for m, value in zip(near, partial_products(near)):
         parts[m] = along_row(value, 2 * m)
     parts[0] = partial_products([0])[0]

time: 52 us -> 47.2 us (0.908)
  waiting for transfers between devices: 21.3 us -> 15 us
  starting transfers between devices: 15.4 us -> 18.1 us
  local copies, waits for them, and re-layouts: 1.58 us -> 0.97 us
    ppermute x10, waiting for transfers between devices: 20.3 us -> 13.9 us  [along_row(): return lax.ppermute(v, 'row', [(i, i ^ bits) for i in range(rows_n)])]
    ppermute x7, starting transfers between devices: 5.43 us -> 6.98 us  [shift(): return lax.ppermute(v, ('row', 'col'), pairs)]
    ppermute x10, starting transfers between devices: 10 us -> 11.1 us  [along_row(): return lax.ppermute(v, 'row', [(i, i ^ bits) for i in range(rows_n)])]
    unnamed x14 -> x20, local copies, waits for them, and re-layouts: 1.58 us -> 0.97 us
    pallas_call x13 -> x12, Pallas kernels: 13.3 us -> 12.8 us  [call(): pl.pallas_call(kernel, out_shape=outs, in_specs=[pl.BlockSpec(memory_spac...]
  transfers between devices with their start and end apart: 17 -> 17, of which waited for: 7 -> 6; matrix products, arithmetic and copies ran while one was open for 0% -> 0% of each run, Pallas kernels for 16% -> 18%
where the time goes in v3:
time: 47.2 us; the launch traced here: 47 us
  starting transfers between devices  18.1 us (38%)
  waiting for transfers between devices  15 us (32%)
  Pallas kernels  12.8 us (27%)
  local copies, waits for them, and re-layouts  0.97 us (2%)
    ppermute x10, waiting for transfers between devices, along_row(): return lax.ppermute(v, 'row', [(i, i ^ bits) for i in range(rows_n)])  13.9 us
    pallas_call x12, Pallas kernels, call(): pl.pallas_call(kernel, out_shape=outs, in_specs=[pl.BlockSpec(memory_spac...  12.8 us
    ppermute x10, starting transfers between devices, along_row(): return lax.ppermute(v, 'row', [(i, i ^ bits) for i in range(rows_n)])  11.1 us
    ppermute x7, starting transfers between devices, shift(): return lax.ppermute(v, ('row', 'col'), pairs)  6.98 us
    ppermute x7, waiting for transfers between devices, shift(): return lax.ppermute(v, ('row', 'col'), pairs)  1.08 us
    unnamed x20, local copies, waits for them, and re-layouts  0.97 us
  transfers between devices with their start and end apart: 17, of which 6 were waited for; matrix products, arithmetic and copies ran while one was open for 0% of the time, Pallas kernels for 18%

profile of v3, /device:TPU:0, one launch (start us, length us, event | category | flops | bytes accessed | tf_op | source)
XLA Modules:
  0.0 47.0 jit_solution(3906296115954820365)
XLA Ops:
  0.0 2.1 %shard_map.82.refs_0_ = bf16[12,48,128]{2,1,0:T(8,128)(2,1)} custom-call(bf16[12,48,128]{2,1,0:T(8,128)(2,1)} %refs_1_.1, s32[1,96]{1,0:T(1,128)} %bitcast.1, bf16[128,512]{1,0:T(8,128)(2,1)} %refs_3_.1), custom_call_target="tpu_custom_call" | custom-call | flops 100000000 | bytes 426368 | tf_op jit(solution)/shard_map/pallas_call | solution.py:26
  2.1 4.1 %collective-permute-start.2 = (bf16[12,48,128]{2,1,0:T(8,128)(2,1)}, bf16[12,48,128]{2,1,0:T(8,128)(2,1)S(1)}, u32[]{:S(2)}, u32[]{:S(2)}) collective-permute-start(bf16[12,48,128]{2,1,0:T(8,128)(2,1)} %shard_map.82.refs_0_), channel_id=1, source_target_pairs={{0,8},{2,10},{4,12},{6,14},{8,0},{10,2},{12,4},{14,6},{1,9},{3,11}... | collective-permute-start | bytes 442376 | tf_op jit(solution)/shard_map/ppermute | solution.py:277
  6.2 1.6 %collective-permute-start.1 = (bf16[12,48,128]{2,1,0:T(8,128)(2,1)}, bf16[12,48,128]{2,1,0:T(8,128)(2,1)S(1)}, u32[]{:S(2)}, u32[]{:S(2)}) collective-permute-start(bf16[12,48,128]{2,1,0:T(8,128)(2,1)} %shard_map.82.refs_0_), channel_id=1, source_target_pairs={{0,4},{2,6},{4,0},{6,2},{8,12},{10,14},{12,8},{14,10},{1,5},{3,7},... | collective-permute-start | bytes 442376 | tf_op jit(solution)/shard_map/ppermute | solution.py:277
  7.8 0.9 %copy-done.1 = bf16[12,48,128]{2,1,0:T(8,128)(2,1)S(1)} copy-done((bf16[12,48,128]{2,1,0:T(8,128)(2,1)S(1)}, bf16[12,48,128]{2,1,0:T(8,128)(2,1)}, u32[]{:S(2)}) %copy-start.1) | copy-done | bytes 147480
  9.3 1.6 %collective-permute-start.10 = (bf16[12,48,128]{2,1,0:T(8,128)(2,1)S(1)}, bf16[12,48,128]{2,1,0:T(8,128)(2,1)S(1)}, u32[]{:S(2)}, u32[]{:S(2)}) collective-permute-start(bf16[12,48,128]{2,1,0:T(8,128)(2,1)S(1)} %get-tuple-element.30.refs_0_), channel_id=1, source_target_pairs={{0,1},{1,0},{2,3},{3,2},{4,5},{5,4},{6,7},{7,6},{8,9},{9,8},{10,11... | collective-permute-start | bytes 442376 | tf_op jit(solution)/shard_map/ppermute | solution.py:285
  10.8 2.7 %collective-permute-done.2.refs_2_ = bf16[12,48,128]{2,1,0:T(8,128)(2,1)S(1)} collective-permute-done((bf16[12,48,128]{2,1,0:T(8,128)(2,1)}, bf16[12,48,128]{2,1,0:T(8,128)(2,1)S(1)}, u32[]{:S(2)}, u32[]{:S(2)}) %collective-permute-start.2) | collective-permute-done | bytes 147488 | tf_op jit(solution)/shard_map/ppermute | solution.py:277
  13.6 0.7 %collective-permute-start.6 = (bf16[12,48,128]{2,1,0:T(8,128)(2,1)S(1)}, bf16[12,48,128]{2,1,0:T(8,128)(2,1)S(1)}, u32[]{:S(2)}, u32[]{:S(2)}) collective-permute-start(bf16[12,48,128]{2,1,0:T(8,128)(2,1)S(1)} %collective-permute-done.2.refs_2_), channel_id=1, source_target_pairs={{0,4},{2,6},{4,0},{6,2},{8,12},{10,14},{12,8},{14,10},{1,5},{3,7},... | collective-permute-start | bytes 442376 | tf_op jit(solution)/shard_map/ppermute | solution.py:277
  14.3 2.3 %shard_map.84 = (bf16[432,128]{1,0:T(8,128)(2,1)S(1)}, bf16[432,128]{1,0:T(8,128)(2,1)S(1)}) custom-call(bf16[12,48,128]{2,1,0:T(8,128)(2,1)S(1)} %get-tuple-element.25.own_left, bf16[12,48,128]{2,1,0:T(8,128)(2,1)S(1)} %collective-permute-done.core_left, bf16[12,48,128]{2,1,0:T(8,128)(2,1)S(1)} %copy-done.2, ...), custom_call_target="tpu_custom_call" | custom-call | flops 750000000 | bytes 958464 | tf_op jit(solution)/shard_map/pallas_call | solution.py:26
  16.6 0.9 %collective-permute-start.5 = (bf16[432,128]{1,0:T(8,128)(2,1)S(1)}, bf16[432,128]{1,0:T(8,128)(2,1)S(1)}, u32[]{:S(2)}, u32[]{:S(2)}) collective-permute-start(bf16[432,128]{1,0:T(8,128)(2,1)S(1)} %get-tuple-element.27), channel_id=1, source_target_pairs={{0,3},{1,2},{2,1},{3,0},{4,7},{5,6},{6,5},{7,4},{8,11},{9,10},{10,... | collective-permute-start | bytes 331784 | tf_op jit(solution)/shard_map/ppermute | solution.py:285
  17.5 0.8 %collective-permute-start.4 = (bf16[432,128]{1,0:T(8,128)(2,1)S(1)}, bf16[432,128]{1,0:T(8,128)(2,1)S(1)}, u32[]{:S(2)}, u32[]{:S(2)}) collective-permute-start(bf16[432,128]{1,0:T(8,128)(2,1)S(1)} %get-tuple-element.27), channel_id=1, source_target_pairs={{0,2},{1,3},{2,0},{3,1},{4,6},{5,7},{6,4},{7,5},{8,10},{9,11},{10,... | collective-permute-start | bytes 331784 | tf_op jit(solution)/shard_map/ppermute | solution.py:285
  18.8 0.9 %shard_map.85 = (bf16[144,128]{1,0:T(8,128)(2,1)S(1)}, bf16[144,128]{1,0:T(8,128)(2,1)S(1)}) custom-call(bf16[12,48,128]{2,1,0:T(8,128)(2,1)S(1)} %get-tuple-element.25.own_left, bf16[12,48,128]{2,1,0:T(8,128)(2,1)S(1)} %collective-permute-done.core_left, bf16[12,48,128]{2,1,0:T(8,128)(2,1)S(1)} %collective-permute-done.6.refs_0_), custom_call_target="tpu_custom_call" | custom-call | flops 250000000 | bytes 516096 | tf_op jit(solution)/shard_map/pallas_call | solution.py:26
  19.7 0.9 %collective-permute-start.9 = (bf16[144,128]{1,0:T(8,128)(2,1)S(1)}, bf16[144,128]{1,0:T(8,128)(2,1)S(1)}, u32[]{:S(2)}, u32[]{:S(2)}) collective-permute-start(bf16[144,128]{1,0:T(8,128)(2,1)S(1)} %get-tuple-element.29), channel_id=1, source_target_pairs={{0,3},{1,2},{2,1},{3,0},{4,7},{5,6},{6,5},{7,4},{8,11},{9,10},{10,... | collective-permute-start | bytes 110600 | tf_op jit(solution)/shard_map/ppermute | solution.py:285
  20.6 0.8 %collective-permute-start.8 = (bf16[144,128]{1,0:T(8,128)(2,1)S(1)}, bf16[144,128]{1,0:T(8,128)(2,1)S(1)}, u32[]{:S(2)}, u32[]{:S(2)}) collective-permute-start(bf16[144,128]{1,0:T(8,128)(2,1)S(1)} %get-tuple-element.29), channel_id=1, source_target_pairs={{0,2},{1,3},{2,0},{3,1},{4,6},{5,7},{6,4},{7,5},{8,10},{9,11},{10,... | collective-permute-start | bytes 110600 | tf_op jit(solution)/shard_map/ppermute | solution.py:285
  22.0 1.5 %collective-permute-start.7 = (bf16[144,128]{1,0:T(8,128)(2,1)S(1)}, bf16[144,128]{1,0:T(8,128)(2,1)S(1)}, u32[]{:S(2)}, u32[]{:S(2)}) collective-permute-start(bf16[144,128]{1,0:T(8,128)(2,1)S(1)} %get-tuple-element.28.refs_4_), channel_id=1, source_target_pairs={{0,1},{1,0},{2,3},{3,2},{4,5},{5,4},{6,7},{7,6},{8,9},{9,8},{10,11... | collective-permute-start | bytes 110600 | tf_op jit(solution)/shard_map/ppermute | solution.py:285
  23.5 0.9 %shard_map.86 = (bf16[12,48,128]{2,1,0:T(8,128)(2,1)S(1)}, f32[12,48,128]{2,1,0:T(8,128)S(1)}, bf16[12,48,128]{2,1,0:T(8,128)(2,1)S(1)}, f32[12,48,128]{2,1,0:T(8,128)S(1)}) custom-call(bf16[12,48,128]{2,1,0:T(8,128)(2,1)S(1)} %get-tuple-element.30.refs_0_, bf16[12,48,128]{2,1,0:T(8,128)(2,1)S(1)} %collective-permute-done.10.refs_1_, ...), custom_call_target="tpu_custom_call" | custom-call | flops 100000000 | bytes 1212416 | tf_op jit(solution)/shard_map/pallas_call | solution.py:26
  24.4 1.1 %shard_map.87 = (bf16[12,48,128]{2,1,0:T(8,128)(2,1)S(1)}, bf16[12,48,128]{2,1,0:T(8,128)(2,1)S(1)}, bf16[12,24,128]{2,1,0:T(8,128)(2,1)S(1)}, bf16[12,24,128]{2,1,0:T(8,128)(2,1)S(1)}) custom-call(bf16[432,128]{1,0:T(8,128)(2,1)S(1)} %get-tuple-element.26.refs_0_, bf16[432,128]{1,0:T(8,128)(2,1)S(1)} %collective-permute-done.3.refs_1_, ...), custom_call_target="tpu_custom_call" | custom-call | flops 300000000 | bytes 1491328 | tf_op jit(solution)/shard_map/pallas_call | solution.py:26
  26.0 1.1 %shard_map.88 = (bf16[12,48,128]{2,1,0:T(8,128)(2,1)S(1)}, bf16[12,48,128]{2,1,0:T(8,128)(2,1)S(1)}, bf16[12,24,128]{2,1,0:T(8,128)(2,1)S(1)}, bf16[12,24,128]{2,1,0:T(8,128)(2,1)S(1)}) custom-call(bf16[432,128]{1,0:T(8,128)(2,1)S(1)} %get-tuple-element.26.refs_0_, bf16[432,128]{1,0:T(8,128)(2,1)S(1)} %collective-permute-done.3.refs_1_, ...), custom_call_target="tpu_custom_call" | custom-call | flops 300000000 | bytes 1933696 | tf_op jit(solution)/shard_map/pallas_call | solution.py:26
  27.8 0.9 %collective-permute-done.14.refs_3_ = bf16[12,24,128]{2,1,0:T(8,128)(2,1)S(1)} collective-permute-done((bf16[12,24,128]{2,1,0:T(8,128)(2,1)S(1)}, bf16[12,24,128]{2,1,0:T(8,128)(2,1)S(1)}, u32[]{:S(2)}, u32[]{:S(2)}) %collective-permute-start.14) | collective-permute-done | bytes 73760 | tf_op jit(solution)/shard_map/ppermute | solution.py:277
  28.7 1.3 %shard_map.91 = (bf16[12,48,128]{2,1,0:T(8,128)(2,1)S(1)}, bf16[12,48,128]{2,1,0:T(8,128)(2,1)S(1)}) custom-call(bf16[12,48,128]{2,1,0:T(8,128)(2,1)S(1)} %get-tuple-element.37.refs_0_, bf16[12,48,128]{2,1,0:T(8,128)(2,1)S(1)} %collective-permute-done.11.refs_1_, bf16[12,24,128]{2,1,0:T(8,128)(2,1)S(1)} %get-tuple-element.40.refs_2_, ...), custom_call_target="tpu_custom_call" | custom-call | flops 400000000 | bytes 737280 | tf_op jit(solution)/shard_map/pallas_call | solution.py:26
  29.9 3.3 %collective-permute-start.15 = (bf16[12,48,128]{2,1,0:T(8,128)(2,1)S(1)}, bf16[12,48,128]{2,1,0:T(8,128)(2,1)S(1)}, u32[]{:S(2)}, u32[]{:S(2)}) collective-permute-start(bf16[12,48,128]{2,1,0:T(8,128)(2,1)S(1)} %get-tuple-element.42), channel_id=1, source_target_pairs={{0,8},{2,10},{4,12},{6,14},{8,0},{10,2},{12,4},{14,6},{1,9},{3,11}... | collective-permute-start | bytes 442376 | tf_op jit(solution)/shard_map/ppermute | solution.py:277
  33.7 0.7 %shard_map.90 = bf16[12,48,128]{2,1,0:T(8,128)(2,1)S(1)} custom-call(bf16[12,48,128]{2,1,0:T(8,128)(2,1)S(1)} %get-tuple-element.37.refs_0_, bf16[12,48,128]{2,1,0:T(8,128)(2,1)S(1)} %collective-permute-done.11.refs_1_, bf16[12,24,128]{2,1,0:T(8,128)(2,1)S(1)} %get-tuple-element.38.refs_2_, bf16[12,24,128]{2,1,0:T(8,128)(2,1)S(1)} %collective-permute-done.12.refs_3_), custom_call_target="tpu_custom_call" | custom-call | flops 200000000 | bytes 589824 | tf_op jit(solution)/shard_map/pallas_call | solution.py:26
  35.7 8.5 %collective-permute-done.15.refs_2_ = bf16[12,48,128]{2,1,0:T(8,128)(2,1)S(1)} collective-permute-done((bf16[12,48,128]{2,1,0:T(8,128)(2,1)S(1)}, bf16[12,48,128]{2,1,0:T(8,128)(2,1)S(1)}, u32[]{:S(2)}, u32[]{:S(2)}) %collective-permute-start.15) | collective-permute-done | bytes 147488 | tf_op jit(solution)/shard_map/ppermute | solution.py:277
  44.1 1.8 %collective-permute-done.13.refs_1_ = bf16[12,48,128]{2,1,0:T(8,128)(2,1)S(1)} collective-permute-done((bf16[12,48,128]{2,1,0:T(8,128)(2,1)S(1)}, bf16[12,48,128]{2,1,0:T(8,128)(2,1)S(1)}, u32[]{:S(2)}, u32[]{:S(2)}) %collective-permute-start.13) | collective-permute-done | bytes 147488 | tf_op jit(solution)/shard_map/ppermute | solution.py:277
  46.0 1.0 %shard_map.93 = bf16[12,48,128]{2,1,0:T(8,128)(2,1)} custom-call(f32[12,48,128]{2,1,0:T(8,128)S(1)} %shard_map.89.refs_0_, bf16[12,48,128]{2,1,0:T(8,128)(2,1)S(1)} %collective-permute-done.13.refs_1_, bf16[12,48,128]{2,1,0:T(8,128)(2,1)S(1)} %collective-permute-done.15.refs_2_, bf16[12,48,128]{2,1,0:T(8,128)(2,1)S(1)} %collective-permute-done.16.refs_3_, ...), custom_call_target="tpu_custom_call" | custom-call | flops 100000000 | bytes 1359872 | tf_op jit(solution)/shard_map/pallas_call | solution.py:26
  (42 shorter events, 4.6 us)
Async XLA Ops:
  0.0 7.8 %copy-start = (bf16[12,48,128]{2,1,0:T(8,128)(2,1)S(1)}, bf16[12,48,128]{2,1,0:T(8,128)(2,1)}, u32[]{:S(2)}) copy-start(bf16[12,48,128]{2,1,0:T(8,128)(2,1)} %refs_1_.1) | copy-start | bytes 442372
  0.0 7.8 %copy-start.3 = (bf16[128,512]{1,0:T(8,128)(2,1)S(1)}, bf16[128,512]{1,0:T(8,128)(2,1)}, u32[]{:S(2)}) copy-start(bf16[128,512]{1,0:T(8,128)(2,1)} %refs_3_.1) | copy-start | bytes 393220
  0.0 7.8 %copy-start.8 = (s32[96]{0:T(128)S(1)}, s32[96]{0:T(128)}, u32[]{:S(2)}) copy-start(s32[96]{0:T(128)} %param.9) | copy-start | bytes 1156
  2.1 11.4 %collective-permute-start.2 = (bf16[12,48,128]{2,1,0:T(8,128)(2,1)}, bf16[12,48,128]{2,1,0:T(8,128)(2,1)S(1)}, u32[]{:S(2)}, u32[]{:S(2)}) collective-permute-start(bf16[12,48,128]{2,1,0:T(8,128)(2,1)} %shard_map.82.refs_0_), channel_id=1, source_target_pairs={{0,8},{2,10},{4,12},{6,14},{8,0},{10,2},{12,4},{14,6},{1,9},{3,11}... | collective-permute-start | bytes 442376 | tf_op jit(solution)/shard_map/ppermute | solution.py:277
  6.2 8.0 %collective-permute-start.1 = (bf16[12,48,128]{2,1,0:T(8,128)(2,1)}, bf16[12,48,128]{2,1,0:T(8,128)(2,1)S(1)}, u32[]{:S(2)}, u32[]{:S(2)}) collective-permute-start(bf16[12,48,128]{2,1,0:T(8,128)(2,1)} %shard_map.82.refs_0_), channel_id=1, source_target_pairs={{0,4},{2,6},{4,0},{6,2},{8,12},{10,14},{12,8},{14,10},{1,5},{3,7},... | collective-permute-start | bytes 442376 | tf_op jit(solution)/shard_map/ppermute | solution.py:277
  8.8 5.5 %copy-start.2 = (bf16[12,48,128]{2,1,0:T(8,128)(2,1)S(1)}, bf16[12,48,128]{2,1,0:T(8,128)(2,1)}, u32[]{:S(2)}) copy-start(bf16[12,48,128]{2,1,0:T(8,128)(2,1)} %shard_map.82.refs_0_) | copy-start | bytes 442372
  9.2 5.1 %collective-permute-start = (bf16[12,48,128]{2,1,0:T(8,128)(2,1)S(1)}, bf16[12,48,128]{2,1,0:T(8,128)(2,1)S(1)}, u32[]{:S(2)}, u32[]{:S(2)}) collective-permute-start(bf16[12,48,128]{2,1,0:T(8,128)(2,1)S(1)} %get-tuple-element.25.own_left), channel_id=1, source_target_pairs={{0,2},{2,0},{4,6},{6,4},{8,10},{10,8},{12,14},{14,12},{1,3},{3,1},... | collective-permute-start | bytes 442376 | tf_op jit(solution)/shard_map/ppermute | solution.py:277
  9.3 11.3 %collective-permute-start.10 = (bf16[12,48,128]{2,1,0:T(8,128)(2,1)S(1)}, bf16[12,48,128]{2,1,0:T(8,128)(2,1)S(1)}, u32[]{:S(2)}, u32[]{:S(2)}) collective-permute-start(bf16[12,48,128]{2,1,0:T(8,128)(2,1)S(1)} %get-tuple-element.30.refs_0_), channel_id=1, source_target_pairs={{0,1},{1,0},{2,3},{3,2},{4,5},{5,4},{6,7},{7,6},{8,9},{9,8},{10,11... | collective-permute-start | bytes 442376 | tf_op jit(solution)/shard_map/ppermute | solution.py:285
  13.6 5.2 %collective-permute-start.6 = (bf16[12,48,128]{2,1,0:T(8,128)(2,1)S(1)}, bf16[12,48,128]{2,1,0:T(8,128)(2,1)S(1)}, u32[]{:S(2)}, u32[]{:S(2)}) collective-permute-start(bf16[12,48,128]{2,1,0:T(8,128)(2,1)S(1)} %collective-permute-done.2.refs_2_), channel_id=1, source_target_pairs={{0,4},{2,6},{4,0},{6,2},{8,12},{10,14},{12,8},{14,10},{1,5},{3,7},... | collective-permute-start | bytes 442376 | tf_op jit(solution)/shard_map/ppermute | solution.py:277
  16.6 5.4 %collective-permute-start.5 = (bf16[432,128]{1,0:T(8,128)(2,1)S(1)}, bf16[432,128]{1,0:T(8,128)(2,1)S(1)}, u32[]{:S(2)}, u32[]{:S(2)}) collective-permute-start(bf16[432,128]{1,0:T(8,128)(2,1)S(1)} %get-tuple-element.27), channel_id=1, source_target_pairs={{0,3},{1,2},{2,1},{3,0},{4,7},{5,6},{6,5},{7,4},{8,11},{9,10},{10,... | collective-permute-start | bytes 331784 | tf_op jit(solution)/shard_map/ppermute | solution.py:285
  17.5 6.9 %collective-permute-start.4 = (bf16[432,128]{1,0:T(8,128)(2,1)S(1)}, bf16[432,128]{1,0:T(8,128)(2,1)S(1)}, u32[]{:S(2)}, u32[]{:S(2)}) collective-permute-start(bf16[432,128]{1,0:T(8,128)(2,1)S(1)} %get-tuple-element.27), channel_id=1, source_target_pairs={{0,2},{1,3},{2,0},{3,1},{4,6},{5,7},{6,4},{7,5},{8,10},{9,11},{10,... | collective-permute-start | bytes 331784 | tf_op jit(solution)/shard_map/ppermute | solution.py:285
  18.3 5.2 %copy-start.9 = (bf16[128,128]{1,0:T(8,128)(2,1)S(1)}, bf16[128,128]{1,0:T(8,128)(2,1)}, u32[]{:S(2)}) copy-start(bf16[128,128]{1,0:T(8,128)(2,1)} %refs_2_.1) | copy-start | bytes 98308
  18.3 6.2 %collective-permute-start.3 = (bf16[432,128]{1,0:T(8,128)(2,1)S(1)}, bf16[432,128]{1,0:T(8,128)(2,1)S(1)}, u32[]{:S(2)}, u32[]{:S(2)}) collective-permute-start(bf16[432,128]{1,0:T(8,128)(2,1)S(1)} %get-tuple-element.26.refs_0_), channel_id=1, source_target_pairs={{0,1},{1,0},{2,3},{3,2},{4,5},{5,4},{6,7},{7,6},{8,9},{9,8},{10,11... | collective-permute-start | bytes 331784 | tf_op jit(solution)/shard_map/ppermute | solution.py:285
  19.7 6.3 %collective-permute-start.9 = (bf16[144,128]{1,0:T(8,128)(2,1)S(1)}, bf16[144,128]{1,0:T(8,128)(2,1)S(1)}, u32[]{:S(2)}, u32[]{:S(2)}) collective-permute-start(bf16[144,128]{1,0:T(8,128)(2,1)S(1)} %get-tuple-element.29), channel_id=1, source_target_pairs={{0,3},{1,2},{2,1},{3,0},{4,7},{5,6},{6,5},{7,4},{8,11},{9,10},{10,... | collective-permute-start | bytes 110600 | tf_op jit(solution)/shard_map/ppermute | solution.py:285
  20.6 5.4 %collective-permute-start.8 = (bf16[144,128]{1,0:T(8,128)(2,1)S(1)}, bf16[144,128]{1,0:T(8,128)(2,1)S(1)}, u32[]{:S(2)}, u32[]{:S(2)}) collective-permute-start(bf16[144,128]{1,0:T(8,128)(2,1)S(1)} %get-tuple-element.29), channel_id=1, source_target_pairs={{0,2},{1,3},{2,0},{3,1},{4,6},{5,7},{6,4},{7,5},{8,10},{9,11},{10,... | collective-permute-start | bytes 110600 | tf_op jit(solution)/shard_map/ppermute | solution.py:285
  22.0 2.5 %copy-start.5 = (bf16[128,128]{1,0:T(8,128)(2,1)S(1)}, bf16[128,128]{1,0:T(8,128)(2,1)}, u32[]{:S(2)}) copy-start(bf16[128,128]{1,0:T(8,128)(2,1)} %refs_11_.1) | copy-start | bytes 98308
  22.0 4.0 %collective-permute-start.7 = (bf16[144,128]{1,0:T(8,128)(2,1)S(1)}, bf16[144,128]{1,0:T(8,128)(2,1)S(1)}, u32[]{:S(2)}, u32[]{:S(2)}) collective-permute-start(bf16[144,128]{1,0:T(8,128)(2,1)S(1)} %get-tuple-element.28.refs_4_), channel_id=1, source_target_pairs={{0,1},{1,0},{2,3},{3,2},{4,5},{5,4},{6,7},{7,6},{8,9},{9,8},{10,11... | collective-permute-start | bytes 110600 | tf_op jit(solution)/shard_map/ppermute | solution.py:285
  27.1 1.5 %collective-permute-start.11 = (bf16[12,48,128]{2,1,0:T(8,128)(2,1)S(1)}, bf16[12,48,128]{2,1,0:T(8,128)(2,1)S(1)}, u32[]{:S(2)}, u32[]{:S(2)}) collective-permute-start(bf16[12,48,128]{2,1,0:T(8,128)(2,1)S(1)} %get-tuple-element.37.refs_0_), channel_id=1, source_target_pairs={{0,2},{2,0},{4,6},{6,4},{8,10},{10,8},{12,14},{14,12},{1,3},{3,1},... | collective-permute-start | bytes 442376 | tf_op jit(solution)/shard_map/ppermute | solution.py:277
  27.2 1.5 %collective-permute-start.14 = (bf16[12,24,128]{2,1,0:T(8,128)(2,1)S(1)}, bf16[12,24,128]{2,1,0:T(8,128)(2,1)S(1)}, u32[]{:S(2)}, u32[]{:S(2)}) collective-permute-start(bf16[12,24,128]{2,1,0:T(8,128)(2,1)S(1)} %get-tuple-element.41), channel_id=1, source_target_pairs={{0,2},{2,0},{4,6},{6,4},{8,10},{10,8},{12,14},{14,12},{1,3},{3,1},... | collective-permute-start | bytes 221192 | tf_op jit(solution)/shard_map/ppermute | solution.py:277
  27.7 6.0 %collective-permute-start.12 = (bf16[12,24,128]{2,1,0:T(8,128)(2,1)S(1)}, bf16[12,24,128]{2,1,0:T(8,128)(2,1)S(1)}, u32[]{:S(2)}, u32[]{:S(2)}) collective-permute-start(bf16[12,24,128]{2,1,0:T(8,128)(2,1)S(1)} %get-tuple-element.39), channel_id=1, source_target_pairs={{0,2},{2,0},{4,6},{6,4},{8,10},{10,8},{12,14},{14,12},{1,3},{3,1},... | collective-permute-start | bytes 221192 | tf_op jit(solution)/shard_map/ppermute | solution.py:277
  29.9 14.2 %collective-permute-start.15 = (bf16[12,48,128]{2,1,0:T(8,128)(2,1)S(1)}, bf16[12,48,128]{2,1,0:T(8,128)(2,1)S(1)}, u32[]{:S(2)}, u32[]{:S(2)}) collective-permute-start(bf16[12,48,128]{2,1,0:T(8,128)(2,1)S(1)} %get-tuple-element.42), channel_id=1, source_target_pairs={{0,8},{2,10},{4,12},{6,14},{8,0},{10,2},{12,4},{14,6},{1,9},{3,11}... | collective-permute-start | bytes 442376 | tf_op jit(solution)/shard_map/ppermute | solution.py:277
  33.2 10.9 %collective-permute-start.16 = (bf16[12,48,128]{2,1,0:T(8,128)(2,1)S(1)}, bf16[12,48,128]{2,1,0:T(8,128)(2,1)S(1)}, u32[]{:S(2)}, u32[]{:S(2)}) collective-permute-start(bf16[12,48,128]{2,1,0:T(8,128)(2,1)S(1)} %get-tuple-element.43), channel_id=1, source_target_pairs={{0,12},{2,14},{4,8},{6,10},{8,4},{10,6},{12,0},{14,2},{1,13},{3,15... | collective-permute-start | bytes 442376 | tf_op jit(solution)/shard_map/ppermute | solution.py:277
  34.3 11.7 %collective-permute-start.13 = (bf16[12,48,128]{2,1,0:T(8,128)(2,1)S(1)}, bf16[12,48,128]{2,1,0:T(8,128)(2,1)S(1)}, u32[]{:S(2)}, u32[]{:S(2)}) collective-permute-start(bf16[12,48,128]{2,1,0:T(8,128)(2,1)S(1)} %shard_map.90), channel_id=1, source_target_pairs={{0,4},{2,6},{4,0},{6,2},{8,12},{10,14},{12,8},{14,10},{1,5},{3,7},... | collective-permute-start | bytes 442376 | tf_op jit(solution)/shard_map/ppermute | solution.py:277
  35.0 11.0 %copy-start.6 = (bf16[128,128]{1,0:T(8,128)(2,1)S(1)}, bf16[128,128]{1,0:T(8,128)(2,1)}, u32[]{:S(2)}) copy-start(bf16[128,128]{1,0:T(8,128)(2,1)} %refs_6_.1) | copy-start | bytes 98308
  (3 other events, 4.4 us)

commit v4 on v3

--- a/solution.py
+++ b/solution.py
@@ -129,37 +129,38 @@
     gate_ref[...] = sigmoid(gate).reshape(gate_ref.shape)
 
 
-def outgoing_kernel(runs, own_left, core_left, *refs):
+def outgoing_kernel(carried, *refs):
+    earlier, (own_left, core_left), refs = refs[:carried], refs[carried : carried + 2], refs[carried + 2 :]
     rights, (mine_ref, other_ref, r_scr, l_scr, o_scr) = refs[:-5], refs[-5:]
     rows, cols, chan = own_left.shape
+    count = len(rights)
+    used = count * rows
+    width = -(-used // 8) * 8
     z, _, _ = place()
-    for out_ref, left in ((mine_ref, own_left), (other_ref, core_left)):
+    begin = earlier[0].shape[0] if carried else 0
+    for m, ref in enumerate(rights):
+        base = ((z % count) ^ m) * rows
+        for j in range(rows):
+            r_scr[pl.ds(base + j, cols, stride=width), :] = ref[j].astype(F32)
+    for n, (out_ref, left) in enumerate(((mine_ref, own_left), (other_ref, core_left))):
         l_scr[...] = left[...].astype(F32).reshape(rows * cols, chan)
-        done = 0
-        for count in runs:
-            used = count * rows
-            width = -(-used // 8) * 8
-            if out_ref is mine_ref or len(runs) > 1:
-                for m, ref in enumerate(rights[done : done + count]):
-                    base = ((z % count) ^ m) * rows
-                    for j in range(rows):
-                        r_scr[pl.ds(base + j, cols, stride=width), :] = ref[j].astype(F32)
-
-            def step(block, totals):
-                for u in range(8):
-                    k = block * 8 + u
-                    right = r_scr[pl.ds(pl.multiple_of(k * width, 8), width), :]
-                    totals = tuple(
-                        t + l_scr[pl.ds(i * cols + k, 1), :] * right for i, t in enumerate(totals)
-                    )
-                return totals
-
-            zero = jnp.zeros((width, chan), F32)
-            totals = lax.fori_loop(0, cols // 8, step, (zero,) * rows)
-            for i, t in enumerate(totals):
-                o_scr[pl.ds(rows * done * rows + i * used, used), :] = t[:used]
-            done += count
-        out_ref[...] = o_scr[...].astype(BF16)
+
+        def step(block, totals):
+            for u in range(8):
+                k = block * 8 + u
+                right = r_scr[pl.ds(pl.multiple_of(k * width, 8), width), :]
+                totals = tuple(
+                    t + l_scr[pl.ds(i * cols + k, 1), :] * right for i, t in enumerate(totals)
+                )
+            return totals
+
+        zero = jnp.zeros((width, chan), F32)
+        totals = lax.fori_loop(0, cols // 8, step, (zero,) * rows)
+        for i, t in enumerate(totals):
+            o_scr[pl.ds(i * used, used), :] = t[:used]
+        if carried:
+            out_ref[pl.ds(0, begin), :] = earlier[n][...]
+        out_ref[pl.ds(begin, rows * used), :] = o_scr[...].astype(BF16)
 
 
 def first_kernel(cols_n, h, groups, *refs):
@@ -319,21 +320,31 @@
         flops=100_000_000,
     )
     core_left = along_row(left, 1)
-    runs = [pieces] * (cols_n - 1) + [1] * (pieces - 1)
-    exchanged = []
-    for counts, blocks in ((runs, list(range(chips - 1))), ([1], [chips - 1])):
-        out = shape((rows * len(blocks) * rows, chan), BF16)
-        mine, other = call(
-            functools.partial(outgoing_kernel, counts),
+    def product(blocks, earlier, wait=()):
+        size = rows * len(blocks) * rows
+        out = shape((size + sum(e.shape[0] for e in earlier[:1]), chan), BF16)
+        return call(
+            functools.partial(
+                after, functools.partial(outgoing_kernel, len(earlier)), len(wait)
+            ),
             [out, out],
-            [left, core_left] + [rights[m] for m in blocks],
+            [*wait, *earlier, left, core_left] + [rights[m] for m in blocks],
             scratch=[
-                pltpu.VMEM((cols * (-(-max(counts) * rows // 8) * 8), chan), F32),
+                pltpu.VMEM((cols * (-(-len(blocks) * rows // 8) * 8), chan), F32),
                 pltpu.VMEM((rows * cols, chan), F32),
-                pltpu.VMEM(out.shape, F32),
+                pltpu.VMEM((size, chan), F32),
             ],
             flops=250_000_000 * len(blocks),
+            outside=range(len(wait)),
         )
+
+    early = []
+    for h in range(cols_n - 1):
+        early = product(range(h * pieces, (h + 1) * pieces), early)
+    for m in range(chips - pieces, chips - 1):
+        early = product([m], early)
+    exchanged = []
+    for mine, other in (early, product([chips - 1], [], gates[1:2])):
         parts = [mine] + [shift(mine, dx, 0) for dx in range(1, cols_n)]
         exchanged.append(parts + [shift(other, dx, 1) for dx in range(cols_n)])
     firsts, lefts = [], []
@@ -362,24 +373,25 @@
 
     def partial_products(steps):
         used = lefts[steps[0] // pieces : steps[-1] // pieces + 1]
+        wait = [] if used[-1] is lefts[-1] else lefts[-1]
         return call(
-            functools.partial(incoming_kernel, steps),
+            functools.partial(after, functools.partial(incoming_kernel, steps), len(wait)),
             [block if m else block32 for m in steps],
-            [right, core_right] + sum(used, []),
+            wait + [right, core_right] + sum(used, []),
             scratch=[
                 pltpu.VMEM((2 * len(used) * rows * pieces * rows, chan), F32),
                 pltpu.VMEM((2 * rows * cols, chan), F32),
             ],
             flops=200_000_000 * len(steps),
+            outside=range(len(wait)),
         )
 
     parts = [None] * chips
-    far, near = list(range(pieces, chips)), list(range(1, pieces))
-    for m, value in zip(far, partial_products(far)):
+    for m, value in enumerate(partial_products(list(range(pieces, chips))), pieces):
         parts[m] = along_row(value, 2 * m)
-    for m, value in zip(near, partial_products(near)):
-        parts[m] = along_row(value, 2 * m)
-    parts[0] = partial_products([0])[0]
+    for m in reversed(range(pieces)):
+        value = partial_products([m])[0]
+        parts[m] = along_row(value, 2 * m) if m else value
     gate = call(gate_kernel, block32, [first, in_gating], flops=50_000_000)
     return call(last_kernel, block, parts + [first, gate, in_final], flops=100_000_000)
 

time: 47.2 us -> 47 us (level)
  starting transfers between devices: 18.1 us -> 17.2 us
  waiting for transfers between devices: 15 us -> 15.9 us
    ppermute x7, starting transfers between devices: 6.98 us -> 5.97 us  [shift(): return lax.ppermute(v, ('row', 'col'), pairs)]
    ppermute x7, waiting for transfers between devices: 1.08 us -> 2 us  [shift(): return lax.ppermute(v, ('row', 'col'), pairs)]
    pallas_call x12 -> x13, Pallas kernels: 12.8 us -> 12.6 us  [call(): pl.pallas_call(kernel, out_shape=outs, in_specs=[pl.BlockSpec(memory_spac...]
where the time goes in v4:
time: 47 us; the launch traced here: 46.8 us
  starting transfers between devices  17.2 us (37%)
  waiting for transfers between devices  15.9 us (34%)
  Pallas kernels  12.6 us (27%)
  local copies, waits for them, and re-layouts  0.97 us (2%)
    ppermute x10, waiting for transfers between devices, along_row(): return lax.ppermute(v, 'row', [(i, i ^ bits) for i in range(rows_n)])  13.9 us
    pallas_call x13, Pallas kernels, call(): pl.pallas_call(kernel, out_shape=outs, in_specs=[pl.BlockSpec(memory_spac...  12.6 us
    ppermute x10, starting transfers between devices, along_row(): return lax.ppermute(v, 'row', [(i, i ^ bits) for i in range(rows_n)])  11.2 us
    ppermute x7, starting transfers between devices, shift(): return lax.ppermute(v, ('row', 'col'), pairs)  5.97 us
    ppermute x7, waiting for transfers between devices, shift(): return lax.ppermute(v, ('row', 'col'), pairs)  2 us
    unnamed x20, local copies, waits for them, and re-layouts  0.97 us
  transfers between devices with their start and end apart: 17, of which 6 were waited for; matrix products, arithmetic and copies ran while one was open for 0% of the time, Pallas kernels for 18%

profile of v4, /device:TPU:0, one launch (start us, length us, event | category | flops | bytes accessed | tf_op | source)
XLA Modules:
  0.0 46.8 jit_solution(9763237817403904669)
XLA Ops:
  0.0 2.1 %shard_map.82.refs_0_.refs_2_ = bf16[12,48,128]{2,1,0:T(8,128)(2,1)} custom-call(bf16[12,48,128]{2,1,0:T(8,128)(2,1)} %refs_1_.1, s32[1,96]{1,0:T(1,128)} %bitcast.1, bf16[128,512]{1,0:T(8,128)(2,1)} %refs_3_.1), custom_call_target="tpu_custom_call" | custom-call | flops 100000000 | bytes 426368 | tf_op jit(solution)/shard_map/pallas_call | solution.py:26
  2.1 4.1 %collective-permute-start.2 = (bf16[12,48,128]{2,1,0:T(8,128)(2,1)}, bf16[12,48,128]{2,1,0:T(8,128)(2,1)S(1)}, u32[]{:S(2)}, u32[]{:S(2)}) collective-permute-start(bf16[12,48,128]{2,1,0:T(8,128)(2,1)} %shard_map.82.refs_0_.refs_2_), channel_id=1, source_target_pairs={{0,8},{2,10},{4,12},{6,14},{8,0},{10,2},{12,4},{14,6},{1,9},{3,11}... | collective-permute-start | bytes 442376 | tf_op jit(solution)/shard_map/ppermute | solution.py:278
  6.2 1.6 %collective-permute-start.1 = (bf16[12,48,128]{2,1,0:T(8,128)(2,1)}, bf16[12,48,128]{2,1,0:T(8,128)(2,1)S(1)}, u32[]{:S(2)}, u32[]{:S(2)}) collective-permute-start(bf16[12,48,128]{2,1,0:T(8,128)(2,1)} %shard_map.82.refs_0_.refs_2_), channel_id=1, source_target_pairs={{0,4},{2,6},{4,0},{6,2},{8,12},{10,14},{12,8},{14,10},{1,5},{3,7},... | collective-permute-start | bytes 442376 | tf_op jit(solution)/shard_map/ppermute | solution.py:278
  7.8 0.9 %copy-done.1 = bf16[12,48,128]{2,1,0:T(8,128)(2,1)S(1)} copy-done((bf16[12,48,128]{2,1,0:T(8,128)(2,1)S(1)}, bf16[12,48,128]{2,1,0:T(8,128)(2,1)}, u32[]{:S(2)}) %copy-start.1) | copy-done | bytes 147480
  9.3 1.6 %collective-permute-start.6 = (bf16[12,48,128]{2,1,0:T(8,128)(2,1)S(1)}, bf16[12,48,128]{2,1,0:T(8,128)(2,1)S(1)}, u32[]{:S(2)}, u32[]{:S(2)}) collective-permute-start(bf16[12,48,128]{2,1,0:T(8,128)(2,1)S(1)} %get-tuple-element.32.refs_0_), channel_id=1, source_target_pairs={{0,1},{1,0},{2,3},{3,2},{4,5},{5,4},{6,7},{7,6},{8,9},{9,8},{10,11... | collective-permute-start | bytes 442376 | tf_op jit(solution)/shard_map/ppermute | solution.py:286
  10.8 2.7 %collective-permute-done.2.refs_4_ = bf16[12,48,128]{2,1,0:T(8,128)(2,1)S(1)} collective-permute-done((bf16[12,48,128]{2,1,0:T(8,128)(2,1)}, bf16[12,48,128]{2,1,0:T(8,128)(2,1)S(1)}, u32[]{:S(2)}, u32[]{:S(2)}) %collective-permute-start.2) | collective-permute-done | bytes 147488 | tf_op jit(solution)/shard_map/ppermute | solution.py:278
  13.6 0.7 %collective-permute-start.7 = (bf16[12,48,128]{2,1,0:T(8,128)(2,1)S(1)}, bf16[12,48,128]{2,1,0:T(8,128)(2,1)S(1)}, u32[]{:S(2)}, u32[]{:S(2)}) collective-permute-start(bf16[12,48,128]{2,1,0:T(8,128)(2,1)S(1)} %collective-permute-done.2.refs_4_), channel_id=1, source_target_pairs={{0,4},{2,6},{4,0},{6,2},{8,12},{10,14},{12,8},{14,10},{1,5},{3,7},... | collective-permute-start | bytes 442376 | tf_op jit(solution)/shard_map/ppermute | solution.py:278
  14.3 1.2 %shard_map.84 = (bf16[288,128]{1,0:T(8,128)(2,1)S(1)}, bf16[288,128]{1,0:T(8,128)(2,1)S(1)}) custom-call(bf16[12,48,128]{2,1,0:T(8,128)(2,1)S(1)} %get-tuple-element.27.refs_0_.refs_2_.refs_1_, bf16[12,48,128]{2,1,0:T(8,128)(2,1)S(1)} %collective-permute-done.refs_1_.refs_3_.refs_2_, bf16[12,48,128]{2,1,0:T(8,128)(2,1)S(1)} %copy-done.2, ...), custom_call_target="tpu_custom_call" | custom-call | flops 500000000 | bytes 737280 | tf_op jit(solution)/shard_map/pallas_call | solution.py:26
  15.5 0.9 %shard_map.85 = (bf16[432,128]{1,0:T(8,128)(2,1)S(1)}, bf16[432,128]{1,0:T(8,128)(2,1)S(1)}) custom-call(bf16[288,128]{1,0:T(8,128)(2,1)S(1)} %get-tuple-element.28.refs_0_, bf16[288,128]{1,0:T(8,128)(2,1)S(1)} %get-tuple-element.29.refs_1_, bf16[12,48,128]{2,1,0:T(8,128)(2,1)S(1)} %get-tuple-element.27.refs_0_.refs_2_.refs_1_, ...), custom_call_target="tpu_custom_call" | custom-call | flops 250000000 | bytes 811008 | tf_op jit(solution)/shard_map/pallas_call | solution.py:26
  16.4 0.9 %collective-permute-start.5 = (bf16[432,128]{1,0:T(8,128)(2,1)S(1)}, bf16[432,128]{1,0:T(8,128)(2,1)S(1)}, u32[]{:S(2)}, u32[]{:S(2)}) collective-permute-start(bf16[432,128]{1,0:T(8,128)(2,1)S(1)} %get-tuple-element.31), channel_id=1, source_target_pairs={{0,3},{1,2},{2,1},{3,0},{4,7},{5,6},{6,5},{7,4},{8,11},{9,10},{10,... | collective-permute-start | bytes 331784 | tf_op jit(solution)/shard_map/ppermute | solution.py:286
  17.3 0.8 %collective-permute-start.4 = (bf16[432,128]{1,0:T(8,128)(2,1)S(1)}, bf16[432,128]{1,0:T(8,128)(2,1)S(1)}, u32[]{:S(2)}, u32[]{:S(2)}) collective-permute-start(bf16[432,128]{1,0:T(8,128)(2,1)S(1)} %get-tuple-element.31), channel_id=1, source_target_pairs={{0,2},{1,3},{2,0},{3,1},{4,6},{5,7},{6,4},{7,5},{8,10},{9,11},{10,... | collective-permute-start | bytes 331784 | tf_op jit(solution)/shard_map/ppermute | solution.py:286
  18.6 0.9 %shard_map.86 = (bf16[12,48,128]{2,1,0:T(8,128)(2,1)S(1)}, f32[12,48,128]{2,1,0:T(8,128)S(1)}, bf16[12,48,128]{2,1,0:T(8,128)(2,1)S(1)}, f32[12,48,128]{2,1,0:T(8,128)S(1)}) custom-call(bf16[12,48,128]{2,1,0:T(8,128)(2,1)S(1)} %get-tuple-element.32.refs_0_, bf16[12,48,128]{2,1,0:T(8,128)(2,1)S(1)} %collective-permute-done.6.refs_1_, ...), custom_call_target="tpu_custom_call" | custom-call | flops 100000000 | bytes 1212416 | tf_op jit(solution)/shard_map/pallas_call | solution.py:26
  19.5 0.9 %shard_map.87 = (bf16[144,128]{1,0:T(8,128)(2,1)S(1)}, bf16[144,128]{1,0:T(8,128)(2,1)S(1)}) custom-call(f32[12,48,128]{2,1,0:T(8,128)S(1)} %get-tuple-element.33.refs_0_.refs_5_, bf16[12,48,128]{2,1,0:T(8,128)(2,1)S(1)} %get-tuple-element.27.refs_0_.refs_2_.refs_1_, bf16[12,48,128]{2,1,0:T(8,128)(2,1)S(1)} %collective-permute-done.refs_1_.refs_3_.refs_2_, ...), custom_call_target="tpu_custom_call" | custom-call | flops 250000000 | bytes 811008 | tf_op jit(solution)/shard_map/pallas_call | solution.py:26
  20.4 1.5 %collective-permute-start.8 = (bf16[144,128]{1,0:T(8,128)(2,1)S(1)}, bf16[144,128]{1,0:T(8,128)(2,1)S(1)}, u32[]{:S(2)}, u32[]{:S(2)}) collective-permute-start(bf16[144,128]{1,0:T(8,128)(2,1)S(1)} %get-tuple-element.34.refs_4_), channel_id=1, source_target_pairs={{0,1},{1,0},{2,3},{3,2},{4,5},{5,4},{6,7},{7,6},{8,9},{9,8},{10,11... | collective-permute-start | bytes 110600 | tf_op jit(solution)/shard_map/ppermute | solution.py:286
  22.6 1.6 %collective-permute-done.3.refs_1_ = bf16[432,128]{1,0:T(8,128)(2,1)S(1)} collective-permute-done((bf16[432,128]{1,0:T(8,128)(2,1)S(1)}, bf16[432,128]{1,0:T(8,128)(2,1)S(1)}, u32[]{:S(2)}, u32[]{:S(2)}) %collective-permute-start.3) | collective-permute-done | bytes 110624 | tf_op jit(solution)/shard_map/ppermute | solution.py:286
  24.3 1.1 %shard_map.88 = (bf16[12,48,128]{2,1,0:T(8,128)(2,1)S(1)}, bf16[12,48,128]{2,1,0:T(8,128)(2,1)S(1)}, bf16[12,24,128]{2,1,0:T(8,128)(2,1)S(1)}, bf16[12,24,128]{2,1,0:T(8,128)(2,1)S(1)}) custom-call(bf16[432,128]{1,0:T(8,128)(2,1)S(1)} %get-tuple-element.30.refs_0_, bf16[432,128]{1,0:T(8,128)(2,1)S(1)} %collective-permute-done.3.refs_1_, ...), custom_call_target="tpu_custom_call" | custom-call | flops 300000000 | bytes 1491328 | tf_op jit(solution)/shard_map/pallas_call | solution.py:26
  25.7 1.1 %shard_map.89 = (bf16[12,48,128]{2,1,0:T(8,128)(2,1)S(1)}, bf16[12,48,128]{2,1,0:T(8,128)(2,1)S(1)}, bf16[12,24,128]{2,1,0:T(8,128)(2,1)S(1)}, bf16[12,24,128]{2,1,0:T(8,128)(2,1)S(1)}) custom-call(bf16[432,128]{1,0:T(8,128)(2,1)S(1)} %get-tuple-element.30.refs_0_, bf16[432,128]{1,0:T(8,128)(2,1)S(1)} %collective-permute-done.3.refs_1_, ...), custom_call_target="tpu_custom_call" | custom-call | flops 300000000 | bytes 1933696 | tf_op jit(solution)/shard_map/pallas_call | solution.py:26
  27.6 0.9 %collective-permute-done.11.refs_1_.refs_3_ = bf16[12,24,128]{2,1,0:T(8,128)(2,1)S(1)} collective-permute-done((bf16[12,24,128]{2,1,0:T(8,128)(2,1)S(1)}, bf16[12,24,128]{2,1,0:T(8,128)(2,1)S(1)}, u32[]{:S(2)}, u32[]{:S(2)}) %collective-permute-start.11) | collective-permute-done | bytes 73760 | tf_op jit(solution)/shard_map/ppermute | solution.py:278
  28.4 1.3 %shard_map.92 = (bf16[12,48,128]{2,1,0:T(8,128)(2,1)S(1)}, bf16[12,48,128]{2,1,0:T(8,128)(2,1)S(1)}) custom-call(bf16[12,48,128]{2,1,0:T(8,128)(2,1)S(1)} %get-tuple-element.43.refs_2_.refs_0_, bf16[12,48,128]{2,1,0:T(8,128)(2,1)S(1)} %collective-permute-done.12.refs_3_.refs_1_, bf16[12,24,128]{2,1,0:T(8,128)(2,1)S(1)} %get-tuple-element.41.refs_0_.refs_2_, ...), custom_call_target="tpu_custom_call" | custom-call | flops 400000000 | bytes 737280 | tf_op jit(solution)/shard_map/pallas_call | solution.py:26
  29.7 3.4 %collective-permute-start.15 = (bf16[12,48,128]{2,1,0:T(8,128)(2,1)S(1)}, bf16[12,48,128]{2,1,0:T(8,128)(2,1)S(1)}, u32[]{:S(2)}, u32[]{:S(2)}) collective-permute-start(bf16[12,48,128]{2,1,0:T(8,128)(2,1)S(1)} %get-tuple-element.46), channel_id=1, source_target_pairs={{0,8},{2,10},{4,12},{6,14},{8,0},{10,2},{12,4},{14,6},{1,9},{3,11}... | collective-permute-start | bytes 442376 | tf_op jit(solution)/shard_map/ppermute | solution.py:278
  33.5 0.7 %shard_map.91 = bf16[12,48,128]{2,1,0:T(8,128)(2,1)S(1)} custom-call(bf16[12,24,128]{2,1,0:T(8,128)(2,1)S(1)} %get-tuple-element.41.refs_0_.refs_2_, bf16[12,24,128]{2,1,0:T(8,128)(2,1)S(1)} %collective-permute-done.11.refs_1_.refs_3_, bf16[12,48,128]{2,1,0:T(8,128)(2,1)S(1)} %get-tuple-element.43.refs_2_.refs_0_, ...), custom_call_target="tpu_custom_call" | custom-call | flops 200000000 | bytes 737280 | tf_op jit(solution)/shard_map/pallas_call | solution.py:26
  35.5 8.5 %collective-permute-done.15.refs_2_ = bf16[12,48,128]{2,1,0:T(8,128)(2,1)S(1)} collective-permute-done((bf16[12,48,128]{2,1,0:T(8,128)(2,1)S(1)}, bf16[12,48,128]{2,1,0:T(8,128)(2,1)S(1)}, u32[]{:S(2)}, u32[]{:S(2)}) %collective-permute-start.15) | collective-permute-done | bytes 147488 | tf_op jit(solution)/shard_map/ppermute | solution.py:278
  44.0 1.8 %collective-permute-done.14.refs_1_ = bf16[12,48,128]{2,1,0:T(8,128)(2,1)S(1)} collective-permute-done((bf16[12,48,128]{2,1,0:T(8,128)(2,1)S(1)}, bf16[12,48,128]{2,1,0:T(8,128)(2,1)S(1)}, u32[]{:S(2)}, u32[]{:S(2)}) %collective-permute-start.14) | collective-permute-done | bytes 147488 | tf_op jit(solution)/shard_map/ppermute | solution.py:278
  45.8 1.0 %shard_map.94 = bf16[12,48,128]{2,1,0:T(8,128)(2,1)} custom-call(f32[12,48,128]{2,1,0:T(8,128)S(1)} %shard_map.90.refs_0_, bf16[12,48,128]{2,1,0:T(8,128)(2,1)S(1)} %collective-permute-done.14.refs_1_, bf16[12,48,128]{2,1,0:T(8,128)(2,1)S(1)} %collective-permute-done.15.refs_2_, bf16[12,48,128]{2,1,0:T(8,128)(2,1)S(1)} %collective-permute-done.16.refs_3_, ...), custom_call_target="tpu_custom_call" | custom-call | flops 100000000 | bytes 1359872 | tf_op jit(solution)/shard_map/pallas_call | solution.py:26
  (43 shorter events, 4.6 us)
Async XLA Ops:
  0.0 7.8 %copy-start = (bf16[12,48,128]{2,1,0:T(8,128)(2,1)S(1)}, bf16[12,48,128]{2,1,0:T(8,128)(2,1)}, u32[]{:S(2)}) copy-start(bf16[12,48,128]{2,1,0:T(8,128)(2,1)} %refs_1_.1) | copy-start | bytes 442372
  0.0 7.8 %copy-start.3 = (bf16[128,512]{1,0:T(8,128)(2,1)S(1)}, bf16[128,512]{1,0:T(8,128)(2,1)}, u32[]{:S(2)}) copy-start(bf16[128,512]{1,0:T(8,128)(2,1)} %refs_3_.1) | copy-start | bytes 393220
  0.0 7.8 %copy-start.8 = (s32[96]{0:T(128)S(1)}, s32[96]{0:T(128)}, u32[]{:S(2)}) copy-start(s32[96]{0:T(128)} %param.9) | copy-start | bytes 1156
  2.1 11.4 %collective-permute-start.2 = (bf16[12,48,128]{2,1,0:T(8,128)(2,1)}, bf16[12,48,128]{2,1,0:T(8,128)(2,1)S(1)}, u32[]{:S(2)}, u32[]{:S(2)}) collective-permute-start(bf16[12,48,128]{2,1,0:T(8,128)(2,1)} %shard_map.82.refs_0_.refs_2_), channel_id=1, source_target_pairs={{0,8},{2,10},{4,12},{6,14},{8,0},{10,2},{12,4},{14,6},{1,9},{3,11}... | collective-permute-start | bytes 442376 | tf_op jit(solution)/shard_map/ppermute | solution.py:278
  6.2 8.0 %collective-permute-start.1 = (bf16[12,48,128]{2,1,0:T(8,128)(2,1)}, bf16[12,48,128]{2,1,0:T(8,128)(2,1)S(1)}, u32[]{:S(2)}, u32[]{:S(2)}) collective-permute-start(bf16[12,48,128]{2,1,0:T(8,128)(2,1)} %shard_map.82.refs_0_.refs_2_), channel_id=1, source_target_pairs={{0,4},{2,6},{4,0},{6,2},{8,12},{10,14},{12,8},{14,10},{1,5},{3,7},... | collective-permute-start | bytes 442376 | tf_op jit(solution)/shard_map/ppermute | solution.py:278
  8.8 5.5 %copy-start.2 = (bf16[12,48,128]{2,1,0:T(8,128)(2,1)S(1)}, bf16[12,48,128]{2,1,0:T(8,128)(2,1)}, u32[]{:S(2)}) copy-start(bf16[12,48,128]{2,1,0:T(8,128)(2,1)} %shard_map.82.refs_0_.refs_2_) | copy-start | bytes 442372
  9.2 5.1 %collective-permute-start = (bf16[12,48,128]{2,1,0:T(8,128)(2,1)S(1)}, bf16[12,48,128]{2,1,0:T(8,128)(2,1)S(1)}, u32[]{:S(2)}, u32[]{:S(2)}) collective-permute-start(bf16[12,48,128]{2,1,0:T(8,128)(2,1)S(1)} %get-tuple-element.27.refs_0_.refs_2_.refs_1_), channel_id=1, source_target_pairs={{0,2},{2,0},{4,6},{6,4},{8,10},{10,8},{12,14},{14,12},{1,3},{3,1},... | collective-permute-start | bytes 442376 | tf_op jit(solution)/shard_map/ppermute | solution.py:278
  9.3 9.3 %collective-permute-start.6 = (bf16[12,48,128]{2,1,0:T(8,128)(2,1)S(1)}, bf16[12,48,128]{2,1,0:T(8,128)(2,1)S(1)}, u32[]{:S(2)}, u32[]{:S(2)}) collective-permute-start(bf16[12,48,128]{2,1,0:T(8,128)(2,1)S(1)} %get-tuple-element.32.refs_0_), channel_id=1, source_target_pairs={{0,1},{1,0},{2,3},{3,2},{4,5},{5,4},{6,7},{7,6},{8,9},{9,8},{10,11... | collective-permute-start | bytes 442376 | tf_op jit(solution)/shard_map/ppermute | solution.py:286
  13.6 5.9 %collective-permute-start.7 = (bf16[12,48,128]{2,1,0:T(8,128)(2,1)S(1)}, bf16[12,48,128]{2,1,0:T(8,128)(2,1)S(1)}, u32[]{:S(2)}, u32[]{:S(2)}) collective-permute-start(bf16[12,48,128]{2,1,0:T(8,128)(2,1)S(1)} %collective-permute-done.2.refs_4_), channel_id=1, source_target_pairs={{0,4},{2,6},{4,0},{6,2},{8,12},{10,14},{12,8},{14,10},{1,5},{3,7},... | collective-permute-start | bytes 442376 | tf_op jit(solution)/shard_map/ppermute | solution.py:278
  16.4 5.5 %collective-permute-start.5 = (bf16[432,128]{1,0:T(8,128)(2,1)S(1)}, bf16[432,128]{1,0:T(8,128)(2,1)S(1)}, u32[]{:S(2)}, u32[]{:S(2)}) collective-permute-start(bf16[432,128]{1,0:T(8,128)(2,1)S(1)} %get-tuple-element.31), channel_id=1, source_target_pairs={{0,3},{1,2},{2,1},{3,0},{4,7},{5,6},{6,5},{7,4},{8,11},{9,10},{10,... | collective-permute-start | bytes 331784 | tf_op jit(solution)/shard_map/ppermute | solution.py:286
  17.3 5.3 %collective-permute-start.4 = (bf16[432,128]{1,0:T(8,128)(2,1)S(1)}, bf16[432,128]{1,0:T(8,128)(2,1)S(1)}, u32[]{:S(2)}, u32[]{:S(2)}) collective-permute-start(bf16[432,128]{1,0:T(8,128)(2,1)S(1)} %get-tuple-element.31), channel_id=1, source_target_pairs={{0,2},{1,3},{2,0},{3,1},{4,6},{5,7},{6,4},{7,5},{8,10},{9,11},{10,... | collective-permute-start | bytes 331784 | tf_op jit(solution)/shard_map/ppermute | solution.py:286
  18.1 6.2 %collective-permute-start.3 = (bf16[432,128]{1,0:T(8,128)(2,1)S(1)}, bf16[432,128]{1,0:T(8,128)(2,1)S(1)}, u32[]{:S(2)}, u32[]{:S(2)}) collective-permute-start(bf16[432,128]{1,0:T(8,128)(2,1)S(1)} %get-tuple-element.30.refs_0_), channel_id=1, source_target_pairs={{0,1},{1,0},{2,3},{3,2},{4,5},{5,4},{6,7},{7,6},{8,9},{9,8},{10,11... | collective-permute-start | bytes 331784 | tf_op jit(solution)/shard_map/ppermute | solution.py:286
  19.5 4.8 %copy-start.4 = (bf16[128,512]{1,0:T(8,128)(2,1)S(1)}, bf16[128,512]{1,0:T(8,128)(2,1)}, u32[]{:S(2)}) copy-start(bf16[128,512]{1,0:T(8,128)(2,1)} %refs_12_.1) | copy-start | bytes 393220
  19.5 4.7 %copy-start.5 = (bf16[128,128]{1,0:T(8,128)(2,1)S(1)}, bf16[128,128]{1,0:T(8,128)(2,1)}, u32[]{:S(2)}) copy-start(bf16[128,128]{1,0:T(8,128)(2,1)} %refs_11_.1) | copy-start | bytes 98308
  20.4 5.0 %collective-permute-start.8 = (bf16[144,128]{1,0:T(8,128)(2,1)S(1)}, bf16[144,128]{1,0:T(8,128)(2,1)S(1)}, u32[]{:S(2)}, u32[]{:S(2)}) collective-permute-start(bf16[144,128]{1,0:T(8,128)(2,1)S(1)} %get-tuple-element.34.refs_4_), channel_id=1, source_target_pairs={{0,1},{1,0},{2,3},{3,2},{4,5},{5,4},{6,7},{7,6},{8,9},{9,8},{10,11... | collective-permute-start | bytes 110600 | tf_op jit(solution)/shard_map/ppermute | solution.py:286
  22.0 3.8 %collective-permute-start.10 = (bf16[144,128]{1,0:T(8,128)(2,1)S(1)}, bf16[144,128]{1,0:T(8,128)(2,1)S(1)}, u32[]{:S(2)}, u32[]{:S(2)}) collective-permute-start(bf16[144,128]{1,0:T(8,128)(2,1)S(1)} %get-tuple-element.35), channel_id=1, source_target_pairs={{0,3},{1,2},{2,1},{3,0},{4,7},{5,6},{6,5},{7,4},{8,11},{9,10},{10,... | collective-permute-start | bytes 110600 | tf_op jit(solution)/shard_map/ppermute | solution.py:286
  22.0 3.8 %collective-permute-start.9 = (bf16[144,128]{1,0:T(8,128)(2,1)S(1)}, bf16[144,128]{1,0:T(8,128)(2,1)S(1)}, u32[]{:S(2)}, u32[]{:S(2)}) collective-permute-start(bf16[144,128]{1,0:T(8,128)(2,1)S(1)} %get-tuple-element.35), channel_id=1, source_target_pairs={{0,2},{1,3},{2,0},{3,1},{4,6},{5,7},{6,4},{7,5},{8,10},{9,11},{10,... | collective-permute-start | bytes 110600 | tf_op jit(solution)/shard_map/ppermute | solution.py:286
  26.9 1.5 %collective-permute-start.12 = (bf16[12,48,128]{2,1,0:T(8,128)(2,1)S(1)}, bf16[12,48,128]{2,1,0:T(8,128)(2,1)S(1)}, u32[]{:S(2)}, u32[]{:S(2)}) collective-permute-start(bf16[12,48,128]{2,1,0:T(8,128)(2,1)S(1)} %get-tuple-element.43.refs_2_.refs_0_), channel_id=1, source_target_pairs={{0,2},{2,0},{4,6},{6,4},{8,10},{10,8},{12,14},{14,12},{1,3},{3,1},... | collective-permute-start | bytes 442376 | tf_op jit(solution)/shard_map/ppermute | solution.py:278
  27.1 1.4 %collective-permute-start.11 = (bf16[12,24,128]{2,1,0:T(8,128)(2,1)S(1)}, bf16[12,24,128]{2,1,0:T(8,128)(2,1)S(1)}, u32[]{:S(2)}, u32[]{:S(2)}) collective-permute-start(bf16[12,24,128]{2,1,0:T(8,128)(2,1)S(1)} %get-tuple-element.42), channel_id=1, source_target_pairs={{0,2},{2,0},{4,6},{6,4},{8,10},{10,8},{12,14},{14,12},{1,3},{3,1},... | collective-permute-start | bytes 221192 | tf_op jit(solution)/shard_map/ppermute | solution.py:278
  27.5 6.0 %collective-permute-start.13 = (bf16[12,24,128]{2,1,0:T(8,128)(2,1)S(1)}, bf16[12,24,128]{2,1,0:T(8,128)(2,1)S(1)}, u32[]{:S(2)}, u32[]{:S(2)}) collective-permute-start(bf16[12,24,128]{2,1,0:T(8,128)(2,1)S(1)} %get-tuple-element.45), channel_id=1, source_target_pairs={{0,2},{2,0},{4,6},{6,4},{8,10},{10,8},{12,14},{14,12},{1,3},{3,1},... | collective-permute-start | bytes 221192 | tf_op jit(solution)/shard_map/ppermute | solution.py:278
  29.7 14.3 %collective-permute-start.15 = (bf16[12,48,128]{2,1,0:T(8,128)(2,1)S(1)}, bf16[12,48,128]{2,1,0:T(8,128)(2,1)S(1)}, u32[]{:S(2)}, u32[]{:S(2)}) collective-permute-start(bf16[12,48,128]{2,1,0:T(8,128)(2,1)S(1)} %get-tuple-element.46), channel_id=1, source_target_pairs={{0,8},{2,10},{4,12},{6,14},{8,0},{10,2},{12,4},{14,6},{1,9},{3,11}... | collective-permute-start | bytes 442376 | tf_op jit(solution)/shard_map/ppermute | solution.py:278
  33.1 10.9 %collective-permute-start.16 = (bf16[12,48,128]{2,1,0:T(8,128)(2,1)S(1)}, bf16[12,48,128]{2,1,0:T(8,128)(2,1)S(1)}, u32[]{:S(2)}, u32[]{:S(2)}) collective-permute-start(bf16[12,48,128]{2,1,0:T(8,128)(2,1)S(1)} %get-tuple-element.47), channel_id=1, source_target_pairs={{0,12},{2,14},{4,8},{6,10},{8,4},{10,6},{12,0},{14,2},{1,13},{3,15... | collective-permute-start | bytes 442376 | tf_op jit(solution)/shard_map/ppermute | solution.py:278
  34.2 11.7 %collective-permute-start.14 = (bf16[12,48,128]{2,1,0:T(8,128)(2,1)S(1)}, bf16[12,48,128]{2,1,0:T(8,128)(2,1)S(1)}, u32[]{:S(2)}, u32[]{:S(2)}) collective-permute-start(bf16[12,48,128]{2,1,0:T(8,128)(2,1)S(1)} %shard_map.91), channel_id=1, source_target_pairs={{0,4},{2,6},{4,0},{6,2},{8,12},{10,14},{12,8},{14,10},{1,5},{3,7},... | collective-permute-start | bytes 442376 | tf_op jit(solution)/shard_map/ppermute | solution.py:278
  34.8 11.0 %copy-start.6 = (bf16[128,128]{1,0:T(8,128)(2,1)S(1)}, bf16[128,128]{1,0:T(8,128)(2,1)}, u32[]{:S(2)}) copy-start(bf16[128,128]{1,0:T(8,128)(2,1)} %refs_6_.1) | copy-start | bytes 98308
  (3 other events, 5.0 us)

commit v5 on v4

--- a/solution.py
+++ b/solution.py
@@ -129,20 +129,19 @@
     gate_ref[...] = sigmoid(gate).reshape(gate_ref.shape)
 
 
-def outgoing_kernel(carried, *refs):
-    earlier, (own_left, core_left), refs = refs[:carried], refs[carried : carried + 2], refs[carried + 2 :]
-    rights, (mine_ref, other_ref, r_scr, l_scr, o_scr) = refs[:-5], refs[-5:]
-    rows, cols, chan = own_left.shape
-    count = len(rights)
-    used = count * rows
+def outgoing_kernel(carried, sides, *refs):
+    earlier, lefts, refs = refs[:carried], refs[carried : carried + sides], refs[carried + sides :]
+    rights, outs, (r_scr, l_scr, o_scr) = refs[: -3 - sides], refs[-3 - sides : -3], refs[-3:]
+    rows, cols, chan = lefts[0].shape
+    blocks = len(rights)
+    used = blocks * rows
     width = -(-used // 8) * 8
     z, _, _ = place()
-    begin = earlier[0].shape[0] if carried else 0
     for m, ref in enumerate(rights):
-        base = ((z % count) ^ m) * rows
+        base = ((z % blocks) ^ m) * rows
         for j in range(rows):
             r_scr[pl.ds(base + j, cols, stride=width), :] = ref[j].astype(F32)
-    for n, (out_ref, left) in enumerate(((mine_ref, own_left), (other_ref, core_left))):
+    for n, (left, out_ref) in enumerate(zip(lefts, outs)):
         l_scr[...] = left[...].astype(F32).reshape(rows * cols, chan)
 
         def step(block, totals):
@@ -158,6 +157,7 @@
         totals = lax.fori_loop(0, cols // 8, step, (zero,) * rows)
         for i, t in enumerate(totals):
             o_scr[pl.ds(i * used, used), :] = t[:used]
+        begin = out_ref.shape[0] - rows * used
         if carried:
             out_ref[pl.ds(0, begin), :] = earlier[n][...]
         out_ref[pl.ds(begin, rows * used), :] = o_scr[...].astype(BF16)
@@ -319,34 +319,39 @@
         pairs + [out_gating],
         flops=100_000_000,
     )
+    gates = list(gates)
     core_left = along_row(left, 1)
-    def product(blocks, earlier, wait=()):
-        size = rows * len(blocks) * rows
-        out = shape((size + sum(e.shape[0] for e in earlier[:1]), chan), BF16)
+    def product(blocks, sides, earlier=()):
+        area = rows * len(blocks) * rows
+        out = shape((area + sum(e.shape[0] for e in earlier[:1]), chan), BF16)
         return call(
-            functools.partial(
-                after, functools.partial(outgoing_kernel, len(earlier)), len(wait)
-            ),
-            [out, out],
-            [*wait, *earlier, left, core_left] + [rights[m] for m in blocks],
+            functools.partial(outgoing_kernel, len(earlier), len(sides)),
+            [out] * len(sides),
+            [*earlier, *sides] + [rights[m] for m in blocks],
             scratch=[
                 pltpu.VMEM((cols * (-(-len(blocks) * rows // 8) * 8), chan), F32),
                 pltpu.VMEM((rows * cols, chan), F32),
-                pltpu.VMEM((size, chan), F32),
+                pltpu.VMEM((area, chan), F32),
             ],
-            flops=250_000_000 * len(blocks),
-            outside=range(len(wait)),
+            flops=125_000_000 * len(blocks) * len(sides),
         )
 
+    both = [left, core_left]
     early = []
     for h in range(cols_n - 1):
-        early = product(range(h * pieces, (h + 1) * pieces), early)
+        early = product(range(h * pieces, (h + 1) * pieces), both, early)
     for m in range(chips - pieces, chips - 1):
-        early = product([m], early)
-    exchanged = []
-    for mine, other in (early, product([chips - 1], [], gates[1:2])):
-        parts = [mine] + [shift(mine, dx, 0) for dx in range(1, cols_n)]
-        exchanged.append(parts + [shift(other, dx, 1) for dx in range(cols_n)])
+        early = product([m], both, early)
+    mine, other = early
+    parts = [mine] + [shift(mine, dx, 0) for dx in range(1, cols_n)]
+    exchanged = [parts + [shift(other, dx, 1) for dx in range(cols_n)]]
+    (mine,) = product([chips - 1], [left])
+    mine, core_left = lax.optimization_barrier((mine, core_left))
+    (other,) = product([chips - 1], [core_left])
+    other_core, gates[1] = lax.optimization_barrier((other, gates[1]))
+    parts = [mine] + [shift(mine, dx, 0) for dx in range(1, cols_n)]
+    parts += [shift(other_core, 0, 1)] + [shift(other, dx, 1) for dx in range(1, cols_n)]
+    exchanged.append(parts)
     firsts, lefts = [], []
     for h in range(cols_n):
         area = rows * rows

time: 47 us -> 47 us (level)
    pallas_call x13 -> x14, Pallas kernels: 12.6 us -> 12.8 us  [call(): pl.pallas_call(kernel, out_shape=outs, in_specs=[pl.BlockSpec(memory_spac...]
where the time goes in v5:
time: 47 us; the launch traced here: 46.8 us
  starting transfers between devices  16.8 us (36%)
  waiting for transfers between devices  16.1 us (34%)
  Pallas kernels  12.8 us (27%)
  local copies, waits for them, and re-layouts  0.97 us (2%)
    ppermute x10, waiting for transfers between devices, along_row(): return lax.ppermute(v, 'row', [(i, i ^ bits) for i in range(rows_n)])  13.9 us
    pallas_call x14, Pallas kernels, call(): pl.pallas_call(kernel, out_shape=outs, in_specs=[pl.BlockSpec(memory_spac...  12.8 us
    ppermute x10, starting transfers between devices, along_row(): return lax.ppermute(v, 'row', [(i, i ^ bits) for i in range(rows_n)])  11.2 us
    ppermute x7, starting transfers between devices, shift(): return lax.ppermute(v, ('row', 'col'), pairs)  5.69 us
    ppermute x7, waiting for transfers between devices, shift(): return lax.ppermute(v, ('row', 'col'), pairs)  2.18 us
    unnamed x20, local copies, waits for them, and re-layouts  0.97 us
  transfers between devices with their start and end apart: 17, of which 6 were waited for; matrix products, arithmetic and copies ran while one was open for 0% of the time, Pallas kernels for 18%

profile of v5, /device:TPU:0, one launch (start us, length us, event | category | flops | bytes accessed | tf_op | source)
XLA Modules:
  0.0 46.8 jit_solution(16629829380055319173)
XLA Ops:
  0.0 2.1 %shard_map.82.refs_0_.refs_2_ = bf16[12,48,128]{2,1,0:T(8,128)(2,1)} custom-call(bf16[12,48,128]{2,1,0:T(8,128)(2,1)} %refs_1_.1, s32[1,96]{1,0:T(1,128)} %bitcast.1, bf16[128,512]{1,0:T(8,128)(2,1)} %refs_3_.1), custom_call_target="tpu_custom_call" | custom-call | flops 100000000 | bytes 426368 | tf_op jit(solution)/shard_map/pallas_call | solution.py:26
  2.1 4.1 %collective-permute-start.2 = (bf16[12,48,128]{2,1,0:T(8,128)(2,1)}, bf16[12,48,128]{2,1,0:T(8,128)(2,1)S(1)}, u32[]{:S(2)}, u32[]{:S(2)}) collective-permute-start(bf16[12,48,128]{2,1,0:T(8,128)(2,1)} %shard_map.82.refs_0_.refs_2_), channel_id=1, source_target_pairs={{0,8},{2,10},{4,12},{6,14},{8,0},{10,2},{12,4},{14,6},{1,9},{3,11}... | collective-permute-start | bytes 442376 | tf_op jit(solution)/shard_map/ppermute | solution.py:278
  6.2 1.6 %collective-permute-start.1 = (bf16[12,48,128]{2,1,0:T(8,128)(2,1)}, bf16[12,48,128]{2,1,0:T(8,128)(2,1)S(1)}, u32[]{:S(2)}, u32[]{:S(2)}) collective-permute-start(bf16[12,48,128]{2,1,0:T(8,128)(2,1)} %shard_map.82.refs_0_.refs_2_), channel_id=1, source_target_pairs={{0,4},{2,6},{4,0},{6,2},{8,12},{10,14},{12,8},{14,10},{1,5},{3,7},... | collective-permute-start | bytes 442376 | tf_op jit(solution)/shard_map/ppermute | solution.py:278
  7.8 0.9 %copy-done.1 = bf16[12,48,128]{2,1,0:T(8,128)(2,1)S(1)} copy-done((bf16[12,48,128]{2,1,0:T(8,128)(2,1)S(1)}, bf16[12,48,128]{2,1,0:T(8,128)(2,1)}, u32[]{:S(2)}) %copy-start.1) | copy-done | bytes 147480
  9.3 1.6 %collective-permute-start.8 = (bf16[12,48,128]{2,1,0:T(8,128)(2,1)S(1)}, bf16[12,48,128]{2,1,0:T(8,128)(2,1)S(1)}, u32[]{:S(2)}, u32[]{:S(2)}) collective-permute-start(bf16[12,48,128]{2,1,0:T(8,128)(2,1)S(1)} %get-tuple-element.36.refs_0_), channel_id=1, source_target_pairs={{0,1},{1,0},{2,3},{3,2},{4,5},{5,4},{6,7},{7,6},{8,9},{9,8},{10,11... | collective-permute-start | bytes 442376 | tf_op jit(solution)/shard_map/ppermute | solution.py:286
  10.8 2.7 %collective-permute-done.2.refs_4_ = bf16[12,48,128]{2,1,0:T(8,128)(2,1)S(1)} collective-permute-done((bf16[12,48,128]{2,1,0:T(8,128)(2,1)}, bf16[12,48,128]{2,1,0:T(8,128)(2,1)S(1)}, u32[]{:S(2)}, u32[]{:S(2)}) %collective-permute-start.2) | collective-permute-done | bytes 147488 | tf_op jit(solution)/shard_map/ppermute | solution.py:278
  13.6 0.7 %collective-permute-start.6 = (bf16[12,48,128]{2,1,0:T(8,128)(2,1)S(1)}, bf16[12,48,128]{2,1,0:T(8,128)(2,1)S(1)}, u32[]{:S(2)}, u32[]{:S(2)}) collective-permute-start(bf16[12,48,128]{2,1,0:T(8,128)(2,1)S(1)} %collective-permute-done.2.refs_4_), channel_id=1, source_target_pairs={{0,4},{2,6},{4,0},{6,2},{8,12},{10,14},{12,8},{14,10},{1,5},{3,7},... | collective-permute-start | bytes 442376 | tf_op jit(solution)/shard_map/ppermute | solution.py:278
  14.3 1.2 %shard_map.84 = (bf16[288,128]{1,0:T(8,128)(2,1)S(1)}, bf16[288,128]{1,0:T(8,128)(2,1)S(1)}) custom-call(bf16[12,48,128]{2,1,0:T(8,128)(2,1)S(1)} %get-tuple-element.29.refs_0_.refs_2_, bf16[12,48,128]{2,1,0:T(8,128)(2,1)S(1)} %collective-permute-done.refs_1_.refs_3_.refs_0_, bf16[12,48,128]{2,1,0:T(8,128)(2,1)S(1)} %copy-done.2, ...), custom_call_target="tpu_custom_call" | custom-call | flops 500000000 | bytes 737280 | tf_op jit(solution)/shard_map/pallas_call | solution.py:26
  15.5 0.9 %shard_map.85 = (bf16[432,128]{1,0:T(8,128)(2,1)S(1)}, bf16[432,128]{1,0:T(8,128)(2,1)S(1)}) custom-call(bf16[288,128]{1,0:T(8,128)(2,1)S(1)} %get-tuple-element.30.refs_0_, bf16[288,128]{1,0:T(8,128)(2,1)S(1)} %get-tuple-element.31.refs_1_, bf16[12,48,128]{2,1,0:T(8,128)(2,1)S(1)} %get-tuple-element.29.refs_0_.refs_2_, ...), custom_call_target="tpu_custom_call" | custom-call | flops 250000000 | bytes 811008 | tf_op jit(solution)/shard_map/pallas_call | solution.py:26
  16.4 0.9 %collective-permute-start.5 = (bf16[432,128]{1,0:T(8,128)(2,1)S(1)}, bf16[432,128]{1,0:T(8,128)(2,1)S(1)}, u32[]{:S(2)}, u32[]{:S(2)}) collective-permute-start(bf16[432,128]{1,0:T(8,128)(2,1)S(1)} %get-tuple-element.33), channel_id=1, source_target_pairs={{0,3},{1,2},{2,1},{3,0},{4,7},{5,6},{6,5},{7,4},{8,11},{9,10},{10,... | collective-permute-start | bytes 331784 | tf_op jit(solution)/shard_map/ppermute | solution.py:286
  17.3 0.8 %collective-permute-start.4 = (bf16[432,128]{1,0:T(8,128)(2,1)S(1)}, bf16[432,128]{1,0:T(8,128)(2,1)S(1)}, u32[]{:S(2)}, u32[]{:S(2)}) collective-permute-start(bf16[432,128]{1,0:T(8,128)(2,1)S(1)} %get-tuple-element.33), channel_id=1, source_target_pairs={{0,2},{1,3},{2,0},{3,1},{4,6},{5,7},{6,4},{7,5},{8,10},{9,11},{10,... | collective-permute-start | bytes 331784 | tf_op jit(solution)/shard_map/ppermute | solution.py:286
  18.6 0.9 %shard_map.88 = (bf16[12,48,128]{2,1,0:T(8,128)(2,1)S(1)}, f32[12,48,128]{2,1,0:T(8,128)S(1)}, bf16[12,48,128]{2,1,0:T(8,128)(2,1)S(1)}, f32[12,48,128]{2,1,0:T(8,128)S(1)}) custom-call(bf16[12,48,128]{2,1,0:T(8,128)(2,1)S(1)} %get-tuple-element.36.refs_0_, bf16[12,48,128]{2,1,0:T(8,128)(2,1)S(1)} %collective-permute-done.8.refs_1_, ...), custom_call_target="tpu_custom_call" | custom-call | flops 100000000 | bytes 1212416 | tf_op jit(solution)/shard_map/pallas_call | solution.py:26
  20.6 0.9 %collective-permute-start.10 = (bf16[144,128]{1,0:T(8,128)(2,1)S(1)}, bf16[144,128]{1,0:T(8,128)(2,1)S(1)}, u32[]{:S(2)}, u32[]{:S(2)}) collective-permute-start(bf16[144,128]{1,0:T(8,128)(2,1)S(1)} %shard_map.87), channel_id=1, source_target_pairs={{0,3},{1,2},{2,1},{3,0},{4,7},{5,6},{6,5},{7,4},{8,11},{9,10},{10,... | collective-permute-start | bytes 110600 | tf_op jit(solution)/shard_map/ppermute | solution.py:286
  21.4 0.8 %collective-permute-start.7 = (bf16[144,128]{1,0:T(8,128)(2,1)S(1)}, bf16[144,128]{1,0:T(8,128)(2,1)S(1)}, u32[]{:S(2)}, u32[]{:S(2)}) collective-permute-start(bf16[144,128]{1,0:T(8,128)(2,1)S(1)} %shard_map.86.refs_4_), channel_id=1, source_target_pairs={{0,1},{1,0},{2,3},{3,2},{4,5},{5,4},{6,7},{7,6},{8,9},{9,8},{10,11... | collective-permute-start | bytes 110600 | tf_op jit(solution)/shard_map/ppermute | solution.py:286
  22.5 1.8 %collective-permute-done.3.refs_1_ = bf16[432,128]{1,0:T(8,128)(2,1)S(1)} collective-permute-done((bf16[432,128]{1,0:T(8,128)(2,1)S(1)}, bf16[432,128]{1,0:T(8,128)(2,1)S(1)}, u32[]{:S(2)}, u32[]{:S(2)}) %collective-permute-start.3) | collective-permute-done | bytes 110624 | tf_op jit(solution)/shard_map/ppermute | solution.py:286
  24.3 1.1 %shard_map.89 = (bf16[12,48,128]{2,1,0:T(8,128)(2,1)S(1)}, bf16[12,48,128]{2,1,0:T(8,128)(2,1)S(1)}, bf16[12,24,128]{2,1,0:T(8,128)(2,1)S(1)}, bf16[12,24,128]{2,1,0:T(8,128)(2,1)S(1)}) custom-call(bf16[432,128]{1,0:T(8,128)(2,1)S(1)} %get-tuple-element.32.refs_0_, bf16[432,128]{1,0:T(8,128)(2,1)S(1)} %collective-permute-done.3.refs_1_, ...), custom_call_target="tpu_custom_call" | custom-call | flops 300000000 | bytes 1491328 | tf_op jit(solution)/shard_map/pallas_call | solution.py:26
  25.8 1.1 %shard_map.90 = (bf16[12,48,128]{2,1,0:T(8,128)(2,1)S(1)}, bf16[12,48,128]{2,1,0:T(8,128)(2,1)S(1)}, bf16[12,24,128]{2,1,0:T(8,128)(2,1)S(1)}, bf16[12,24,128]{2,1,0:T(8,128)(2,1)S(1)}) custom-call(bf16[432,128]{1,0:T(8,128)(2,1)S(1)} %get-tuple-element.32.refs_0_, bf16[432,128]{1,0:T(8,128)(2,1)S(1)} %collective-permute-done.3.refs_1_, ...), custom_call_target="tpu_custom_call" | custom-call | flops 300000000 | bytes 1933696 | tf_op jit(solution)/shard_map/pallas_call | solution.py:26
  27.6 0.9 %collective-permute-done.11.refs_1_.refs_3_ = bf16[12,24,128]{2,1,0:T(8,128)(2,1)S(1)} collective-permute-done((bf16[12,24,128]{2,1,0:T(8,128)(2,1)S(1)}, bf16[12,24,128]{2,1,0:T(8,128)(2,1)S(1)}, u32[]{:S(2)}, u32[]{:S(2)}) %collective-permute-start.11) | collective-permute-done | bytes 73760 | tf_op jit(solution)/shard_map/ppermute | solution.py:278
  28.5 1.3 %shard_map.93 = (bf16[12,48,128]{2,1,0:T(8,128)(2,1)S(1)}, bf16[12,48,128]{2,1,0:T(8,128)(2,1)S(1)}) custom-call(bf16[12,48,128]{2,1,0:T(8,128)(2,1)S(1)} %get-tuple-element.47.refs_2_.refs_0_, bf16[12,48,128]{2,1,0:T(8,128)(2,1)S(1)} %collective-permute-done.12.refs_3_.refs_1_, bf16[12,24,128]{2,1,0:T(8,128)(2,1)S(1)} %get-tuple-element.45.refs_0_.refs_2_, ...), custom_call_target="tpu_custom_call" | custom-call | flops 400000000 | bytes 737280 | tf_op jit(solution)/shard_map/pallas_call | solution.py:26
  29.8 3.3 %collective-permute-start.15 = (bf16[12,48,128]{2,1,0:T(8,128)(2,1)S(1)}, bf16[12,48,128]{2,1,0:T(8,128)(2,1)S(1)}, u32[]{:S(2)}, u32[]{:S(2)}) collective-permute-start(bf16[12,48,128]{2,1,0:T(8,128)(2,1)S(1)} %get-tuple-element.50), channel_id=1, source_target_pairs={{0,8},{2,10},{4,12},{6,14},{8,0},{10,2},{12,4},{14,6},{1,9},{3,11}... | collective-permute-start | bytes 442376 | tf_op jit(solution)/shard_map/ppermute | solution.py:278
  33.5 0.7 %shard_map.92 = bf16[12,48,128]{2,1,0:T(8,128)(2,1)S(1)} custom-call(bf16[12,24,128]{2,1,0:T(8,128)(2,1)S(1)} %get-tuple-element.45.refs_0_.refs_2_, bf16[12,24,128]{2,1,0:T(8,128)(2,1)S(1)} %collective-permute-done.11.refs_1_.refs_3_, bf16[12,48,128]{2,1,0:T(8,128)(2,1)S(1)} %get-tuple-element.47.refs_2_.refs_0_, ...), custom_call_target="tpu_custom_call" | custom-call | flops 200000000 | bytes 737280 | tf_op jit(solution)/shard_map/pallas_call | solution.py:26
  35.5 8.5 %collective-permute-done.15.refs_2_ = bf16[12,48,128]{2,1,0:T(8,128)(2,1)S(1)} collective-permute-done((bf16[12,48,128]{2,1,0:T(8,128)(2,1)S(1)}, bf16[12,48,128]{2,1,0:T(8,128)(2,1)S(1)}, u32[]{:S(2)}, u32[]{:S(2)}) %collective-permute-start.15) | collective-permute-done | bytes 147488 | tf_op jit(solution)/shard_map/ppermute | solution.py:278
  44.0 1.8 %collective-permute-done.14.refs_1_ = bf16[12,48,128]{2,1,0:T(8,128)(2,1)S(1)} collective-permute-done((bf16[12,48,128]{2,1,0:T(8,128)(2,1)S(1)}, bf16[12,48,128]{2,1,0:T(8,128)(2,1)S(1)}, u32[]{:S(2)}, u32[]{:S(2)}) %collective-permute-start.14) | collective-permute-done | bytes 147488 | tf_op jit(solution)/shard_map/ppermute | solution.py:278
  45.8 1.0 %shard_map.95 = bf16[12,48,128]{2,1,0:T(8,128)(2,1)} custom-call(f32[12,48,128]{2,1,0:T(8,128)S(1)} %shard_map.91.refs_0_, bf16[12,48,128]{2,1,0:T(8,128)(2,1)S(1)} %collective-permute-done.14.refs_1_, bf16[12,48,128]{2,1,0:T(8,128)(2,1)S(1)} %collective-permute-done.15.refs_2_, bf16[12,48,128]{2,1,0:T(8,128)(2,1)S(1)} %collective-permute-done.16.refs_3_, ...), custom_call_target="tpu_custom_call" | custom-call | flops 100000000 | bytes 1359872 | tf_op jit(solution)/shard_map/pallas_call | solution.py:26
  (44 shorter events, 5.2 us)
Async XLA Ops:
  0.0 7.8 %copy-start = (bf16[12,48,128]{2,1,0:T(8,128)(2,1)S(1)}, bf16[12,48,128]{2,1,0:T(8,128)(2,1)}, u32[]{:S(2)}) copy-start(bf16[12,48,128]{2,1,0:T(8,128)(2,1)} %refs_1_.1) | copy-start | bytes 442372
  0.0 7.8 %copy-start.3 = (bf16[128,512]{1,0:T(8,128)(2,1)S(1)}, bf16[128,512]{1,0:T(8,128)(2,1)}, u32[]{:S(2)}) copy-start(bf16[128,512]{1,0:T(8,128)(2,1)} %refs_3_.1) | copy-start | bytes 393220
  0.0 7.8 %copy-start.8 = (s32[96]{0:T(128)S(1)}, s32[96]{0:T(128)}, u32[]{:S(2)}) copy-start(s32[96]{0:T(128)} %param.9) | copy-start | bytes 1156
  2.1 11.4 %collective-permute-start.2 = (bf16[12,48,128]{2,1,0:T(8,128)(2,1)}, bf16[12,48,128]{2,1,0:T(8,128)(2,1)S(1)}, u32[]{:S(2)}, u32[]{:S(2)}) collective-permute-start(bf16[12,48,128]{2,1,0:T(8,128)(2,1)} %shard_map.82.refs_0_.refs_2_), channel_id=1, source_target_pairs={{0,8},{2,10},{4,12},{6,14},{8,0},{10,2},{12,4},{14,6},{1,9},{3,11}... | collective-permute-start | bytes 442376 | tf_op jit(solution)/shard_map/ppermute | solution.py:278
  6.2 8.0 %collective-permute-start.1 = (bf16[12,48,128]{2,1,0:T(8,128)(2,1)}, bf16[12,48,128]{2,1,0:T(8,128)(2,1)S(1)}, u32[]{:S(2)}, u32[]{:S(2)}) collective-permute-start(bf16[12,48,128]{2,1,0:T(8,128)(2,1)} %shard_map.82.refs_0_.refs_2_), channel_id=1, source_target_pairs={{0,4},{2,6},{4,0},{6,2},{8,12},{10,14},{12,8},{14,10},{1,5},{3,7},... | collective-permute-start | bytes 442376 | tf_op jit(solution)/shard_map/ppermute | solution.py:278
  8.8 5.5 %copy-start.2 = (bf16[12,48,128]{2,1,0:T(8,128)(2,1)S(1)}, bf16[12,48,128]{2,1,0:T(8,128)(2,1)}, u32[]{:S(2)}) copy-start(bf16[12,48,128]{2,1,0:T(8,128)(2,1)} %shard_map.82.refs_0_.refs_2_) | copy-start | bytes 442372
  9.2 5.1 %collective-permute-start = (bf16[12,48,128]{2,1,0:T(8,128)(2,1)S(1)}, bf16[12,48,128]{2,1,0:T(8,128)(2,1)S(1)}, u32[]{:S(2)}, u32[]{:S(2)}) collective-permute-start(bf16[12,48,128]{2,1,0:T(8,128)(2,1)S(1)} %get-tuple-element.29.refs_0_.refs_2_), channel_id=1, source_target_pairs={{0,2},{2,0},{4,6},{6,4},{8,10},{10,8},{12,14},{14,12},{1,3},{3,1},... | collective-permute-start | bytes 442376 | tf_op jit(solution)/shard_map/ppermute | solution.py:278
  9.3 9.3 %collective-permute-start.8 = (bf16[12,48,128]{2,1,0:T(8,128)(2,1)S(1)}, bf16[12,48,128]{2,1,0:T(8,128)(2,1)S(1)}, u32[]{:S(2)}, u32[]{:S(2)}) collective-permute-start(bf16[12,48,128]{2,1,0:T(8,128)(2,1)S(1)} %get-tuple-element.36.refs_0_), channel_id=1, source_target_pairs={{0,1},{1,0},{2,3},{3,2},{4,5},{5,4},{6,7},{7,6},{8,9},{9,8},{10,11... | collective-permute-start | bytes 442376 | tf_op jit(solution)/shard_map/ppermute | solution.py:286
  13.6 5.9 %collective-permute-start.6 = (bf16[12,48,128]{2,1,0:T(8,128)(2,1)S(1)}, bf16[12,48,128]{2,1,0:T(8,128)(2,1)S(1)}, u32[]{:S(2)}, u32[]{:S(2)}) collective-permute-start(bf16[12,48,128]{2,1,0:T(8,128)(2,1)S(1)} %collective-permute-done.2.refs_4_), channel_id=1, source_target_pairs={{0,4},{2,6},{4,0},{6,2},{8,12},{10,14},{12,8},{14,10},{1,5},{3,7},... | collective-permute-start | bytes 442376 | tf_op jit(solution)/shard_map/ppermute | solution.py:278
  16.4 5.8 %collective-permute-start.5 = (bf16[432,128]{1,0:T(8,128)(2,1)S(1)}, bf16[432,128]{1,0:T(8,128)(2,1)S(1)}, u32[]{:S(2)}, u32[]{:S(2)}) collective-permute-start(bf16[432,128]{1,0:T(8,128)(2,1)S(1)} %get-tuple-element.33), channel_id=1, source_target_pairs={{0,3},{1,2},{2,1},{3,0},{4,7},{5,6},{6,5},{7,4},{8,11},{9,10},{10,... | collective-permute-start | bytes 331784 | tf_op jit(solution)/shard_map/ppermute | solution.py:286
  17.3 5.2 %collective-permute-start.4 = (bf16[432,128]{1,0:T(8,128)(2,1)S(1)}, bf16[432,128]{1,0:T(8,128)(2,1)S(1)}, u32[]{:S(2)}, u32[]{:S(2)}) collective-permute-start(bf16[432,128]{1,0:T(8,128)(2,1)S(1)} %get-tuple-element.33), channel_id=1, source_target_pairs={{0,2},{1,3},{2,0},{3,1},{4,6},{5,7},{6,4},{7,5},{8,10},{9,11},{10,... | collective-permute-start | bytes 331784 | tf_op jit(solution)/shard_map/ppermute | solution.py:286
  18.1 6.2 %collective-permute-start.3 = (bf16[432,128]{1,0:T(8,128)(2,1)S(1)}, bf16[432,128]{1,0:T(8,128)(2,1)S(1)}, u32[]{:S(2)}, u32[]{:S(2)}) collective-permute-start(bf16[432,128]{1,0:T(8,128)(2,1)S(1)} %get-tuple-element.32.refs_0_), channel_id=1, source_target_pairs={{0,1},{1,0},{2,3},{3,2},{4,5},{5,4},{6,7},{7,6},{8,9},{9,8},{10,11... | collective-permute-start | bytes 331784 | tf_op jit(solution)/shard_map/ppermute | solution.py:286
  20.0 4.2 %copy-start.4 = (bf16[128,512]{1,0:T(8,128)(2,1)S(1)}, bf16[128,512]{1,0:T(8,128)(2,1)}, u32[]{:S(2)}) copy-start(bf16[128,512]{1,0:T(8,128)(2,1)} %refs_12_.1) | copy-start | bytes 393220
  20.0 4.2 %copy-start.5 = (bf16[128,128]{1,0:T(8,128)(2,1)S(1)}, bf16[128,128]{1,0:T(8,128)(2,1)}, u32[]{:S(2)}) copy-start(bf16[128,128]{1,0:T(8,128)(2,1)} %refs_11_.1) | copy-start | bytes 98308
  20.6 4.8 %collective-permute-start.10 = (bf16[144,128]{1,0:T(8,128)(2,1)S(1)}, bf16[144,128]{1,0:T(8,128)(2,1)S(1)}, u32[]{:S(2)}, u32[]{:S(2)}) collective-permute-start(bf16[144,128]{1,0:T(8,128)(2,1)S(1)} %shard_map.87), channel_id=1, source_target_pairs={{0,3},{1,2},{2,1},{3,0},{4,7},{5,6},{6,5},{7,4},{8,11},{9,10},{10,... | collective-permute-start | bytes 110600 | tf_op jit(solution)/shard_map/ppermute | solution.py:286
  21.4 4.4 %collective-permute-start.7 = (bf16[144,128]{1,0:T(8,128)(2,1)S(1)}, bf16[144,128]{1,0:T(8,128)(2,1)S(1)}, u32[]{:S(2)}, u32[]{:S(2)}) collective-permute-start(bf16[144,128]{1,0:T(8,128)(2,1)S(1)} %shard_map.86.refs_4_), channel_id=1, source_target_pairs={{0,1},{1,0},{2,3},{3,2},{4,5},{5,4},{6,7},{7,6},{8,9},{9,8},{10,11... | collective-permute-start | bytes 110600 | tf_op jit(solution)/shard_map/ppermute | solution.py:286
  22.2 3.6 %collective-permute-start.9 = (bf16[144,128]{1,0:T(8,128)(2,1)S(1)}, bf16[144,128]{1,0:T(8,128)(2,1)S(1)}, u32[]{:S(2)}, u32[]{:S(2)}) collective-permute-start(bf16[144,128]{1,0:T(8,128)(2,1)S(1)} %shard_map.87), channel_id=1, source_target_pairs={{0,2},{1,3},{2,0},{3,1},{4,6},{5,7},{6,4},{7,5},{8,10},{9,11},{10,... | collective-permute-start | bytes 110600 | tf_op jit(solution)/shard_map/ppermute | solution.py:286
  26.9 1.5 %collective-permute-start.12 = (bf16[12,48,128]{2,1,0:T(8,128)(2,1)S(1)}, bf16[12,48,128]{2,1,0:T(8,128)(2,1)S(1)}, u32[]{:S(2)}, u32[]{:S(2)}) collective-permute-start(bf16[12,48,128]{2,1,0:T(8,128)(2,1)S(1)} %get-tuple-element.47.refs_2_.refs_0_), channel_id=1, source_target_pairs={{0,2},{2,0},{4,6},{6,4},{8,10},{10,8},{12,14},{14,12},{1,3},{3,1},... | collective-permute-start | bytes 442376 | tf_op jit(solution)/shard_map/ppermute | solution.py:278
  27.1 1.4 %collective-permute-start.11 = (bf16[12,24,128]{2,1,0:T(8,128)(2,1)S(1)}, bf16[12,24,128]{2,1,0:T(8,128)(2,1)S(1)}, u32[]{:S(2)}, u32[]{:S(2)}) collective-permute-start(bf16[12,24,128]{2,1,0:T(8,128)(2,1)S(1)} %get-tuple-element.46), channel_id=1, source_target_pairs={{0,2},{2,0},{4,6},{6,4},{8,10},{10,8},{12,14},{14,12},{1,3},{3,1},... | collective-permute-start | bytes 221192 | tf_op jit(solution)/shard_map/ppermute | solution.py:278
  27.5 6.0 %collective-permute-start.13 = (bf16[12,24,128]{2,1,0:T(8,128)(2,1)S(1)}, bf16[12,24,128]{2,1,0:T(8,128)(2,1)S(1)}, u32[]{:S(2)}, u32[]{:S(2)}) collective-permute-start(bf16[12,24,128]{2,1,0:T(8,128)(2,1)S(1)} %get-tuple-element.49), channel_id=1, source_target_pairs={{0,2},{2,0},{4,6},{6,4},{8,10},{10,8},{12,14},{14,12},{1,3},{3,1},... | collective-permute-start | bytes 221192 | tf_op jit(solution)/shard_map/ppermute | solution.py:278
  29.8 14.2 %collective-permute-start.15 = (bf16[12,48,128]{2,1,0:T(8,128)(2,1)S(1)}, bf16[12,48,128]{2,1,0:T(8,128)(2,1)S(1)}, u32[]{:S(2)}, u32[]{:S(2)}) collective-permute-start(bf16[12,48,128]{2,1,0:T(8,128)(2,1)S(1)} %get-tuple-element.50), channel_id=1, source_target_pairs={{0,8},{2,10},{4,12},{6,14},{8,0},{10,2},{12,4},{14,6},{1,9},{3,11}... | collective-permute-start | bytes 442376 | tf_op jit(solution)/shard_map/ppermute | solution.py:278
  33.1 10.9 %collective-permute-start.16 = (bf16[12,48,128]{2,1,0:T(8,128)(2,1)S(1)}, bf16[12,48,128]{2,1,0:T(8,128)(2,1)S(1)}, u32[]{:S(2)}, u32[]{:S(2)}) collective-permute-start(bf16[12,48,128]{2,1,0:T(8,128)(2,1)S(1)} %get-tuple-element.51), channel_id=1, source_target_pairs={{0,12},{2,14},{4,8},{6,10},{8,4},{10,6},{12,0},{14,2},{1,13},{3,15... | collective-permute-start | bytes 442376 | tf_op jit(solution)/shard_map/ppermute | solution.py:278
  34.2 11.7 %collective-permute-start.14 = (bf16[12,48,128]{2,1,0:T(8,128)(2,1)S(1)}, bf16[12,48,128]{2,1,0:T(8,128)(2,1)S(1)}, u32[]{:S(2)}, u32[]{:S(2)}) collective-permute-start(bf16[12,48,128]{2,1,0:T(8,128)(2,1)S(1)} %shard_map.92), channel_id=1, source_target_pairs={{0,4},{2,6},{4,0},{6,2},{8,12},{10,14},{12,8},{14,10},{1,5},{3,7},... | collective-permute-start | bytes 442376 | tf_op jit(solution)/shard_map/ppermute | solution.py:278
  34.8 11.0 %copy-start.6 = (bf16[128,128]{1,0:T(8,128)(2,1)S(1)}, bf16[128,128]{1,0:T(8,128)(2,1)}, u32[]{:S(2)}) copy-start(bf16[128,128]{1,0:T(8,128)(2,1)} %refs_6_.1) | copy-start | bytes 98308
  (3 other events, 5.0 us)

commit v6 on v5

--- a/solution.py
+++ b/solution.py
@@ -313,13 +313,6 @@
         outside=(0,),
     )
     pairs = [pair_copy] + [shift(pair_copy, dx, 0) for dx in range(1, cols_n)]
-    gates = call(
-        functools.partial(gates_kernel, cols_n),
-        [block, block32] * cols_n,
-        pairs + [out_gating],
-        flops=100_000_000,
-    )
-    gates = list(gates)
     core_left = along_row(left, 1)
     def product(blocks, sides, earlier=()):
         area = rows * len(blocks) * rows
@@ -344,13 +337,23 @@
         early = product([m], both, early)
     mine, other = early
     parts = [mine] + [shift(mine, dx, 0) for dx in range(1, cols_n)]
-    exchanged = [parts + [shift(other, dx, 1) for dx in range(cols_n)]]
+    across = [shift(other, dx, 1) for dx in range(1, cols_n)]
+    other_core = other
     (mine,) = product([chips - 1], [left])
     mine, core_left = lax.optimization_barrier((mine, core_left))
     (other,) = product([chips - 1], [core_left])
-    other_core, gates[1] = lax.optimization_barrier((other, gates[1]))
+    other, out_gating = lax.optimization_barrier((other, out_gating))
+    gates = call(
+        functools.partial(gates_kernel, cols_n),
+        [block, block32] * cols_n,
+        pairs + [out_gating],
+        flops=100_000_000,
+    )
+    gates = list(gates)
+    other_core, last_core, gates[1] = lax.optimization_barrier((other_core, other, gates[1]))
+    exchanged = [parts + [shift(other_core, 0, 1)] + across]
     parts = [mine] + [shift(mine, dx, 0) for dx in range(1, cols_n)]
-    parts += [shift(other_core, 0, 1)] + [shift(other, dx, 1) for dx in range(1, cols_n)]
+    parts += [shift(last_core, 0, 1)] + [shift(other, dx, 1) for dx in range(1, cols_n)]
     exchanged.append(parts)
     firsts, lefts = [], []
     for h in range(cols_n):

time: 47 us -> 48.3 us (1.028)
  waiting for transfers between devices: 16.1 us -> 17.1 us
    ppermute x10, waiting for transfers between devices: 13.9 us -> 15.2 us  [along_row(): return lax.ppermute(v, 'row', [(i, i ^ bits) for i in range(rows_n)])]
where the time goes in v6:
time: 48.3 us; the launch traced here: 48 us
  waiting for transfers between devices  17.1 us (35%)
  starting transfers between devices  16.8 us (35%)
  Pallas kernels  12.8 us (27%)
  local copies, waits for them, and re-layouts  1.17 us (2%)
    ppermute x10, waiting for transfers between devices, along_row(): return lax.ppermute(v, 'row', [(i, i ^ bits) for i in range(rows_n)])  15.2 us
    pallas_call x14, Pallas kernels, call(): pl.pallas_call(kernel, out_shape=outs, in_specs=[pl.BlockSpec(memory_spac...  12.8 us
    ppermute x10, starting transfers between devices, along_row(): return lax.ppermute(v, 'row', [(i, i ^ bits) for i in range(rows_n)])  11.5 us
    ppermute x7, starting transfers between devices, shift(): return lax.ppermute(v, ('row', 'col'), pairs)  5.35 us
    ppermute x7, waiting for transfers between devices, shift(): return lax.ppermute(v, ('row', 'col'), pairs)  1.87 us
    unnamed x20, local copies, waits for them, and re-layouts  1.17 us
  transfers between devices with their start and end apart: 17, of which 6 were waited for; matrix products, arithmetic and copies ran while one was open for 0% of the time, Pallas kernels for 18%

profile of v6, /device:TPU:0, one launch (start us, length us, event | category | flops | bytes accessed | tf_op | source)
XLA Modules:
  0.0 48.0 jit_solution(14063407094920163640)
XLA Ops:
  0.0 2.1 %shard_map.82.refs_0_.refs_2_ = bf16[12,48,128]{2,1,0:T(8,128)(2,1)} custom-call(bf16[12,48,128]{2,1,0:T(8,128)(2,1)} %refs_1_.1, s32[1,96]{1,0:T(1,128)} %bitcast.1, bf16[128,512]{1,0:T(8,128)(2,1)} %refs_3_.1), custom_call_target="tpu_custom_call" | custom-call | flops 100000000 | bytes 426368 | tf_op jit(solution)/shard_map/pallas_call | solution.py:26
  2.1 4.1 %collective-permute-start.2 = (bf16[12,48,128]{2,1,0:T(8,128)(2,1)}, bf16[12,48,128]{2,1,0:T(8,128)(2,1)S(1)}, u32[]{:S(2)}, u32[]{:S(2)}) collective-permute-start(bf16[12,48,128]{2,1,0:T(8,128)(2,1)} %shard_map.82.refs_0_.refs_2_), channel_id=1, source_target_pairs={{0,8},{2,10},{4,12},{6,14},{8,0},{10,2},{12,4},{14,6},{1,9},{3,11}... | collective-permute-start | bytes 442376 | tf_op jit(solution)/shard_map/ppermute | solution.py:278
  6.2 1.6 %collective-permute-start.1 = (bf16[12,48,128]{2,1,0:T(8,128)(2,1)}, bf16[12,48,128]{2,1,0:T(8,128)(2,1)S(1)}, u32[]{:S(2)}, u32[]{:S(2)}) collective-permute-start(bf16[12,48,128]{2,1,0:T(8,128)(2,1)} %shard_map.82.refs_0_.refs_2_), channel_id=1, source_target_pairs={{0,4},{2,6},{4,0},{6,2},{8,12},{10,14},{12,8},{14,10},{1,5},{3,7},... | collective-permute-start | bytes 442376 | tf_op jit(solution)/shard_map/ppermute | solution.py:278
  7.8 0.9 %copy-done.1 = bf16[12,48,128]{2,1,0:T(8,128)(2,1)S(1)} copy-done((bf16[12,48,128]{2,1,0:T(8,128)(2,1)S(1)}, bf16[12,48,128]{2,1,0:T(8,128)(2,1)}, u32[]{:S(2)}) %copy-start.1) | copy-done | bytes 147480
  9.3 4.3 %collective-permute-done.2.refs_4_ = bf16[12,48,128]{2,1,0:T(8,128)(2,1)S(1)} collective-permute-done((bf16[12,48,128]{2,1,0:T(8,128)(2,1)}, bf16[12,48,128]{2,1,0:T(8,128)(2,1)S(1)}, u32[]{:S(2)}, u32[]{:S(2)}) %collective-permute-start.2) | collective-permute-done | bytes 147488 | tf_op jit(solution)/shard_map/ppermute | solution.py:278
  13.6 0.7 %collective-permute-start.4 = (bf16[12,48,128]{2,1,0:T(8,128)(2,1)S(1)}, bf16[12,48,128]{2,1,0:T(8,128)(2,1)S(1)}, u32[]{:S(2)}, u32[]{:S(2)}) collective-permute-start(bf16[12,48,128]{2,1,0:T(8,128)(2,1)S(1)} %collective-permute-done.2.refs_4_), channel_id=1, source_target_pairs={{0,4},{2,6},{4,0},{6,2},{8,12},{10,14},{12,8},{14,10},{1,5},{3,7},... | collective-permute-start | bytes 442376 | tf_op jit(solution)/shard_map/ppermute | solution.py:278
  14.3 1.5 %collective-permute-start.5 = (bf16[12,48,128]{2,1,0:T(8,128)(2,1)S(1)}, bf16[12,48,128]{2,1,0:T(8,128)(2,1)S(1)}, u32[]{:S(2)}, u32[]{:S(2)}) collective-permute-start(bf16[12,48,128]{2,1,0:T(8,128)(2,1)S(1)} %get-tuple-element.39.refs_0_), channel_id=1, source_target_pairs={{0,1},{1,0},{2,3},{3,2},{4,5},{5,4},{6,7},{7,6},{8,9},{9,8},{10,11... | collective-permute-start | bytes 442376 | tf_op jit(solution)/shard_map/ppermute | solution.py:286
  15.8 1.2 %shard_map.84 = (bf16[288,128]{1,0:T(8,128)(2,1)S(1)}, bf16[288,128]{1,0:T(8,128)(2,1)S(1)}) custom-call(bf16[12,48,128]{2,1,0:T(8,128)(2,1)S(1)} %get-tuple-element.32.refs_0_.refs_2_, bf16[12,48,128]{2,1,0:T(8,128)(2,1)S(1)} %collective-permute-done.refs_1_.refs_3_.refs_0_, bf16[12,48,128]{2,1,0:T(8,128)(2,1)S(1)} %copy-done.2, ...), custom_call_target="tpu_custom_call" | custom-call | flops 500000000 | bytes 737280 | tf_op jit(solution)/shard_map/pallas_call | solution.py:26
  17.0 0.9 %shard_map.85 = (bf16[432,128]{1,0:T(8,128)(2,1)S(1)}, bf16[432,128]{1,0:T(8,128)(2,1)S(1)}) custom-call(bf16[288,128]{1,0:T(8,128)(2,1)S(1)} %get-tuple-element.33.refs_0_, bf16[288,128]{1,0:T(8,128)(2,1)S(1)} %get-tuple-element.34.refs_1_, bf16[12,48,128]{2,1,0:T(8,128)(2,1)S(1)} %get-tuple-element.32.refs_0_.refs_2_, ...), custom_call_target="tpu_custom_call" | custom-call | flops 250000000 | bytes 811008 | tf_op jit(solution)/shard_map/pallas_call | solution.py:26
  18.0 1.1 %collective-permute-start.3 = (bf16[432,128]{1,0:T(8,128)(2,1)S(1)}, bf16[432,128]{1,0:T(8,128)(2,1)S(1)}, u32[]{:S(2)}, u32[]{:S(2)}) collective-permute-start(bf16[432,128]{1,0:T(8,128)(2,1)S(1)} %get-tuple-element.35.refs_0_), channel_id=1, source_target_pairs={{0,1},{1,0},{2,3},{3,2},{4,5},{5,4},{6,7},{7,6},{8,9},{9,8},{10,11... | collective-permute-start | bytes 331784 | tf_op jit(solution)/shard_map/ppermute | solution.py:286
  20.3 0.9 %shard_map.88 = (bf16[12,48,128]{2,1,0:T(8,128)(2,1)S(1)}, f32[12,48,128]{2,1,0:T(8,128)S(1)}, bf16[12,48,128]{2,1,0:T(8,128)(2,1)S(1)}, f32[12,48,128]{2,1,0:T(8,128)S(1)}) custom-call(bf16[12,48,128]{2,1,0:T(8,128)(2,1)S(1)} %get-tuple-element.39.refs_0_, bf16[12,48,128]{2,1,0:T(8,128)(2,1)S(1)} %collective-permute-done.5.refs_1_, ...), custom_call_target="tpu_custom_call" | custom-call | flops 100000000 | bytes 1212416 | tf_op jit(solution)/shard_map/pallas_call | solution.py:26
  21.2 0.8 %collective-permute-start.6 = (bf16[432,128]{1,0:T(8,128)(2,1)S(1)}, bf16[432,128]{1,0:T(8,128)(2,1)S(1)}, u32[]{:S(2)}, u32[]{:S(2)}) collective-permute-start(bf16[432,128]{1,0:T(8,128)(2,1)S(1)} %get-tuple-element.42), channel_id=1, source_target_pairs={{0,2},{1,3},{2,0},{3,1},{4,6},{5,7},{6,4},{7,5},{8,10},{9,11},{10,... | collective-permute-start | bytes 331784 | tf_op jit(solution)/shard_map/ppermute | solution.py:286
  22.6 1.2 %collective-permute-start.8 = (bf16[144,128]{1,0:T(8,128)(2,1)S(1)}, bf16[144,128]{1,0:T(8,128)(2,1)S(1)}, u32[]{:S(2)}, u32[]{:S(2)}) collective-permute-start(bf16[144,128]{1,0:T(8,128)(2,1)S(1)} %shard_map.86.refs_4_), channel_id=1, source_target_pairs={{0,1},{1,0},{2,3},{3,2},{4,5},{5,4},{6,7},{7,6},{8,9},{9,8},{10,11... | collective-permute-start | bytes 110600 | tf_op jit(solution)/shard_map/ppermute | solution.py:286
  23.9 1.1 %collective-permute-done.3.refs_1_ = bf16[432,128]{1,0:T(8,128)(2,1)S(1)} collective-permute-done((bf16[432,128]{1,0:T(8,128)(2,1)S(1)}, bf16[432,128]{1,0:T(8,128)(2,1)S(1)}, u32[]{:S(2)}, u32[]{:S(2)}) %collective-permute-start.3) | collective-permute-done | bytes 110624 | tf_op jit(solution)/shard_map/ppermute | solution.py:286
  25.1 1.1 %shard_map.89 = (bf16[12,48,128]{2,1,0:T(8,128)(2,1)S(1)}, bf16[12,48,128]{2,1,0:T(8,128)(2,1)S(1)}, bf16[12,24,128]{2,1,0:T(8,128)(2,1)S(1)}, bf16[12,24,128]{2,1,0:T(8,128)(2,1)S(1)}) custom-call(bf16[432,128]{1,0:T(8,128)(2,1)S(1)} %get-tuple-element.35.refs_0_, bf16[432,128]{1,0:T(8,128)(2,1)S(1)} %collective-permute-done.3.refs_1_, ...), custom_call_target="tpu_custom_call" | custom-call | flops 300000000 | bytes 1491328 | tf_op jit(solution)/shard_map/pallas_call | solution.py:26
  26.2 0.7 %collective-permute-done.8.refs_5_ = bf16[144,128]{1,0:T(8,128)(2,1)S(1)} collective-permute-done((bf16[144,128]{1,0:T(8,128)(2,1)S(1)}, bf16[144,128]{1,0:T(8,128)(2,1)S(1)}, u32[]{:S(2)}, u32[]{:S(2)}) %collective-permute-start.8) | collective-permute-done | bytes 36896 | tf_op jit(solution)/shard_map/ppermute | solution.py:286
  26.9 1.1 %shard_map.90 = (bf16[12,48,128]{2,1,0:T(8,128)(2,1)S(1)}, bf16[12,48,128]{2,1,0:T(8,128)(2,1)S(1)}, bf16[12,24,128]{2,1,0:T(8,128)(2,1)S(1)}, bf16[12,24,128]{2,1,0:T(8,128)(2,1)S(1)}) custom-call(bf16[432,128]{1,0:T(8,128)(2,1)S(1)} %get-tuple-element.35.refs_0_, bf16[432,128]{1,0:T(8,128)(2,1)S(1)} %collective-permute-done.3.refs_1_, ...), custom_call_target="tpu_custom_call" | custom-call | flops 300000000 | bytes 1933696 | tf_op jit(solution)/shard_map/pallas_call | solution.py:26
  28.7 0.9 %collective-permute-done.11.refs_1_.refs_3_ = bf16[12,24,128]{2,1,0:T(8,128)(2,1)S(1)} collective-permute-done((bf16[12,24,128]{2,1,0:T(8,128)(2,1)S(1)}, bf16[12,24,128]{2,1,0:T(8,128)(2,1)S(1)}, u32[]{:S(2)}, u32[]{:S(2)}) %collective-permute-start.11) | collective-permute-done | bytes 73760 | tf_op jit(solution)/shard_map/ppermute | solution.py:278
  29.6 1.3 %shard_map.93 = (bf16[12,48,128]{2,1,0:T(8,128)(2,1)S(1)}, bf16[12,48,128]{2,1,0:T(8,128)(2,1)S(1)}) custom-call(bf16[12,48,128]{2,1,0:T(8,128)(2,1)S(1)} %get-tuple-element.53.refs_2_.refs_0_, bf16[12,48,128]{2,1,0:T(8,128)(2,1)S(1)} %collective-permute-done.12.refs_3_.refs_1_, bf16[12,24,128]{2,1,0:T(8,128)(2,1)S(1)} %get-tuple-element.51.refs_0_.refs_2_, ...), custom_call_target="tpu_custom_call" | custom-call | flops 400000000 | bytes 737280 | tf_op jit(solution)/shard_map/pallas_call | solution.py:26
  30.9 3.3 %collective-permute-start.15 = (bf16[12,48,128]{2,1,0:T(8,128)(2,1)S(1)}, bf16[12,48,128]{2,1,0:T(8,128)(2,1)S(1)}, u32[]{:S(2)}, u32[]{:S(2)}) collective-permute-start(bf16[12,48,128]{2,1,0:T(8,128)(2,1)S(1)} %get-tuple-element.56), channel_id=1, source_target_pairs={{0,8},{2,10},{4,12},{6,14},{8,0},{10,2},{12,4},{14,6},{1,9},{3,11}... | collective-permute-start | bytes 442376 | tf_op jit(solution)/shard_map/ppermute | solution.py:278
  34.6 0.7 %shard_map.92 = bf16[12,48,128]{2,1,0:T(8,128)(2,1)S(1)} custom-call(bf16[12,24,128]{2,1,0:T(8,128)(2,1)S(1)} %get-tuple-element.51.refs_0_.refs_2_, bf16[12,24,128]{2,1,0:T(8,128)(2,1)S(1)} %collective-permute-done.11.refs_1_.refs_3_, bf16[12,48,128]{2,1,0:T(8,128)(2,1)S(1)} %get-tuple-element.53.refs_2_.refs_0_, ...), custom_call_target="tpu_custom_call" | custom-call | flops 200000000 | bytes 737280 | tf_op jit(solution)/shard_map/pallas_call | solution.py:26
  36.9 8.2 %collective-permute-done.15.refs_2_ = bf16[12,48,128]{2,1,0:T(8,128)(2,1)S(1)} collective-permute-done((bf16[12,48,128]{2,1,0:T(8,128)(2,1)S(1)}, bf16[12,48,128]{2,1,0:T(8,128)(2,1)S(1)}, u32[]{:S(2)}, u32[]{:S(2)}) %collective-permute-start.15) | collective-permute-done | bytes 147488 | tf_op jit(solution)/shard_map/ppermute | solution.py:278
  45.2 1.8 %collective-permute-done.14.refs_1_ = bf16[12,48,128]{2,1,0:T(8,128)(2,1)S(1)} collective-permute-done((bf16[12,48,128]{2,1,0:T(8,128)(2,1)S(1)}, bf16[12,48,128]{2,1,0:T(8,128)(2,1)S(1)}, u32[]{:S(2)}, u32[]{:S(2)}) %collective-permute-start.14) | collective-permute-done | bytes 147488 | tf_op jit(solution)/shard_map/ppermute | solution.py:278
  47.0 1.0 %shard_map.95 = bf16[12,48,128]{2,1,0:T(8,128)(2,1)} custom-call(f32[12,48,128]{2,1,0:T(8,128)S(1)} %shard_map.91.refs_0_, bf16[12,48,128]{2,1,0:T(8,128)(2,1)S(1)} %collective-permute-done.14.refs_1_, bf16[12,48,128]{2,1,0:T(8,128)(2,1)S(1)} %collective-permute-done.15.refs_2_, bf16[12,48,128]{2,1,0:T(8,128)(2,1)S(1)} %collective-permute-done.16.refs_3_, ...), custom_call_target="tpu_custom_call" | custom-call | flops 100000000 | bytes 1359872 | tf_op jit(solution)/shard_map/pallas_call | solution.py:26
  (44 shorter events, 5.3 us)
Async XLA Ops:
  0.0 7.8 %copy-start = (bf16[12,48,128]{2,1,0:T(8,128)(2,1)S(1)}, bf16[12,48,128]{2,1,0:T(8,128)(2,1)}, u32[]{:S(2)}) copy-start(bf16[12,48,128]{2,1,0:T(8,128)(2,1)} %refs_1_.1) | copy-start | bytes 442372
  0.0 7.8 %copy-start.3 = (bf16[128,512]{1,0:T(8,128)(2,1)S(1)}, bf16[128,512]{1,0:T(8,128)(2,1)}, u32[]{:S(2)}) copy-start(bf16[128,512]{1,0:T(8,128)(2,1)} %refs_3_.1) | copy-start | bytes 393220
  0.0 7.8 %copy-start.8 = (s32[96]{0:T(128)S(1)}, s32[96]{0:T(128)}, u32[]{:S(2)}) copy-start(s32[96]{0:T(128)} %param.9) | copy-start | bytes 1156
  2.1 11.4 %collective-permute-start.2 = (bf16[12,48,128]{2,1,0:T(8,128)(2,1)}, bf16[12,48,128]{2,1,0:T(8,128)(2,1)S(1)}, u32[]{:S(2)}, u32[]{:S(2)}) collective-permute-start(bf16[12,48,128]{2,1,0:T(8,128)(2,1)} %shard_map.82.refs_0_.refs_2_), channel_id=1, source_target_pairs={{0,8},{2,10},{4,12},{6,14},{8,0},{10,2},{12,4},{14,6},{1,9},{3,11}... | collective-permute-start | bytes 442376 | tf_op jit(solution)/shard_map/ppermute | solution.py:278
  6.2 9.5 %collective-permute-start.1 = (bf16[12,48,128]{2,1,0:T(8,128)(2,1)}, bf16[12,48,128]{2,1,0:T(8,128)(2,1)S(1)}, u32[]{:S(2)}, u32[]{:S(2)}) collective-permute-start(bf16[12,48,128]{2,1,0:T(8,128)(2,1)} %shard_map.82.refs_0_.refs_2_), channel_id=1, source_target_pairs={{0,4},{2,6},{4,0},{6,2},{8,12},{10,14},{12,8},{14,10},{1,5},{3,7},... | collective-permute-start | bytes 442376 | tf_op jit(solution)/shard_map/ppermute | solution.py:278
  8.8 7.0 %copy-start.2 = (bf16[12,48,128]{2,1,0:T(8,128)(2,1)S(1)}, bf16[12,48,128]{2,1,0:T(8,128)(2,1)}, u32[]{:S(2)}) copy-start(bf16[12,48,128]{2,1,0:T(8,128)(2,1)} %shard_map.82.refs_0_.refs_2_) | copy-start | bytes 442372
  9.2 6.6 %collective-permute-start = (bf16[12,48,128]{2,1,0:T(8,128)(2,1)S(1)}, bf16[12,48,128]{2,1,0:T(8,128)(2,1)S(1)}, u32[]{:S(2)}, u32[]{:S(2)}) collective-permute-start(bf16[12,48,128]{2,1,0:T(8,128)(2,1)S(1)} %get-tuple-element.32.refs_0_.refs_2_), channel_id=1, source_target_pairs={{0,2},{2,0},{4,6},{6,4},{8,10},{10,8},{12,14},{14,12},{1,3},{3,1},... | collective-permute-start | bytes 442376 | tf_op jit(solution)/shard_map/ppermute | solution.py:278
  13.6 5.5 %collective-permute-start.4 = (bf16[12,48,128]{2,1,0:T(8,128)(2,1)S(1)}, bf16[12,48,128]{2,1,0:T(8,128)(2,1)S(1)}, u32[]{:S(2)}, u32[]{:S(2)}) collective-permute-start(bf16[12,48,128]{2,1,0:T(8,128)(2,1)S(1)} %collective-permute-done.2.refs_4_), channel_id=1, source_target_pairs={{0,4},{2,6},{4,0},{6,2},{8,12},{10,14},{12,8},{14,10},{1,5},{3,7},... | collective-permute-start | bytes 442376 | tf_op jit(solution)/shard_map/ppermute | solution.py:278
  14.3 5.8 %collective-permute-start.5 = (bf16[12,48,128]{2,1,0:T(8,128)(2,1)S(1)}, bf16[12,48,128]{2,1,0:T(8,128)(2,1)S(1)}, u32[]{:S(2)}, u32[]{:S(2)}) collective-permute-start(bf16[12,48,128]{2,1,0:T(8,128)(2,1)S(1)} %get-tuple-element.39.refs_0_), channel_id=1, source_target_pairs={{0,1},{1,0},{2,3},{3,2},{4,5},{5,4},{6,7},{7,6},{8,9},{9,8},{10,11... | collective-permute-start | bytes 442376 | tf_op jit(solution)/shard_map/ppermute | solution.py:286
  17.9 5.8 %collective-permute-start.7 = (bf16[432,128]{1,0:T(8,128)(2,1)S(1)}, bf16[432,128]{1,0:T(8,128)(2,1)S(1)}, u32[]{:S(2)}, u32[]{:S(2)}) collective-permute-start(bf16[432,128]{1,0:T(8,128)(2,1)S(1)} %get-tuple-element.42), channel_id=1, source_target_pairs={{0,3},{1,2},{2,1},{3,0},{4,7},{5,6},{6,5},{7,4},{8,11},{9,10},{10,... | collective-permute-start | bytes 331784 | tf_op jit(solution)/shard_map/ppermute | solution.py:286
  18.0 7.1 %collective-permute-start.3 = (bf16[432,128]{1,0:T(8,128)(2,1)S(1)}, bf16[432,128]{1,0:T(8,128)(2,1)S(1)}, u32[]{:S(2)}, u32[]{:S(2)}) collective-permute-start(bf16[432,128]{1,0:T(8,128)(2,1)S(1)} %get-tuple-element.35.refs_0_), channel_id=1, source_target_pairs={{0,1},{1,0},{2,3},{3,2},{4,5},{5,4},{6,7},{7,6},{8,9},{9,8},{10,11... | collective-permute-start | bytes 331784 | tf_op jit(solution)/shard_map/ppermute | solution.py:286
  20.1 5.0 %copy-start.4 = (bf16[128,512]{1,0:T(8,128)(2,1)S(1)}, bf16[128,512]{1,0:T(8,128)(2,1)}, u32[]{:S(2)}) copy-start(bf16[128,512]{1,0:T(8,128)(2,1)} %refs_12_.1) | copy-start | bytes 393220
  20.1 5.0 %copy-start.5 = (bf16[128,128]{1,0:T(8,128)(2,1)S(1)}, bf16[128,128]{1,0:T(8,128)(2,1)}, u32[]{:S(2)}) copy-start(bf16[128,128]{1,0:T(8,128)(2,1)} %refs_11_.1) | copy-start | bytes 98308
  21.2 3.9 %collective-permute-start.6 = (bf16[432,128]{1,0:T(8,128)(2,1)S(1)}, bf16[432,128]{1,0:T(8,128)(2,1)S(1)}, u32[]{:S(2)}, u32[]{:S(2)}) collective-permute-start(bf16[432,128]{1,0:T(8,128)(2,1)S(1)} %get-tuple-element.42), channel_id=1, source_target_pairs={{0,2},{1,3},{2,0},{3,1},{4,6},{5,7},{6,4},{7,5},{8,10},{9,11},{10,... | collective-permute-start | bytes 331784 | tf_op jit(solution)/shard_map/ppermute | solution.py:286
  22.0 4.2 %collective-permute-start.10 = (bf16[144,128]{1,0:T(8,128)(2,1)S(1)}, bf16[144,128]{1,0:T(8,128)(2,1)S(1)}, u32[]{:S(2)}, u32[]{:S(2)}) collective-permute-start(bf16[144,128]{1,0:T(8,128)(2,1)S(1)} %shard_map.87), channel_id=1, source_target_pairs={{0,3},{1,2},{2,1},{3,0},{4,7},{5,6},{6,5},{7,4},{8,11},{9,10},{10,... | collective-permute-start | bytes 110600 | tf_op jit(solution)/shard_map/ppermute | solution.py:286
  22.6 4.4 %collective-permute-start.8 = (bf16[144,128]{1,0:T(8,128)(2,1)S(1)}, bf16[144,128]{1,0:T(8,128)(2,1)S(1)}, u32[]{:S(2)}, u32[]{:S(2)}) collective-permute-start(bf16[144,128]{1,0:T(8,128)(2,1)S(1)} %shard_map.86.refs_4_), channel_id=1, source_target_pairs={{0,1},{1,0},{2,3},{3,2},{4,5},{5,4},{6,7},{7,6},{8,9},{9,8},{10,11... | collective-permute-start | bytes 110600 | tf_op jit(solution)/shard_map/ppermute | solution.py:286
  23.7 3.2 %collective-permute-start.9 = (bf16[144,128]{1,0:T(8,128)(2,1)S(1)}, bf16[144,128]{1,0:T(8,128)(2,1)S(1)}, u32[]{:S(2)}, u32[]{:S(2)}) collective-permute-start(bf16[144,128]{1,0:T(8,128)(2,1)S(1)} %shard_map.87), channel_id=1, source_target_pairs={{0,2},{1,3},{2,0},{3,1},{4,6},{5,7},{6,4},{7,5},{8,10},{9,11},{10,... | collective-permute-start | bytes 110600 | tf_op jit(solution)/shard_map/ppermute | solution.py:286
  28.1 1.5 %collective-permute-start.12 = (bf16[12,48,128]{2,1,0:T(8,128)(2,1)S(1)}, bf16[12,48,128]{2,1,0:T(8,128)(2,1)S(1)}, u32[]{:S(2)}, u32[]{:S(2)}) collective-permute-start(bf16[12,48,128]{2,1,0:T(8,128)(2,1)S(1)} %get-tuple-element.53.refs_2_.refs_0_), channel_id=1, source_target_pairs={{0,2},{2,0},{4,6},{6,4},{8,10},{10,8},{12,14},{14,12},{1,3},{3,1},... | collective-permute-start | bytes 442376 | tf_op jit(solution)/shard_map/ppermute | solution.py:278
  28.2 1.4 %collective-permute-start.11 = (bf16[12,24,128]{2,1,0:T(8,128)(2,1)S(1)}, bf16[12,24,128]{2,1,0:T(8,128)(2,1)S(1)}, u32[]{:S(2)}, u32[]{:S(2)}) collective-permute-start(bf16[12,24,128]{2,1,0:T(8,128)(2,1)S(1)} %get-tuple-element.52), channel_id=1, source_target_pairs={{0,2},{2,0},{4,6},{6,4},{8,10},{10,8},{12,14},{14,12},{1,3},{3,1},... | collective-permute-start | bytes 221192 | tf_op jit(solution)/shard_map/ppermute | solution.py:278
  28.6 6.0 %collective-permute-start.13 = (bf16[12,24,128]{2,1,0:T(8,128)(2,1)S(1)}, bf16[12,24,128]{2,1,0:T(8,128)(2,1)S(1)}, u32[]{:S(2)}, u32[]{:S(2)}) collective-permute-start(bf16[12,24,128]{2,1,0:T(8,128)(2,1)S(1)} %get-tuple-element.55), channel_id=1, source_target_pairs={{0,2},{2,0},{4,6},{6,4},{8,10},{10,8},{12,14},{14,12},{1,3},{3,1},... | collective-permute-start | bytes 221192 | tf_op jit(solution)/shard_map/ppermute | solution.py:278
  30.9 14.3 %collective-permute-start.15 = (bf16[12,48,128]{2,1,0:T(8,128)(2,1)S(1)}, bf16[12,48,128]{2,1,0:T(8,128)(2,1)S(1)}, u32[]{:S(2)}, u32[]{:S(2)}) collective-permute-start(bf16[12,48,128]{2,1,0:T(8,128)(2,1)S(1)} %get-tuple-element.56), channel_id=1, source_target_pairs={{0,8},{2,10},{4,12},{6,14},{8,0},{10,2},{12,4},{14,6},{1,9},{3,11}... | collective-permute-start | bytes 442376 | tf_op jit(solution)/shard_map/ppermute | solution.py:278
  34.2 11.0 %collective-permute-start.16 = (bf16[12,48,128]{2,1,0:T(8,128)(2,1)S(1)}, bf16[12,48,128]{2,1,0:T(8,128)(2,1)S(1)}, u32[]{:S(2)}, u32[]{:S(2)}) collective-permute-start(bf16[12,48,128]{2,1,0:T(8,128)(2,1)S(1)} %get-tuple-element.57), channel_id=1, source_target_pairs={{0,12},{2,14},{4,8},{6,10},{8,4},{10,6},{12,0},{14,2},{1,13},{3,15... | collective-permute-start | bytes 442376 | tf_op jit(solution)/shard_map/ppermute | solution.py:278
  35.3 11.7 %collective-permute-start.14 = (bf16[12,48,128]{2,1,0:T(8,128)(2,1)S(1)}, bf16[12,48,128]{2,1,0:T(8,128)(2,1)S(1)}, u32[]{:S(2)}, u32[]{:S(2)}) collective-permute-start(bf16[12,48,128]{2,1,0:T(8,128)(2,1)S(1)} %shard_map.92), channel_id=1, source_target_pairs={{0,4},{2,6},{4,0},{6,2},{8,12},{10,14},{12,8},{14,10},{1,5},{3,7},... | collective-permute-start | bytes 442376 | tf_op jit(solution)/shard_map/ppermute | solution.py:278
  36.2 10.8 %copy-start.6 = (bf16[128,128]{1,0:T(8,128)(2,1)S(1)}, bf16[128,128]{1,0:T(8,128)(2,1)}, u32[]{:S(2)}) copy-start(bf16[128,128]{1,0:T(8,128)(2,1)} %refs_6_.1) | copy-start | bytes 98308
  (3 other events, 2.9 us)

commit v7 on v6

--- a/solution.py
+++ b/solution.py
@@ -337,8 +337,7 @@
         early = product([m], both, early)
     mine, other = early
     parts = [mine] + [shift(mine, dx, 0) for dx in range(1, cols_n)]
-    across = [shift(other, dx, 1) for dx in range(1, cols_n)]
-    other_core = other
+    exchanged = [parts + [shift(other, dx, 1) for dx in range(cols_n)]]
     (mine,) = product([chips - 1], [left])
     mine, core_left = lax.optimization_barrier((mine, core_left))
     (other,) = product([chips - 1], [core_left])
@@ -350,10 +349,9 @@
         flops=100_000_000,
     )
     gates = list(gates)
-    other_core, last_core, gates[1] = lax.optimization_barrier((other_core, other, gates[1]))
-    exchanged = [parts + [shift(other_core, 0, 1)] + across]
+    other_core, gates[1] = lax.optimization_barrier((other, gates[1]))
     parts = [mine] + [shift(mine, dx, 0) for dx in range(1, cols_n)]
-    parts += [shift(last_core, 0, 1)] + [shift(other, dx, 1) for dx in range(1, cols_n)]
+    parts += [shift(other_core, 0, 1)] + [shift(other, dx, 1) for dx in range(1, cols_n)]
     exchanged.append(parts)
     firsts, lefts = [], []
     for h in range(cols_n):

time: 48.3 us -> 47 us (0.973)
  waiting for transfers between devices: 17.1 us -> 16 us
    ppermute x10, waiting for transfers between devices: 15.2 us -> 14 us  [along_row(): return lax.ppermute(v, 'row', [(i, i ^ bits) for i in range(rows_n)])]
  transfers between devices with their start and end apart: 17 -> 17, of which waited for: 6 -> 7; matrix products, arithmetic and copies ran while one was open for 0% -> 0% of each run, Pallas kernels for 18% -> 18%
where the time goes in v7:
time: 47 us; the launch traced here: 46.8 us
  starting transfers between devices  16.9 us (36%)
  waiting for transfers between devices  16 us (34%)
  Pallas kernels  12.8 us (27%)
  local copies, waits for them, and re-layouts  0.97 us (2%)
    ppermute x10, waiting for transfers between devices, along_row(): return lax.ppermute(v, 'row', [(i, i ^ bits) for i in range(rows_n)])  14 us
    pallas_call x14, Pallas kernels, call(): pl.pallas_call(kernel, out_shape=outs, in_specs=[pl.BlockSpec(memory_spac...  12.8 us
    ppermute x10, starting transfers between devices, along_row(): return lax.ppermute(v, 'row', [(i, i ^ bits) for i in range(rows_n)])  11.2 us
    ppermute x7, starting transfers between devices, shift(): return lax.ppermute(v, ('row', 'col'), pairs)  5.75 us
    ppermute x7, waiting for transfers between devices, shift(): return lax.ppermute(v, ('row', 'col'), pairs)  2.02 us
    unnamed x20, local copies, waits for them, and re-layouts  0.97 us
  transfers between devices with their start and end apart: 17, of which 7 were waited for; matrix products, arithmetic and copies ran while one was open for 0% of the time, Pallas kernels for 18%

profile of v7, /device:TPU:0, one launch (start us, length us, event | category | flops | bytes accessed | tf_op | source)
XLA Modules:
  0.0 46.8 jit_solution(17848688365757240525)
XLA Ops:
  0.0 2.1 %shard_map.82.refs_0_.refs_2_ = bf16[12,48,128]{2,1,0:T(8,128)(2,1)} custom-call(bf16[12,48,128]{2,1,0:T(8,128)(2,1)} %refs_1_.1, s32[1,96]{1,0:T(1,128)} %bitcast.1, bf16[128,512]{1,0:T(8,128)(2,1)} %refs_3_.1), custom_call_target="tpu_custom_call" | custom-call | flops 100000000 | bytes 426368 | tf_op jit(solution)/shard_map/pallas_call | solution.py:26
  2.1 4.1 %collective-permute-start.2 = (bf16[12,48,128]{2,1,0:T(8,128)(2,1)}, bf16[12,48,128]{2,1,0:T(8,128)(2,1)S(1)}, u32[]{:S(2)}, u32[]{:S(2)}) collective-permute-start(bf16[12,48,128]{2,1,0:T(8,128)(2,1)} %shard_map.82.refs_0_.refs_2_), channel_id=1, source_target_pairs={{0,8},{2,10},{4,12},{6,14},{8,0},{10,2},{12,4},{14,6},{1,9},{3,11}... | collective-permute-start | bytes 442376 | tf_op jit(solution)/shard_map/ppermute | solution.py:278
  6.2 1.6 %collective-permute-start.1 = (bf16[12,48,128]{2,1,0:T(8,128)(2,1)}, bf16[12,48,128]{2,1,0:T(8,128)(2,1)S(1)}, u32[]{:S(2)}, u32[]{:S(2)}) collective-permute-start(bf16[12,48,128]{2,1,0:T(8,128)(2,1)} %shard_map.82.refs_0_.refs_2_), channel_id=1, source_target_pairs={{0,4},{2,6},{4,0},{6,2},{8,12},{10,14},{12,8},{14,10},{1,5},{3,7},... | collective-permute-start | bytes 442376 | tf_op jit(solution)/shard_map/ppermute | solution.py:278
  7.8 0.9 %copy-done.1 = bf16[12,48,128]{2,1,0:T(8,128)(2,1)S(1)} copy-done((bf16[12,48,128]{2,1,0:T(8,128)(2,1)S(1)}, bf16[12,48,128]{2,1,0:T(8,128)(2,1)}, u32[]{:S(2)}) %copy-start.1) | copy-done | bytes 147480
  9.3 1.6 %collective-permute-start.8 = (bf16[12,48,128]{2,1,0:T(8,128)(2,1)S(1)}, bf16[12,48,128]{2,1,0:T(8,128)(2,1)S(1)}, u32[]{:S(2)}, u32[]{:S(2)}) collective-permute-start(bf16[12,48,128]{2,1,0:T(8,128)(2,1)S(1)} %get-tuple-element.39.refs_0_), channel_id=1, source_target_pairs={{0,1},{1,0},{2,3},{3,2},{4,5},{5,4},{6,7},{7,6},{8,9},{9,8},{10,11... | collective-permute-start | bytes 442376 | tf_op jit(solution)/shard_map/ppermute | solution.py:286
  10.8 2.7 %collective-permute-done.2.refs_4_ = bf16[12,48,128]{2,1,0:T(8,128)(2,1)S(1)} collective-permute-done((bf16[12,48,128]{2,1,0:T(8,128)(2,1)}, bf16[12,48,128]{2,1,0:T(8,128)(2,1)S(1)}, u32[]{:S(2)}, u32[]{:S(2)}) %collective-permute-start.2) | collective-permute-done | bytes 147488 | tf_op jit(solution)/shard_map/ppermute | solution.py:278
  13.6 0.7 %collective-permute-start.6 = (bf16[12,48,128]{2,1,0:T(8,128)(2,1)S(1)}, bf16[12,48,128]{2,1,0:T(8,128)(2,1)S(1)}, u32[]{:S(2)}, u32[]{:S(2)}) collective-permute-start(bf16[12,48,128]{2,1,0:T(8,128)(2,1)S(1)} %collective-permute-done.2.refs_4_), channel_id=1, source_target_pairs={{0,4},{2,6},{4,0},{6,2},{8,12},{10,14},{12,8},{14,10},{1,5},{3,7},... | collective-permute-start | bytes 442376 | tf_op jit(solution)/shard_map/ppermute | solution.py:278
  14.3 1.2 %shard_map.84 = (bf16[288,128]{1,0:T(8,128)(2,1)S(1)}, bf16[288,128]{1,0:T(8,128)(2,1)S(1)}) custom-call(bf16[12,48,128]{2,1,0:T(8,128)(2,1)S(1)} %get-tuple-element.31.refs_0_.refs_2_, bf16[12,48,128]{2,1,0:T(8,128)(2,1)S(1)} %collective-permute-done.refs_1_.refs_3_.refs_0_, bf16[12,48,128]{2,1,0:T(8,128)(2,1)S(1)} %copy-done.2, ...), custom_call_target="tpu_custom_call" | custom-call | flops 500000000 | bytes 737280 | tf_op jit(solution)/shard_map/pallas_call | solution.py:26
  15.5 0.9 %shard_map.85 = (bf16[432,128]{1,0:T(8,128)(2,1)S(1)}, bf16[432,128]{1,0:T(8,128)(2,1)S(1)}) custom-call(bf16[288,128]{1,0:T(8,128)(2,1)S(1)} %get-tuple-element.32.refs_0_, bf16[288,128]{1,0:T(8,128)(2,1)S(1)} %get-tuple-element.33.refs_1_, bf16[12,48,128]{2,1,0:T(8,128)(2,1)S(1)} %get-tuple-element.31.refs_0_.refs_2_, ...), custom_call_target="tpu_custom_call" | custom-call | flops 250000000 | bytes 811008 | tf_op jit(solution)/shard_map/pallas_call | solution.py:26
  16.4 0.9 %collective-permute-start.5 = (bf16[432,128]{1,0:T(8,128)(2,1)S(1)}, bf16[432,128]{1,0:T(8,128)(2,1)S(1)}, u32[]{:S(2)}, u32[]{:S(2)}) collective-permute-start(bf16[432,128]{1,0:T(8,128)(2,1)S(1)} %get-tuple-element.35), channel_id=1, source_target_pairs={{0,3},{1,2},{2,1},{3,0},{4,7},{5,6},{6,5},{7,4},{8,11},{9,10},{10,... | collective-permute-start | bytes 331784 | tf_op jit(solution)/shard_map/ppermute | solution.py:286
  17.3 0.8 %collective-permute-start.4 = (bf16[432,128]{1,0:T(8,128)(2,1)S(1)}, bf16[432,128]{1,0:T(8,128)(2,1)S(1)}, u32[]{:S(2)}, u32[]{:S(2)}) collective-permute-start(bf16[432,128]{1,0:T(8,128)(2,1)S(1)} %get-tuple-element.35), channel_id=1, source_target_pairs={{0,2},{1,3},{2,0},{3,1},{4,6},{5,7},{6,4},{7,5},{8,10},{9,11},{10,... | collective-permute-start | bytes 331784 | tf_op jit(solution)/shard_map/ppermute | solution.py:286
  19.8 0.8 %collective-permute-start.10 = (bf16[144,128]{1,0:T(8,128)(2,1)S(1)}, bf16[144,128]{1,0:T(8,128)(2,1)S(1)}, u32[]{:S(2)}, u32[]{:S(2)}) collective-permute-start(bf16[144,128]{1,0:T(8,128)(2,1)S(1)} %shard_map.87), channel_id=1, source_target_pairs={{0,3},{1,2},{2,1},{3,0},{4,7},{5,6},{6,5},{7,4},{8,11},{9,10},{10,... | collective-permute-start | bytes 110600 | tf_op jit(solution)/shard_map/ppermute | solution.py:286
  20.6 0.9 %collective-permute-start.7 = (bf16[144,128]{1,0:T(8,128)(2,1)S(1)}, bf16[144,128]{1,0:T(8,128)(2,1)S(1)}, u32[]{:S(2)}, u32[]{:S(2)}) collective-permute-start(bf16[144,128]{1,0:T(8,128)(2,1)S(1)} %shard_map.86.refs_4_), channel_id=1, source_target_pairs={{0,1},{1,0},{2,3},{3,2},{4,5},{5,4},{6,7},{7,6},{8,9},{9,8},{10,11... | collective-permute-start | bytes 110600 | tf_op jit(solution)/shard_map/ppermute | solution.py:286
  21.5 0.9 %shard_map.88 = (bf16[12,48,128]{2,1,0:T(8,128)(2,1)S(1)}, f32[12,48,128]{2,1,0:T(8,128)S(1)}, bf16[12,48,128]{2,1,0:T(8,128)(2,1)S(1)}, f32[12,48,128]{2,1,0:T(8,128)S(1)}) custom-call(bf16[12,48,128]{2,1,0:T(8,128)(2,1)S(1)} %get-tuple-element.39.refs_0_, bf16[12,48,128]{2,1,0:T(8,128)(2,1)S(1)} %collective-permute-done.8.refs_1_, ...), custom_call_target="tpu_custom_call" | custom-call | flops 100000000 | bytes 1212416 | tf_op jit(solution)/shard_map/pallas_call | solution.py:26
  22.6 1.6 %collective-permute-done.3.refs_1_ = bf16[432,128]{1,0:T(8,128)(2,1)S(1)} collective-permute-done((bf16[432,128]{1,0:T(8,128)(2,1)S(1)}, bf16[432,128]{1,0:T(8,128)(2,1)S(1)}, u32[]{:S(2)}, u32[]{:S(2)}) %collective-permute-start.3) | collective-permute-done | bytes 110624 | tf_op jit(solution)/shard_map/ppermute | solution.py:286
  24.3 1.1 %shard_map.89 = (bf16[12,48,128]{2,1,0:T(8,128)(2,1)S(1)}, bf16[12,48,128]{2,1,0:T(8,128)(2,1)S(1)}, bf16[12,24,128]{2,1,0:T(8,128)(2,1)S(1)}, bf16[12,24,128]{2,1,0:T(8,128)(2,1)S(1)}) custom-call(bf16[432,128]{1,0:T(8,128)(2,1)S(1)} %get-tuple-element.34.refs_0_, bf16[432,128]{1,0:T(8,128)(2,1)S(1)} %collective-permute-done.3.refs_1_, ...), custom_call_target="tpu_custom_call" | custom-call | flops 300000000 | bytes 1491328 | tf_op jit(solution)/shard_map/pallas_call | solution.py:26
  25.8 1.1 %shard_map.90 = (bf16[12,48,128]{2,1,0:T(8,128)(2,1)S(1)}, bf16[12,48,128]{2,1,0:T(8,128)(2,1)S(1)}, bf16[12,24,128]{2,1,0:T(8,128)(2,1)S(1)}, bf16[12,24,128]{2,1,0:T(8,128)(2,1)S(1)}) custom-call(bf16[432,128]{1,0:T(8,128)(2,1)S(1)} %get-tuple-element.34.refs_0_, bf16[432,128]{1,0:T(8,128)(2,1)S(1)} %collective-permute-done.3.refs_1_, ...), custom_call_target="tpu_custom_call" | custom-call | flops 300000000 | bytes 1933696 | tf_op jit(solution)/shard_map/pallas_call | solution.py:26
  27.6 0.9 %collective-permute-done.11.refs_1_.refs_3_ = bf16[12,24,128]{2,1,0:T(8,128)(2,1)S(1)} collective-permute-done((bf16[12,24,128]{2,1,0:T(8,128)(2,1)S(1)}, bf16[12,24,128]{2,1,0:T(8,128)(2,1)S(1)}, u32[]{:S(2)}, u32[]{:S(2)}) %collective-permute-start.11) | collective-permute-done | bytes 73760 | tf_op jit(solution)/shard_map/ppermute | solution.py:278
  28.5 1.3 %shard_map.93 = (bf16[12,48,128]{2,1,0:T(8,128)(2,1)S(1)}, bf16[12,48,128]{2,1,0:T(8,128)(2,1)S(1)}) custom-call(bf16[12,48,128]{2,1,0:T(8,128)(2,1)S(1)} %get-tuple-element.51.refs_2_.refs_0_, bf16[12,48,128]{2,1,0:T(8,128)(2,1)S(1)} %collective-permute-done.12.refs_3_.refs_1_, bf16[12,24,128]{2,1,0:T(8,128)(2,1)S(1)} %get-tuple-element.49.refs_0_.refs_2_, ...), custom_call_target="tpu_custom_call" | custom-call | flops 400000000 | bytes 737280 | tf_op jit(solution)/shard_map/pallas_call | solution.py:26
  29.7 3.3 %collective-permute-start.15 = (bf16[12,48,128]{2,1,0:T(8,128)(2,1)S(1)}, bf16[12,48,128]{2,1,0:T(8,128)(2,1)S(1)}, u32[]{:S(2)}, u32[]{:S(2)}) collective-permute-start(bf16[12,48,128]{2,1,0:T(8,128)(2,1)S(1)} %get-tuple-element.54), channel_id=1, source_target_pairs={{0,8},{2,10},{4,12},{6,14},{8,0},{10,2},{12,4},{14,6},{1,9},{3,11}... | collective-permute-start | bytes 442376 | tf_op jit(solution)/shard_map/ppermute | solution.py:278
  33.5 0.7 %shard_map.92 = bf16[12,48,128]{2,1,0:T(8,128)(2,1)S(1)} custom-call(bf16[12,24,128]{2,1,0:T(8,128)(2,1)S(1)} %get-tuple-element.49.refs_0_.refs_2_, bf16[12,24,128]{2,1,0:T(8,128)(2,1)S(1)} %collective-permute-done.11.refs_1_.refs_3_, bf16[12,48,128]{2,1,0:T(8,128)(2,1)S(1)} %get-tuple-element.51.refs_2_.refs_0_, ...), custom_call_target="tpu_custom_call" | custom-call | flops 200000000 | bytes 737280 | tf_op jit(solution)/shard_map/pallas_call | solution.py:26
  35.5 8.5 %collective-permute-done.15.refs_2_ = bf16[12,48,128]{2,1,0:T(8,128)(2,1)S(1)} collective-permute-done((bf16[12,48,128]{2,1,0:T(8,128)(2,1)S(1)}, bf16[12,48,128]{2,1,0:T(8,128)(2,1)S(1)}, u32[]{:S(2)}, u32[]{:S(2)}) %collective-permute-start.15) | collective-permute-done | bytes 147488 | tf_op jit(solution)/shard_map/ppermute | solution.py:278
  44.0 1.8 %collective-permute-done.14.refs_1_ = bf16[12,48,128]{2,1,0:T(8,128)(2,1)S(1)} collective-permute-done((bf16[12,48,128]{2,1,0:T(8,128)(2,1)S(1)}, bf16[12,48,128]{2,1,0:T(8,128)(2,1)S(1)}, u32[]{:S(2)}, u32[]{:S(2)}) %collective-permute-start.14) | collective-permute-done | bytes 147488 | tf_op jit(solution)/shard_map/ppermute | solution.py:278
  45.8 1.0 %shard_map.95 = bf16[12,48,128]{2,1,0:T(8,128)(2,1)} custom-call(f32[12,48,128]{2,1,0:T(8,128)S(1)} %shard_map.91.refs_0_, bf16[12,48,128]{2,1,0:T(8,128)(2,1)S(1)} %collective-permute-done.14.refs_1_, bf16[12,48,128]{2,1,0:T(8,128)(2,1)S(1)} %collective-permute-done.15.refs_2_, bf16[12,48,128]{2,1,0:T(8,128)(2,1)S(1)} %collective-permute-done.16.refs_3_, ...), custom_call_target="tpu_custom_call" | custom-call | flops 100000000 | bytes 1359872 | tf_op jit(solution)/shard_map/pallas_call | solution.py:26
  (44 shorter events, 5.3 us)
Async XLA Ops:
  0.0 7.8 %copy-start = (bf16[12,48,128]{2,1,0:T(8,128)(2,1)S(1)}, bf16[12,48,128]{2,1,0:T(8,128)(2,1)}, u32[]{:S(2)}) copy-start(bf16[12,48,128]{2,1,0:T(8,128)(2,1)} %refs_1_.1) | copy-start | bytes 442372
  0.0 7.8 %copy-start.3 = (bf16[128,512]{1,0:T(8,128)(2,1)S(1)}, bf16[128,512]{1,0:T(8,128)(2,1)}, u32[]{:S(2)}) copy-start(bf16[128,512]{1,0:T(8,128)(2,1)} %refs_3_.1) | copy-start | bytes 393220
  0.0 7.8 %copy-start.8 = (s32[96]{0:T(128)S(1)}, s32[96]{0:T(128)}, u32[]{:S(2)}) copy-start(s32[96]{0:T(128)} %param.9) | copy-start | bytes 1156
  2.1 11.4 %collective-permute-start.2 = (bf16[12,48,128]{2,1,0:T(8,128)(2,1)}, bf16[12,48,128]{2,1,0:T(8,128)(2,1)S(1)}, u32[]{:S(2)}, u32[]{:S(2)}) collective-permute-start(bf16[12,48,128]{2,1,0:T(8,128)(2,1)} %shard_map.82.refs_0_.refs_2_), channel_id=1, source_target_pairs={{0,8},{2,10},{4,12},{6,14},{8,0},{10,2},{12,4},{14,6},{1,9},{3,11}... | collective-permute-start | bytes 442376 | tf_op jit(solution)/shard_map/ppermute | solution.py:278
  6.2 8.0 %collective-permute-start.1 = (bf16[12,48,128]{2,1,0:T(8,128)(2,1)}, bf16[12,48,128]{2,1,0:T(8,128)(2,1)S(1)}, u32[]{:S(2)}, u32[]{:S(2)}) collective-permute-start(bf16[12,48,128]{2,1,0:T(8,128)(2,1)} %shard_map.82.refs_0_.refs_2_), channel_id=1, source_target_pairs={{0,4},{2,6},{4,0},{6,2},{8,12},{10,14},{12,8},{14,10},{1,5},{3,7},... | collective-permute-start | bytes 442376 | tf_op jit(solution)/shard_map/ppermute | solution.py:278
  8.8 5.5 %copy-start.2 = (bf16[12,48,128]{2,1,0:T(8,128)(2,1)S(1)}, bf16[12,48,128]{2,1,0:T(8,128)(2,1)}, u32[]{:S(2)}) copy-start(bf16[12,48,128]{2,1,0:T(8,128)(2,1)} %shard_map.82.refs_0_.refs_2_) | copy-start | bytes 442372
  9.2 5.1 %collective-permute-start = (bf16[12,48,128]{2,1,0:T(8,128)(2,1)S(1)}, bf16[12,48,128]{2,1,0:T(8,128)(2,1)S(1)}, u32[]{:S(2)}, u32[]{:S(2)}) collective-permute-start(bf16[12,48,128]{2,1,0:T(8,128)(2,1)S(1)} %get-tuple-element.31.refs_0_.refs_2_), channel_id=1, source_target_pairs={{0,2},{2,0},{4,6},{6,4},{8,10},{10,8},{12,14},{14,12},{1,3},{3,1},... | collective-permute-start | bytes 442376 | tf_op jit(solution)/shard_map/ppermute | solution.py:278
  9.3 11.3 %collective-permute-start.8 = (bf16[12,48,128]{2,1,0:T(8,128)(2,1)S(1)}, bf16[12,48,128]{2,1,0:T(8,128)(2,1)S(1)}, u32[]{:S(2)}, u32[]{:S(2)}) collective-permute-start(bf16[12,48,128]{2,1,0:T(8,128)(2,1)S(1)} %get-tuple-element.39.refs_0_), channel_id=1, source_target_pairs={{0,1},{1,0},{2,3},{3,2},{4,5},{5,4},{6,7},{7,6},{8,9},{9,8},{10,11... | collective-permute-start | bytes 442376 | tf_op jit(solution)/shard_map/ppermute | solution.py:286
  13.6 5.1 %collective-permute-start.6 = (bf16[12,48,128]{2,1,0:T(8,128)(2,1)S(1)}, bf16[12,48,128]{2,1,0:T(8,128)(2,1)S(1)}, u32[]{:S(2)}, u32[]{:S(2)}) collective-permute-start(bf16[12,48,128]{2,1,0:T(8,128)(2,1)S(1)} %collective-permute-done.2.refs_4_), channel_id=1, source_target_pairs={{0,4},{2,6},{4,0},{6,2},{8,12},{10,14},{12,8},{14,10},{1,5},{3,7},... | collective-permute-start | bytes 442376 | tf_op jit(solution)/shard_map/ppermute | solution.py:278
  16.4 5.9 %collective-permute-start.5 = (bf16[432,128]{1,0:T(8,128)(2,1)S(1)}, bf16[432,128]{1,0:T(8,128)(2,1)S(1)}, u32[]{:S(2)}, u32[]{:S(2)}) collective-permute-start(bf16[432,128]{1,0:T(8,128)(2,1)S(1)} %get-tuple-element.35), channel_id=1, source_target_pairs={{0,3},{1,2},{2,1},{3,0},{4,7},{5,6},{6,5},{7,4},{8,11},{9,10},{10,... | collective-permute-start | bytes 331784 | tf_op jit(solution)/shard_map/ppermute | solution.py:286
  17.3 5.3 %collective-permute-start.4 = (bf16[432,128]{1,0:T(8,128)(2,1)S(1)}, bf16[432,128]{1,0:T(8,128)(2,1)S(1)}, u32[]{:S(2)}, u32[]{:S(2)}) collective-permute-start(bf16[432,128]{1,0:T(8,128)(2,1)S(1)} %get-tuple-element.35), channel_id=1, source_target_pairs={{0,2},{1,3},{2,0},{3,1},{4,6},{5,7},{6,4},{7,5},{8,10},{9,11},{10,... | collective-permute-start | bytes 331784 | tf_op jit(solution)/shard_map/ppermute | solution.py:286
  18.1 6.2 %collective-permute-start.3 = (bf16[432,128]{1,0:T(8,128)(2,1)S(1)}, bf16[432,128]{1,0:T(8,128)(2,1)S(1)}, u32[]{:S(2)}, u32[]{:S(2)}) collective-permute-start(bf16[432,128]{1,0:T(8,128)(2,1)S(1)} %get-tuple-element.34.refs_0_), channel_id=1, source_target_pairs={{0,1},{1,0},{2,3},{3,2},{4,5},{5,4},{6,7},{7,6},{8,9},{9,8},{10,11... | collective-permute-start | bytes 331784 | tf_op jit(solution)/shard_map/ppermute | solution.py:286
  19.7 4.5 %copy-start.4 = (bf16[128,512]{1,0:T(8,128)(2,1)S(1)}, bf16[128,512]{1,0:T(8,128)(2,1)}, u32[]{:S(2)}) copy-start(bf16[128,512]{1,0:T(8,128)(2,1)} %refs_12_.1) | copy-start | bytes 393220
  19.8 4.5 %copy-start.5 = (bf16[128,128]{1,0:T(8,128)(2,1)S(1)}, bf16[128,128]{1,0:T(8,128)(2,1)}, u32[]{:S(2)}) copy-start(bf16[128,128]{1,0:T(8,128)(2,1)} %refs_11_.1) | copy-start | bytes 98308
  19.8 5.6 %collective-permute-start.10 = (bf16[144,128]{1,0:T(8,128)(2,1)S(1)}, bf16[144,128]{1,0:T(8,128)(2,1)S(1)}, u32[]{:S(2)}, u32[]{:S(2)}) collective-permute-start(bf16[144,128]{1,0:T(8,128)(2,1)S(1)} %shard_map.87), channel_id=1, source_target_pairs={{0,3},{1,2},{2,1},{3,0},{4,7},{5,6},{6,5},{7,4},{8,11},{9,10},{10,... | collective-permute-start | bytes 110600 | tf_op jit(solution)/shard_map/ppermute | solution.py:286
  20.6 5.2 %collective-permute-start.7 = (bf16[144,128]{1,0:T(8,128)(2,1)S(1)}, bf16[144,128]{1,0:T(8,128)(2,1)S(1)}, u32[]{:S(2)}, u32[]{:S(2)}) collective-permute-start(bf16[144,128]{1,0:T(8,128)(2,1)S(1)} %shard_map.86.refs_4_), channel_id=1, source_target_pairs={{0,1},{1,0},{2,3},{3,2},{4,5},{5,4},{6,7},{7,6},{8,9},{9,8},{10,11... | collective-permute-start | bytes 110600 | tf_op jit(solution)/shard_map/ppermute | solution.py:286
  22.3 3.4 %collective-permute-start.9 = (bf16[144,128]{1,0:T(8,128)(2,1)S(1)}, bf16[144,128]{1,0:T(8,128)(2,1)S(1)}, u32[]{:S(2)}, u32[]{:S(2)}) collective-permute-start(bf16[144,128]{1,0:T(8,128)(2,1)S(1)} %shard_map.87), channel_id=1, source_target_pairs={{0,2},{1,3},{2,0},{3,1},{4,6},{5,7},{6,4},{7,5},{8,10},{9,11},{10,... | collective-permute-start | bytes 110600 | tf_op jit(solution)/shard_map/ppermute | solution.py:286
  26.9 1.5 %collective-permute-start.12 = (bf16[12,48,128]{2,1,0:T(8,128)(2,1)S(1)}, bf16[12,48,128]{2,1,0:T(8,128)(2,1)S(1)}, u32[]{:S(2)}, u32[]{:S(2)}) collective-permute-start(bf16[12,48,128]{2,1,0:T(8,128)(2,1)S(1)} %get-tuple-element.51.refs_2_.refs_0_), channel_id=1, source_target_pairs={{0,2},{2,0},{4,6},{6,4},{8,10},{10,8},{12,14},{14,12},{1,3},{3,1},... | collective-permute-start | bytes 442376 | tf_op jit(solution)/shard_map/ppermute | solution.py:278
  27.1 1.4 %collective-permute-start.11 = (bf16[12,24,128]{2,1,0:T(8,128)(2,1)S(1)}, bf16[12,24,128]{2,1,0:T(8,128)(2,1)S(1)}, u32[]{:S(2)}, u32[]{:S(2)}) collective-permute-start(bf16[12,24,128]{2,1,0:T(8,128)(2,1)S(1)} %get-tuple-element.50), channel_id=1, source_target_pairs={{0,2},{2,0},{4,6},{6,4},{8,10},{10,8},{12,14},{14,12},{1,3},{3,1},... | collective-permute-start | bytes 221192 | tf_op jit(solution)/shard_map/ppermute | solution.py:278
  27.5 6.0 %collective-permute-start.13 = (bf16[12,24,128]{2,1,0:T(8,128)(2,1)S(1)}, bf16[12,24,128]{2,1,0:T(8,128)(2,1)S(1)}, u32[]{:S(2)}, u32[]{:S(2)}) collective-permute-start(bf16[12,24,128]{2,1,0:T(8,128)(2,1)S(1)} %get-tuple-element.53), channel_id=1, source_target_pairs={{0,2},{2,0},{4,6},{6,4},{8,10},{10,8},{12,14},{14,12},{1,3},{3,1},... | collective-permute-start | bytes 221192 | tf_op jit(solution)/shard_map/ppermute | solution.py:278
  29.7 14.2 %collective-permute-start.15 = (bf16[12,48,128]{2,1,0:T(8,128)(2,1)S(1)}, bf16[12,48,128]{2,1,0:T(8,128)(2,1)S(1)}, u32[]{:S(2)}, u32[]{:S(2)}) collective-permute-start(bf16[12,48,128]{2,1,0:T(8,128)(2,1)S(1)} %get-tuple-element.54), channel_id=1, source_target_pairs={{0,8},{2,10},{4,12},{6,14},{8,0},{10,2},{12,4},{14,6},{1,9},{3,11}... | collective-permute-start | bytes 442376 | tf_op jit(solution)/shard_map/ppermute | solution.py:278
  33.1 10.9 %collective-permute-start.16 = (bf16[12,48,128]{2,1,0:T(8,128)(2,1)S(1)}, bf16[12,48,128]{2,1,0:T(8,128)(2,1)S(1)}, u32[]{:S(2)}, u32[]{:S(2)}) collective-permute-start(bf16[12,48,128]{2,1,0:T(8,128)(2,1)S(1)} %get-tuple-element.55), channel_id=1, source_target_pairs={{0,12},{2,14},{4,8},{6,10},{8,4},{10,6},{12,0},{14,2},{1,13},{3,15... | collective-permute-start | bytes 442376 | tf_op jit(solution)/shard_map/ppermute | solution.py:278
  34.1 11.7 %collective-permute-start.14 = (bf16[12,48,128]{2,1,0:T(8,128)(2,1)S(1)}, bf16[12,48,128]{2,1,0:T(8,128)(2,1)S(1)}, u32[]{:S(2)}, u32[]{:S(2)}) collective-permute-start(bf16[12,48,128]{2,1,0:T(8,128)(2,1)S(1)} %shard_map.92), channel_id=1, source_target_pairs={{0,4},{2,6},{4,0},{6,2},{8,12},{10,14},{12,8},{14,10},{1,5},{3,7},... | collective-permute-start | bytes 442376 | tf_op jit(solution)/shard_map/ppermute | solution.py:278
  34.8 11.0 %copy-start.6 = (bf16[128,128]{1,0:T(8,128)(2,1)S(1)}, bf16[128,128]{1,0:T(8,128)(2,1)}, u32[]{:S(2)}) copy-start(bf16[128,128]{1,0:T(8,128)(2,1)} %refs_6_.1) | copy-start | bytes 98308
  (3 other events, 4.2 us)

commit v8 on v7

--- a/solution.py
+++ b/solution.py
@@ -210,11 +210,8 @@
 
 
 def incoming_kernel(steps, *refs):
-    own_right, core_right = refs[:2]
-    count = (len(refs) - 4 - len(steps)) // 2
-    lefts = refs[2 : 2 + 2 * count]
-    outs = refs[2 + 2 * count : -2]
-    l_scr, r_scr = refs[-2:]
+    outs, (l_scr, r_scr) = refs[-2 - len(steps) : -2], refs[-2:]
+    own_right, core_right, *lefts = refs[: -2 - len(steps)]
     rows, cols, chan = own_right.shape
     width = lefts[0].shape[1]
     pieces = width // rows
@@ -223,10 +220,10 @@
         r_scr[pl.ds(n * rows * cols, rows * cols), :] = ref[...].astype(F32).reshape(-1, chan)
     for n, ref in enumerate(lefts):
         l_scr[pl.ds(n * rows * width, rows * width), :] = ref[...].astype(F32).reshape(-1, chan)
-    for m, out_ref in zip(steps, outs):
-        block = m // pieces - steps[0] // pieces
-        base = block * (2 * rows * width) + ((z ^ m) % pieces) * rows
-        for group in range(0, rows, 6):
+    for (m, begin, count), out_ref in zip(steps, outs):
+        block = m // pieces - steps[0][0] // pieces
+        base = block * (2 * rows * width) + ((z ^ m) % pieces) * rows + begin
+        for group in range(0, count, 6):
 
             def step(k, totals):
                 right = r_scr[pl.ds(pl.multiple_of(k * cols, 8), cols), :]
@@ -236,17 +233,18 @@
                 )
 
             zero = jnp.zeros((cols, chan), F32)
-            totals = lax.fori_loop(0, 2 * rows, step, (zero,) * 6, unroll=4)
+            totals = lax.fori_loop(0, 2 * rows, step, (zero,) * min(6, count - group), unroll=4)
             for i, t in enumerate(totals):
                 out_ref[group + i] = t.astype(out_ref.dtype)
 
 
-def last_kernel(*refs):
+def last_kernel(whole, upper, *refs):
     parts, (first_ref, gate_ref, final_ref, out_ref) = refs[:-4], refs[-4:]
     rows, cols, chan = first_ref.shape
-    product = parts[0][...].astype(F32)
-    for ref in parts[1:]:
-        product = product + ref[...].astype(F32)
+    product = sum(ref[...].astype(F32) for ref in parts[:whole])
+    top = sum(ref[...].astype(F32) for ref in parts[whole : whole + upper])
+    low = sum(ref[...].astype(F32) for ref in parts[whole + upper :])
+    product = product + jnp.concatenate([top, low], axis=0)
     mixed = layer_norm(product).astype(BF16).reshape(rows * cols, chan)
     update = jnp.dot(mixed, final_ref[...], preferred_element_type=F32)
     first = first_ref[...].astype(F32).reshape(rows * cols, chan)
@@ -378,28 +376,41 @@
     core_right = along_row(right, 1)
 
     def partial_products(steps):
-        used = lefts[steps[0] // pieces : steps[-1] // pieces + 1]
+        used = lefts[steps[0][0] // pieces : steps[-1][0] // pieces + 1]
         wait = [] if used[-1] is lefts[-1] else lefts[-1]
         return call(
             functools.partial(after, functools.partial(incoming_kernel, steps), len(wait)),
-            [block if m else block32 for m in steps],
+            [shape((count, cols, chan), BF16 if m else F32) for m, _, count in steps],
             wait + [right, core_right] + sum(used, []),
             scratch=[
                 pltpu.VMEM((2 * len(used) * rows * pieces * rows, chan), F32),
                 pltpu.VMEM((2 * rows * cols, chan), F32),
             ],
-            flops=200_000_000 * len(steps),
+            flops=20_000_000 * sum(count for *_, count in steps),
             outside=range(len(wait)),
         )
 
-    parts = [None] * chips
-    for m, value in enumerate(partial_products(list(range(pieces, chips))), pieces):
-        parts[m] = along_row(value, 2 * m)
-    for m in reversed(range(pieces)):
-        value = partial_products([m])[0]
-        parts[m] = along_row(value, 2 * m) if m else value
+    cut = rows // 2
+    top, low = [], []
+    for h in range(1, cols_n):
+        blocks = range(h * pieces, (h + 1) * pieces)
+        relayed = partial_products([(m, cut, rows - cut) for m in blocks[1:]])
+        relayed = [along_row(v, 2 * p) for p, v in enumerate(relayed, 1)]
+        *direct, own = partial_products(
+            [(m, 0, cut) for m in blocks] + [(blocks[0], cut, rows - cut)]
+        )
+        top += [along_row(v, 2 * m) for m, v in zip(blocks, direct)]
+        total = sum((v.astype(F32) for v in relayed), own.astype(F32)).astype(BF16)
+        low.append(along_row(total, 2 * blocks[0]))
+    near = [partial_products([(m, 0, rows)])[0] for m in range(pieces)]
+    near = [along_row(v, 2 * m) if m else v for m, v in enumerate(near)]
     gate = call(gate_kernel, block32, [first, in_gating], flops=50_000_000)
-    return call(last_kernel, block, parts + [first, gate, in_final], flops=100_000_000)
+    return call(
+        functools.partial(last_kernel, len(near), len(top)),
+        block,
+        near + top + low + [first, gate, in_final],
+        flops=100_000_000,
+    )
 
 
 def solution(mesh):

time: 47 us -> 45.5 us (0.968)
  waiting for transfers between devices: 16 us -> 10.5 us
  starting transfers between devices: 16.9 us -> 20.8 us
    ppermute x10 -> x12, waiting for transfers between devices: 14 us -> 8.52 us  [along_row(): return lax.ppermute(v, 'row', [(i, i ^ bits) for i in range(rows_n)])]
    ppermute x10 -> x12, starting transfers between devices: 11.2 us -> 15 us  [along_row(): return lax.ppermute(v, 'row', [(i, i ^ bits) for i in range(rows_n)])]
    pallas_call x14 -> x15, Pallas kernels: 12.8 us -> 12.8 us  [call(): pl.pallas_call(kernel, out_shape=outs, in_specs=[pl.BlockSpec(memory_spac...]
  transfers between devices with their start and end apart: 17 -> 19, of which waited for: 7 -> 8; matrix products, arithmetic and copies ran while one was open for 0% -> 0% of each run, Pallas kernels for 18% -> 19%
where the time goes in v8:
time: 45.5 us; the launch traced here: 45.3 us
  starting transfers between devices  20.8 us (46%)
  Pallas kernels  12.8 us (28%)
  waiting for transfers between devices  10.5 us (23%)
  local copies, waits for them, and re-layouts  0.97 us (2%)
    ppermute x12, starting transfers between devices, along_row(): return lax.ppermute(v, 'row', [(i, i ^ bits) for i in range(rows_n)])  15 us
    pallas_call x15, Pallas kernels, call(): pl.pallas_call(kernel, out_shape=outs, in_specs=[pl.BlockSpec(memory_spac...  12.8 us
    ppermute x12, waiting for transfers between devices, along_row(): return lax.ppermute(v, 'row', [(i, i ^ bits) for i in range(rows_n)])  8.52 us
    ppermute x7, starting transfers between devices, shift(): return lax.ppermute(v, ('row', 'col'), pairs)  5.75 us
    ppermute x7, waiting for transfers between devices, shift(): return lax.ppermute(v, ('row', 'col'), pairs)  2.02 us
    unnamed x20, local copies, waits for them, and re-layouts  0.97 us
  transfers between devices with their start and end apart: 19, of which 8 were waited for; matrix products, arithmetic and copies ran while one was open for 0% of the time, Pallas kernels for 19%

profile of v8, /device:TPU:0, one launch (start us, length us, event | category | flops | bytes accessed | tf_op | source)
XLA Modules:
  0.0 45.3 jit_solution(16126143895294845987)
XLA Ops:
  0.0 2.1 %shard_map.82.refs_0_.refs_2_ = bf16[12,48,128]{2,1,0:T(8,128)(2,1)} custom-call(bf16[12,48,128]{2,1,0:T(8,128)(2,1)} %refs_1_.1, s32[1,96]{1,0:T(1,128)} %bitcast.1, bf16[128,512]{1,0:T(8,128)(2,1)} %refs_3_.1), custom_call_target="tpu_custom_call" | custom-call | flops 100000000 | bytes 426368 | tf_op jit(solution)/shard_map/pallas_call | solution.py:26
  2.1 4.1 %collective-permute-start.2 = (bf16[12,48,128]{2,1,0:T(8,128)(2,1)}, bf16[12,48,128]{2,1,0:T(8,128)(2,1)S(1)}, u32[]{:S(2)}, u32[]{:S(2)}) collective-permute-start(bf16[12,48,128]{2,1,0:T(8,128)(2,1)} %shard_map.82.refs_0_.refs_2_), channel_id=1, source_target_pairs={{0,8},{2,10},{4,12},{6,14},{8,0},{10,2},{12,4},{14,6},{1,9},{3,11}... | collective-permute-start | bytes 442376 | tf_op jit(solution)/shard_map/ppermute | solution.py:276
  6.2 1.6 %collective-permute-start.1 = (bf16[12,48,128]{2,1,0:T(8,128)(2,1)}, bf16[12,48,128]{2,1,0:T(8,128)(2,1)S(1)}, u32[]{:S(2)}, u32[]{:S(2)}) collective-permute-start(bf16[12,48,128]{2,1,0:T(8,128)(2,1)} %shard_map.82.refs_0_.refs_2_), channel_id=1, source_target_pairs={{0,4},{2,6},{4,0},{6,2},{8,12},{10,14},{12,8},{14,10},{1,5},{3,7},... | collective-permute-start | bytes 442376 | tf_op jit(solution)/shard_map/ppermute | solution.py:276
  7.8 0.9 %copy-done.1 = bf16[12,48,128]{2,1,0:T(8,128)(2,1)S(1)} copy-done((bf16[12,48,128]{2,1,0:T(8,128)(2,1)S(1)}, bf16[12,48,128]{2,1,0:T(8,128)(2,1)}, u32[]{:S(2)}) %copy-start.1) | copy-done | bytes 147480
  9.3 1.6 %collective-permute-start.8 = (bf16[12,48,128]{2,1,0:T(8,128)(2,1)S(1)}, bf16[12,48,128]{2,1,0:T(8,128)(2,1)S(1)}, u32[]{:S(2)}, u32[]{:S(2)}) collective-permute-start(bf16[12,48,128]{2,1,0:T(8,128)(2,1)S(1)} %get-tuple-element.40.refs_0_), channel_id=1, source_target_pairs={{0,1},{1,0},{2,3},{3,2},{4,5},{5,4},{6,7},{7,6},{8,9},{9,8},{10,11... | collective-permute-start | bytes 442376 | tf_op jit(solution)/shard_map/ppermute | solution.py:284
  10.8 2.7 %collective-permute-done.2.refs_4_ = bf16[12,48,128]{2,1,0:T(8,128)(2,1)S(1)} collective-permute-done((bf16[12,48,128]{2,1,0:T(8,128)(2,1)}, bf16[12,48,128]{2,1,0:T(8,128)(2,1)S(1)}, u32[]{:S(2)}, u32[]{:S(2)}) %collective-permute-start.2) | collective-permute-done | bytes 147488 | tf_op jit(solution)/shard_map/ppermute | solution.py:276
  14.3 1.2 %shard_map.84 = (bf16[288,128]{1,0:T(8,128)(2,1)S(1)}, bf16[288,128]{1,0:T(8,128)(2,1)S(1)}) custom-call(bf16[12,48,128]{2,1,0:T(8,128)(2,1)S(1)} %get-tuple-element.32.refs_0_.refs_2_, bf16[12,48,128]{2,1,0:T(8,128)(2,1)S(1)} %collective-permute-done.refs_1_.refs_3_.refs_0_, bf16[12,48,128]{2,1,0:T(8,128)(2,1)S(1)} %copy-done.2, ...), custom_call_target="tpu_custom_call" | custom-call | flops 500000000 | bytes 737280 | tf_op jit(solution)/shard_map/pallas_call | solution.py:26
  15.5 0.9 %shard_map.85 = (bf16[432,128]{1,0:T(8,128)(2,1)S(1)}, bf16[432,128]{1,0:T(8,128)(2,1)S(1)}) custom-call(bf16[288,128]{1,0:T(8,128)(2,1)S(1)} %get-tuple-element.33.refs_0_, bf16[288,128]{1,0:T(8,128)(2,1)S(1)} %get-tuple-element.34.refs_1_, bf16[12,48,128]{2,1,0:T(8,128)(2,1)S(1)} %get-tuple-element.32.refs_0_.refs_2_, ...), custom_call_target="tpu_custom_call" | custom-call | flops 250000000 | bytes 811008 | tf_op jit(solution)/shard_map/pallas_call | solution.py:26
  16.4 0.9 %collective-permute-start.5 = (bf16[432,128]{1,0:T(8,128)(2,1)S(1)}, bf16[432,128]{1,0:T(8,128)(2,1)S(1)}, u32[]{:S(2)}, u32[]{:S(2)}) collective-permute-start(bf16[432,128]{1,0:T(8,128)(2,1)S(1)} %get-tuple-element.36), channel_id=1, source_target_pairs={{0,3},{1,2},{2,1},{3,0},{4,7},{5,6},{6,5},{7,4},{8,11},{9,10},{10,... | collective-permute-start | bytes 331784 | tf_op jit(solution)/shard_map/ppermute | solution.py:284
  17.3 0.8 %collective-permute-start.4 = (bf16[432,128]{1,0:T(8,128)(2,1)S(1)}, bf16[432,128]{1,0:T(8,128)(2,1)S(1)}, u32[]{:S(2)}, u32[]{:S(2)}) collective-permute-start(bf16[432,128]{1,0:T(8,128)(2,1)S(1)} %get-tuple-element.36), channel_id=1, source_target_pairs={{0,2},{1,3},{2,0},{3,1},{4,6},{5,7},{6,4},{7,5},{8,10},{9,11},{10,... | collective-permute-start | bytes 331784 | tf_op jit(solution)/shard_map/ppermute | solution.py:284
  19.8 0.8 %collective-permute-start.10 = (bf16[144,128]{1,0:T(8,128)(2,1)S(1)}, bf16[144,128]{1,0:T(8,128)(2,1)S(1)}, u32[]{:S(2)}, u32[]{:S(2)}) collective-permute-start(bf16[144,128]{1,0:T(8,128)(2,1)S(1)} %shard_map.87), channel_id=1, source_target_pairs={{0,3},{1,2},{2,1},{3,0},{4,7},{5,6},{6,5},{7,4},{8,11},{9,10},{10,... | collective-permute-start | bytes 110600 | tf_op jit(solution)/shard_map/ppermute | solution.py:284
  20.6 0.9 %collective-permute-start.7 = (bf16[144,128]{1,0:T(8,128)(2,1)S(1)}, bf16[144,128]{1,0:T(8,128)(2,1)S(1)}, u32[]{:S(2)}, u32[]{:S(2)}) collective-permute-start(bf16[144,128]{1,0:T(8,128)(2,1)S(1)} %shard_map.86.refs_4_), channel_id=1, source_target_pairs={{0,1},{1,0},{2,3},{3,2},{4,5},{5,4},{6,7},{7,6},{8,9},{9,8},{10,11... | collective-permute-start | bytes 110600 | tf_op jit(solution)/shard_map/ppermute | solution.py:284
  21.5 0.9 %shard_map.88 = (bf16[12,48,128]{2,1,0:T(8,128)(2,1)S(1)}, f32[12,48,128]{2,1,0:T(8,128)S(1)}, bf16[12,48,128]{2,1,0:T(8,128)(2,1)S(1)}, f32[12,48,128]{2,1,0:T(8,128)S(1)}) custom-call(bf16[12,48,128]{2,1,0:T(8,128)(2,1)S(1)} %get-tuple-element.40.refs_0_, bf16[12,48,128]{2,1,0:T(8,128)(2,1)S(1)} %collective-permute-done.8.refs_1_, ...), custom_call_target="tpu_custom_call" | custom-call | flops 100000000 | bytes 1212416 | tf_op jit(solution)/shard_map/pallas_call | solution.py:26
  22.6 1.6 %collective-permute-done.3.refs_1_ = bf16[432,128]{1,0:T(8,128)(2,1)S(1)} collective-permute-done((bf16[432,128]{1,0:T(8,128)(2,1)S(1)}, bf16[432,128]{1,0:T(8,128)(2,1)S(1)}, u32[]{:S(2)}, u32[]{:S(2)}) %collective-permute-start.3) | collective-permute-done | bytes 110624 | tf_op jit(solution)/shard_map/ppermute | solution.py:284
  24.3 1.1 %shard_map.89 = (bf16[12,48,128]{2,1,0:T(8,128)(2,1)S(1)}, bf16[12,48,128]{2,1,0:T(8,128)(2,1)S(1)}, bf16[12,24,128]{2,1,0:T(8,128)(2,1)S(1)}, bf16[12,24,128]{2,1,0:T(8,128)(2,1)S(1)}) custom-call(bf16[432,128]{1,0:T(8,128)(2,1)S(1)} %get-tuple-element.35.refs_0_, bf16[432,128]{1,0:T(8,128)(2,1)S(1)} %collective-permute-done.3.refs_1_, ...), custom_call_target="tpu_custom_call" | custom-call | flops 300000000 | bytes 1491328 | tf_op jit(solution)/shard_map/pallas_call | solution.py:26
  25.8 1.1 %shard_map.90 = (bf16[12,48,128]{2,1,0:T(8,128)(2,1)S(1)}, bf16[12,48,128]{2,1,0:T(8,128)(2,1)S(1)}, bf16[12,24,128]{2,1,0:T(8,128)(2,1)S(1)}, bf16[12,24,128]{2,1,0:T(8,128)(2,1)S(1)}) custom-call(bf16[432,128]{1,0:T(8,128)(2,1)S(1)} %get-tuple-element.35.refs_0_, bf16[432,128]{1,0:T(8,128)(2,1)S(1)} %collective-permute-done.3.refs_1_, ...), custom_call_target="tpu_custom_call" | custom-call | flops 300000000 | bytes 1933696 | tf_op jit(solution)/shard_map/pallas_call | solution.py:26
  27.6 0.9 %collective-permute-done.11.refs_1_.refs_3_ = bf16[12,24,128]{2,1,0:T(8,128)(2,1)S(1)} collective-permute-done((bf16[12,24,128]{2,1,0:T(8,128)(2,1)S(1)}, bf16[12,24,128]{2,1,0:T(8,128)(2,1)S(1)}, u32[]{:S(2)}, u32[]{:S(2)}) %collective-permute-start.11) | collective-permute-done | bytes 73760 | tf_op jit(solution)/shard_map/ppermute | solution.py:276
  28.8 1.4 %collective-permute-start.17 = (bf16[6,48,128]{2,1,0:T(8,128)(2,1)S(1)}, bf16[6,48,128]{2,1,0:T(8,128)(2,1)S(1)}, u32[]{:S(2)}, u32[]{:S(2)}) collective-permute-start(bf16[6,48,128]{2,1,0:T(8,128)(2,1)S(1)} %shard_map.94), channel_id=1, source_target_pairs={{0,4},{2,6},{4,0},{6,2},{8,12},{10,14},{12,8},{14,10},{1,5},{3,7},... | collective-permute-start | bytes 221192 | tf_op jit(solution)/shard_map/ppermute | solution.py:276
  30.2 1.0 %shard_map.93 = (bf16[6,48,128]{2,1,0:T(8,128)(2,1)S(1)}, bf16[6,48,128]{2,1,0:T(8,128)(2,1)S(1)}, bf16[6,48,128]{2,1,0:T(8,128)(2,1)S(1)}) custom-call(bf16[12,48,128]{2,1,0:T(8,128)(2,1)S(1)} %get-tuple-element.52.refs_2_.refs_0_, bf16[12,48,128]{2,1,0:T(8,128)(2,1)S(1)} %collective-permute-done.12.refs_3_.refs_1_, ...), custom_call_target="tpu_custom_call" | custom-call | flops 360000000 | bytes 663552 | tf_op jit(solution)/shard_map/pallas_call | solution.py:26
  31.2 2.0 %collective-permute-start.15 = (bf16[6,48,128]{2,1,0:T(8,128)(2,1)S(1)}, bf16[6,48,128]{2,1,0:T(8,128)(2,1)S(1)}, u32[]{:S(2)}, u32[]{:S(2)}) collective-permute-start(bf16[6,48,128]{2,1,0:T(8,128)(2,1)S(1)} %get-tuple-element.55), channel_id=1, source_target_pairs={{0,8},{2,10},{4,12},{6,14},{8,0},{10,2},{12,4},{14,6},{1,9},{3,11}... | collective-permute-start | bytes 221192 | tf_op jit(solution)/shard_map/ppermute | solution.py:276
  33.2 1.5 %collective-permute-start.16 = (bf16[6,48,128]{2,1,0:T(8,128)(2,1)S(1)}, bf16[6,48,128]{2,1,0:T(8,128)(2,1)S(1)}, u32[]{:S(2)}, u32[]{:S(2)}) collective-permute-start(bf16[6,48,128]{2,1,0:T(8,128)(2,1)S(1)} %get-tuple-element.56), channel_id=1, source_target_pairs={{0,12},{2,14},{4,8},{6,10},{8,4},{10,6},{12,0},{14,2},{1,13},{3,15... | collective-permute-start | bytes 221192 | tf_op jit(solution)/shard_map/ppermute | solution.py:276
  36.0 2.4 %collective-permute-start.18 = (bf16[6,48,128]{2,1,0:T(8,128)(2,1)S(1)}, bf16[6,48,128]{2,1,0:T(8,128)(2,1)S(1)}, u32[]{:S(2)}, u32[]{:S(2)}) collective-permute-start(bf16[6,48,128]{2,1,0:T(8,128)(2,1)S(1)} %add_convert_fusion), channel_id=1, source_target_pairs={{0,8},{2,10},{4,12},{6,14},{8,0},{10,2},{12,4},{14,6},{1,9},{3,11}... | collective-permute-start | bytes 221192 | tf_op jit(solution)/shard_map/ppermute | solution.py:276
  39.8 4.5 %collective-permute-done.18.refs_4_ = bf16[6,48,128]{2,1,0:T(8,128)(2,1)S(1)} collective-permute-done((bf16[6,48,128]{2,1,0:T(8,128)(2,1)S(1)}, bf16[6,48,128]{2,1,0:T(8,128)(2,1)S(1)}, u32[]{:S(2)}, u32[]{:S(2)}) %collective-permute-start.18) | collective-permute-done | bytes 73760 | tf_op jit(solution)/shard_map/ppermute | solution.py:276
  44.3 1.0 %shard_map.96 = bf16[12,48,128]{2,1,0:T(8,128)(2,1)} custom-call(f32[12,48,128]{2,1,0:T(8,128)S(1)} %shard_map.91.refs_0_, bf16[12,48,128]{2,1,0:T(8,128)(2,1)S(1)} %collective-permute-done.14.refs_1_, bf16[6,48,128]{2,1,0:T(8,128)(2,1)S(1)} %collective-permute-done.15.refs_2_, bf16[6,48,128]{2,1,0:T(8,128)(2,1)S(1)} %collective-permute-done.16.refs_3_, ...), custom_call_target="tpu_custom_call" | custom-call | flops 100000000 | bytes 1286144 | tf_op jit(solution)/shard_map/pallas_call | solution.py:26
  (50 shorter events, 7.3 us)
Async XLA Ops:
  0.0 7.8 %copy-start = (bf16[12,48,128]{2,1,0:T(8,128)(2,1)S(1)}, bf16[12,48,128]{2,1,0:T(8,128)(2,1)}, u32[]{:S(2)}) copy-start(bf16[12,48,128]{2,1,0:T(8,128)(2,1)} %refs_1_.1) | copy-start | bytes 442372
  0.0 7.8 %copy-start.3 = (bf16[128,512]{1,0:T(8,128)(2,1)S(1)}, bf16[128,512]{1,0:T(8,128)(2,1)}, u32[]{:S(2)}) copy-start(bf16[128,512]{1,0:T(8,128)(2,1)} %refs_3_.1) | copy-start | bytes 393220
  0.0 7.8 %copy-start.8 = (s32[96]{0:T(128)S(1)}, s32[96]{0:T(128)}, u32[]{:S(2)}) copy-start(s32[96]{0:T(128)} %param.9) | copy-start | bytes 1156
  2.1 11.4 %collective-permute-start.2 = (bf16[12,48,128]{2,1,0:T(8,128)(2,1)}, bf16[12,48,128]{2,1,0:T(8,128)(2,1)S(1)}, u32[]{:S(2)}, u32[]{:S(2)}) collective-permute-start(bf16[12,48,128]{2,1,0:T(8,128)(2,1)} %shard_map.82.refs_0_.refs_2_), channel_id=1, source_target_pairs={{0,8},{2,10},{4,12},{6,14},{8,0},{10,2},{12,4},{14,6},{1,9},{3,11}... | collective-permute-start | bytes 442376 | tf_op jit(solution)/shard_map/ppermute | solution.py:276
  6.2 8.0 %collective-permute-start.1 = (bf16[12,48,128]{2,1,0:T(8,128)(2,1)}, bf16[12,48,128]{2,1,0:T(8,128)(2,1)S(1)}, u32[]{:S(2)}, u32[]{:S(2)}) collective-permute-start(bf16[12,48,128]{2,1,0:T(8,128)(2,1)} %shard_map.82.refs_0_.refs_2_), channel_id=1, source_target_pairs={{0,4},{2,6},{4,0},{6,2},{8,12},{10,14},{12,8},{14,10},{1,5},{3,7},... | collective-permute-start | bytes 442376 | tf_op jit(solution)/shard_map/ppermute | solution.py:276
  8.8 5.5 %copy-start.2 = (bf16[12,48,128]{2,1,0:T(8,128)(2,1)S(1)}, bf16[12,48,128]{2,1,0:T(8,128)(2,1)}, u32[]{:S(2)}) copy-start(bf16[12,48,128]{2,1,0:T(8,128)(2,1)} %shard_map.82.refs_0_.refs_2_) | copy-start | bytes 442372
  9.2 5.1 %collective-permute-start = (bf16[12,48,128]{2,1,0:T(8,128)(2,1)S(1)}, bf16[12,48,128]{2,1,0:T(8,128)(2,1)S(1)}, u32[]{:S(2)}, u32[]{:S(2)}) collective-permute-start(bf16[12,48,128]{2,1,0:T(8,128)(2,1)S(1)} %get-tuple-element.32.refs_0_.refs_2_), channel_id=1, source_target_pairs={{0,2},{2,0},{4,6},{6,4},{8,10},{10,8},{12,14},{14,12},{1,3},{3,1},... | collective-permute-start | bytes 442376 | tf_op jit(solution)/shard_map/ppermute | solution.py:276
  9.3 11.3 %collective-permute-start.8 = (bf16[12,48,128]{2,1,0:T(8,128)(2,1)S(1)}, bf16[12,48,128]{2,1,0:T(8,128)(2,1)S(1)}, u32[]{:S(2)}, u32[]{:S(2)}) collective-permute-start(bf16[12,48,128]{2,1,0:T(8,128)(2,1)S(1)} %get-tuple-element.40.refs_0_), channel_id=1, source_target_pairs={{0,1},{1,0},{2,3},{3,2},{4,5},{5,4},{6,7},{7,6},{8,9},{9,8},{10,11... | collective-permute-start | bytes 442376 | tf_op jit(solution)/shard_map/ppermute | solution.py:284
  13.6 5.1 %collective-permute-start.6 = (bf16[12,48,128]{2,1,0:T(8,128)(2,1)S(1)}, bf16[12,48,128]{2,1,0:T(8,128)(2,1)S(1)}, u32[]{:S(2)}, u32[]{:S(2)}) collective-permute-start(bf16[12,48,128]{2,1,0:T(8,128)(2,1)S(1)} %collective-permute-done.2.refs_4_), channel_id=1, source_target_pairs={{0,4},{2,6},{4,0},{6,2},{8,12},{10,14},{12,8},{14,10},{1,5},{3,7},... | collective-permute-start | bytes 442376 | tf_op jit(solution)/shard_map/ppermute | solution.py:276
  16.4 5.9 %collective-permute-start.5 = (bf16[432,128]{1,0:T(8,128)(2,1)S(1)}, bf16[432,128]{1,0:T(8,128)(2,1)S(1)}, u32[]{:S(2)}, u32[]{:S(2)}) collective-permute-start(bf16[432,128]{1,0:T(8,128)(2,1)S(1)} %get-tuple-element.36), channel_id=1, source_target_pairs={{0,3},{1,2},{2,1},{3,0},{4,7},{5,6},{6,5},{7,4},{8,11},{9,10},{10,... | collective-permute-start | bytes 331784 | tf_op jit(solution)/shard_map/ppermute | solution.py:284
  17.3 5.3 %collective-permute-start.4 = (bf16[432,128]{1,0:T(8,128)(2,1)S(1)}, bf16[432,128]{1,0:T(8,128)(2,1)S(1)}, u32[]{:S(2)}, u32[]{:S(2)}) collective-permute-start(bf16[432,128]{1,0:T(8,128)(2,1)S(1)} %get-tuple-element.36), channel_id=1, source_target_pairs={{0,2},{1,3},{2,0},{3,1},{4,6},{5,7},{6,4},{7,5},{8,10},{9,11},{10,... | collective-permute-start | bytes 331784 | tf_op jit(solution)/shard_map/ppermute | solution.py:284
  18.1 6.2 %collective-permute-start.3 = (bf16[432,128]{1,0:T(8,128)(2,1)S(1)}, bf16[432,128]{1,0:T(8,128)(2,1)S(1)}, u32[]{:S(2)}, u32[]{:S(2)}) collective-permute-start(bf16[432,128]{1,0:T(8,128)(2,1)S(1)} %get-tuple-element.35.refs_0_), channel_id=1, source_target_pairs={{0,1},{1,0},{2,3},{3,2},{4,5},{5,4},{6,7},{7,6},{8,9},{9,8},{10,11... | collective-permute-start | bytes 331784 | tf_op jit(solution)/shard_map/ppermute | solution.py:284
  19.8 5.6 %collective-permute-start.10 = (bf16[144,128]{1,0:T(8,128)(2,1)S(1)}, bf16[144,128]{1,0:T(8,128)(2,1)S(1)}, u32[]{:S(2)}, u32[]{:S(2)}) collective-permute-start(bf16[144,128]{1,0:T(8,128)(2,1)S(1)} %shard_map.87), channel_id=1, source_target_pairs={{0,3},{1,2},{2,1},{3,0},{4,7},{5,6},{6,5},{7,4},{8,11},{9,10},{10,... | collective-permute-start | bytes 110600 | tf_op jit(solution)/shard_map/ppermute | solution.py:284
  20.6 5.2 %collective-permute-start.7 = (bf16[144,128]{1,0:T(8,128)(2,1)S(1)}, bf16[144,128]{1,0:T(8,128)(2,1)S(1)}, u32[]{:S(2)}, u32[]{:S(2)}) collective-permute-start(bf16[144,128]{1,0:T(8,128)(2,1)S(1)} %shard_map.86.refs_4_), channel_id=1, source_target_pairs={{0,1},{1,0},{2,3},{3,2},{4,5},{5,4},{6,7},{7,6},{8,9},{9,8},{10,11... | collective-permute-start | bytes 110600 | tf_op jit(solution)/shard_map/ppermute | solution.py:284
  22.3 3.4 %collective-permute-start.9 = (bf16[144,128]{1,0:T(8,128)(2,1)S(1)}, bf16[144,128]{1,0:T(8,128)(2,1)S(1)}, u32[]{:S(2)}, u32[]{:S(2)}) collective-permute-start(bf16[144,128]{1,0:T(8,128)(2,1)S(1)} %shard_map.87), channel_id=1, source_target_pairs={{0,2},{1,3},{2,0},{3,1},{4,6},{5,7},{6,4},{7,5},{8,10},{9,11},{10,... | collective-permute-start | bytes 110600 | tf_op jit(solution)/shard_map/ppermute | solution.py:284
  26.9 1.5 %collective-permute-start.12 = (bf16[12,48,128]{2,1,0:T(8,128)(2,1)S(1)}, bf16[12,48,128]{2,1,0:T(8,128)(2,1)S(1)}, u32[]{:S(2)}, u32[]{:S(2)}) collective-permute-start(bf16[12,48,128]{2,1,0:T(8,128)(2,1)S(1)} %get-tuple-element.52.refs_2_.refs_0_), channel_id=1, source_target_pairs={{0,2},{2,0},{4,6},{6,4},{8,10},{10,8},{12,14},{14,12},{1,3},{3,1},... | collective-permute-start | bytes 442376 | tf_op jit(solution)/shard_map/ppermute | solution.py:276
  27.1 1.4 %collective-permute-start.11 = (bf16[12,24,128]{2,1,0:T(8,128)(2,1)S(1)}, bf16[12,24,128]{2,1,0:T(8,128)(2,1)S(1)}, u32[]{:S(2)}, u32[]{:S(2)}) collective-permute-start(bf16[12,24,128]{2,1,0:T(8,128)(2,1)S(1)} %get-tuple-element.51), channel_id=1, source_target_pairs={{0,2},{2,0},{4,6},{6,4},{8,10},{10,8},{12,14},{14,12},{1,3},{3,1},... | collective-permute-start | bytes 221192 | tf_op jit(solution)/shard_map/ppermute | solution.py:276
  27.5 7.2 %collective-permute-start.13 = (bf16[12,24,128]{2,1,0:T(8,128)(2,1)S(1)}, bf16[12,24,128]{2,1,0:T(8,128)(2,1)S(1)}, u32[]{:S(2)}, u32[]{:S(2)}) collective-permute-start(bf16[12,24,128]{2,1,0:T(8,128)(2,1)S(1)} %get-tuple-element.54), channel_id=1, source_target_pairs={{0,2},{2,0},{4,6},{6,4},{8,10},{10,8},{12,14},{14,12},{1,3},{3,1},... | collective-permute-start | bytes 221192 | tf_op jit(solution)/shard_map/ppermute | solution.py:276
  28.8 7.1 %collective-permute-start.17 = (bf16[6,48,128]{2,1,0:T(8,128)(2,1)S(1)}, bf16[6,48,128]{2,1,0:T(8,128)(2,1)S(1)}, u32[]{:S(2)}, u32[]{:S(2)}) collective-permute-start(bf16[6,48,128]{2,1,0:T(8,128)(2,1)S(1)} %shard_map.94), channel_id=1, source_target_pairs={{0,4},{2,6},{4,0},{6,2},{8,12},{10,14},{12,8},{14,10},{1,5},{3,7},... | collective-permute-start | bytes 221192 | tf_op jit(solution)/shard_map/ppermute | solution.py:276
  31.2 8.5 %collective-permute-start.15 = (bf16[6,48,128]{2,1,0:T(8,128)(2,1)S(1)}, bf16[6,48,128]{2,1,0:T(8,128)(2,1)S(1)}, u32[]{:S(2)}, u32[]{:S(2)}) collective-permute-start(bf16[6,48,128]{2,1,0:T(8,128)(2,1)S(1)} %get-tuple-element.55), channel_id=1, source_target_pairs={{0,8},{2,10},{4,12},{6,14},{8,0},{10,2},{12,4},{14,6},{1,9},{3,11}... | collective-permute-start | bytes 221192 | tf_op jit(solution)/shard_map/ppermute | solution.py:276
  33.2 6.6 %collective-permute-start.16 = (bf16[6,48,128]{2,1,0:T(8,128)(2,1)S(1)}, bf16[6,48,128]{2,1,0:T(8,128)(2,1)S(1)}, u32[]{:S(2)}, u32[]{:S(2)}) collective-permute-start(bf16[6,48,128]{2,1,0:T(8,128)(2,1)S(1)} %get-tuple-element.56), channel_id=1, source_target_pairs={{0,12},{2,14},{4,8},{6,10},{8,4},{10,6},{12,0},{14,2},{1,13},{3,15... | collective-permute-start | bytes 221192 | tf_op jit(solution)/shard_map/ppermute | solution.py:276
  35.4 8.9 %collective-permute-start.14 = (bf16[12,48,128]{2,1,0:T(8,128)(2,1)S(1)}, bf16[12,48,128]{2,1,0:T(8,128)(2,1)S(1)}, u32[]{:S(2)}, u32[]{:S(2)}) collective-permute-start(bf16[12,48,128]{2,1,0:T(8,128)(2,1)S(1)} %shard_map.92), channel_id=1, source_target_pairs={{0,4},{2,6},{4,0},{6,2},{8,12},{10,14},{12,8},{14,10},{1,5},{3,7},... | collective-permute-start | bytes 442376 | tf_op jit(solution)/shard_map/ppermute | solution.py:276
  36.0 8.3 %collective-permute-start.18 = (bf16[6,48,128]{2,1,0:T(8,128)(2,1)S(1)}, bf16[6,48,128]{2,1,0:T(8,128)(2,1)S(1)}, u32[]{:S(2)}, u32[]{:S(2)}) collective-permute-start(bf16[6,48,128]{2,1,0:T(8,128)(2,1)S(1)} %add_convert_fusion), channel_id=1, source_target_pairs={{0,8},{2,10},{4,12},{6,14},{8,0},{10,2},{12,4},{14,6},{1,9},{3,11}... | collective-permute-start | bytes 221192 | tf_op jit(solution)/shard_map/ppermute | solution.py:276
  38.8 5.5 %copy-start.6 = (bf16[128,128]{1,0:T(8,128)(2,1)S(1)}, bf16[128,128]{1,0:T(8,128)(2,1)}, u32[]{:S(2)}) copy-start(bf16[128,128]{1,0:T(8,128)(2,1)} %refs_7_.3) | copy-start | bytes 98308
  (5 other events, 14.7 us)

commit v9 on v8

--- a/solution.py
+++ b/solution.py
@@ -10,7 +10,6 @@
 F32, BF16 = jnp.float32, jnp.bfloat16
 VMEM = pl.BlockSpec(memory_space=pltpu.VMEM)
 LIMIT = 40 * 1024 * 1024
-FULL = 63 * 1024 * 1024
 
 
 def after(kernel, count, *refs):
@@ -286,7 +285,7 @@
     right = call(
         opening_kernel,
         block,
-        [pair_rep, mask, out_project],
+        [pltpu.with_memory_space_constraint(v, pltpu.HBM) for v in (pair_rep, mask, out_project)],
         scratch=[
             pltpu.VMEM(pair_rep.shape, BF16),
             pltpu.VMEM(mask.shape, jnp.int32),
@@ -295,7 +294,6 @@
         ],
         flops=100_000_000,
         outside=(0, 1, 2),
-        limit=FULL,
     )
     rights = {0: right}
     bit = chips // 2

time: 45.5 us -> 44.6 us (0.980)
  local copies, waits for them, and re-layouts: 0.97 us -> 0.04 us
  waiting for transfers between devices: 10.5 us -> 11.3 us
  Pallas kernels: 12.8 us -> 12.2 us
    unnamed x20 -> x16, local copies, waits for them, and re-layouts: 0.97 us -> 0.04 us
    ppermute x12, waiting for transfers between devices: 8.52 us -> 9.35 us  [along_row(): return lax.ppermute(v, 'row', [(i, i ^ bits) for i in range(rows_n)])]
    pallas_call x15, Pallas kernels: 12.8 us -> 12.2 us  [call(): pl.pallas_call(kernel, out_shape=outs, in_specs=[pl.BlockSpec(memory_spac...]
where the time goes in v9:
time: 44.6 us; the launch traced here: 44.5 us
  starting transfers between devices  20.8 us (47%)
  Pallas kernels  12.2 us (27%)
  waiting for transfers between devices  11.3 us (25%)
    ppermute x12, starting transfers between devices, along_row(): return lax.ppermute(v, 'row', [(i, i ^ bits) for i in range(rows_n)])  15 us
    pallas_call x15, Pallas kernels, call(): pl.pallas_call(kernel, out_shape=outs, in_specs=[pl.BlockSpec(memory_spac...  12.2 us
    ppermute x12, waiting for transfers between devices, along_row(): return lax.ppermute(v, 'row', [(i, i ^ bits) for i in range(rows_n)])  9.35 us
    ppermute x7, starting transfers between devices, shift(): return lax.ppermute(v, ('row', 'col'), pairs)  5.76 us
    ppermute x7, waiting for transfers between devices, shift(): return lax.ppermute(v, ('row', 'col'), pairs)  1.91 us
  transfers between devices with their start and end apart: 19, of which 8 were waited for; matrix products, arithmetic and copies ran while one was open for 0% of the time, Pallas kernels for 19%

profile of v9, /device:TPU:0, one launch (start us, length us, event | category | flops | bytes accessed | tf_op | source)
XLA Modules:
  0.0 44.5 jit_solution(10961991381809059888)
XLA Ops:
  0.0 1.5 %shard_map.82.refs_0_.refs_2_ = bf16[12,48,128]{2,1,0:T(8,128)(2,1)S(1)} custom-call(bf16[12,48,128]{2,1,0:T(8,128)(2,1)} %refs_1_.1, s32[1,96]{1,0:T(1,128)} %bitcast.1, bf16[128,512]{1,0:T(8,128)(2,1)} %refs_3_.1), custom_call_target="tpu_custom_call" | custom-call | flops 100000000 | bytes 426368 | tf_op jit(solution)/shard_map/pallas_call | solution.py:25
  1.5 4.1 %collective-permute-start.2 = (bf16[12,48,128]{2,1,0:T(8,128)(2,1)S(1)}, bf16[12,48,128]{2,1,0:T(8,128)(2,1)S(1)}, u32[]{:S(2)}, u32[]{:S(2)}) collective-permute-start(bf16[12,48,128]{2,1,0:T(8,128)(2,1)S(1)} %shard_map.82.refs_0_.refs_2_), channel_id=1, source_target_pairs={{0,8},{2,10},{4,12},{6,14},{8,0},{10,2},{12,4},{14,6},{1,9},{3,11}... | collective-permute-start | bytes 442376 | tf_op jit(solution)/shard_map/ppermute | solution.py:275
  5.6 1.6 %collective-permute-start.1 = (bf16[12,48,128]{2,1,0:T(8,128)(2,1)S(1)}, bf16[12,48,128]{2,1,0:T(8,128)(2,1)S(1)}, u32[]{:S(2)}, u32[]{:S(2)}) collective-permute-start(bf16[12,48,128]{2,1,0:T(8,128)(2,1)S(1)} %shard_map.82.refs_0_.refs_2_), channel_id=1, source_target_pairs={{0,4},{2,6},{4,0},{6,2},{8,12},{10,14},{12,8},{14,10},{1,5},{3,7},... | collective-permute-start | bytes 442376 | tf_op jit(solution)/shard_map/ppermute | solution.py:275
  7.7 1.6 %collective-permute-start.8 = (bf16[12,48,128]{2,1,0:T(8,128)(2,1)S(1)}, bf16[12,48,128]{2,1,0:T(8,128)(2,1)S(1)}, u32[]{:S(2)}, u32[]{:S(2)}) collective-permute-start(bf16[12,48,128]{2,1,0:T(8,128)(2,1)S(1)} %get-tuple-element.40.refs_0_), channel_id=1, source_target_pairs={{0,1},{1,0},{2,3},{3,2},{4,5},{5,4},{6,7},{7,6},{8,9},{9,8},{10,11... | collective-permute-start | bytes 442376 | tf_op jit(solution)/shard_map/ppermute | solution.py:283
  9.3 3.4 %collective-permute-done.2.refs_4_ = bf16[12,48,128]{2,1,0:T(8,128)(2,1)S(1)} collective-permute-done((bf16[12,48,128]{2,1,0:T(8,128)(2,1)S(1)}, bf16[12,48,128]{2,1,0:T(8,128)(2,1)S(1)}, u32[]{:S(2)}, u32[]{:S(2)}) %collective-permute-start.2) | collective-permute-done | bytes 147488 | tf_op jit(solution)/shard_map/ppermute | solution.py:275
  13.3 1.2 %shard_map.84 = (bf16[288,128]{1,0:T(8,128)(2,1)S(1)}, bf16[288,128]{1,0:T(8,128)(2,1)S(1)}) custom-call(bf16[12,48,128]{2,1,0:T(8,128)(2,1)S(1)} %get-tuple-element.32.refs_0_.refs_2_, bf16[12,48,128]{2,1,0:T(8,128)(2,1)S(1)} %collective-permute-done.refs_1_.refs_3_.refs_0_, bf16[12,48,128]{2,1,0:T(8,128)(2,1)S(1)} %shard_map.82.refs_0_.refs_2_, ...), custom_call_target="tpu_custom_call" | custom-call | flops 500000000 | bytes 737280 | tf_op jit(solution)/shard_map/pallas_call | solution.py:25
  14.5 0.9 %shard_map.85 = (bf16[432,128]{1,0:T(8,128)(2,1)S(1)}, bf16[432,128]{1,0:T(8,128)(2,1)S(1)}) custom-call(bf16[288,128]{1,0:T(8,128)(2,1)S(1)} %get-tuple-element.33.refs_0_, bf16[288,128]{1,0:T(8,128)(2,1)S(1)} %get-tuple-element.34.refs_1_, bf16[12,48,128]{2,1,0:T(8,128)(2,1)S(1)} %get-tuple-element.32.refs_0_.refs_2_, ...), custom_call_target="tpu_custom_call" | custom-call | flops 250000000 | bytes 811008 | tf_op jit(solution)/shard_map/pallas_call | solution.py:25
  15.4 0.9 %collective-permute-start.5 = (bf16[432,128]{1,0:T(8,128)(2,1)S(1)}, bf16[432,128]{1,0:T(8,128)(2,1)S(1)}, u32[]{:S(2)}, u32[]{:S(2)}) collective-permute-start(bf16[432,128]{1,0:T(8,128)(2,1)S(1)} %get-tuple-element.36), channel_id=1, source_target_pairs={{0,3},{1,2},{2,1},{3,0},{4,7},{5,6},{6,5},{7,4},{8,11},{9,10},{10,... | collective-permute-start | bytes 331784 | tf_op jit(solution)/shard_map/ppermute | solution.py:283
  16.3 0.8 %collective-permute-start.4 = (bf16[432,128]{1,0:T(8,128)(2,1)S(1)}, bf16[432,128]{1,0:T(8,128)(2,1)S(1)}, u32[]{:S(2)}, u32[]{:S(2)}) collective-permute-start(bf16[432,128]{1,0:T(8,128)(2,1)S(1)} %get-tuple-element.36), channel_id=1, source_target_pairs={{0,2},{1,3},{2,0},{3,1},{4,6},{5,7},{6,4},{7,5},{8,10},{9,11},{10,... | collective-permute-start | bytes 331784 | tf_op jit(solution)/shard_map/ppermute | solution.py:283
  18.9 0.7 %collective-permute-start.10 = (bf16[144,128]{1,0:T(8,128)(2,1)S(1)}, bf16[144,128]{1,0:T(8,128)(2,1)S(1)}, u32[]{:S(2)}, u32[]{:S(2)}) collective-permute-start(bf16[144,128]{1,0:T(8,128)(2,1)S(1)} %shard_map.87), channel_id=1, source_target_pairs={{0,3},{1,2},{2,1},{3,0},{4,7},{5,6},{6,5},{7,4},{8,11},{9,10},{10,... | collective-permute-start | bytes 110600 | tf_op jit(solution)/shard_map/ppermute | solution.py:283
  19.6 1.0 %collective-permute-start.7 = (bf16[144,128]{1,0:T(8,128)(2,1)S(1)}, bf16[144,128]{1,0:T(8,128)(2,1)S(1)}, u32[]{:S(2)}, u32[]{:S(2)}) collective-permute-start(bf16[144,128]{1,0:T(8,128)(2,1)S(1)} %shard_map.86.refs_4_), channel_id=1, source_target_pairs={{0,1},{1,0},{2,3},{3,2},{4,5},{5,4},{6,7},{7,6},{8,9},{9,8},{10,11... | collective-permute-start | bytes 110600 | tf_op jit(solution)/shard_map/ppermute | solution.py:283
  20.6 0.9 %shard_map.88 = (bf16[12,48,128]{2,1,0:T(8,128)(2,1)S(1)}, f32[12,48,128]{2,1,0:T(8,128)S(1)}, bf16[12,48,128]{2,1,0:T(8,128)(2,1)S(1)}, f32[12,48,128]{2,1,0:T(8,128)S(1)}) custom-call(bf16[12,48,128]{2,1,0:T(8,128)(2,1)S(1)} %get-tuple-element.40.refs_0_, bf16[12,48,128]{2,1,0:T(8,128)(2,1)S(1)} %collective-permute-done.8.refs_1_, ...), custom_call_target="tpu_custom_call" | custom-call | flops 100000000 | bytes 1212416 | tf_op jit(solution)/shard_map/pallas_call | solution.py:25
  21.8 1.5 %collective-permute-done.3.refs_1_ = bf16[432,128]{1,0:T(8,128)(2,1)S(1)} collective-permute-done((bf16[432,128]{1,0:T(8,128)(2,1)S(1)}, bf16[432,128]{1,0:T(8,128)(2,1)S(1)}, u32[]{:S(2)}, u32[]{:S(2)}) %collective-permute-start.3) | collective-permute-done | bytes 110624 | tf_op jit(solution)/shard_map/ppermute | solution.py:283
  23.3 1.1 %shard_map.89 = (bf16[12,48,128]{2,1,0:T(8,128)(2,1)S(1)}, bf16[12,48,128]{2,1,0:T(8,128)(2,1)S(1)}, bf16[12,24,128]{2,1,0:T(8,128)(2,1)S(1)}, bf16[12,24,128]{2,1,0:T(8,128)(2,1)S(1)}) custom-call(bf16[432,128]{1,0:T(8,128)(2,1)S(1)} %get-tuple-element.35.refs_0_, bf16[432,128]{1,0:T(8,128)(2,1)S(1)} %collective-permute-done.3.refs_1_, ...), custom_call_target="tpu_custom_call" | custom-call | flops 300000000 | bytes 1491328 | tf_op jit(solution)/shard_map/pallas_call | solution.py:25
  24.8 1.1 %shard_map.90 = (bf16[12,48,128]{2,1,0:T(8,128)(2,1)S(1)}, bf16[12,48,128]{2,1,0:T(8,128)(2,1)S(1)}, bf16[12,24,128]{2,1,0:T(8,128)(2,1)S(1)}, bf16[12,24,128]{2,1,0:T(8,128)(2,1)S(1)}) custom-call(bf16[432,128]{1,0:T(8,128)(2,1)S(1)} %get-tuple-element.35.refs_0_, bf16[432,128]{1,0:T(8,128)(2,1)S(1)} %collective-permute-done.3.refs_1_, ...), custom_call_target="tpu_custom_call" | custom-call | flops 300000000 | bytes 1933696 | tf_op jit(solution)/shard_map/pallas_call | solution.py:25
  26.6 0.9 %collective-permute-done.11.refs_1_.refs_3_ = bf16[12,24,128]{2,1,0:T(8,128)(2,1)S(1)} collective-permute-done((bf16[12,24,128]{2,1,0:T(8,128)(2,1)S(1)}, bf16[12,24,128]{2,1,0:T(8,128)(2,1)S(1)}, u32[]{:S(2)}, u32[]{:S(2)}) %collective-permute-start.11) | collective-permute-done | bytes 73760 | tf_op jit(solution)/shard_map/ppermute | solution.py:275
  27.9 1.5 %collective-permute-start.17 = (bf16[6,48,128]{2,1,0:T(8,128)(2,1)S(1)}, bf16[6,48,128]{2,1,0:T(8,128)(2,1)S(1)}, u32[]{:S(2)}, u32[]{:S(2)}) collective-permute-start(bf16[6,48,128]{2,1,0:T(8,128)(2,1)S(1)} %shard_map.94), channel_id=1, source_target_pairs={{0,4},{2,6},{4,0},{6,2},{8,12},{10,14},{12,8},{14,10},{1,5},{3,7},... | collective-permute-start | bytes 221192 | tf_op jit(solution)/shard_map/ppermute | solution.py:275
  29.3 1.0 %shard_map.93 = (bf16[6,48,128]{2,1,0:T(8,128)(2,1)S(1)}, bf16[6,48,128]{2,1,0:T(8,128)(2,1)S(1)}, bf16[6,48,128]{2,1,0:T(8,128)(2,1)S(1)}) custom-call(bf16[12,48,128]{2,1,0:T(8,128)(2,1)S(1)} %get-tuple-element.52.refs_2_.refs_0_, bf16[12,48,128]{2,1,0:T(8,128)(2,1)S(1)} %collective-permute-done.12.refs_3_.refs_1_, ...), custom_call_target="tpu_custom_call" | custom-call | flops 360000000 | bytes 663552 | tf_op jit(solution)/shard_map/pallas_call | solution.py:25
  30.3 2.0 %collective-permute-start.15 = (bf16[6,48,128]{2,1,0:T(8,128)(2,1)S(1)}, bf16[6,48,128]{2,1,0:T(8,128)(2,1)S(1)}, u32[]{:S(2)}, u32[]{:S(2)}) collective-permute-start(bf16[6,48,128]{2,1,0:T(8,128)(2,1)S(1)} %get-tuple-element.55), channel_id=1, source_target_pairs={{0,8},{2,10},{4,12},{6,14},{8,0},{10,2},{12,4},{14,6},{1,9},{3,11}... | collective-permute-start | bytes 221192 | tf_op jit(solution)/shard_map/ppermute | solution.py:275
  32.3 1.5 %collective-permute-start.16 = (bf16[6,48,128]{2,1,0:T(8,128)(2,1)S(1)}, bf16[6,48,128]{2,1,0:T(8,128)(2,1)S(1)}, u32[]{:S(2)}, u32[]{:S(2)}) collective-permute-start(bf16[6,48,128]{2,1,0:T(8,128)(2,1)S(1)} %get-tuple-element.56), channel_id=1, source_target_pairs={{0,12},{2,14},{4,8},{6,10},{8,4},{10,6},{12,0},{14,2},{1,13},{3,15... | collective-permute-start | bytes 221192 | tf_op jit(solution)/shard_map/ppermute | solution.py:275
  33.9 0.7 %shard_map.92 = bf16[12,48,128]{2,1,0:T(8,128)(2,1)S(1)} custom-call(bf16[12,24,128]{2,1,0:T(8,128)(2,1)S(1)} %get-tuple-element.50.refs_0_.refs_2_, bf16[12,24,128]{2,1,0:T(8,128)(2,1)S(1)} %collective-permute-done.11.refs_1_.refs_3_, bf16[12,48,128]{2,1,0:T(8,128)(2,1)S(1)} %get-tuple-element.52.refs_2_.refs_0_, ...), custom_call_target="tpu_custom_call" | custom-call | flops 240000000 | bytes 737280 | tf_op jit(solution)/shard_map/pallas_call | solution.py:25
  35.1 2.4 %collective-permute-start.18 = (bf16[6,48,128]{2,1,0:T(8,128)(2,1)S(1)}, bf16[6,48,128]{2,1,0:T(8,128)(2,1)S(1)}, u32[]{:S(2)}, u32[]{:S(2)}) collective-permute-start(bf16[6,48,128]{2,1,0:T(8,128)(2,1)S(1)} %add_convert_fusion), channel_id=1, source_target_pairs={{0,8},{2,10},{4,12},{6,14},{8,0},{10,2},{12,4},{14,6},{1,9},{3,11}... | collective-permute-start | bytes 221192 | tf_op jit(solution)/shard_map/ppermute | solution.py:275
  39.0 4.5 %collective-permute-done.18.refs_4_ = bf16[6,48,128]{2,1,0:T(8,128)(2,1)S(1)} collective-permute-done((bf16[6,48,128]{2,1,0:T(8,128)(2,1)S(1)}, bf16[6,48,128]{2,1,0:T(8,128)(2,1)S(1)}, u32[]{:S(2)}, u32[]{:S(2)}) %collective-permute-start.18) | collective-permute-done | bytes 73760 | tf_op jit(solution)/shard_map/ppermute | solution.py:275
  43.4 1.0 %shard_map.96 = bf16[12,48,128]{2,1,0:T(8,128)(2,1)} custom-call(f32[12,48,128]{2,1,0:T(8,128)S(1)} %shard_map.91.refs_0_, bf16[12,48,128]{2,1,0:T(8,128)(2,1)S(1)} %collective-permute-done.14.refs_1_, bf16[6,48,128]{2,1,0:T(8,128)(2,1)S(1)} %collective-permute-done.15.refs_2_, bf16[6,48,128]{2,1,0:T(8,128)(2,1)S(1)} %collective-permute-done.16.refs_3_, ...), custom_call_target="tpu_custom_call" | custom-call | flops 100000000 | bytes 1286144 | tf_op jit(solution)/shard_map/pallas_call | solution.py:25
  (46 shorter events, 6.6 us)
Async XLA Ops:
  0.0 7.2 %copy-start = (bf16[12,48,128]{2,1,0:T(8,128)(2,1)S(1)}, bf16[12,48,128]{2,1,0:T(8,128)(2,1)}, u32[]{:S(2)}) copy-start(bf16[12,48,128]{2,1,0:T(8,128)(2,1)} %refs_1_.1) | copy-start | bytes 442372
  0.0 7.2 %copy-start.1 = (bf16[128,512]{1,0:T(8,128)(2,1)S(1)}, bf16[128,512]{1,0:T(8,128)(2,1)}, u32[]{:S(2)}) copy-start(bf16[128,512]{1,0:T(8,128)(2,1)} %refs_3_.1) | copy-start | bytes 393220
  0.0 7.2 %copy-start.6 = (s32[96]{0:T(128)S(1)}, s32[96]{0:T(128)}, u32[]{:S(2)}) copy-start(s32[96]{0:T(128)} %param.9) | copy-start | bytes 1156
  1.5 11.2 %collective-permute-start.2 = (bf16[12,48,128]{2,1,0:T(8,128)(2,1)S(1)}, bf16[12,48,128]{2,1,0:T(8,128)(2,1)S(1)}, u32[]{:S(2)}, u32[]{:S(2)}) collective-permute-start(bf16[12,48,128]{2,1,0:T(8,128)(2,1)S(1)} %shard_map.82.refs_0_.refs_2_), channel_id=1, source_target_pairs={{0,8},{2,10},{4,12},{6,14},{8,0},{10,2},{12,4},{14,6},{1,9},{3,11}... | collective-permute-start | bytes 442376 | tf_op jit(solution)/shard_map/ppermute | solution.py:275
  5.6 7.7 %collective-permute-start.1 = (bf16[12,48,128]{2,1,0:T(8,128)(2,1)S(1)}, bf16[12,48,128]{2,1,0:T(8,128)(2,1)S(1)}, u32[]{:S(2)}, u32[]{:S(2)}) collective-permute-start(bf16[12,48,128]{2,1,0:T(8,128)(2,1)S(1)} %shard_map.82.refs_0_.refs_2_), channel_id=1, source_target_pairs={{0,4},{2,6},{4,0},{6,2},{8,12},{10,14},{12,8},{14,10},{1,5},{3,7},... | collective-permute-start | bytes 442376 | tf_op jit(solution)/shard_map/ppermute | solution.py:275
  7.6 5.7 %collective-permute-start = (bf16[12,48,128]{2,1,0:T(8,128)(2,1)S(1)}, bf16[12,48,128]{2,1,0:T(8,128)(2,1)S(1)}, u32[]{:S(2)}, u32[]{:S(2)}) collective-permute-start(bf16[12,48,128]{2,1,0:T(8,128)(2,1)S(1)} %get-tuple-element.32.refs_0_.refs_2_), channel_id=1, source_target_pairs={{0,2},{2,0},{4,6},{6,4},{8,10},{10,8},{12,14},{14,12},{1,3},{3,1},... | collective-permute-start | bytes 442376 | tf_op jit(solution)/shard_map/ppermute | solution.py:275
  7.7 11.9 %collective-permute-start.8 = (bf16[12,48,128]{2,1,0:T(8,128)(2,1)S(1)}, bf16[12,48,128]{2,1,0:T(8,128)(2,1)S(1)}, u32[]{:S(2)}, u32[]{:S(2)}) collective-permute-start(bf16[12,48,128]{2,1,0:T(8,128)(2,1)S(1)} %get-tuple-element.40.refs_0_), channel_id=1, source_target_pairs={{0,1},{1,0},{2,3},{3,2},{4,5},{5,4},{6,7},{7,6},{8,9},{9,8},{10,11... | collective-permute-start | bytes 442376 | tf_op jit(solution)/shard_map/ppermute | solution.py:283
  12.7 5.1 %collective-permute-start.6 = (bf16[12,48,128]{2,1,0:T(8,128)(2,1)S(1)}, bf16[12,48,128]{2,1,0:T(8,128)(2,1)S(1)}, u32[]{:S(2)}, u32[]{:S(2)}) collective-permute-start(bf16[12,48,128]{2,1,0:T(8,128)(2,1)S(1)} %collective-permute-done.2.refs_4_), channel_id=1, source_target_pairs={{0,4},{2,6},{4,0},{6,2},{8,12},{10,14},{12,8},{14,10},{1,5},{3,7},... | collective-permute-start | bytes 442376 | tf_op jit(solution)/shard_map/ppermute | solution.py:275
  15.4 6.0 %collective-permute-start.5 = (bf16[432,128]{1,0:T(8,128)(2,1)S(1)}, bf16[432,128]{1,0:T(8,128)(2,1)S(1)}, u32[]{:S(2)}, u32[]{:S(2)}) collective-permute-start(bf16[432,128]{1,0:T(8,128)(2,1)S(1)} %get-tuple-element.36), channel_id=1, source_target_pairs={{0,3},{1,2},{2,1},{3,0},{4,7},{5,6},{6,5},{7,4},{8,11},{9,10},{10,... | collective-permute-start | bytes 331784 | tf_op jit(solution)/shard_map/ppermute | solution.py:283
  16.3 5.4 %collective-permute-start.4 = (bf16[432,128]{1,0:T(8,128)(2,1)S(1)}, bf16[432,128]{1,0:T(8,128)(2,1)S(1)}, u32[]{:S(2)}, u32[]{:S(2)}) collective-permute-start(bf16[432,128]{1,0:T(8,128)(2,1)S(1)} %get-tuple-element.36), channel_id=1, source_target_pairs={{0,2},{1,3},{2,0},{3,1},{4,6},{5,7},{6,4},{7,5},{8,10},{9,11},{10,... | collective-permute-start | bytes 331784 | tf_op jit(solution)/shard_map/ppermute | solution.py:283
  17.1 6.2 %collective-permute-start.3 = (bf16[432,128]{1,0:T(8,128)(2,1)S(1)}, bf16[432,128]{1,0:T(8,128)(2,1)S(1)}, u32[]{:S(2)}, u32[]{:S(2)}) collective-permute-start(bf16[432,128]{1,0:T(8,128)(2,1)S(1)} %get-tuple-element.35.refs_0_), channel_id=1, source_target_pairs={{0,1},{1,0},{2,3},{3,2},{4,5},{5,4},{6,7},{7,6},{8,9},{9,8},{10,11... | collective-permute-start | bytes 331784 | tf_op jit(solution)/shard_map/ppermute | solution.py:283
  18.9 4.4 %copy-start.2 = (bf16[128,512]{1,0:T(8,128)(2,1)S(1)}, bf16[128,512]{1,0:T(8,128)(2,1)}, u32[]{:S(2)}) copy-start(bf16[128,512]{1,0:T(8,128)(2,1)} %refs_12_.1) | copy-start | bytes 393220
  18.9 5.5 %collective-permute-start.10 = (bf16[144,128]{1,0:T(8,128)(2,1)S(1)}, bf16[144,128]{1,0:T(8,128)(2,1)S(1)}, u32[]{:S(2)}, u32[]{:S(2)}) collective-permute-start(bf16[144,128]{1,0:T(8,128)(2,1)S(1)} %shard_map.87), channel_id=1, source_target_pairs={{0,3},{1,2},{2,1},{3,0},{4,7},{5,6},{6,5},{7,4},{8,11},{9,10},{10,... | collective-permute-start | bytes 110600 | tf_op jit(solution)/shard_map/ppermute | solution.py:283
  19.6 5.2 %collective-permute-start.7 = (bf16[144,128]{1,0:T(8,128)(2,1)S(1)}, bf16[144,128]{1,0:T(8,128)(2,1)S(1)}, u32[]{:S(2)}, u32[]{:S(2)}) collective-permute-start(bf16[144,128]{1,0:T(8,128)(2,1)S(1)} %shard_map.86.refs_4_), channel_id=1, source_target_pairs={{0,1},{1,0},{2,3},{3,2},{4,5},{5,4},{6,7},{7,6},{8,9},{9,8},{10,11... | collective-permute-start | bytes 110600 | tf_op jit(solution)/shard_map/ppermute | solution.py:283
  21.5 3.3 %collective-permute-start.9 = (bf16[144,128]{1,0:T(8,128)(2,1)S(1)}, bf16[144,128]{1,0:T(8,128)(2,1)S(1)}, u32[]{:S(2)}, u32[]{:S(2)}) collective-permute-start(bf16[144,128]{1,0:T(8,128)(2,1)S(1)} %shard_map.87), channel_id=1, source_target_pairs={{0,2},{1,3},{2,0},{3,1},{4,6},{5,7},{6,4},{7,5},{8,10},{9,11},{10,... | collective-permute-start | bytes 110600 | tf_op jit(solution)/shard_map/ppermute | solution.py:283
  25.9 1.5 %collective-permute-start.12 = (bf16[12,48,128]{2,1,0:T(8,128)(2,1)S(1)}, bf16[12,48,128]{2,1,0:T(8,128)(2,1)S(1)}, u32[]{:S(2)}, u32[]{:S(2)}) collective-permute-start(bf16[12,48,128]{2,1,0:T(8,128)(2,1)S(1)} %get-tuple-element.52.refs_2_.refs_0_), channel_id=1, source_target_pairs={{0,2},{2,0},{4,6},{6,4},{8,10},{10,8},{12,14},{14,12},{1,3},{3,1},... | collective-permute-start | bytes 442376 | tf_op jit(solution)/shard_map/ppermute | solution.py:275
  26.1 1.4 %collective-permute-start.11 = (bf16[12,24,128]{2,1,0:T(8,128)(2,1)S(1)}, bf16[12,24,128]{2,1,0:T(8,128)(2,1)S(1)}, u32[]{:S(2)}, u32[]{:S(2)}) collective-permute-start(bf16[12,24,128]{2,1,0:T(8,128)(2,1)S(1)} %get-tuple-element.51), channel_id=1, source_target_pairs={{0,2},{2,0},{4,6},{6,4},{8,10},{10,8},{12,14},{14,12},{1,3},{3,1},... | collective-permute-start | bytes 221192 | tf_op jit(solution)/shard_map/ppermute | solution.py:275
  26.5 7.3 %collective-permute-start.13 = (bf16[12,24,128]{2,1,0:T(8,128)(2,1)S(1)}, bf16[12,24,128]{2,1,0:T(8,128)(2,1)S(1)}, u32[]{:S(2)}, u32[]{:S(2)}) collective-permute-start(bf16[12,24,128]{2,1,0:T(8,128)(2,1)S(1)} %get-tuple-element.54), channel_id=1, source_target_pairs={{0,2},{2,0},{4,6},{6,4},{8,10},{10,8},{12,14},{14,12},{1,3},{3,1},... | collective-permute-start | bytes 221192 | tf_op jit(solution)/shard_map/ppermute | solution.py:275
  27.9 7.2 %collective-permute-start.17 = (bf16[6,48,128]{2,1,0:T(8,128)(2,1)S(1)}, bf16[6,48,128]{2,1,0:T(8,128)(2,1)S(1)}, u32[]{:S(2)}, u32[]{:S(2)}) collective-permute-start(bf16[6,48,128]{2,1,0:T(8,128)(2,1)S(1)} %shard_map.94), channel_id=1, source_target_pairs={{0,4},{2,6},{4,0},{6,2},{8,12},{10,14},{12,8},{14,10},{1,5},{3,7},... | collective-permute-start | bytes 221192 | tf_op jit(solution)/shard_map/ppermute | solution.py:275
  30.3 8.5 %collective-permute-start.15 = (bf16[6,48,128]{2,1,0:T(8,128)(2,1)S(1)}, bf16[6,48,128]{2,1,0:T(8,128)(2,1)S(1)}, u32[]{:S(2)}, u32[]{:S(2)}) collective-permute-start(bf16[6,48,128]{2,1,0:T(8,128)(2,1)S(1)} %get-tuple-element.55), channel_id=1, source_target_pairs={{0,8},{2,10},{4,12},{6,14},{8,0},{10,2},{12,4},{14,6},{1,9},{3,11}... | collective-permute-start | bytes 221192 | tf_op jit(solution)/shard_map/ppermute | solution.py:275
  32.3 6.6 %collective-permute-start.16 = (bf16[6,48,128]{2,1,0:T(8,128)(2,1)S(1)}, bf16[6,48,128]{2,1,0:T(8,128)(2,1)S(1)}, u32[]{:S(2)}, u32[]{:S(2)}) collective-permute-start(bf16[6,48,128]{2,1,0:T(8,128)(2,1)S(1)} %get-tuple-element.56), channel_id=1, source_target_pairs={{0,12},{2,14},{4,8},{6,10},{8,4},{10,6},{12,0},{14,2},{1,13},{3,15... | collective-permute-start | bytes 221192 | tf_op jit(solution)/shard_map/ppermute | solution.py:275
  34.5 8.9 %collective-permute-start.14 = (bf16[12,48,128]{2,1,0:T(8,128)(2,1)S(1)}, bf16[12,48,128]{2,1,0:T(8,128)(2,1)S(1)}, u32[]{:S(2)}, u32[]{:S(2)}) collective-permute-start(bf16[12,48,128]{2,1,0:T(8,128)(2,1)S(1)} %shard_map.92), channel_id=1, source_target_pairs={{0,4},{2,6},{4,0},{6,2},{8,12},{10,14},{12,8},{14,10},{1,5},{3,7},... | collective-permute-start | bytes 442376 | tf_op jit(solution)/shard_map/ppermute | solution.py:275
  35.1 8.3 %collective-permute-start.18 = (bf16[6,48,128]{2,1,0:T(8,128)(2,1)S(1)}, bf16[6,48,128]{2,1,0:T(8,128)(2,1)S(1)}, u32[]{:S(2)}, u32[]{:S(2)}) collective-permute-start(bf16[6,48,128]{2,1,0:T(8,128)(2,1)S(1)} %add_convert_fusion), channel_id=1, source_target_pairs={{0,8},{2,10},{4,12},{6,14},{8,0},{10,2},{12,4},{14,6},{1,9},{3,11}... | collective-permute-start | bytes 221192 | tf_op jit(solution)/shard_map/ppermute | solution.py:275
  37.9 5.5 %copy-start.4 = (bf16[128,128]{1,0:T(8,128)(2,1)S(1)}, bf16[128,128]{1,0:T(8,128)(2,1)}, u32[]{:S(2)}) copy-start(bf16[128,128]{1,0:T(8,128)(2,1)} %refs_7_.3) | copy-start | bytes 98308
  (3 other events, 9.1 us)

commit v10 on v9

--- a/solution.py
+++ b/solution.py
@@ -144,8 +144,8 @@
         l_scr[...] = left[...].astype(F32).reshape(rows * cols, chan)
 
         def step(block, totals):
-            for u in range(8):
-                k = block * 8 + u
+            for u in range(16):
+                k = block * 16 + u
                 right = r_scr[pl.ds(pl.multiple_of(k * width, 8), width), :]
                 totals = tuple(
                     t + l_scr[pl.ds(i * cols + k, 1), :] * right for i, t in enumerate(totals)
@@ -153,7 +153,7 @@
             return totals
 
         zero = jnp.zeros((width, chan), F32)
-        totals = lax.fori_loop(0, cols // 8, step, (zero,) * rows)
+        totals = lax.fori_loop(0, cols // 16, step, (zero,) * rows)
         for i, t in enumerate(totals):
             o_scr[pl.ds(i * used, used), :] = t[:used]
         begin = out_ref.shape[0] - rows * used
@@ -197,7 +197,11 @@
             for q in range(pieces):
                 part = scr[pl.ds(i * cols + (2 * q + side) * rows, rows), :]
                 half_scr[pl.ds((i * pieces + q) * rows, rows), :] = part
-        out_ref[...] = half_scr[...].astype(BF16).reshape(out_ref.shape)
+        half_block = half_scr[...].astype(BF16)
+        if out_ref is other_ref and h == cols_n - 1:
+            out_ref[pl.ds(rows, rows // 2)] = half_block.reshape(rows // 2, cols, chan)
+        else:
+            out_ref[...] = half_block.reshape(out_ref.shape)
     right = gated(normed, w_ref[:, width:], mask_ref, rows, cols, block)
     right_ref[...] = right.astype(BF16).reshape(right_ref.shape)
     for g in range(len(earlier) // 2):
@@ -207,18 +211,24 @@
             first_ref[...] = earlier[2 * g][...]
             right_ref[...] = earlier[2 * g + 1][...]
 
+    if h == cols_n - 1:
+        other_ref[pl.ds(0, rows)] = right_ref[...]
+
 
 def incoming_kernel(steps, *refs):
     outs, (l_scr, r_scr) = refs[-2 - len(steps) : -2], refs[-2:]
-    own_right, core_right, *lefts = refs[: -2 - len(steps)]
+    own_right, packed, *lefts = refs[: -2 - len(steps)]
     rows, cols, chan = own_right.shape
     width = lefts[0].shape[1]
     pieces = width // rows
     z, _, _ = place()
-    for n, ref in enumerate((own_right, core_right)):
-        r_scr[pl.ds(n * rows * cols, rows * cols), :] = ref[...].astype(F32).reshape(-1, chan)
-    for n, ref in enumerate(lefts):
-        l_scr[pl.ds(n * rows * width, rows * width), :] = ref[...].astype(F32).reshape(-1, chan)
+    for n, value in enumerate((own_right[...], packed[pl.ds(0, rows)])):
+        r_scr[pl.ds(n * rows * cols, rows * cols), :] = value.astype(F32).reshape(-1, chan)
+    lefts = [ref[...] for ref in lefts]
+    if len(lefts) == 1:
+        lefts.append(packed[pl.ds(rows, rows // 2)])
+    for n, value in enumerate(lefts):
+        l_scr[pl.ds(n * rows * width, rows * width), :] = value.astype(F32).reshape(-1, chan)
     for (m, begin, count), out_ref in zip(steps, outs):
         block = m // pieces - steps[0][0] // pieces
         base = block * (2 * rows * width) + ((z ^ m) % pieces) * rows + begin
@@ -232,7 +242,7 @@
                 )
 
             zero = jnp.zeros((cols, chan), F32)
-            totals = lax.fori_loop(0, 2 * rows, step, (zero,) * min(6, count - group), unroll=4)
+            totals = lax.fori_loop(0, 2 * rows, step, (zero,) * min(6, count - group), unroll=12)
             for i, t in enumerate(totals):
                 out_ref[group + i] = t.astype(out_ref.dtype)
 
@@ -270,6 +280,7 @@
     block = shape((rows, cols, chan), BF16)
     block32 = shape((rows, cols, chan), F32)
     half = (rows, pieces * rows, chan)
+    packed = (rows + rows // 2, cols, chan)
 
     def along_row(v, bits):
         return lax.ppermute(v, "row", [(i, i ^ bits) for i in range(rows_n)])
@@ -360,7 +371,7 @@
             parts, earlier = exchanged[0] * (pieces - 1) + exchanged[1], firsts
         first, right, left_mine, left_other = call(
             functools.partial(first_kernel, cols_n, h, groups),
-            [block, block, shape(half, BF16), shape(half, BF16)],
+            [block, block, shape(half, BF16), shape(half if h < cols_n - 1 else packed, BF16)],
             parts + list(gates[2 * h : 2 * h + 2]) + [mask, out_final, in_project] + earlier,
             scratch=[
                 pltpu.VMEM((rows * cols, chan), F32),
@@ -369,17 +380,16 @@
             flops=300_000_000,
         )
         firsts += [first, right]
-        lefts.append([left_mine, along_row(left_other, 1)])
-
-    core_right = along_row(right, 1)
+        arrived = along_row(left_other, 1)
+        lefts.append([left_mine, arrived] if h < cols_n - 1 else [left_mine])
 
     def partial_products(steps):
         used = lefts[steps[0][0] // pieces : steps[-1][0] // pieces + 1]
-        wait = [] if used[-1] is lefts[-1] else lefts[-1]
+        wait = []
         return call(
             functools.partial(after, functools.partial(incoming_kernel, steps), len(wait)),
             [shape((count, cols, chan), BF16 if m else F32) for m, _, count in steps],
-            wait + [right, core_right] + sum(used, []),
+            wait + [right, arrived] + sum(used, []),
             scratch=[
                 pltpu.VMEM((2 * len(used) * rows * pieces * rows, chan), F32),
                 pltpu.VMEM((2 * rows * cols, chan), F32),

time: 44.6 us -> 44.2 us (level)
  Pallas kernels: 12.2 us -> 11.7 us
    pallas_call x15, Pallas kernels: 12.2 us -> 11.7 us  [call(): pl.pallas_call(kernel, out_shape=outs, in_specs=[pl.BlockSpec(memory_spac...]
    ppermute x12 -> x11, waiting for transfers between devices: 9.35 us -> 9.66 us  [along_row(): return lax.ppermute(v, 'row', [(i, i ^ bits) for i in range(rows_n)])]
    ppermute x12 -> x11, starting transfers between devices: 15 us -> 15 us  [along_row(): return lax.ppermute(v, 'row', [(i, i ^ bits) for i in range(rows_n)])]
  transfers between devices with their start and end apart: 19 -> 18, of which waited for: 8 -> 7; matrix products, arithmetic and copies ran while one was open for 0% -> 0% of each run, Pallas kernels for 19% -> 18%
where the time goes in v10:
time: 44.2 us; the launch traced here: 44.1 us
  starting transfers between devices  20.7 us (47%)
  Pallas kernels  11.7 us (26%)
  waiting for transfers between devices  11.5 us (26%)
    ppermute x11, starting transfers between devices, along_row(): return lax.ppermute(v, 'row', [(i, i ^ bits) for i in range(rows_n)])  15 us
    pallas_call x15, Pallas kernels, call(): pl.pallas_call(kernel, out_shape=outs, in_specs=[pl.BlockSpec(memory_spac...  11.7 us
    ppermute x11, waiting for transfers between devices, along_row(): return lax.ppermute(v, 'row', [(i, i ^ bits) for i in range(rows_n)])  9.66 us
    ppermute x7, starting transfers between devices, shift(): return lax.ppermute(v, ('row', 'col'), pairs)  5.76 us
    ppermute x7, waiting for transfers between devices, shift(): return lax.ppermute(v, ('row', 'col'), pairs)  1.83 us
  transfers between devices with their start and end apart: 18, of which 7 were waited for; matrix products, arithmetic and copies ran while one was open for 0% of the time, Pallas kernels for 18%

profile of v10, /device:TPU:0, one launch (start us, length us, event | category | flops | bytes accessed | tf_op | source)
XLA Modules:
  0.0 44.1 jit_solution(5652179104745671241)
XLA Ops:
  0.0 1.5 %shard_map.82.refs_0_.refs_2_ = bf16[12,48,128]{2,1,0:T(8,128)(2,1)S(1)} custom-call(bf16[12,48,128]{2,1,0:T(8,128)(2,1)} %refs_1_.1, s32[1,96]{1,0:T(1,128)} %bitcast.1, bf16[128,512]{1,0:T(8,128)(2,1)} %refs_3_.1), custom_call_target="tpu_custom_call" | custom-call | flops 100000000 | bytes 426368 | tf_op jit(solution)/shard_map/pallas_call | solution.py:25
  1.5 4.1 %collective-permute-start.2 = (bf16[12,48,128]{2,1,0:T(8,128)(2,1)S(1)}, bf16[12,48,128]{2,1,0:T(8,128)(2,1)S(1)}, u32[]{:S(2)}, u32[]{:S(2)}) collective-permute-start(bf16[12,48,128]{2,1,0:T(8,128)(2,1)S(1)} %shard_map.82.refs_0_.refs_2_), channel_id=1, source_target_pairs={{0,8},{2,10},{4,12},{6,14},{8,0},{10,2},{12,4},{14,6},{1,9},{3,11}... | collective-permute-start | bytes 442376 | tf_op jit(solution)/shard_map/ppermute | solution.py:286
  5.6 1.6 %collective-permute-start.1 = (bf16[12,48,128]{2,1,0:T(8,128)(2,1)S(1)}, bf16[12,48,128]{2,1,0:T(8,128)(2,1)S(1)}, u32[]{:S(2)}, u32[]{:S(2)}) collective-permute-start(bf16[12,48,128]{2,1,0:T(8,128)(2,1)S(1)} %shard_map.82.refs_0_.refs_2_), channel_id=1, source_target_pairs={{0,4},{2,6},{4,0},{6,2},{8,12},{10,14},{12,8},{14,10},{1,5},{3,7},... | collective-permute-start | bytes 442376 | tf_op jit(solution)/shard_map/ppermute | solution.py:286
  7.7 1.6 %collective-permute-start.8 = (bf16[12,48,128]{2,1,0:T(8,128)(2,1)S(1)}, bf16[12,48,128]{2,1,0:T(8,128)(2,1)S(1)}, u32[]{:S(2)}, u32[]{:S(2)}) collective-permute-start(bf16[12,48,128]{2,1,0:T(8,128)(2,1)S(1)} %get-tuple-element.40.refs_0_), channel_id=1, source_target_pairs={{0,1},{1,0},{2,3},{3,2},{4,5},{5,4},{6,7},{7,6},{8,9},{9,8},{10,11... | collective-permute-start | bytes 442376 | tf_op jit(solution)/shard_map/ppermute | solution.py:294
  9.3 3.4 %collective-permute-done.2.refs_4_ = bf16[12,48,128]{2,1,0:T(8,128)(2,1)S(1)} collective-permute-done((bf16[12,48,128]{2,1,0:T(8,128)(2,1)S(1)}, bf16[12,48,128]{2,1,0:T(8,128)(2,1)S(1)}, u32[]{:S(2)}, u32[]{:S(2)}) %collective-permute-start.2) | collective-permute-done | bytes 147488 | tf_op jit(solution)/shard_map/ppermute | solution.py:286
  12.7 0.6 %collective-permute-start.6 = (bf16[12,48,128]{2,1,0:T(8,128)(2,1)S(1)}, bf16[12,48,128]{2,1,0:T(8,128)(2,1)S(1)}, u32[]{:S(2)}, u32[]{:S(2)}) collective-permute-start(bf16[12,48,128]{2,1,0:T(8,128)(2,1)S(1)} %collective-permute-done.2.refs_4_), channel_id=1, source_target_pairs={{0,4},{2,6},{4,0},{6,2},{8,12},{10,14},{12,8},{14,10},{1,5},{3,7},... | collective-permute-start | bytes 442376 | tf_op jit(solution)/shard_map/ppermute | solution.py:286
  13.3 1.1 %shard_map.84 = (bf16[288,128]{1,0:T(8,128)(2,1)S(1)}, bf16[288,128]{1,0:T(8,128)(2,1)S(1)}) custom-call(bf16[12,48,128]{2,1,0:T(8,128)(2,1)S(1)} %get-tuple-element.32.refs_0_.refs_2_, bf16[12,48,128]{2,1,0:T(8,128)(2,1)S(1)} %collective-permute-done.refs_1_.refs_3_.refs_0_, bf16[12,48,128]{2,1,0:T(8,128)(2,1)S(1)} %shard_map.82.refs_0_.refs_2_, ...), custom_call_target="tpu_custom_call" | custom-call | flops 500000000 | bytes 737280 | tf_op jit(solution)/shard_map/pallas_call | solution.py:25
  14.5 0.8 %shard_map.85 = (bf16[432,128]{1,0:T(8,128)(2,1)S(1)}, bf16[432,128]{1,0:T(8,128)(2,1)S(1)}) custom-call(bf16[288,128]{1,0:T(8,128)(2,1)S(1)} %get-tuple-element.33.refs_0_, bf16[288,128]{1,0:T(8,128)(2,1)S(1)} %get-tuple-element.34.refs_1_, bf16[12,48,128]{2,1,0:T(8,128)(2,1)S(1)} %get-tuple-element.32.refs_0_.refs_2_, ...), custom_call_target="tpu_custom_call" | custom-call | flops 250000000 | bytes 811008 | tf_op jit(solution)/shard_map/pallas_call | solution.py:25
  15.3 0.9 %collective-permute-start.5 = (bf16[432,128]{1,0:T(8,128)(2,1)S(1)}, bf16[432,128]{1,0:T(8,128)(2,1)S(1)}, u32[]{:S(2)}, u32[]{:S(2)}) collective-permute-start(bf16[432,128]{1,0:T(8,128)(2,1)S(1)} %get-tuple-element.36), channel_id=1, source_target_pairs={{0,3},{1,2},{2,1},{3,0},{4,7},{5,6},{6,5},{7,4},{8,11},{9,10},{10,... | collective-permute-start | bytes 331784 | tf_op jit(solution)/shard_map/ppermute | solution.py:294
  16.2 0.8 %collective-permute-start.4 = (bf16[432,128]{1,0:T(8,128)(2,1)S(1)}, bf16[432,128]{1,0:T(8,128)(2,1)S(1)}, u32[]{:S(2)}, u32[]{:S(2)}) collective-permute-start(bf16[432,128]{1,0:T(8,128)(2,1)S(1)} %get-tuple-element.36), channel_id=1, source_target_pairs={{0,2},{1,3},{2,0},{3,1},{4,6},{5,7},{6,4},{7,5},{8,10},{9,11},{10,... | collective-permute-start | bytes 331784 | tf_op jit(solution)/shard_map/ppermute | solution.py:294
  19.4 1.1 %collective-permute-start.7 = (bf16[144,128]{1,0:T(8,128)(2,1)S(1)}, bf16[144,128]{1,0:T(8,128)(2,1)S(1)}, u32[]{:S(2)}, u32[]{:S(2)}) collective-permute-start(bf16[144,128]{1,0:T(8,128)(2,1)S(1)} %shard_map.86.refs_4_), channel_id=1, source_target_pairs={{0,1},{1,0},{2,3},{3,2},{4,5},{5,4},{6,7},{7,6},{8,9},{9,8},{10,11... | collective-permute-start | bytes 110600 | tf_op jit(solution)/shard_map/ppermute | solution.py:294
  20.6 0.9 %shard_map.88 = (bf16[12,48,128]{2,1,0:T(8,128)(2,1)S(1)}, f32[12,48,128]{2,1,0:T(8,128)S(1)}, bf16[12,48,128]{2,1,0:T(8,128)(2,1)S(1)}, f32[12,48,128]{2,1,0:T(8,128)S(1)}) custom-call(bf16[12,48,128]{2,1,0:T(8,128)(2,1)S(1)} %get-tuple-element.40.refs_0_, bf16[12,48,128]{2,1,0:T(8,128)(2,1)S(1)} %collective-permute-done.8.refs_1_, ...), custom_call_target="tpu_custom_call" | custom-call | flops 100000000 | bytes 1212416 | tf_op jit(solution)/shard_map/pallas_call | solution.py:25
  21.7 1.4 %collective-permute-done.3.refs_1_ = bf16[432,128]{1,0:T(8,128)(2,1)S(1)} collective-permute-done((bf16[432,128]{1,0:T(8,128)(2,1)S(1)}, bf16[432,128]{1,0:T(8,128)(2,1)S(1)}, u32[]{:S(2)}, u32[]{:S(2)}) %collective-permute-start.3) | collective-permute-done | bytes 110624 | tf_op jit(solution)/shard_map/ppermute | solution.py:294
  23.1 1.1 %shard_map.89 = (bf16[12,48,128]{2,1,0:T(8,128)(2,1)S(1)}, bf16[12,48,128]{2,1,0:T(8,128)(2,1)S(1)}, bf16[12,24,128]{2,1,0:T(8,128)(2,1)S(1)}, bf16[12,24,128]{2,1,0:T(8,128)(2,1)S(1)}) custom-call(bf16[432,128]{1,0:T(8,128)(2,1)S(1)} %get-tuple-element.35.refs_0_, bf16[432,128]{1,0:T(8,128)(2,1)S(1)} %collective-permute-done.3.refs_1_, ...), custom_call_target="tpu_custom_call" | custom-call | flops 300000000 | bytes 1491328 | tf_op jit(solution)/shard_map/pallas_call | solution.py:25
  24.7 1.1 %shard_map.90 = (bf16[12,48,128]{2,1,0:T(8,128)(2,1)S(1)}, bf16[12,48,128]{2,1,0:T(8,128)(2,1)S(1)}, bf16[12,24,128]{2,1,0:T(8,128)(2,1)S(1)}, bf16[18,48,128]{2,1,0:T(8,128)(2,1)S(1)}) custom-call(bf16[432,128]{1,0:T(8,128)(2,1)S(1)} %get-tuple-element.35.refs_0_, bf16[432,128]{1,0:T(8,128)(2,1)S(1)} %collective-permute-done.3.refs_1_, ...), custom_call_target="tpu_custom_call" | custom-call | flops 300000000 | bytes 2081152 | tf_op jit(solution)/shard_map/pallas_call | solution.py:25
  26.4 1.0 %collective-permute-done.11.refs_1_ = bf16[18,48,128]{2,1,0:T(8,128)(2,1)S(1)} collective-permute-done((bf16[18,48,128]{2,1,0:T(8,128)(2,1)S(1)}, bf16[18,48,128]{2,1,0:T(8,128)(2,1)S(1)}, u32[]{:S(2)}, u32[]{:S(2)}) %collective-permute-start.11) | collective-permute-done | bytes 221216 | tf_op jit(solution)/shard_map/ppermute | solution.py:286
  27.7 1.5 %collective-permute-start.16 = (bf16[6,48,128]{2,1,0:T(8,128)(2,1)S(1)}, bf16[6,48,128]{2,1,0:T(8,128)(2,1)S(1)}, u32[]{:S(2)}, u32[]{:S(2)}) collective-permute-start(bf16[6,48,128]{2,1,0:T(8,128)(2,1)S(1)} %shard_map.94), channel_id=1, source_target_pairs={{0,4},{2,6},{4,0},{6,2},{8,12},{10,14},{12,8},{14,10},{1,5},{3,7},... | collective-permute-start | bytes 221192 | tf_op jit(solution)/shard_map/ppermute | solution.py:286
  29.2 0.8 %shard_map.93 = (bf16[6,48,128]{2,1,0:T(8,128)(2,1)S(1)}, bf16[6,48,128]{2,1,0:T(8,128)(2,1)S(1)}, bf16[6,48,128]{2,1,0:T(8,128)(2,1)S(1)}) custom-call(bf16[12,48,128]{2,1,0:T(8,128)(2,1)S(1)} %get-tuple-element.50.refs_0_, bf16[18,48,128]{2,1,0:T(8,128)(2,1)S(1)} %collective-permute-done.11.refs_1_, bf16[12,24,128]{2,1,0:T(8,128)(2,1)S(1)} %get-tuple-element.54.refs_2_), custom_call_target="tpu_custom_call" | custom-call | flops 360000000 | bytes 663552 | tf_op jit(solution)/shard_map/pallas_call | solution.py:25
  30.0 2.0 %collective-permute-start.14 = (bf16[6,48,128]{2,1,0:T(8,128)(2,1)S(1)}, bf16[6,48,128]{2,1,0:T(8,128)(2,1)S(1)}, u32[]{:S(2)}, u32[]{:S(2)}) collective-permute-start(bf16[6,48,128]{2,1,0:T(8,128)(2,1)S(1)} %get-tuple-element.55), channel_id=1, source_target_pairs={{0,8},{2,10},{4,12},{6,14},{8,0},{10,2},{12,4},{14,6},{1,9},{3,11}... | collective-permute-start | bytes 221192 | tf_op jit(solution)/shard_map/ppermute | solution.py:286
  32.0 1.5 %collective-permute-start.15 = (bf16[6,48,128]{2,1,0:T(8,128)(2,1)S(1)}, bf16[6,48,128]{2,1,0:T(8,128)(2,1)S(1)}, u32[]{:S(2)}, u32[]{:S(2)}) collective-permute-start(bf16[6,48,128]{2,1,0:T(8,128)(2,1)S(1)} %get-tuple-element.56), channel_id=1, source_target_pairs={{0,12},{2,14},{4,8},{6,10},{8,4},{10,6},{12,0},{14,2},{1,13},{3,15... | collective-permute-start | bytes 221192 | tf_op jit(solution)/shard_map/ppermute | solution.py:286
  34.7 2.4 %collective-permute-start.17 = (bf16[6,48,128]{2,1,0:T(8,128)(2,1)S(1)}, bf16[6,48,128]{2,1,0:T(8,128)(2,1)S(1)}, u32[]{:S(2)}, u32[]{:S(2)}) collective-permute-start(bf16[6,48,128]{2,1,0:T(8,128)(2,1)S(1)} %add_convert_fusion), channel_id=1, source_target_pairs={{0,8},{2,10},{4,12},{6,14},{8,0},{10,2},{12,4},{14,6},{1,9},{3,11}... | collective-permute-start | bytes 221192 | tf_op jit(solution)/shard_map/ppermute | solution.py:286
  38.1 0.8 %collective-permute-done.15.refs_3_ = bf16[6,48,128]{2,1,0:T(8,128)(2,1)S(1)} collective-permute-done((bf16[6,48,128]{2,1,0:T(8,128)(2,1)S(1)}, bf16[6,48,128]{2,1,0:T(8,128)(2,1)S(1)}, u32[]{:S(2)}, u32[]{:S(2)}) %collective-permute-start.15) | collective-permute-done | bytes 73760 | tf_op jit(solution)/shard_map/ppermute | solution.py:286
  38.9 4.1 %collective-permute-done.17.refs_4_ = bf16[6,48,128]{2,1,0:T(8,128)(2,1)S(1)} collective-permute-done((bf16[6,48,128]{2,1,0:T(8,128)(2,1)S(1)}, bf16[6,48,128]{2,1,0:T(8,128)(2,1)S(1)}, u32[]{:S(2)}, u32[]{:S(2)}) %collective-permute-start.17) | collective-permute-done | bytes 73760 | tf_op jit(solution)/shard_map/ppermute | solution.py:286
  43.1 1.0 %shard_map.96 = bf16[12,48,128]{2,1,0:T(8,128)(2,1)} custom-call(f32[12,48,128]{2,1,0:T(8,128)S(1)} %shard_map.91.refs_0_, bf16[12,48,128]{2,1,0:T(8,128)(2,1)S(1)} %collective-permute-done.13.refs_1_, bf16[6,48,128]{2,1,0:T(8,128)(2,1)S(1)} %collective-permute-done.14.refs_2_, bf16[6,48,128]{2,1,0:T(8,128)(2,1)S(1)} %collective-permute-done.15.refs_3_, ...), custom_call_target="tpu_custom_call" | custom-call | flops 100000000 | bytes 1286144 | tf_op jit(solution)/shard_map/pallas_call | solution.py:25
  (44 shorter events, 6.7 us)
Async XLA Ops:
  0.0 7.2 %copy-start = (bf16[12,48,128]{2,1,0:T(8,128)(2,1)S(1)}, bf16[12,48,128]{2,1,0:T(8,128)(2,1)}, u32[]{:S(2)}) copy-start(bf16[12,48,128]{2,1,0:T(8,128)(2,1)} %refs_1_.1) | copy-start | bytes 442372
  0.0 7.2 %copy-start.1 = (bf16[128,512]{1,0:T(8,128)(2,1)S(1)}, bf16[128,512]{1,0:T(8,128)(2,1)}, u32[]{:S(2)}) copy-start(bf16[128,512]{1,0:T(8,128)(2,1)} %refs_3_.1) | copy-start | bytes 393220
  0.0 7.2 %copy-start.6 = (s32[96]{0:T(128)S(1)}, s32[96]{0:T(128)}, u32[]{:S(2)}) copy-start(s32[96]{0:T(128)} %param.9) | copy-start | bytes 1156
  1.5 11.2 %collective-permute-start.2 = (bf16[12,48,128]{2,1,0:T(8,128)(2,1)S(1)}, bf16[12,48,128]{2,1,0:T(8,128)(2,1)S(1)}, u32[]{:S(2)}, u32[]{:S(2)}) collective-permute-start(bf16[12,48,128]{2,1,0:T(8,128)(2,1)S(1)} %shard_map.82.refs_0_.refs_2_), channel_id=1, source_target_pairs={{0,8},{2,10},{4,12},{6,14},{8,0},{10,2},{12,4},{14,6},{1,9},{3,11}... | collective-permute-start | bytes 442376 | tf_op jit(solution)/shard_map/ppermute | solution.py:286
  5.6 7.7 %collective-permute-start.1 = (bf16[12,48,128]{2,1,0:T(8,128)(2,1)S(1)}, bf16[12,48,128]{2,1,0:T(8,128)(2,1)S(1)}, u32[]{:S(2)}, u32[]{:S(2)}) collective-permute-start(bf16[12,48,128]{2,1,0:T(8,128)(2,1)S(1)} %shard_map.82.refs_0_.refs_2_), channel_id=1, source_target_pairs={{0,4},{2,6},{4,0},{6,2},{8,12},{10,14},{12,8},{14,10},{1,5},{3,7},... | collective-permute-start | bytes 442376 | tf_op jit(solution)/shard_map/ppermute | solution.py:286
  7.6 5.7 %collective-permute-start = (bf16[12,48,128]{2,1,0:T(8,128)(2,1)S(1)}, bf16[12,48,128]{2,1,0:T(8,128)(2,1)S(1)}, u32[]{:S(2)}, u32[]{:S(2)}) collective-permute-start(bf16[12,48,128]{2,1,0:T(8,128)(2,1)S(1)} %get-tuple-element.32.refs_0_.refs_2_), channel_id=1, source_target_pairs={{0,2},{2,0},{4,6},{6,4},{8,10},{10,8},{12,14},{14,12},{1,3},{3,1},... | collective-permute-start | bytes 442376 | tf_op jit(solution)/shard_map/ppermute | solution.py:286
  7.7 11.7 %collective-permute-start.8 = (bf16[12,48,128]{2,1,0:T(8,128)(2,1)S(1)}, bf16[12,48,128]{2,1,0:T(8,128)(2,1)S(1)}, u32[]{:S(2)}, u32[]{:S(2)}) collective-permute-start(bf16[12,48,128]{2,1,0:T(8,128)(2,1)S(1)} %get-tuple-element.40.refs_0_), channel_id=1, source_target_pairs={{0,1},{1,0},{2,3},{3,2},{4,5},{5,4},{6,7},{7,6},{8,9},{9,8},{10,11... | collective-permute-start | bytes 442376 | tf_op jit(solution)/shard_map/ppermute | solution.py:294
  12.7 5.1 %collective-permute-start.6 = (bf16[12,48,128]{2,1,0:T(8,128)(2,1)S(1)}, bf16[12,48,128]{2,1,0:T(8,128)(2,1)S(1)}, u32[]{:S(2)}, u32[]{:S(2)}) collective-permute-start(bf16[12,48,128]{2,1,0:T(8,128)(2,1)S(1)} %collective-permute-done.2.refs_4_), channel_id=1, source_target_pairs={{0,4},{2,6},{4,0},{6,2},{8,12},{10,14},{12,8},{14,10},{1,5},{3,7},... | collective-permute-start | bytes 442376 | tf_op jit(solution)/shard_map/ppermute | solution.py:286
  15.3 6.1 %collective-permute-start.5 = (bf16[432,128]{1,0:T(8,128)(2,1)S(1)}, bf16[432,128]{1,0:T(8,128)(2,1)S(1)}, u32[]{:S(2)}, u32[]{:S(2)}) collective-permute-start(bf16[432,128]{1,0:T(8,128)(2,1)S(1)} %get-tuple-element.36), channel_id=1, source_target_pairs={{0,3},{1,2},{2,1},{3,0},{4,7},{5,6},{6,5},{7,4},{8,11},{9,10},{10,... | collective-permute-start | bytes 331784 | tf_op jit(solution)/shard_map/ppermute | solution.py:294
  16.2 5.5 %collective-permute-start.4 = (bf16[432,128]{1,0:T(8,128)(2,1)S(1)}, bf16[432,128]{1,0:T(8,128)(2,1)S(1)}, u32[]{:S(2)}, u32[]{:S(2)}) collective-permute-start(bf16[432,128]{1,0:T(8,128)(2,1)S(1)} %get-tuple-element.36), channel_id=1, source_target_pairs={{0,2},{1,3},{2,0},{3,1},{4,6},{5,7},{6,4},{7,5},{8,10},{9,11},{10,... | collective-permute-start | bytes 331784 | tf_op jit(solution)/shard_map/ppermute | solution.py:294
  17.0 6.2 %collective-permute-start.3 = (bf16[432,128]{1,0:T(8,128)(2,1)S(1)}, bf16[432,128]{1,0:T(8,128)(2,1)S(1)}, u32[]{:S(2)}, u32[]{:S(2)}) collective-permute-start(bf16[432,128]{1,0:T(8,128)(2,1)S(1)} %get-tuple-element.35.refs_0_), channel_id=1, source_target_pairs={{0,1},{1,0},{2,3},{3,2},{4,5},{5,4},{6,7},{7,6},{8,9},{9,8},{10,11... | collective-permute-start | bytes 331784 | tf_op jit(solution)/shard_map/ppermute | solution.py:294
  18.8 4.3 %copy-start.2 = (bf16[128,512]{1,0:T(8,128)(2,1)S(1)}, bf16[128,512]{1,0:T(8,128)(2,1)}, u32[]{:S(2)}) copy-start(bf16[128,512]{1,0:T(8,128)(2,1)} %refs_12_.1) | copy-start | bytes 393220
  18.8 4.3 %copy-start.3 = (bf16[128,128]{1,0:T(8,128)(2,1)S(1)}, bf16[128,128]{1,0:T(8,128)(2,1)}, u32[]{:S(2)}) copy-start(bf16[128,128]{1,0:T(8,128)(2,1)} %refs_11_.1) | copy-start | bytes 98308
  18.9 5.4 %collective-permute-start.10 = (bf16[144,128]{1,0:T(8,128)(2,1)S(1)}, bf16[144,128]{1,0:T(8,128)(2,1)S(1)}, u32[]{:S(2)}, u32[]{:S(2)}) collective-permute-start(bf16[144,128]{1,0:T(8,128)(2,1)S(1)} %shard_map.87), channel_id=1, source_target_pairs={{0,3},{1,2},{2,1},{3,0},{4,7},{5,6},{6,5},{7,4},{8,11},{9,10},{10,... | collective-permute-start | bytes 110600 | tf_op jit(solution)/shard_map/ppermute | solution.py:294
  19.4 5.3 %collective-permute-start.7 = (bf16[144,128]{1,0:T(8,128)(2,1)S(1)}, bf16[144,128]{1,0:T(8,128)(2,1)S(1)}, u32[]{:S(2)}, u32[]{:S(2)}) collective-permute-start(bf16[144,128]{1,0:T(8,128)(2,1)S(1)} %shard_map.86.refs_4_), channel_id=1, source_target_pairs={{0,1},{1,0},{2,3},{3,2},{4,5},{5,4},{6,7},{7,6},{8,9},{9,8},{10,11... | collective-permute-start | bytes 110600 | tf_op jit(solution)/shard_map/ppermute | solution.py:294
  21.4 3.3 %collective-permute-start.9 = (bf16[144,128]{1,0:T(8,128)(2,1)S(1)}, bf16[144,128]{1,0:T(8,128)(2,1)S(1)}, u32[]{:S(2)}, u32[]{:S(2)}) collective-permute-start(bf16[144,128]{1,0:T(8,128)(2,1)S(1)} %shard_map.87), channel_id=1, source_target_pairs={{0,2},{1,3},{2,0},{3,1},{4,6},{5,7},{6,4},{7,5},{8,10},{9,11},{10,... | collective-permute-start | bytes 110600 | tf_op jit(solution)/shard_map/ppermute | solution.py:294
  25.8 1.5 %collective-permute-start.11 = (bf16[18,48,128]{2,1,0:T(8,128)(2,1)S(1)}, bf16[18,48,128]{2,1,0:T(8,128)(2,1)S(1)}, u32[]{:S(2)}, u32[]{:S(2)}) collective-permute-start(bf16[18,48,128]{2,1,0:T(8,128)(2,1)S(1)} %get-tuple-element.51), channel_id=1, source_target_pairs={{0,2},{2,0},{4,6},{6,4},{8,10},{10,8},{12,14},{14,12},{1,3},{3,1},... | collective-permute-start | bytes 663560 | tf_op jit(solution)/shard_map/ppermute | solution.py:286
  26.0 7.6 %collective-permute-start.12 = (bf16[12,24,128]{2,1,0:T(8,128)(2,1)S(1)}, bf16[12,24,128]{2,1,0:T(8,128)(2,1)S(1)}, u32[]{:S(2)}, u32[]{:S(2)}) collective-permute-start(bf16[12,24,128]{2,1,0:T(8,128)(2,1)S(1)} %get-tuple-element.53), channel_id=1, source_target_pairs={{0,2},{2,0},{4,6},{6,4},{8,10},{10,8},{12,14},{14,12},{1,3},{3,1},... | collective-permute-start | bytes 221192 | tf_op jit(solution)/shard_map/ppermute | solution.py:286
  27.7 7.0 %collective-permute-start.16 = (bf16[6,48,128]{2,1,0:T(8,128)(2,1)S(1)}, bf16[6,48,128]{2,1,0:T(8,128)(2,1)S(1)}, u32[]{:S(2)}, u32[]{:S(2)}) collective-permute-start(bf16[6,48,128]{2,1,0:T(8,128)(2,1)S(1)} %shard_map.94), channel_id=1, source_target_pairs={{0,4},{2,6},{4,0},{6,2},{8,12},{10,14},{12,8},{14,10},{1,5},{3,7},... | collective-permute-start | bytes 221192 | tf_op jit(solution)/shard_map/ppermute | solution.py:286
  30.0 8.1 %collective-permute-start.14 = (bf16[6,48,128]{2,1,0:T(8,128)(2,1)S(1)}, bf16[6,48,128]{2,1,0:T(8,128)(2,1)S(1)}, u32[]{:S(2)}, u32[]{:S(2)}) collective-permute-start(bf16[6,48,128]{2,1,0:T(8,128)(2,1)S(1)} %get-tuple-element.55), channel_id=1, source_target_pairs={{0,8},{2,10},{4,12},{6,14},{8,0},{10,2},{12,4},{14,6},{1,9},{3,11}... | collective-permute-start | bytes 221192 | tf_op jit(solution)/shard_map/ppermute | solution.py:286
  32.0 6.9 %collective-permute-start.15 = (bf16[6,48,128]{2,1,0:T(8,128)(2,1)S(1)}, bf16[6,48,128]{2,1,0:T(8,128)(2,1)S(1)}, u32[]{:S(2)}, u32[]{:S(2)}) collective-permute-start(bf16[6,48,128]{2,1,0:T(8,128)(2,1)S(1)} %get-tuple-element.56), channel_id=1, source_target_pairs={{0,12},{2,14},{4,8},{6,10},{8,4},{10,6},{12,0},{14,2},{1,13},{3,15... | collective-permute-start | bytes 221192 | tf_op jit(solution)/shard_map/ppermute | solution.py:286
  34.1 8.9 %collective-permute-start.13 = (bf16[12,48,128]{2,1,0:T(8,128)(2,1)S(1)}, bf16[12,48,128]{2,1,0:T(8,128)(2,1)S(1)}, u32[]{:S(2)}, u32[]{:S(2)}) collective-permute-start(bf16[12,48,128]{2,1,0:T(8,128)(2,1)S(1)} %shard_map.92), channel_id=1, source_target_pairs={{0,4},{2,6},{4,0},{6,2},{8,12},{10,14},{12,8},{14,10},{1,5},{3,7},... | collective-permute-start | bytes 442376 | tf_op jit(solution)/shard_map/ppermute | solution.py:286
  34.7 8.3 %collective-permute-start.17 = (bf16[6,48,128]{2,1,0:T(8,128)(2,1)S(1)}, bf16[6,48,128]{2,1,0:T(8,128)(2,1)S(1)}, u32[]{:S(2)}, u32[]{:S(2)}) collective-permute-start(bf16[6,48,128]{2,1,0:T(8,128)(2,1)S(1)} %add_convert_fusion), channel_id=1, source_target_pairs={{0,8},{2,10},{4,12},{6,14},{8,0},{10,2},{12,4},{14,6},{1,9},{3,11}... | collective-permute-start | bytes 221192 | tf_op jit(solution)/shard_map/ppermute | solution.py:286
  37.5 5.5 %copy-start.4 = (bf16[128,128]{1,0:T(8,128)(2,1)S(1)}, bf16[128,128]{1,0:T(8,128)(2,1)}, u32[]{:S(2)}) copy-start(bf16[128,128]{1,0:T(8,128)(2,1)} %refs_7_.3) | copy-start | bytes 98308
  (2 other events, 4.7 us)

commit v11 on v10

--- a/solution.py
+++ b/solution.py
@@ -242,7 +242,7 @@
                 )
 
             zero = jnp.zeros((cols, chan), F32)
-            totals = lax.fori_loop(0, 2 * rows, step, (zero,) * min(6, count - group), unroll=12)
+            totals = lax.fori_loop(0, 2 * rows, step, (zero,) * min(6, count - group), unroll=24)
             for i, t in enumerate(totals):
                 out_ref[group + i] = t.astype(out_ref.dtype)
 

time: 44.2 us -> 44.1 us (level)
  no operation moved by 1% of the time
where the time goes in v11:
time: 44.1 us; the launch traced here: 44 us
  starting transfers between devices  20.7 us (47%)
  waiting for transfers between devices  11.6 us (26%)
  Pallas kernels  11.4 us (26%)
    ppermute x11, starting transfers between devices, along_row(): return lax.ppermute(v, 'row', [(i, i ^ bits) for i in range(rows_n)])  15 us
    pallas_call x15, Pallas kernels, call(): pl.pallas_call(kernel, out_shape=outs, in_specs=[pl.BlockSpec(memory_spac...  11.4 us
    ppermute x11, waiting for transfers between devices, along_row(): return lax.ppermute(v, 'row', [(i, i ^ bits) for i in range(rows_n)])  9.76 us
    ppermute x7, starting transfers between devices, shift(): return lax.ppermute(v, ('row', 'col'), pairs)  5.76 us
    ppermute x7, waiting for transfers between devices, shift(): return lax.ppermute(v, ('row', 'col'), pairs)  1.83 us
  transfers between devices with their start and end apart: 18, of which 7 were waited for; matrix products, arithmetic and copies ran while one was open for 0% of the time, Pallas kernels for 18%

profile of v11, /device:TPU:0, one launch (start us, length us, event | category | flops | bytes accessed | tf_op | source)
XLA Modules:
  0.0 44.0 jit_solution(3938197057706422108)
XLA Ops:
  0.0 1.5 %shard_map.82.refs_0_.refs_2_ = bf16[12,48,128]{2,1,0:T(8,128)(2,1)S(1)} custom-call(bf16[12,48,128]{2,1,0:T(8,128)(2,1)} %refs_1_.1, s32[1,96]{1,0:T(1,128)} %bitcast.1, bf16[128,512]{1,0:T(8,128)(2,1)} %refs_3_.1), custom_call_target="tpu_custom_call" | custom-call | flops 100000000 | bytes 426368 | tf_op jit(solution)/shard_map/pallas_call | solution.py:25
  1.5 4.1 %collective-permute-start.2 = (bf16[12,48,128]{2,1,0:T(8,128)(2,1)S(1)}, bf16[12,48,128]{2,1,0:T(8,128)(2,1)S(1)}, u32[]{:S(2)}, u32[]{:S(2)}) collective-permute-start(bf16[12,48,128]{2,1,0:T(8,128)(2,1)S(1)} %shard_map.82.refs_0_.refs_2_), channel_id=1, source_target_pairs={{0,8},{2,10},{4,12},{6,14},{8,0},{10,2},{12,4},{14,6},{1,9},{3,11}... | collective-permute-start | bytes 442376 | tf_op jit(solution)/shard_map/ppermute | solution.py:286
  5.6 1.6 %collective-permute-start.1 = (bf16[12,48,128]{2,1,0:T(8,128)(2,1)S(1)}, bf16[12,48,128]{2,1,0:T(8,128)(2,1)S(1)}, u32[]{:S(2)}, u32[]{:S(2)}) collective-permute-start(bf16[12,48,128]{2,1,0:T(8,128)(2,1)S(1)} %shard_map.82.refs_0_.refs_2_), channel_id=1, source_target_pairs={{0,4},{2,6},{4,0},{6,2},{8,12},{10,14},{12,8},{14,10},{1,5},{3,7},... | collective-permute-start | bytes 442376 | tf_op jit(solution)/shard_map/ppermute | solution.py:286
  7.7 1.6 %collective-permute-start.8 = (bf16[12,48,128]{2,1,0:T(8,128)(2,1)S(1)}, bf16[12,48,128]{2,1,0:T(8,128)(2,1)S(1)}, u32[]{:S(2)}, u32[]{:S(2)}) collective-permute-start(bf16[12,48,128]{2,1,0:T(8,128)(2,1)S(1)} %get-tuple-element.40.refs_0_), channel_id=1, source_target_pairs={{0,1},{1,0},{2,3},{3,2},{4,5},{5,4},{6,7},{7,6},{8,9},{9,8},{10,11... | collective-permute-start | bytes 442376 | tf_op jit(solution)/shard_map/ppermute | solution.py:294
  9.3 3.4 %collective-permute-done.2.refs_4_ = bf16[12,48,128]{2,1,0:T(8,128)(2,1)S(1)} collective-permute-done((bf16[12,48,128]{2,1,0:T(8,128)(2,1)S(1)}, bf16[12,48,128]{2,1,0:T(8,128)(2,1)S(1)}, u32[]{:S(2)}, u32[]{:S(2)}) %collective-permute-start.2) | collective-permute-done | bytes 147488 | tf_op jit(solution)/shard_map/ppermute | solution.py:286
  12.7 0.6 %collective-permute-start.6 = (bf16[12,48,128]{2,1,0:T(8,128)(2,1)S(1)}, bf16[12,48,128]{2,1,0:T(8,128)(2,1)S(1)}, u32[]{:S(2)}, u32[]{:S(2)}) collective-permute-start(bf16[12,48,128]{2,1,0:T(8,128)(2,1)S(1)} %collective-permute-done.2.refs_4_), channel_id=1, source_target_pairs={{0,4},{2,6},{4,0},{6,2},{8,12},{10,14},{12,8},{14,10},{1,5},{3,7},... | collective-permute-start | bytes 442376 | tf_op jit(solution)/shard_map/ppermute | solution.py:286
  13.3 1.1 %shard_map.84 = (bf16[288,128]{1,0:T(8,128)(2,1)S(1)}, bf16[288,128]{1,0:T(8,128)(2,1)S(1)}) custom-call(bf16[12,48,128]{2,1,0:T(8,128)(2,1)S(1)} %get-tuple-element.32.refs_0_.refs_2_, bf16[12,48,128]{2,1,0:T(8,128)(2,1)S(1)} %collective-permute-done.refs_1_.refs_3_.refs_0_, bf16[12,48,128]{2,1,0:T(8,128)(2,1)S(1)} %shard_map.82.refs_0_.refs_2_, ...), custom_call_target="tpu_custom_call" | custom-call | flops 500000000 | bytes 737280 | tf_op jit(solution)/shard_map/pallas_call | solution.py:25
  14.5 0.8 %shard_map.85 = (bf16[432,128]{1,0:T(8,128)(2,1)S(1)}, bf16[432,128]{1,0:T(8,128)(2,1)S(1)}) custom-call(bf16[288,128]{1,0:T(8,128)(2,1)S(1)} %get-tuple-element.33.refs_0_, bf16[288,128]{1,0:T(8,128)(2,1)S(1)} %get-tuple-element.34.refs_1_, bf16[12,48,128]{2,1,0:T(8,128)(2,1)S(1)} %get-tuple-element.32.refs_0_.refs_2_, ...), custom_call_target="tpu_custom_call" | custom-call | flops 250000000 | bytes 811008 | tf_op jit(solution)/shard_map/pallas_call | solution.py:25
  15.3 0.9 %collective-permute-start.5 = (bf16[432,128]{1,0:T(8,128)(2,1)S(1)}, bf16[432,128]{1,0:T(8,128)(2,1)S(1)}, u32[]{:S(2)}, u32[]{:S(2)}) collective-permute-start(bf16[432,128]{1,0:T(8,128)(2,1)S(1)} %get-tuple-element.36), channel_id=1, source_target_pairs={{0,3},{1,2},{2,1},{3,0},{4,7},{5,6},{6,5},{7,4},{8,11},{9,10},{10,... | collective-permute-start | bytes 331784 | tf_op jit(solution)/shard_map/ppermute | solution.py:294
  16.2 0.8 %collective-permute-start.4 = (bf16[432,128]{1,0:T(8,128)(2,1)S(1)}, bf16[432,128]{1,0:T(8,128)(2,1)S(1)}, u32[]{:S(2)}, u32[]{:S(2)}) collective-permute-start(bf16[432,128]{1,0:T(8,128)(2,1)S(1)} %get-tuple-element.36), channel_id=1, source_target_pairs={{0,2},{1,3},{2,0},{3,1},{4,6},{5,7},{6,4},{7,5},{8,10},{9,11},{10,... | collective-permute-start | bytes 331784 | tf_op jit(solution)/shard_map/ppermute | solution.py:294
  19.4 1.1 %collective-permute-start.7 = (bf16[144,128]{1,0:T(8,128)(2,1)S(1)}, bf16[144,128]{1,0:T(8,128)(2,1)S(1)}, u32[]{:S(2)}, u32[]{:S(2)}) collective-permute-start(bf16[144,128]{1,0:T(8,128)(2,1)S(1)} %shard_map.86.refs_4_), channel_id=1, source_target_pairs={{0,1},{1,0},{2,3},{3,2},{4,5},{5,4},{6,7},{7,6},{8,9},{9,8},{10,11... | collective-permute-start | bytes 110600 | tf_op jit(solution)/shard_map/ppermute | solution.py:294
  20.6 0.9 %shard_map.88 = (bf16[12,48,128]{2,1,0:T(8,128)(2,1)S(1)}, f32[12,48,128]{2,1,0:T(8,128)S(1)}, bf16[12,48,128]{2,1,0:T(8,128)(2,1)S(1)}, f32[12,48,128]{2,1,0:T(8,128)S(1)}) custom-call(bf16[12,48,128]{2,1,0:T(8,128)(2,1)S(1)} %get-tuple-element.40.refs_0_, bf16[12,48,128]{2,1,0:T(8,128)(2,1)S(1)} %collective-permute-done.8.refs_1_, ...), custom_call_target="tpu_custom_call" | custom-call | flops 100000000 | bytes 1212416 | tf_op jit(solution)/shard_map/pallas_call | solution.py:25
  21.7 1.4 %collective-permute-done.3.refs_1_ = bf16[432,128]{1,0:T(8,128)(2,1)S(1)} collective-permute-done((bf16[432,128]{1,0:T(8,128)(2,1)S(1)}, bf16[432,128]{1,0:T(8,128)(2,1)S(1)}, u32[]{:S(2)}, u32[]{:S(2)}) %collective-permute-start.3) | collective-permute-done | bytes 110624 | tf_op jit(solution)/shard_map/ppermute | solution.py:294
  23.1 1.1 %shard_map.89 = (bf16[12,48,128]{2,1,0:T(8,128)(2,1)S(1)}, bf16[12,48,128]{2,1,0:T(8,128)(2,1)S(1)}, bf16[12,24,128]{2,1,0:T(8,128)(2,1)S(1)}, bf16[12,24,128]{2,1,0:T(8,128)(2,1)S(1)}) custom-call(bf16[432,128]{1,0:T(8,128)(2,1)S(1)} %get-tuple-element.35.refs_0_, bf16[432,128]{1,0:T(8,128)(2,1)S(1)} %collective-permute-done.3.refs_1_, ...), custom_call_target="tpu_custom_call" | custom-call | flops 300000000 | bytes 1491328 | tf_op jit(solution)/shard_map/pallas_call | solution.py:25
  24.7 1.1 %shard_map.90 = (bf16[12,48,128]{2,1,0:T(8,128)(2,1)S(1)}, bf16[12,48,128]{2,1,0:T(8,128)(2,1)S(1)}, bf16[12,24,128]{2,1,0:T(8,128)(2,1)S(1)}, bf16[18,48,128]{2,1,0:T(8,128)(2,1)S(1)}) custom-call(bf16[432,128]{1,0:T(8,128)(2,1)S(1)} %get-tuple-element.35.refs_0_, bf16[432,128]{1,0:T(8,128)(2,1)S(1)} %collective-permute-done.3.refs_1_, ...), custom_call_target="tpu_custom_call" | custom-call | flops 300000000 | bytes 2081152 | tf_op jit(solution)/shard_map/pallas_call | solution.py:25
  26.4 1.0 %collective-permute-done.11.refs_1_ = bf16[18,48,128]{2,1,0:T(8,128)(2,1)S(1)} collective-permute-done((bf16[18,48,128]{2,1,0:T(8,128)(2,1)S(1)}, bf16[18,48,128]{2,1,0:T(8,128)(2,1)S(1)}, u32[]{:S(2)}, u32[]{:S(2)}) %collective-permute-start.11) | collective-permute-done | bytes 221216 | tf_op jit(solution)/shard_map/ppermute | solution.py:286
  27.7 1.5 %collective-permute-start.16 = (bf16[6,48,128]{2,1,0:T(8,128)(2,1)S(1)}, bf16[6,48,128]{2,1,0:T(8,128)(2,1)S(1)}, u32[]{:S(2)}, u32[]{:S(2)}) collective-permute-start(bf16[6,48,128]{2,1,0:T(8,128)(2,1)S(1)} %shard_map.94), channel_id=1, source_target_pairs={{0,4},{2,6},{4,0},{6,2},{8,12},{10,14},{12,8},{14,10},{1,5},{3,7},... | collective-permute-start | bytes 221192 | tf_op jit(solution)/shard_map/ppermute | solution.py:286
  29.1 0.7 %shard_map.93 = (bf16[6,48,128]{2,1,0:T(8,128)(2,1)S(1)}, bf16[6,48,128]{2,1,0:T(8,128)(2,1)S(1)}, bf16[6,48,128]{2,1,0:T(8,128)(2,1)S(1)}) custom-call(bf16[12,48,128]{2,1,0:T(8,128)(2,1)S(1)} %get-tuple-element.50.refs_0_, bf16[18,48,128]{2,1,0:T(8,128)(2,1)S(1)} %collective-permute-done.11.refs_1_, bf16[12,24,128]{2,1,0:T(8,128)(2,1)S(1)} %get-tuple-element.54.refs_2_), custom_call_target="tpu_custom_call" | custom-call | flops 360000000 | bytes 663552 | tf_op jit(solution)/shard_map/pallas_call | solution.py:25
  29.9 2.0 %collective-permute-start.14 = (bf16[6,48,128]{2,1,0:T(8,128)(2,1)S(1)}, bf16[6,48,128]{2,1,0:T(8,128)(2,1)S(1)}, u32[]{:S(2)}, u32[]{:S(2)}) collective-permute-start(bf16[6,48,128]{2,1,0:T(8,128)(2,1)S(1)} %get-tuple-element.55), channel_id=1, source_target_pairs={{0,8},{2,10},{4,12},{6,14},{8,0},{10,2},{12,4},{14,6},{1,9},{3,11}... | collective-permute-start | bytes 221192 | tf_op jit(solution)/shard_map/ppermute | solution.py:286
  31.9 1.5 %collective-permute-start.15 = (bf16[6,48,128]{2,1,0:T(8,128)(2,1)S(1)}, bf16[6,48,128]{2,1,0:T(8,128)(2,1)S(1)}, u32[]{:S(2)}, u32[]{:S(2)}) collective-permute-start(bf16[6,48,128]{2,1,0:T(8,128)(2,1)S(1)} %get-tuple-element.56), channel_id=1, source_target_pairs={{0,12},{2,14},{4,8},{6,10},{8,4},{10,6},{12,0},{14,2},{1,13},{3,15... | collective-permute-start | bytes 221192 | tf_op jit(solution)/shard_map/ppermute | solution.py:286
  34.6 2.4 %collective-permute-start.17 = (bf16[6,48,128]{2,1,0:T(8,128)(2,1)S(1)}, bf16[6,48,128]{2,1,0:T(8,128)(2,1)S(1)}, u32[]{:S(2)}, u32[]{:S(2)}) collective-permute-start(bf16[6,48,128]{2,1,0:T(8,128)(2,1)S(1)} %add_convert_fusion), channel_id=1, source_target_pairs={{0,8},{2,10},{4,12},{6,14},{8,0},{10,2},{12,4},{14,6},{1,9},{3,11}... | collective-permute-start | bytes 221192 | tf_op jit(solution)/shard_map/ppermute | solution.py:286
  37.9 0.9 %collective-permute-done.15.refs_3_ = bf16[6,48,128]{2,1,0:T(8,128)(2,1)S(1)} collective-permute-done((bf16[6,48,128]{2,1,0:T(8,128)(2,1)S(1)}, bf16[6,48,128]{2,1,0:T(8,128)(2,1)S(1)}, u32[]{:S(2)}, u32[]{:S(2)}) %collective-permute-start.15) | collective-permute-done | bytes 73760 | tf_op jit(solution)/shard_map/ppermute | solution.py:286
  38.9 4.1 %collective-permute-done.17.refs_4_ = bf16[6,48,128]{2,1,0:T(8,128)(2,1)S(1)} collective-permute-done((bf16[6,48,128]{2,1,0:T(8,128)(2,1)S(1)}, bf16[6,48,128]{2,1,0:T(8,128)(2,1)S(1)}, u32[]{:S(2)}, u32[]{:S(2)}) %collective-permute-start.17) | collective-permute-done | bytes 73760 | tf_op jit(solution)/shard_map/ppermute | solution.py:286
  42.9 1.0 %shard_map.96 = bf16[12,48,128]{2,1,0:T(8,128)(2,1)} custom-call(f32[12,48,128]{2,1,0:T(8,128)S(1)} %shard_map.91.refs_0_, bf16[12,48,128]{2,1,0:T(8,128)(2,1)S(1)} %collective-permute-done.13.refs_1_, bf16[6,48,128]{2,1,0:T(8,128)(2,1)S(1)} %collective-permute-done.14.refs_2_, bf16[6,48,128]{2,1,0:T(8,128)(2,1)S(1)} %collective-permute-done.15.refs_3_, ...), custom_call_target="tpu_custom_call" | custom-call | flops 100000000 | bytes 1286144 | tf_op jit(solution)/shard_map/pallas_call | solution.py:25
  (44 shorter events, 6.5 us)
Async XLA Ops:
  0.0 7.2 %copy-start = (bf16[12,48,128]{2,1,0:T(8,128)(2,1)S(1)}, bf16[12,48,128]{2,1,0:T(8,128)(2,1)}, u32[]{:S(2)}) copy-start(bf16[12,48,128]{2,1,0:T(8,128)(2,1)} %refs_1_.1) | copy-start | bytes 442372
  0.0 7.2 %copy-start.1 = (bf16[128,512]{1,0:T(8,128)(2,1)S(1)}, bf16[128,512]{1,0:T(8,128)(2,1)}, u32[]{:S(2)}) copy-start(bf16[128,512]{1,0:T(8,128)(2,1)} %refs_3_.1) | copy-start | bytes 393220
  0.0 7.2 %copy-start.6 = (s32[96]{0:T(128)S(1)}, s32[96]{0:T(128)}, u32[]{:S(2)}) copy-start(s32[96]{0:T(128)} %param.9) | copy-start | bytes 1156
  1.5 11.2 %collective-permute-start.2 = (bf16[12,48,128]{2,1,0:T(8,128)(2,1)S(1)}, bf16[12,48,128]{2,1,0:T(8,128)(2,1)S(1)}, u32[]{:S(2)}, u32[]{:S(2)}) collective-permute-start(bf16[12,48,128]{2,1,0:T(8,128)(2,1)S(1)} %shard_map.82.refs_0_.refs_2_), channel_id=1, source_target_pairs={{0,8},{2,10},{4,12},{6,14},{8,0},{10,2},{12,4},{14,6},{1,9},{3,11}... | collective-permute-start | bytes 442376 | tf_op jit(solution)/shard_map/ppermute | solution.py:286
  5.6 7.7 %collective-permute-start.1 = (bf16[12,48,128]{2,1,0:T(8,128)(2,1)S(1)}, bf16[12,48,128]{2,1,0:T(8,128)(2,1)S(1)}, u32[]{:S(2)}, u32[]{:S(2)}) collective-permute-start(bf16[12,48,128]{2,1,0:T(8,128)(2,1)S(1)} %shard_map.82.refs_0_.refs_2_), channel_id=1, source_target_pairs={{0,4},{2,6},{4,0},{6,2},{8,12},{10,14},{12,8},{14,10},{1,5},{3,7},... | collective-permute-start | bytes 442376 | tf_op jit(solution)/shard_map/ppermute | solution.py:286
  7.6 5.7 %collective-permute-start = (bf16[12,48,128]{2,1,0:T(8,128)(2,1)S(1)}, bf16[12,48,128]{2,1,0:T(8,128)(2,1)S(1)}, u32[]{:S(2)}, u32[]{:S(2)}) collective-permute-start(bf16[12,48,128]{2,1,0:T(8,128)(2,1)S(1)} %get-tuple-element.32.refs_0_.refs_2_), channel_id=1, source_target_pairs={{0,2},{2,0},{4,6},{6,4},{8,10},{10,8},{12,14},{14,12},{1,3},{3,1},... | collective-permute-start | bytes 442376 | tf_op jit(solution)/shard_map/ppermute | solution.py:286
  7.7 11.7 %collective-permute-start.8 = (bf16[12,48,128]{2,1,0:T(8,128)(2,1)S(1)}, bf16[12,48,128]{2,1,0:T(8,128)(2,1)S(1)}, u32[]{:S(2)}, u32[]{:S(2)}) collective-permute-start(bf16[12,48,128]{2,1,0:T(8,128)(2,1)S(1)} %get-tuple-element.40.refs_0_), channel_id=1, source_target_pairs={{0,1},{1,0},{2,3},{3,2},{4,5},{5,4},{6,7},{7,6},{8,9},{9,8},{10,11... | collective-permute-start | bytes 442376 | tf_op jit(solution)/shard_map/ppermute | solution.py:294
  12.7 5.1 %collective-permute-start.6 = (bf16[12,48,128]{2,1,0:T(8,128)(2,1)S(1)}, bf16[12,48,128]{2,1,0:T(8,128)(2,1)S(1)}, u32[]{:S(2)}, u32[]{:S(2)}) collective-permute-start(bf16[12,48,128]{2,1,0:T(8,128)(2,1)S(1)} %collective-permute-done.2.refs_4_), channel_id=1, source_target_pairs={{0,4},{2,6},{4,0},{6,2},{8,12},{10,14},{12,8},{14,10},{1,5},{3,7},... | collective-permute-start | bytes 442376 | tf_op jit(solution)/shard_map/ppermute | solution.py:286
  15.3 6.1 %collective-permute-start.5 = (bf16[432,128]{1,0:T(8,128)(2,1)S(1)}, bf16[432,128]{1,0:T(8,128)(2,1)S(1)}, u32[]{:S(2)}, u32[]{:S(2)}) collective-permute-start(bf16[432,128]{1,0:T(8,128)(2,1)S(1)} %get-tuple-element.36), channel_id=1, source_target_pairs={{0,3},{1,2},{2,1},{3,0},{4,7},{5,6},{6,5},{7,4},{8,11},{9,10},{10,... | collective-permute-start | bytes 331784 | tf_op jit(solution)/shard_map/ppermute | solution.py:294
  16.2 5.5 %collective-permute-start.4 = (bf16[432,128]{1,0:T(8,128)(2,1)S(1)}, bf16[432,128]{1,0:T(8,128)(2,1)S(1)}, u32[]{:S(2)}, u32[]{:S(2)}) collective-permute-start(bf16[432,128]{1,0:T(8,128)(2,1)S(1)} %get-tuple-element.36), channel_id=1, source_target_pairs={{0,2},{1,3},{2,0},{3,1},{4,6},{5,7},{6,4},{7,5},{8,10},{9,11},{10,... | collective-permute-start | bytes 331784 | tf_op jit(solution)/shard_map/ppermute | solution.py:294
  17.0 6.2 %collective-permute-start.3 = (bf16[432,128]{1,0:T(8,128)(2,1)S(1)}, bf16[432,128]{1,0:T(8,128)(2,1)S(1)}, u32[]{:S(2)}, u32[]{:S(2)}) collective-permute-start(bf16[432,128]{1,0:T(8,128)(2,1)S(1)} %get-tuple-element.35.refs_0_), channel_id=1, source_target_pairs={{0,1},{1,0},{2,3},{3,2},{4,5},{5,4},{6,7},{7,6},{8,9},{9,8},{10,11... | collective-permute-start | bytes 331784 | tf_op jit(solution)/shard_map/ppermute | solution.py:294
  18.8 4.3 %copy-start.2 = (bf16[128,512]{1,0:T(8,128)(2,1)S(1)}, bf16[128,512]{1,0:T(8,128)(2,1)}, u32[]{:S(2)}) copy-start(bf16[128,512]{1,0:T(8,128)(2,1)} %refs_12_.1) | copy-start | bytes 393220
  18.8 4.3 %copy-start.3 = (bf16[128,128]{1,0:T(8,128)(2,1)S(1)}, bf16[128,128]{1,0:T(8,128)(2,1)}, u32[]{:S(2)}) copy-start(bf16[128,128]{1,0:T(8,128)(2,1)} %refs_11_.1) | copy-start | bytes 98308
  18.9 5.4 %collective-permute-start.10 = (bf16[144,128]{1,0:T(8,128)(2,1)S(1)}, bf16[144,128]{1,0:T(8,128)(2,1)S(1)}, u32[]{:S(2)}, u32[]{:S(2)}) collective-permute-start(bf16[144,128]{1,0:T(8,128)(2,1)S(1)} %shard_map.87), channel_id=1, source_target_pairs={{0,3},{1,2},{2,1},{3,0},{4,7},{5,6},{6,5},{7,4},{8,11},{9,10},{10,... | collective-permute-start | bytes 110600 | tf_op jit(solution)/shard_map/ppermute | solution.py:294
  19.4 5.3 %collective-permute-start.7 = (bf16[144,128]{1,0:T(8,128)(2,1)S(1)}, bf16[144,128]{1,0:T(8,128)(2,1)S(1)}, u32[]{:S(2)}, u32[]{:S(2)}) collective-permute-start(bf16[144,128]{1,0:T(8,128)(2,1)S(1)} %shard_map.86.refs_4_), channel_id=1, source_target_pairs={{0,1},{1,0},{2,3},{3,2},{4,5},{5,4},{6,7},{7,6},{8,9},{9,8},{10,11... | collective-permute-start | bytes 110600 | tf_op jit(solution)/shard_map/ppermute | solution.py:294
  21.4 3.3 %collective-permute-start.9 = (bf16[144,128]{1,0:T(8,128)(2,1)S(1)}, bf16[144,128]{1,0:T(8,128)(2,1)S(1)}, u32[]{:S(2)}, u32[]{:S(2)}) collective-permute-start(bf16[144,128]{1,0:T(8,128)(2,1)S(1)} %shard_map.87), channel_id=1, source_target_pairs={{0,2},{1,3},{2,0},{3,1},{4,6},{5,7},{6,4},{7,5},{8,10},{9,11},{10,... | collective-permute-start | bytes 110600 | tf_op jit(solution)/shard_map/ppermute | solution.py:294
  25.8 1.5 %collective-permute-start.11 = (bf16[18,48,128]{2,1,0:T(8,128)(2,1)S(1)}, bf16[18,48,128]{2,1,0:T(8,128)(2,1)S(1)}, u32[]{:S(2)}, u32[]{:S(2)}) collective-permute-start(bf16[18,48,128]{2,1,0:T(8,128)(2,1)S(1)} %get-tuple-element.51), channel_id=1, source_target_pairs={{0,2},{2,0},{4,6},{6,4},{8,10},{10,8},{12,14},{14,12},{1,3},{3,1},... | collective-permute-start | bytes 663560 | tf_op jit(solution)/shard_map/ppermute | solution.py:286
  26.0 7.5 %collective-permute-start.12 = (bf16[12,24,128]{2,1,0:T(8,128)(2,1)S(1)}, bf16[12,24,128]{2,1,0:T(8,128)(2,1)S(1)}, u32[]{:S(2)}, u32[]{:S(2)}) collective-permute-start(bf16[12,24,128]{2,1,0:T(8,128)(2,1)S(1)} %get-tuple-element.53), channel_id=1, source_target_pairs={{0,2},{2,0},{4,6},{6,4},{8,10},{10,8},{12,14},{14,12},{1,3},{3,1},... | collective-permute-start | bytes 221192 | tf_op jit(solution)/shard_map/ppermute | solution.py:286
  27.7 6.9 %collective-permute-start.16 = (bf16[6,48,128]{2,1,0:T(8,128)(2,1)S(1)}, bf16[6,48,128]{2,1,0:T(8,128)(2,1)S(1)}, u32[]{:S(2)}, u32[]{:S(2)}) collective-permute-start(bf16[6,48,128]{2,1,0:T(8,128)(2,1)S(1)} %shard_map.94), channel_id=1, source_target_pairs={{0,4},{2,6},{4,0},{6,2},{8,12},{10,14},{12,8},{14,10},{1,5},{3,7},... | collective-permute-start | bytes 221192 | tf_op jit(solution)/shard_map/ppermute | solution.py:286
  29.9 8.1 %collective-permute-start.14 = (bf16[6,48,128]{2,1,0:T(8,128)(2,1)S(1)}, bf16[6,48,128]{2,1,0:T(8,128)(2,1)S(1)}, u32[]{:S(2)}, u32[]{:S(2)}) collective-permute-start(bf16[6,48,128]{2,1,0:T(8,128)(2,1)S(1)} %get-tuple-element.55), channel_id=1, source_target_pairs={{0,8},{2,10},{4,12},{6,14},{8,0},{10,2},{12,4},{14,6},{1,9},{3,11}... | collective-permute-start | bytes 221192 | tf_op jit(solution)/shard_map/ppermute | solution.py:286
  31.9 6.9 %collective-permute-start.15 = (bf16[6,48,128]{2,1,0:T(8,128)(2,1)S(1)}, bf16[6,48,128]{2,1,0:T(8,128)(2,1)S(1)}, u32[]{:S(2)}, u32[]{:S(2)}) collective-permute-start(bf16[6,48,128]{2,1,0:T(8,128)(2,1)S(1)} %get-tuple-element.56), channel_id=1, source_target_pairs={{0,12},{2,14},{4,8},{6,10},{8,4},{10,6},{12,0},{14,2},{1,13},{3,15... | collective-permute-start | bytes 221192 | tf_op jit(solution)/shard_map/ppermute | solution.py:286
  34.0 9.0 %collective-permute-start.13 = (bf16[12,48,128]{2,1,0:T(8,128)(2,1)S(1)}, bf16[12,48,128]{2,1,0:T(8,128)(2,1)S(1)}, u32[]{:S(2)}, u32[]{:S(2)}) collective-permute-start(bf16[12,48,128]{2,1,0:T(8,128)(2,1)S(1)} %shard_map.92), channel_id=1, source_target_pairs={{0,4},{2,6},{4,0},{6,2},{8,12},{10,14},{12,8},{14,10},{1,5},{3,7},... | collective-permute-start | bytes 442376 | tf_op jit(solution)/shard_map/ppermute | solution.py:286
  34.6 8.4 %collective-permute-start.17 = (bf16[6,48,128]{2,1,0:T(8,128)(2,1)S(1)}, bf16[6,48,128]{2,1,0:T(8,128)(2,1)S(1)}, u32[]{:S(2)}, u32[]{:S(2)}) collective-permute-start(bf16[6,48,128]{2,1,0:T(8,128)(2,1)S(1)} %add_convert_fusion), channel_id=1, source_target_pairs={{0,8},{2,10},{4,12},{6,14},{8,0},{10,2},{12,4},{14,6},{1,9},{3,11}... | collective-permute-start | bytes 221192 | tf_op jit(solution)/shard_map/ppermute | solution.py:286
  37.4 5.6 %copy-start.4 = (bf16[128,128]{1,0:T(8,128)(2,1)S(1)}, bf16[128,128]{1,0:T(8,128)(2,1)}, u32[]{:S(2)}) copy-start(bf16[128,128]{1,0:T(8,128)(2,1)} %refs_7_.3) | copy-start | bytes 98308
  (2 other events, 4.7 us)
